TPU v7x, 128 devices: a whole 4x4x4 slice. The times are simulated.
128 devices in a mesh: space: 32 (over z_lo, x, y), chan: 4 (over z_hi, core).
Axes of the slice: x: 4, y: 4, z: 4 (z_hi: 2, z_lo: 2; z = z_hi * 2 + z_lo), core: 2. Of those that a mesh axis runs over, the one named last changes fastest.
Arguments:
- volume: bfloat16 [4, 512, 32, 512], P(None, 'space', 'chan'), may hold values from -6 to 6
- kernel_one: bfloat16 [3, 3, 3, 4, 32], replicated, may hold values from -0.625 to 0.625
- kernel_two: bfloat16 [3, 3, 3, 32, 64], replicated, may hold values from -0.21875 to 0.21875
- kernel_three: bfloat16 [3, 3, 3, 64, 128], P(None, None, None, 'chan'), may hold values from -0.15625 to 0.15625
- kernel_four: bfloat16 [3, 3, 3, 128, 256], P(None, None, None, 'chan'), may hold values from -0.109375 to 0.109375
- cotangent: bfloat16 [256, 128, 8, 128], P('chan', 'space'), may hold values from -0.15625 to 0.15625
Outputs:
- features: bfloat16 [256, 128, 8, 128], P('chan', 'space')
- grad_one: float32 [3, 3, 3, 4, 32], replicated
- grad_two: float32 [3, 3, 3, 32, 64], replicated
- grad_three: float32 [3, 3, 3, 64, 128], P(None, None, None, 'chan')
- grad_four: float32 [3, 3, 3, 128, 256], P(None, None, None, 'chan')
All inputs are finite; a program needn't handle non-finite values.
Results may differ from a plain program's by a relative error of at most 0.014.
Values may be sent and summed in bfloat16 or wider, within the bound.
No kernel may reach another device: no remote copies, remote signals or barrier semaphores. Data moves between devices by JAX's collectives and lax.ppermute only.
A program may use at most 192 MiB of HBM per device.

v0:
```python
import jax
import jax.numpy as jnp
from jax import lax
from jax.sharding import PartitionSpec as P

NUMBERS = ("NCDHW", "DHWIO", "NCDHW")
WEIGHT_NUMBERS = ("NCDHW", "OIDHW", "NCDHW")
STRIDED = ((0, 0), (0, 0), (0, 1))
SAME_HW = ((0, 0), (1, 1), (1, 1))
SPREAD_PADS = ((2, 2), (2, 2), (2, 1))


def passed_along(block, axis, distance):
    devices = range(lax.axis_size(axis))
    route = [(i - distance, i) for i in devices if i - distance in devices]
    return lax.ppermute(block, axis, route)


def with_halo(block, sides, width):
    for axis, dim in sides:
        count = lax.axis_size(axis)
        forward = [(i, i + 1) for i in range(count - 1)]
        backward = [(target, source) for source, target in forward]
        low = lax.ppermute(
            lax.slice_in_dim(block, block.shape[dim] - width, None, axis=dim), axis, forward
        )
        high = lax.ppermute(lax.slice_in_dim(block, 0, width, axis=dim), axis, backward)
        block = jnp.concatenate([low, block, high], axis=dim)
    return block


def convolve(field, kernel, stride, pads):
    result = lax.conv_general_dilated(
        field[None],
        kernel,
        (stride, stride, stride),
        pads,
        dimension_numbers=NUMBERS,
        preferred_element_type=jnp.float32,
    )
    return result[0]


def silu_slope(value):
    sigma = jax.nn.sigmoid(value)
    return sigma * (1.0 + value * (1.0 - sigma))


def extend(field):
    below = passed_along(field[:, :1], "space", -1)
    field = jnp.concatenate([field, below], 1)
    beside = passed_along(field[:, :, :1], "chan", -1)
    return jnp.concatenate([field, beside], 2)


def fold_back(gradient):
    beside = passed_along(gradient[:, :, -1:], "chan", 1)
    gradient = gradient[:, :, :-1]
    gradient = gradient.at[:, :, :1].add(beside)
    below = passed_along(gradient[:, -1:], "space", 1)
    gradient = gradient[:, :-1]
    return gradient.at[:, :1].add(below)


def depth_halo(field):
    return with_halo(field, (("space", 1),), 1)


def gather_filters(gradient):
    return lax.all_gather(gradient, "chan", axis=0, tiled=True)


def weight_grad(padded, gradient, stride, pads):
    result = lax.conv_general_dilated(
        padded[:, None],
        gradient[:, None],
        (1, 1, 1),
        pads,
        rhs_dilation=(stride, stride, stride),
        dimension_numbers=WEIGHT_NUMBERS,
        preferred_element_type=jnp.float32,
    )
    return jnp.transpose(result, (2, 3, 4, 0, 1))


def transposed(gradient_halo, kernel):
    flipped = jnp.swapaxes(kernel[::-1, ::-1, ::-1], 3, 4)
    return convolve(gradient_halo, flipped, 1, SAME_HW)


def spread_back(gradient, kernel):
    flipped = jnp.swapaxes(kernel[::-1, ::-1, ::-1], 3, 4)
    result = lax.conv_general_dilated(
        gradient[None],
        flipped,
        (1, 1, 1),
        SPREAD_PADS,
        lhs_dilation=(2, 2, 2),
        dimension_numbers=NUMBERS,
        preferred_element_type=jnp.float32,
    )
    return result[0]


def per_device(volume, kernel_one, kernel_two, kernel_three, kernel_four, cotangent):
    padded_one = extend(volume)
    pre_one = convolve(padded_one, kernel_one, 2, STRIDED)
    act_one = jax.nn.silu(pre_one).astype(jnp.bfloat16)
    padded_two = extend(act_one)
    pre_two = convolve(padded_two, kernel_two, 2, STRIDED)
    act_two = jax.nn.silu(pre_two).astype(jnp.bfloat16)
    padded_three = depth_halo(
        lax.all_to_all(act_two, "chan", split_axis=0, concat_axis=2, tiled=True)
    )
    pre_three = lax.psum_scatter(
        convolve(padded_three, kernel_three, 1, SAME_HW), "chan", scatter_dimension=0, tiled=True
    )
    act_three = jax.nn.silu(pre_three).astype(jnp.bfloat16)
    padded_four = depth_halo(act_three)
    pre_four = lax.psum_scatter(
        convolve(padded_four, kernel_four, 1, SAME_HW), "chan", scatter_dimension=0, tiled=True
    )
    features = jax.nn.silu(pre_four).astype(jnp.bfloat16)
    back_four = (cotangent.astype(jnp.float32) * silu_slope(pre_four)).astype(jnp.bfloat16)
    all_four = gather_filters(back_four)
    grad_four = weight_grad(padded_four, all_four, 1, SAME_HW)
    into_three = transposed(depth_halo(all_four), kernel_four)
    back_three = (into_three * silu_slope(pre_three)).astype(jnp.bfloat16)
    all_three = gather_filters(back_three)
    grad_three = weight_grad(padded_three, all_three, 1, SAME_HW)
    into_blocks = transposed(depth_halo(all_three), kernel_three)
    into_two = lax.all_to_all(into_blocks, "chan", split_axis=2, concat_axis=0, tiled=True)
    back_two = (into_two * silu_slope(pre_two)).astype(jnp.bfloat16)
    grad_two = weight_grad(padded_two, back_two, 2, STRIDED)
    into_padded = spread_back(back_two, kernel_two)
    into_one = fold_back(into_padded)
    back_one = (into_one * silu_slope(pre_one)).astype(jnp.bfloat16)
    grad_one = weight_grad(padded_one, back_one, 2, STRIDED)
    grad_one, grad_two = lax.psum((grad_one, grad_two), ("space", "chan"))
    grad_three, grad_four = lax.psum((grad_three, grad_four), "space")
    return (features, grad_one, grad_two, grad_three, grad_four)


def solution(mesh):
    in_specs = (
        P(None, "space", "chan", None),
        P(),
        P(),
        P(None, None, None, "chan", None),
        P(None, None, None, "chan", None),
        P("chan", "space", None, None),
    )
    out_specs = (
        P("chan", "space", None, None),
        P(),
        P(),
        P(None, None, None, "chan", None),
        P(None, None, None, "chan", None),
    )
    return jax.shard_map(
        per_device, mesh=mesh, in_specs=in_specs, out_specs=out_specs, check_vma=False
    )
```

profile of v0, /device:TPU:0, one launch (start us, length us, event | category | flops | bytes accessed | tf_op | source)
XLA Modules:
  0.0 1014.9 jit_solution(16684021504414875110)
XLA Ops:
  20.2 10.7 %copy.235 = bf16[4,17,9,1,8,66]{4,0,5,2,1,3:T(4,128)(2,1)} copy(bf16[4,17,9,1,8,66]{5,4,1,2,0,3:T(8,128)(2,1)S(1)} %reshape.218) | data formatting | bytes 1292544 | tf_op jit(solution)/shard_map/conv_general_dilated | solution.py:33
  32.1 32.7 %broadcast_select_fusion.2 = f32[8,4,8,33,32]{4,2,3,1,0:T(8,128)} fusion(pred[8,33]{0,1:T(8,128)(4,1)S(1)} %copy-done.19, bf16[3,3,3,4,32]{4,3,2,1,0:T(4,128)(2,1)S(1)} %copy-done.18, bf16[4,17,9,1,7,2]{4,0,5,2,1,3:T(4,128)(2,1)S(1)} %slice.143, bf16[4,17,9,1,8,66]{4,0,5,2,1,3:T(4,128)(2,1)} %copy.235), kind=kOutput, calls=%fused_computation.29 | convolution fusion | flops 60660480 | bytes 1751928 | tf_op jit(solution)/shard_map/conv_general_dilated | solution.py:33
  64.9 5.7 copy.236
  75.7 4.9 collective-permute-done.2
  82.0 5.2 collective-permute-done.3
  93.3 4.6 copy.238
  98.9 4.6 add_multiply_fusion
  104.2 12.4 %all_to_all.39 = bf16[64,4,2,128]{3,1,2,0:T(4,128)(2,1)S(1)} all-to-all(bf16[64,4,2,128]{3,1,2,0:T(4,128)(2,1)S(1)} %copy.241), channel_id=1, replica_groups=mesh['space'=32,'chan'=4] {'chan'}, dimensions={0} | all-to-all | bytes 262144 | tf_op jit(solution)/shard_map/all_to_all | solution.py:113
  121.8 5.5 collective-permute-done.5
  141.0 47.2 %reduce-scatter.3.cloned.1.call-done = f32[32,4,8,128]{3,2,1,0:T(8,128)} async-done(((f32[128,4,8,128]{3,2,1,0:T(8,128)}), f32[32,4,8,128]{3,2,1,0:T(8,128)}) %reduce-scatter.3.cloned.1.call-update) | async-done | bytes 524304 | tf_op jit(solution)/shard_map/reduce_scatter | solution.py:115
  209.3 5.6 copy.253
  215.0 54.4 %reduce-scatter.5.cloned.1.call-done = f32[64,4,8,128]{3,2,1,0:T(8,128)} async-done(((f32[256,4,8,128]{3,2,1,0:T(8,128)}), f32[64,4,8,128]{3,2,1,0:T(8,128)}) %reduce-scatter.5.cloned.1.call-update) | async-done | bytes 1048592 | tf_op jit(solution)/shard_map/reduce_scatter | solution.py:120
  272.2 26.1 %all-gather.3.cloned.1.call-done = bf16[256,4,8,128]{3,2,1,0:T(8,128)(2,1)} async-done(((bf16[64,4,8,128]{3,2,1,0:T(8,128)(2,1)}), bf16[256,4,8,128]{3,2,1,0:T(8,128)(2,1)}) %all-gather.3.cloned.1.call-update) | async-done | bytes 2097168 | tf_op jit(solution)/shard_map/all_gather | solution.py:70
  307.3 9.8 collective-permute-done.8
  322.7 17.0 %fusion.50 = f32[4,8,8,17,32]{4,2,3,1,0:T(8,128)S(1)} fusion(bf16[3,3,3,32,256]{4,3,2,1,0:T(8,128)(2,1)S(1)} %copy-done, bf16[256,6,8,1,7,2]{0,4,5,2,1,3:T(8,128)(2,1)S(1)} %slice.158, bf16[256,6,8,1,8,17]{0,4,5,2,1,3:T(8,128)(2,1)S(1)} %copy.259, pred[8,17]{0,1:T(8,128)(4,1)S(1)} %copy-done.20), kind=kOutput, calls=%fused_computation.53 | convolution fusion | flops 1776099328 | bytes 4685960 | tf_op jit(solution)/shard_map/conv_general_dilated | solution.py:33
  344.0 23.8 %all-gather.5.cloned.1.call-done = bf16[128,4,8,128]{3,2,1,0:T(8,128)(2,1)} async-done(((bf16[32,4,8,128]{3,2,1,0:T(8,128)(2,1)}), bf16[128,4,8,128]{3,2,1,0:T(8,128)(2,1)}) %all-gather.5.cloned.1.call-update) | async-done | bytes 1048592 | tf_op jit(solution)/shard_map/all_gather | solution.py:70
  376.6 57.0 %copy.277 = bf16[4,1,17,9,512]{0,1,4,3,2:T(2,128)(2,1)} copy(bf16[4,1,17,9,512]{4,2,3,0,1:T(8,128)(2,1)S(1)} %copy-done.7) | data formatting | bytes 1253376 | tf_op jit(solution)/shard_map/broadcast_in_dim | solution.py:75
  435.9 8.9 copy.280
  444.7 5.5 copy.283
  453.8 5.0 copy.286
  460.8 9.6 fusion.47
  479.2 30.1 %fusion.121 = f32[3,3,3,32,256]{4,3,2,1,0:T(8,128)} fusion(bf16[32,1,6,8,128]{0,1,4,3,2:T(2,128)(2,1)} %copy.285, bf16[256,1,4,8,128]{0,1,4,3,2:T(2,128)(2,1)} %copy.286), kind=kOutput, calls=%fused_computation.145 | convolution fusion | flops 1652293632 | bytes 3375104 | tf_op jit(solution)/shard_map/transpose | solution.py:83
  514.0 7.4 broadcast_select_fusion
  521.5 8.5 copy.276
  529.9 5.3 reshape.180
  539.1 14.5 %fusion.119 = f32[3,3,3,32,64]{4,3,2,1,0:T(8,128)} fusion(bf16[32,1,9,5,256]{0,1,4,3,2:T(2,128)(2,1)} %copy.280, bf16[64,1,4,2,128]{0,1,4,3,2:T(2,128)(2,1)S(1)} %copy.281), kind=kOutput, calls=%fused_computation.143 | convolution fusion | flops 112951296 | bytes 1089536 | tf_op jit(solution)/shard_map/transpose | solution.py:83
  553.9 4.8 collective-permute-start.13
  558.6 29.5 %fusion.120 = f32[3,3,3,16,128]{4,3,2,1,0:T(8,128)} fusion(bf16[16,1,6,8,128]{0,1,4,3,2:T(2,128)(2,1)} %copy.283, bf16[128,1,4,8,128]{0,1,4,3,2:T(2,128)(2,1)} %copy.284), kind=kOutput, calls=%fused_computation.144 | convolution fusion | flops 413073408 | bytes 1466368 | tf_op jit(solution)/shard_map/transpose | solution.py:83
  589.9 7.3 copy.278
  597.2 87.7 %fusion.118 = f32[3,3,3,4,32]{4,3,2,1,0:T(4,128)S(1)} fusion(bf16[4,1,17,9,512]{0,1,4,3,2:T(2,128)(2,1)} %copy.277, bf16[32,1,8,4,256]{0,1,4,3,2:T(2,128)(2,1)} %copy.278), kind=kOutput, calls=%fused_computation.142 | convolution fusion | flops 56549376 | bytes 1164800 | tf_op jit(solution)/shard_map/transpose | solution.py:83
  684.9 71.0 %psum.28 = f32[3,3,3,4,32]{4,3,2,1,0:T(4,128)} all-reduce(f32[3,3,3,4,32]{4,3,2,1,0:T(4,128)S(1)} %fusion.118), channel_id=1, replica_groups=mesh['space'=32,'chan'=4] {'space','chan'}, use_global_device_ids=true, to_apply=%region_2.3 | all-reduce | flops 3456 | bytes 27648 | tf_op jit(solution)/shard_map/psum | solution.py:139
  755.9 246.4 %all-reduce.6.cloned.1.call-done = (f32[3,3,3,16,128]{4,3,2,1,0:T(8,128)}, f32[3,3,3,32,256]{4,3,2,1,0:T(8,128)}) async-done(((f32[3,3,3,16,128]{4,3,2,1,0:T(8,128)}, f32[3,3,3,32,256]{4,3,2,1,0:T(8,128)}), (f32[3,3,3,16,128]{4,3,2,1,0:T(8,128)}, f32[3,3,3,32,256]{4,3,2,1,0:T(8,128)})) %all-reduce.6.cloned.1.call-update) | async-done | bytes 1105936 | tf_op jit(solution)/shard_map/psum | solution.py:140
  (169 shorter events, 131.4 us)
Async XLA Ops:
  7.2 194.2 %copy-start = (bf16[3,3,3,32,256]{4,3,2,1,0:T(8,128)(2,1)S(1)}, bf16[3,3,3,32,256]{4,3,2,1,0:T(8,128)(2,1)}, u32[]{:S(2)}) copy-start(bf16[3,3,3,32,256]{4,3,2,1,0:T(8,128)(2,1)} %param.14) | copy-start | bytes 1327108
  7.2 181.0 %reduce-scatter.3.cloned.1.call-start = ((), (), s32[]{:S(2)}) async-start(), calls=%async_computation.4 | async-start | bytes 2621440 | tf_op jit(solution)/shard_map/reduce_scatter | solution.py:115
  8.1 6.2 collective-permute-start
  14.4 3.2 collective-permute-start.1
  20.2 12.0 %copy-start.18 = (bf16[3,3,3,4,32]{4,3,2,1,0:T(4,128)(2,1)S(1)}, bf16[3,3,3,4,32]{4,3,2,1,0:T(4,128)(2,1)}, u32[]{:S(2)}) copy-start(bf16[3,3,3,4,32]{4,3,2,1,0:T(4,128)(2,1)} %param.11) | copy-start | bytes 20740
  20.2 12.0 %copy-start.19 = (pred[8,33]{0,1:T(8,128)(4,1)S(1)}, pred[8,33]{0,1:T(8,128)(4,1)}, u32[]{:S(2)}) copy-start(pred[8,33]{0,1:T(8,128)(4,1)} %constant.98) | copy-start | bytes 796
  74.0 14.2 %copy-start.2 = (f32[8,4,1,264,32]{3,4,1,0,2:T(8,128)}, f32[8,4,1,264,32]{3,4,1,0,2:T(8,128)S(1)}, u32[]{:S(2)}) copy-start(f32[8,4,1,264,32]{3,4,1,0,2:T(8,128)S(1)} %reshape.138) | copy-start | bytes 3244036
  74.4 6.2 collective-permute-start.2
  80.5 6.7 collective-permute-start.3
  104.0 23.9 %copy-start.9 = (f32[4,2,1,128,64]{3,4,1,0,2:T(8,128)}, f32[4,2,1,128,64]{3,4,1,0,2:T(8,128)S(1)}, u32[]{:S(2)}) copy-start(f32[4,2,1,128,64]{3,4,1,0,2:T(8,128)S(1)} %copy.296) | copy-start | bytes 786436
  116.7 5.1 collective-permute-start.4
  120.2 7.0 collective-permute-start.5
  141.0 128.4 %reduce-scatter.5.cloned.1.call-start = ((), (), s32[]{:S(2)}) async-start(), calls=%async_computation.5 | async-start | bytes 5242880 | tf_op jit(solution)/shard_map/reduce_scatter | solution.py:120
  189.4 5.3 collective-permute-start.6
  192.8 6.2 collective-permute-start.7
  214.9 54.5 %copy-start.14 = (bf16[64,4,8,128]{3,2,1,0:T(8,128)(2,1)S(1)}, bf16[64,4,8,128]{3,2,1,0:T(8,128)(2,1)}, u32[]{:S(2)}) copy-start(bf16[64,4,8,128]{3,2,1,0:T(8,128)(2,1)} %param.15) | copy-start | bytes 1572868
  214.9 83.4 %all-gather.3.cloned.1.call-start = ((), (), s32[]{:S(2)}) async-start(), calls=%async_computation.6 | async-start | bytes 2621440 | tf_op jit(solution)/shard_map/all_gather | solution.py:70
  272.2 95.6 %all-gather.5.cloned.1.call-start = ((), (), s32[]{:S(2)}) async-start(), calls=%async_computation.7 | async-start | bytes 1310720 | tf_op jit(solution)/shard_map/all_gather | solution.py:70
  302.2 15.0 %collective-permute-start.8 = (bf16[256,1,8,128]{0,2,3,1:T(8,128)(2,1)S(1)}, bf16[256,1,8,128]{0,2,3,1:T(8,128)(2,1)S(1)}, u32[]{:S(2)}, u32[]{:S(2)}) collective-permute-start(bf16[256,1,8,128]{0,2,3,1:T(8,128)(2,1)S(1)} %get-tuple-element.46), channel_id=1, source_target_pairs={{0,4},{4,8},{8,12},{12,16},{16,20},{20,24},{24,28},{28,32},{32,36}... | collective-permute-start | bytes 1572872 | tf_op jit(solution)/shard_map/ppermute | solution.py:24
  305.6 15.7 %collective-permute-start.9 = (bf16[256,1,8,128]{0,2,3,1:T(8,128)(2,1)S(1)}, bf16[256,1,8,128]{0,2,3,1:T(8,128)(2,1)S(1)}, u32[]{:S(2)}, u32[]{:S(2)}) collective-permute-start(bf16[256,1,8,128]{0,2,3,1:T(8,128)(2,1)S(1)} %get-tuple-element.47), channel_id=1, source_target_pairs={{4,0},{8,4},{12,8},{16,12},{20,16},{24,20},{28,24},{32,28},{36,32}... | collective-permute-start | bytes 1572872 | tf_op jit(solution)/shard_map/ppermute | solution.py:27
  340.2 36.3 %copy-start.7 = (bf16[4,1,17,9,512]{4,2,3,0,1:T(8,128)(2,1)S(1)}, bf16[4,1,17,9,512]{4,2,3,0,1:T(8,128)(2,1)}, u32[]{:S(2)}) copy-start(bf16[4,1,17,9,512]{4,2,3,0,1:T(8,128)(2,1)} %get-tuple-element.52) | copy-start | bytes 1880068
  370.0 63.5 %copy-start.5 = (bf16[128,4,8,128]{0,2,3,1:T(8,128)(2,1)}, bf16[128,4,8,128]{0,2,3,1:T(8,128)(2,1)S(1)}, u32[]{:S(2)}) copy-start(bf16[128,4,8,128]{0,2,3,1:T(8,128)(2,1)S(1)} %copy.262) | copy-start | bytes 3145732
  370.9 87.9 %collective-permute-start.10 = (bf16[128,1,8,128]{0,2,3,1:T(8,128)(2,1)}, bf16[128,1,8,128]{0,2,3,1:T(8,128)(2,1)}, u32[]{:S(2)}, u32[]{:S(2)}) collective-permute-start(bf16[128,1,8,128]{0,2,3,1:T(8,128)(2,1)} %get-tuple-element.48), channel_id=1, source_target_pairs={{0,4},{4,8},{8,12},{12,16},{16,20},{20,24},{24,28},{28,32},{32,36}... | collective-permute-start | bytes 786440 | tf_op jit(solution)/shard_map/ppermute | solution.py:24
  375.0 83.8 %collective-permute-start.11 = (bf16[128,1,8,128]{0,2,3,1:T(8,128)(2,1)}, bf16[128,1,8,128]{0,2,3,1:T(8,128)(2,1)}, u32[]{:S(2)}, u32[]{:S(2)}) collective-permute-start(bf16[128,1,8,128]{0,2,3,1:T(8,128)(2,1)} %get-tuple-element.49), channel_id=1, source_target_pairs={{4,0},{8,4},{12,8},{16,12},{20,16},{24,20},{28,24},{32,28},{36,32}... | collective-permute-start | bytes 786440 | tf_op jit(solution)/shard_map/ppermute | solution.py:27
  444.7 9.1 copy-start.4
  474.7 37.3 %all-to-all-start.1 = ((f32[16,4,8,128]{3,0,1,2:T(8,128)}), f32[16,4,8,128]{3,0,1,2:T(8,128)}, u32[]{:S(2)}, u32[]{:S(2)}) async-start(f32[16,4,8,128]{3,0,1,2:T(8,128)} %copy.268), calls=%async_computation.3 | async-start | bytes 524288 | tf_op jit(solution)/shard_map/all_to_all | solution.py:132
  478.7 277.2 %all-reduce.4.cloned.1.call-start = ((), (), s32[]{:S(2)}) async-start(), calls=%async_computation.8 | async-start | bytes 884736 | tf_op jit(solution)/shard_map/psum | solution.py:139
  479.2 30.1 %copy-start.6 = (bf16[128,4,8,128]{3,2,1,0:T(8,128)(2,1)S(1)}, bf16[128,4,8,128]{3,2,1,0:T(8,128)(2,1)}, u32[]{:S(2)}) copy-start(bf16[128,4,8,128]{3,2,1,0:T(8,128)(2,1)} %all-gather.5.cloned.1.call-done) | copy-start | bytes 3145732
  536.8 17.0 %collective-permute-start.12 = (f32[32,9,1,256]{3,0,2,1:T(8,128)S(1)}, f32[32,9,1,256]{3,0,2,1:T(8,128)S(1)}, u32[]{:S(2)}, u32[]{:S(2)}) collective-permute-start(f32[32,9,1,256]{3,0,2,1:T(8,128)S(1)} %slice.169), channel_id=1, source_target_pairs={{0,1},{1,2},{2,3},{4,5},{5,6},{6,7},{8,9},{9,10},{10,11},{12,13},{... | collective-permute-start | bytes 884744 | tf_op jit(solution)/shard_map/ppermute | solution.py:16
  553.7 448.6 %all-reduce.6.cloned.1.call-start = ((), (), s32[]{:S(2)}) async-start(), calls=%async_computation.9 | async-start | bytes 2211840 | tf_op jit(solution)/shard_map/psum | solution.py:140
  553.9 34.5 %collective-permute-start.13 = (f32[32,1,4,256]{3,0,2,1:T(8,128)S(1)}, f32[32,1,4,256]{3,0,2,1:T(8,128)S(1)}, u32[]{:S(2)}, u32[]{:S(2)}) collective-permute-start(f32[32,1,4,256]{3,0,2,1:T(8,128)S(1)} %slice.172), channel_id=1, source_target_pairs={{0,4},{4,8},{8,12},{12,16},{16,20},{20,24},{24,28},{28,32},{32,36}... | collective-permute-start | bytes 393224 | tf_op jit(solution)/shard_map/ppermute | solution.py:16
  597.2 410.7 %copy-start.1 = (bf16[3,3,3,32,256]{4,3,2,1,0:T(8,128)(2,1)S(1)}, bf16[3,3,3,32,256]{4,3,2,1,0:T(8,128)(2,1)}, u32[]{:S(2)}) copy-start(bf16[3,3,3,32,256]{4,3,2,1,0:T(8,128)(2,1)} %param.14) | copy-start | bytes 1327108
  (10 other events, 46.4 us)
Sparse Core Ops, SparseCore 0:
  141.1 47.0 reduce-scatter.2
  215.1 54.3 reduce-scatter.4
  272.3 25.9 all-gather.2
  344.1 23.6 all-gather.4
  553.9 145.6 all-reduce.3
  702.7 299.5 all-reduce.5
where the time goes:
time: 1030 us; the launch traced here: 1010 us
  waiting for transfers between devices  438 us (43%)
  matrix products  242 us (23%)
  local copies, waits for them, and re-layouts  187 us (18%)
  blocking collectives  83.4 us (8%)
  starting transfers between devices  37.5 us (4%)
  between operations  15.1 us (1%)
  other arithmetic  12.4 us (1%)
    psum x1, waiting for transfers between devices, per_device(): grad_three, grad_four = lax.psum((grad_three, grad_four), 'space')  246 us
    transpose x4, matrix products, weight_grad(): return jnp.transpose(result, (2, 3, 4, 0, 1))  162 us
    broadcast_in_dim x4, local copies, waits for them, and re-layouts, weight_grad(): padded[:, None]  74.9 us
    conv_general_dilated x6, matrix products, convolve(): lax.conv_general_dilated(field[None], kernel, (stride, stride, stride), p...  72.7 us
    psum x1, blocking collectives, per_device(): grad_one, grad_two = lax.psum((grad_one, grad_two), ('space', 'chan'))  71 us
    reduce_scatter x1, waiting for transfers between devices, per_device(): lax.psum_scatter(convolve(padded_four, kernel_four, 1, SAME_HW), 'chan',...  54.4 us
    all_gather x2, waiting for transfers between devices, gather_filters(): return lax.all_gather(gradient, 'chan', axis=0, tiled=True)  49.9 us
    reduce_scatter x1, waiting for transfers between devices, per_device(): lax.psum_scatter(convolve(padded_three, kernel_three, 1, SAME_HW), 'chan'...  47.2 us
  transfers between devices with their start and end apart: 21, of which 15 were waited for; matrix products, arithmetic and copies ran while one was open for 25% of the time, Pallas kernels for 0%

commit v1 on v0

v1 whole, which is shorter than its diff:
```python
import functools

import jax
import jax.numpy as jnp
import numpy as np
from jax import lax
from jax.experimental import pallas as pl
from jax.experimental.pallas import tpu as pltpu
from jax.sharding import PartitionSpec as P

BF = jnp.bfloat16
F32 = jnp.float32
BOTH = ("space", "chan")
LANES = 128
VMEM_LIMIT = 48 * 1024 * 1024


def mm(left, right):
    return lax.dot_general(left, right, (((1,), (0,)), ((), ())), preferred_element_type=F32)


def mm_nt(left, right):
    return lax.dot_general(left, right, (((1,), (1,)), ((), ())), preferred_element_type=F32)


def lane_of(shape):
    return lax.broadcasted_iota(jnp.int32, shape, len(shape) - 1)


def shifted(value, step):
    width = value.shape[1]
    turned = pltpu.roll(value, step % width, 1)
    edge = 0 if step == 1 else LANES - 1
    return jnp.where(lane_of(value.shape) % LANES == edge, 0.0, turned)


def activate(pre):
    sigma = jax.nn.sigmoid(pre)
    return pre * sigma, sigma * (1.0 + pre * (1.0 - sigma))


def call(kernel, outs, args, scratch=(), flops=0):
    smem = pl.BlockSpec(memory_space=pltpu.SMEM)
    vmem = pl.BlockSpec(memory_space=pltpu.VMEM)
    size = sum(a.size * a.dtype.itemsize for a in args)
    size += sum(int(np.prod(s)) * jnp.dtype(t).itemsize for s, t in outs)
    return pl.pallas_call(
        kernel,
        out_shape=[jax.ShapeDtypeStruct(s, t) for s, t in outs],
        in_specs=[smem if a.dtype == jnp.int32 else vmem for a in args],
        out_specs=[vmem] * len(outs),
        scratch_shapes=[pltpu.VMEM(s, t) for s, t in scratch],
        compiler_params=pltpu.CompilerParams(vmem_limit_bytes=VMEM_LIMIT),
        cost_estimate=pl.CostEstimate(flops=flops, bytes_accessed=size, transcendentals=0),
    )(*args)


def first_layers_kernel(vol, phases, rows, w_one, w_two, field, act_one, slope_one, act_two, slope_two):
    for d in range(19):
        block = jnp.reshape(vol[:, d], (64, 512))
        split = mm(block, phases[...]).astype(BF)
        stacked = jnp.concatenate([split[:, p * 128 : p * 128 + 128] for p in range(5)], 0)
        field[d] = mm(rows[...], stacked).astype(BF)
    for d in range(9):
        columns = []
        for h in range(5):
            parts = [field[2 * d + a, h * 64 : h * 64 + 96] for a in range(3)]
            columns.append(jnp.concatenate(parts, 0))
        pre = mm(w_one[...], jnp.concatenate(columns, 1))
        act, slope = activate(pre)
        if d < 8:
            slope_one[d] = slope[:, :512]
        beside = shifted(act[:32], -1)
        for h in range(5):
            lanes = slice(h * 128, h * 128 + 128)
            act_one[d, h * 96 : h * 96 + 64] = act[:, lanes].astype(BF)
            act_one[d, h * 96 + 64 : h * 96 + 96] = beside[:, lanes].astype(BF)
    for d in range(4):
        columns = []
        for h in range(2):
            parts = [act_one[2 * d + a, h * 192 : h * 192 + 288] for a in range(3)]
            columns.append(jnp.concatenate(parts, 0))
        pre = mm(w_two[...], jnp.concatenate(columns, 1))
        act, slope = activate(pre)
        act_two[d] = act.astype(BF)
        slope_two[d] = slope


def taps_of(field, d, start, width):
    parts = []
    for a in range(3):
        for b in range(3):
            parts.append(field[d + a, :, pl.ds(start + b * LANES, width)])
    return jnp.concatenate(parts, 0)


def shift_sum(product, channels):
    low = product[:channels]
    mid = product[channels : 2 * channels]
    high = product[2 * channels :]
    return shifted(low, 1) + mid + shifted(high, -1)


def clear_rims(field):
    depth, channels, lanes = field.shape
    rim = jnp.zeros((depth, channels, LANES), BF)
    field[:, :, :LANES] = rim
    field[:, :, lanes - LANES :] = rim


def assemble(field, me, pieces, channels):
    clear_rims(field)
    for near, far in ((0, 1), (2, 3)):
        for k in (near, far):
            body, up, down = pieces[k]
            at = pl.multiple_of((me ^ k) * channels, channels)
            field[0, pl.ds(at, channels), LANES : 9 * LANES] = up
            for d in range(4):
                field[d + 1, pl.ds(at, channels), LANES : 9 * LANES] = body[d]
            field[5, pl.ds(at, channels), LANES : 9 * LANES] = down


def pieces_of(own, own_up, own_down, across, across_up, across_down, core, rest):
    return {
        0: (own, own_up[0], own_down[0]),
        2: (across, across_up[0], across_down[0]),
        1: (core, rest[4], rest[5]),
        3: (rest, rest[6], rest[7]),
    }


def third_kernel(me_ref, *refs):
    blocks, weights = refs[:8], refs[8]
    act, slope, field = refs[9:]
    me = me_ref[0]
    clear_rims(field)
    pieces = pieces_of(*blocks)
    for k in range(4):
        body, up, down = pieces[k]
        at = pl.multiple_of(LANES + (me ^ k) * (2 * LANES), LANES)
        lanes = pl.ds(at, 2 * LANES)
        field[0, :, lanes] = up
        for d in range(4):
            field[d + 1, :, lanes] = body[d]
        field[5, :, lanes] = down
    for d in range(4):
        product = mm(weights[...], taps_of(field, d, 0, 1024))
        value, steep = activate(shift_sum(product, 32))
        act[d] = value.astype(BF)
        slope[d] = steep


def fourth_kernel(me_ref, *refs):
    blocks, weights, cotangent = refs[:8], refs[8], refs[9]
    features, back, field = refs[10:]
    assemble(field, me_ref[0], pieces_of(*blocks), 32)
    for d in range(4):
        product = mm(weights[...], taps_of(field, d, 0, 1024))
        value, steep = activate(shift_sum(product, 64))
        features[d] = value.astype(BF)
        back[d] = (cotangent[d].astype(F32) * steep).astype(BF)


def flipped_weights(kernel):
    columns = []
    for a in range(3):
        for b in range(3):
            taps = [((2 - a) * 3 + 2 - b) * 3 + 2 - c for c in range(3)]
            columns.append(jnp.concatenate([kernel[t] for t in taps], 0))
    return jnp.concatenate(columns, 1)


def into_three_kernel(me_ref, *refs):
    blocks, kernel, slope = refs[:8], refs[8], refs[9]
    back, field = refs[10:]
    assemble(field, me_ref[0], pieces_of(*blocks), 64)
    weights = flipped_weights(kernel)
    for d in range(4):
        product = mm(weights, taps_of(field, d, 0, 1024))
        back[d] = (shift_sum(product, 32) * slope[d]).astype(BF)


def into_two_kernel(me_ref, *refs):
    blocks, kernel, slope = refs[:8], refs[8], refs[9]
    back, field = refs[10:]
    me = me_ref[0]
    assemble(field, me, pieces_of(*blocks), 32)
    weights = flipped_weights(kernel)
    start = pl.multiple_of(me * (2 * LANES), LANES)
    for d in range(4):
        product = mm(weights, taps_of(field, d, start, 2 * LANES))
        back[d] = (shift_sum(product, 64) * slope[d]).astype(BF)


def three_shifts(value):
    wide = value.astype(F32)
    return jnp.concatenate([shifted(wide, 1).astype(BF), value, shifted(wide, -1).astype(BF)], 0)


def filter_grad(wide, gradient, grad):
    total = None
    for d in range(4):
        term = mm_nt(taps_of(wide, d, 0, 1024), gradient[d + 1, :, LANES : 9 * LANES])
        total = term if total is None else total + term
    grad[...] = total.astype(grad.dtype)


def grad_four_kernel(own, up, down, gradient, grad, wide):
    clear_rims(wide)
    inside = slice(LANES, 9 * LANES)
    wide[0, :, inside] = three_shifts(up[0])
    for d in range(4):
        wide[d + 1, :, inside] = three_shifts(own[d])
    wide[5, :, inside] = three_shifts(down[0])
    filter_grad(wide, gradient, grad)


def grad_three_kernel(me_ref, field, gradient, grad, wide):
    clear_rims(wide)
    inside = slice(LANES, 9 * LANES)
    at = pl.multiple_of(me_ref[0] * 16, 16)
    for d in range(6):
        wide[d, :, inside] = three_shifts(field[d, pl.ds(at, 16), inside])
    filter_grad(wide, gradient, grad)


def last_kernel(back, plane, row, corner, act_one, slope_one, field, w_back, grads, wide, back_one):
    def place(d, h, value):
        wide[d, h, :64] = value
        wide[d, h, 64:] = shifted(value.astype(F32), 1).astype(BF)

    place(0, 0, corner[0])
    for h in range(2):
        place(0, h + 1, plane[0, :, h * 128 : h * 128 + 128])
    for d in range(4):
        place(d + 1, 0, row[d])
        for h in range(2):
            place(d + 1, h + 1, back[d, :, h * 128 : h * 128 + 128])
    for d_odd in range(2):
        for h_odd in range(2):
            taps = [(a, b) for a in ((1,) if d_odd else (0, 2)) for b in ((1,) if h_odd else (0, 2))]
            weights = jnp.concatenate([w_back[a * 3 + b] for a, b in taps], 1)
            columns = []
            for d in range(4):
                for h in range(2):
                    parts = [wide[d + 1 - a // 2, h + 1 - b // 2] for a, b in taps]
                    columns.append(jnp.concatenate(parts, 0))
            into = mm(weights, jnp.concatenate(columns, 1))
            for d in range(4):
                for h in range(2):
                    at = (d * 2 + h) * 128
                    lanes = slice((2 * h + h_odd) * 128, (2 * h + h_odd) * 128 + 128)
                    d_one = 2 * d + d_odd
                    value = into[:, at : at + 128] * slope_one[d_one, :, lanes]
                    back_one[d_one, :, lanes] = value.astype(BF)
    two = None
    for d in range(4):
        columns = []
        for h in range(2):
            parts = [act_one[2 * d + a, h * 192 : h * 192 + 288] for a in range(3)]
            columns.append(jnp.concatenate(parts, 0))
        term = mm_nt(jnp.concatenate(columns, 1), back[d])
        two = term if two is None else two + term
    one = None
    for d in range(8):
        columns = []
        for h in range(4):
            parts = [field[2 * d + a, h * 64 : h * 64 + 96] for a in range(3)]
            columns.append(jnp.concatenate(parts, 0))
        term = mm_nt(jnp.concatenate(columns, 1), back_one[d])
        one = term if one is None else one + term
    both = jnp.concatenate([two, one], 0)
    grads[:576] = jnp.concatenate([both[:576], both[576:]], 1)
    grads[576:] = jnp.zeros((448, 128), F32)


def moved(block, depth_step, chan_of):
    depth, chans = lax.axis_size("space"), lax.axis_size("chan")
    route = []
    for s in range(depth):
        for c in range(chans):
            to = chan_of(c)
            if 0 <= s + depth_step < depth and 0 <= to < chans:
                route.append((s * chans + c, (s + depth_step) * chans + to))
    return lax.ppermute(block, BOTH, route)


def gathered(own):
    first, last = own[:1], own[3:]
    across = moved(own, 0, lambda c: c ^ 2)
    own_up = moved(last, 1, lambda c: c)
    own_down = moved(first, -1, lambda c: c)
    across_up = moved(last, 1, lambda c: c ^ 2)
    across_down = moved(first, -1, lambda c: c ^ 2)
    core = moved(own, 0, lambda c: c ^ 1)
    rest = jnp.concatenate([across, own_up, own_down, across_up, across_down], 0)
    rest = moved(rest, 0, lambda c: c ^ 1)
    return [own, own_up, own_down, across, across_up, across_down, core, rest]


def summed(parts, axis):
    count = parts.shape[0]
    terms = lax.all_to_all(parts, axis, 0, 0)
    total = jnp.sum(terms.astype(F32), 0).astype(parts.dtype)
    return lax.all_to_all(jnp.broadcast_to(total[None], (count,) + total.shape), axis, 0, 0)


def phase_matrix():
    pick = np.zeros((512, 640), np.float32)
    for p in range(5):
        for w in range(128):
            if 4 * w + p < 512:
                pick[4 * w + p, p * 128 + w] = 1.0
    return jnp.asarray(pick, BF)


def row_matrix():
    pick = np.zeros((11, 8, 4, 5, 4, 16), np.float32)
    for h in range(11):
        for p in range(5):
            for i in range(4):
                pick[h, p, i, p, i, h] = 1.0
    return jnp.asarray(pick.reshape(352, 320), BF)


def per_device(volume, kernel_one, kernel_two, kernel_three, kernel_four, cotangent):
    me = lax.axis_index("chan").astype(jnp.int32)[None]
    below = moved(volume[:, :3], -1, lambda c: c)
    beside = moved(volume[:, :, :3], 0, lambda c: c - 1)
    corner = moved(volume[:, :3, :3], -1, lambda c: c - 1)
    tall = jnp.concatenate([volume, below], 1)
    side = jnp.pad(jnp.concatenate([beside, corner], 1), ((0, 0), (0, 0), (0, 5), (0, 0)))
    tall = jnp.concatenate([tall, side], 2)

    even = jnp.pad(kernel_one, ((0, 0), (0, 0), (0, 5), (0, 0), (0, 0)))
    odd = jnp.pad(kernel_one, ((0, 0), (0, 0), (2, 3), (0, 0), (0, 0)))
    w_one = jnp.stack([even, odd]).reshape(2, 288, 32).transpose(0, 2, 1).reshape(64, 288)
    w_two = kernel_two.reshape(864, 64).T
    field, act_one, slope_one, act_two, slope_two = call(
        first_layers_kernel,
        [((19, 352, 128), BF), ((9, 480, 128), BF), ((8, 64, 512), F32), ((4, 64, 256), BF), ((4, 64, 256), F32)],
        [tall, phase_matrix(), row_matrix(), w_one, w_two],
    )

    all_kernel_three = lax.all_gather(kernel_three, "chan", axis=3, tiled=True)
    mine = lax.dynamic_slice_in_dim(all_kernel_three, lax.axis_index("chan") * 32, 32, axis=4)
    w_three = jnp.transpose(mine, (2, 4, 0, 1, 3)).reshape(96, 576)
    mine = lax.all_to_all(kernel_four, "chan", split_axis=4, concat_axis=3, tiled=True)
    w_four = jnp.transpose(mine, (2, 4, 0, 1, 3)).reshape(192, 1152)
    cotangent = jnp.transpose(cotangent.reshape(64, 4, 1024), (1, 0, 2))

    act_three, slope_three, field_three = call(
        third_kernel,
        [((4, 32, 1024), BF), ((4, 32, 1024), F32), ((6, 64, 1280), BF)],
        [me, *gathered(act_two), w_three],
    )
    blocks = gathered(act_three)
    features, back_four = call(
        fourth_kernel,
        [((4, 64, 1024), BF), ((4, 64, 1024), BF)],
        [me, *blocks, w_four, cotangent],
        [((6, 128, 1280), BF)],
    )
    features = jnp.transpose(features, (1, 0, 2)).reshape(64, 4, 8, 128)
    back_three, all_four = call(
        into_three_kernel,
        [((4, 32, 1024), BF), ((6, 256, 1280), BF)],
        [me, *gathered(back_four), kernel_four.reshape(27, 32, 256), slope_three],
    )
    (grad_four,) = call(
        grad_four_kernel,
        [((864, 256), BF)],
        [*blocks[:3], all_four],
        [((6, 96, 1280), BF)],
        flops=2 * 864 * 256 * 4096,
    )
    back_two, all_three = call(
        into_two_kernel,
        [((4, 64, 256), BF), ((6, 128, 1280), BF)],
        [me, *gathered(back_three), all_kernel_three.reshape(27, 64, 128), slope_two],
    )
    (grad_three,) = call(
        grad_three_kernel,
        [((432, 128), BF)],
        [me, field_three, all_three],
        [((6, 48, 1280), BF)],
        flops=2 * 432 * 128 * 4096,
    )
    plane = moved(back_two[3:], 1, lambda c: c)
    row = moved(back_two[:, :, 128:], 0, lambda c: c + 1)
    corner = moved(back_two[3:, :, 128:], 1, lambda c: c + 1)
    top = jnp.concatenate([kernel_two[:, :, 0], kernel_two[:, :, 2]], 3)
    bottom = jnp.pad(kernel_two[:, :, 1], ((0, 0), (0, 0), (0, 0), (0, 64)))
    w_back = jnp.concatenate([top, bottom], 2).reshape(9, 64, 128)
    (grads,) = call(
        last_kernel,
        [((1024, 128), F32)],
        [back_two, plane, row, corner, act_one, slope_one, field, w_back],
        [((5, 3, 128, 128), BF), ((8, 64, 512), BF)],
    )
    grad_four = summed(grad_four.reshape(32, 27, 256), "space").astype(F32)
    grad_four = grad_four.reshape(3, 3, 3, 32, 256)
    grad_three = summed(grad_three.reshape(32, 27, 64), "space").astype(F32)
    grad_three = grad_three.reshape(3, 3, 3, 16, 128)
    grads = summed(grads.reshape(128, 8, 128), BOTH).reshape(1024, 128)
    grads = jnp.concatenate([grads[:576, :64], grads[:576, 64:]], 0)
    grad_two = grads[:864].reshape(3, 3, 3, 32, 64)
    phases = grads[864:].reshape(3, 3, 8, 4, 64)
    grad_one = phases[:, :, 0:3, :, :32] + phases[:, :, 2:5, :, 32:]
    return (features, grad_one, grad_two, grad_three, grad_four)


def solution(mesh):
    in_specs = (
        P(None, "space", "chan", None),
        P(),
        P(),
        P(None, None, None, "chan", None),
        P(None, None, None, "chan", None),
        P("chan", "space", None, None),
    )
    out_specs = (
        P("chan", "space", None, None),
        P(),
        P(),
        P(None, None, None, "chan", None),
        P(None, None, None, "chan", None),
    )
    return jax.shard_map(
        per_device, mesh=mesh, in_specs=in_specs, out_specs=out_specs, check_vma=False
    )
```

time: 1030 us -> 297 us (0.29); the launches traced: 1010 us -> 294 us
  waiting for transfers between devices: 438 us -> 75.4 us
  matrix products: 242 us -> 0 us
  local copies, waits for them, and re-layouts: 187 us -> 62.5 us
  starting transfers between devices: 37.5 us -> 118 us
  blocking collectives: 83.4 us -> 8.5 us
  Pallas kernels: 0 us -> 24 us
  between operations: 15.1 us -> 1.46 us
    psum x2 -> x0, waiting for transfers between devices: 246 us -> none  [the longest x1 246 us: per_device(): grad_three, grad_four = lax.psum((grad_three, grad_four), 'space')]
    transpose x4 -> x0, matrix products: 162 us -> none  [weight_grad(): return jnp.transpose(result, (2, 3, 4, 0, 1))]
    reduce_scatter x2 -> x0, waiting for transfers between devices: 102 us -> none  [the longest x1 54.4 us: per_device(): lax.psum_scatter(convolve(padded_four, kernel_four, 1, SAME_HW), 'chan',...]
    broadcast_in_dim x13 -> x3, local copies, waits for them, and re-layouts: 91.9 us -> 1.77 us  [summed(): jnp.broadcast_to(total[None], (count,) + total.shape)]
    conv_general_dilated x7 -> x0, matrix products: 80.2 us -> none  [the longest x6 72.7 us: convolve(): lax.conv_general_dilated(field[None], kernel, (stride, stride, stride), p...]
    psum x1 -> x0, blocking collectives: 71 us -> none  [per_device(): grad_one, grad_two = lax.psum((grad_one, grad_two), ('space', 'chan'))]
    conv_general_dilated x29 -> x0, local copies, waits for them, and re-layouts: 59 us -> none  [the longest x25 45.1 us: convolve(): lax.conv_general_dilated(field[None], kernel, (stride, stride, stride), p...]
    all_gather x2 -> x0, waiting for transfers between devices: 49.9 us -> none  [gather_filters(): return lax.all_gather(gradient, 'chan', axis=0, tiled=True)]
  transfers between devices with their start and end apart: 21 -> 41, of which waited for: 15 -> 15; matrix products, arithmetic and copies ran while one was open for 25% -> 17% of each run, Pallas kernels for 0% -> 2%
where the time goes in v1:
time: 297 us; the launch traced here: 294 us
  starting transfers between devices  118 us (40%)
  waiting for transfers between devices  75.4 us (25%)
  local copies, waits for them, and re-layouts  62.5 us (21%)
  Pallas kernels  24 us (8%)
  blocking collectives  8.5 us (3%)
  other arithmetic  4.25 us (1%)
    ppermute x34, starting transfers between devices, moved(): return lax.ppermute(block, BOTH, route)  72 us
    unnamed x93, local copies, waits for them, and re-layouts  35.7 us
    ppermute x34, waiting for transfers between devices, moved(): return lax.ppermute(block, BOTH, route)  29.8 us
    all_to_all x3, starting transfers between devices, summed(): terms = lax.all_to_all(parts, axis, 0, 0)  27.8 us
    pallas_call x8, Pallas kernels, call(): pl.pallas_call(kernel, out_shape=[jax.ShapeDtypeStruct(s, t) for s, t in...  24 us
    all_to_all x3, waiting for transfers between devices, summed(): terms = lax.all_to_all(parts, axis, 0, 0)  22 us
    all_to_all x3, waiting for transfers between devices, summed(): lax.all_to_all(jnp.broadcast_to(total[None], (count,) + total.shape), axi...  17 us
    all_to_all x3, starting transfers between devices, summed(): lax.all_to_all(jnp.broadcast_to(total[None], (count,) + total.shape), axi...  14.3 us
  transfers between devices with their start and end apart: 41, of which 15 were waited for; matrix products, arithmetic and copies ran while one was open for 17% of the time, Pallas kernels for 2%

profile of v1, /device:TPU:0, one launch (start us, length us, event | category | flops | bytes accessed | tf_op | source)
XLA Modules:
  0.0 293.6 jit_solution(8600734299957156609)
XLA Ops:
  9.1 4.1 %collective-permute-done = bf16[4,3,8,512]{3,2,1,0:T(8,128)(2,1)S(1)} collective-permute-done((bf16[4,3,8,512]{3,2,1,0:T(8,128)(2,1)S(1)}, bf16[4,3,8,512]{3,2,1,0:T(8,128)(2,1)S(1)}, u32[]{:S(2)}, u32[]{:S(2)}) %collective-permute-start) | collective-permute-done | bytes 98336 | tf_op jit(solution)/shard_map/ppermute | solution.py:285
  13.5 6.8 %shard_map.119 = (bf16[19,352,128]{2,1,0:T(8,128)(2,1)}, bf16[9,480,128]{2,1,0:T(8,128)(2,1)S(1)}, f32[8,64,512]{2,1,0:T(8,128)S(1)}, bf16[4,64,256]{2,1,0:T(8,128)(2,1)S(1)}, f32[4,64,256]{2,1,0:T(8,128)S(1)}) custom-call(bf16[4,19,16,512]{3,2,1,0:T(8,128)(2,1)S(1)} %pad_maximum_fusion.vol, bf16[512,640]{1,0:T(8,128)(2,1)S(1)} %copy-done.6, ...), custom_call_target="tpu_custom_call" | custom-call | bytes 6533120 | tf_op jit(solution)/shard_map/pallas_call | solution.py:47
  21.3 5.2 %collective-permute-start.5 = (bf16[4,64,256]{2,1,0:T(8,128)(2,1)S(1)}, bf16[4,64,256]{2,1,0:T(8,128)(2,1)S(1)}, u32[]{:S(2)}, u32[]{:S(2)}) collective-permute-start(bf16[4,64,256]{2,1,0:T(8,128)(2,1)S(1)} %get-tuple-element.19.refs_0_), channel_id=1, source_target_pairs={{0,2},{1,3},{2,0},{3,1},{4,6},{5,7},{6,4},{7,5},{8,10},{9,11},{10,... | collective-permute-start | bytes 393224 | tf_op jit(solution)/shard_map/ppermute | solution.py:285
  26.5 3.6 %collective-permute-start.3 = (bf16[1,64,256]{2,1,0:T(8,128)(2,1)S(1)}, bf16[1,64,256]{2,1,0:T(8,128)(2,1)S(1)}, u32[]{:S(2)}, u32[]{:S(2)}) collective-permute-start(bf16[1,64,256]{2,1,0:T(8,128)(2,1)S(1)} %get-tuple-element.60), channel_id=1, source_target_pairs={{0,4},{1,5},{2,6},{3,7},{4,8},{5,9},{6,10},{7,11},{8,12},{9,13},{1... | collective-permute-start | bytes 98312 | tf_op jit(solution)/shard_map/ppermute | solution.py:285
  41.6 3.6 %collective-permute-done.7.refs_5_ = bf16[1,64,256]{2,1,0:T(8,128)(2,1)S(1)} collective-permute-done((bf16[1,64,256]{2,1,0:T(8,128)(2,1)S(1)}, bf16[1,64,256]{2,1,0:T(8,128)(2,1)S(1)}, u32[]{:S(2)}, u32[]{:S(2)}) %collective-permute-start.7) | collective-permute-done | bytes 32800 | tf_op jit(solution)/shard_map/ppermute | solution.py:285
  45.8 8.5 %all_gather.3 = bf16[3,3,3,64,128]{4,3,2,1,0:T(8,128)(2,1)S(1)} all-gather(bf16[3,3,3,16,128]{4,3,2,1,0:T(8,128)(2,1)S(1)} %copy-done.33), channel_id=1, replica_groups=mesh['space'=32,'chan'=4] {'chan'}, dimensions={3}, use_global_device_ids=true | all-gather | bytes 552960 | tf_op jit(solution)/shard_map/all_gather | solution.py:345
  64.0 6.0 %collective-permute-start.10 = (bf16[1,32,1024]{2,1,0:T(8,128)(2,1)S(1)}, bf16[1,32,1024]{2,1,0:T(8,128)(2,1)S(1)}, u32[]{:S(2)}, u32[]{:S(2)}) collective-permute-start(bf16[1,32,1024]{2,1,0:T(8,128)(2,1)S(1)} %get-tuple-element.55), channel_id=1, source_target_pairs={{0,4},{1,5},{2,6},{3,7},{4,8},{5,9},{6,10},{7,11},{8,12},{9,13},{1... | collective-permute-start | bytes 196616 | tf_op jit(solution)/shard_map/ppermute | solution.py:285
  69.9 3.6 %collective-permute-start.13 = (bf16[1,32,1024]{2,1,0:T(8,128)(2,1)S(1)}, bf16[1,32,1024]{2,1,0:T(8,128)(2,1)S(1)}, u32[]{:S(2)}, u32[]{:S(2)}) collective-permute-start(bf16[1,32,1024]{2,1,0:T(8,128)(2,1)S(1)} %get-tuple-element.55), channel_id=1, source_target_pairs={{0,6},{1,7},{2,4},{3,5},{4,10},{5,11},{6,8},{7,9},{8,14},{9,15},{1... | collective-permute-start | bytes 196616 | tf_op jit(solution)/shard_map/ppermute | solution.py:285
  89.4 4.4 %reshape.99 = bf16[4,2,27648]{2,1,0:T(2,128)(2,1)} reshape(bf16[256,3,3,3,32]{4,3,2,1,0:T(4,128)(2,1)} %bitcast.55) | data formatting | bytes 884736
  100.1 6.6 %all-to-all-done = bf16[4,2,27648]{2,1,0:T(2,128)(2,1)S(1)} async-done(((bf16[4,2,27648]{2,1,0:T(2,128)(2,1)}), bf16[4,2,27648]{2,1,0:T(2,128)(2,1)S(1)}, u32[]{:S(2)}, u32[]{:S(2)}) %all-to-all-start) | async-done | bytes 442400 | tf_op jit(solution)/shard_map/all_to_all | solution.py:348
  109.4 4.0 %copy.37 = bf16[3,3,3,32,4,64]{5,3,4,2,1,0:T(8,128)(2,1)} copy(bf16[3,3,3,32,4,64]{3,2,1,0,5,4:T(4,128)(2,1)} %bitcast.54) | data formatting | bytes 884736 | tf_op jit(solution)/shard_map/all_to_all | solution.py:348
  119.7 3.8 %shard_map.121 = (bf16[4,64,1024]{2,1,0:T(8,128)(2,1)S(1)}, bf16[4,64,1024]{2,1,0:T(8,128)(2,1)S(1)}) custom-call(s32[1]{0:T(128)} %bitcast.me_ref, bf16[4,32,1024]{2,1,0:T(8,128)(2,1)S(1)} %get-tuple-element.20.refs_0_.own, bf16[1,32,1024]{2,1,0:T(8,128)(2,1)S(1)} %collective-permute-done.10.refs_1_.up, bf16[1,32,1024]{2,1,0:T(8,128)(2,1)S(1)} %copy-done.17, ...), custom_call_target="tpu_custom_call" | custom-call | bytes 3588100 | tf_op jit(solution)/shard_map/pallas_call | solution.py:47
  124.7 4.8 %collective-permute-start.17 = (bf16[1,64,1024]{2,1,0:T(8,128)(2,1)S(1)}, bf16[1,64,1024]{2,1,0:T(8,128)(2,1)S(1)}, u32[]{:S(2)}, u32[]{:S(2)}) collective-permute-start(bf16[1,64,1024]{2,1,0:T(8,128)(2,1)S(1)} %get-tuple-element.51), channel_id=1, source_target_pairs={{0,4},{1,5},{2,6},{3,7},{4,8},{5,9},{6,10},{7,11},{8,12},{9,13},{1... | collective-permute-start | bytes 393224 | tf_op jit(solution)/shard_map/ppermute | solution.py:285
  129.6 6.5 %collective-permute-start.20 = (bf16[1,64,1024]{2,1,0:T(8,128)(2,1)S(1)}, bf16[1,64,1024]{2,1,0:T(8,128)(2,1)S(1)}, u32[]{:S(2)}, u32[]{:S(2)}) collective-permute-start(bf16[1,64,1024]{2,1,0:T(8,128)(2,1)S(1)} %get-tuple-element.51), channel_id=1, source_target_pairs={{0,6},{1,7},{2,4},{3,5},{4,10},{5,11},{6,8},{7,9},{8,14},{9,15},{1... | collective-permute-start | bytes 393224 | tf_op jit(solution)/shard_map/ppermute | solution.py:285
  139.4 5.0 %collective-permute-done.18.refs_2_ = bf16[1,64,1024]{2,1,0:T(8,128)(2,1)S(1)} collective-permute-done((bf16[1,64,1024]{2,1,0:T(8,128)(2,1)S(1)}, bf16[1,64,1024]{2,1,0:T(8,128)(2,1)S(1)}, u32[]{:S(2)}, u32[]{:S(2)}) %collective-permute-start.18) | collective-permute-done | bytes 131104 | tf_op jit(solution)/shard_map/ppermute | solution.py:285
  144.5 3.6 %collective-permute-done.21.refs_5_ = bf16[1,64,1024]{2,1,0:T(8,128)(2,1)S(1)} collective-permute-done((bf16[1,64,1024]{2,1,0:T(8,128)(2,1)S(1)}, bf16[1,64,1024]{2,1,0:T(8,128)(2,1)S(1)}, u32[]{:S(2)}, u32[]{:S(2)}) %collective-permute-start.21) | collective-permute-done | bytes 131104 | tf_op jit(solution)/shard_map/ppermute | solution.py:285
  151.6 5.4 %shard_map.122 = (bf16[4,32,1024]{2,1,0:T(8,128)(2,1)S(1)}, bf16[6,256,1280]{2,1,0:T(8,128)(2,1)}) custom-call(s32[1]{0:T(128)} %bitcast.me_ref, bf16[4,64,1024]{2,1,0:T(8,128)(2,1)S(1)} %get-tuple-element.22.refs_0_, bf16[1,64,1024]{2,1,0:T(8,128)(2,1)S(1)} %collective-permute-done.17.refs_1_, bf16[1,64,1024]{2,1,0:T(8,128)(2,1)S(1)} %collective-permute-done.18.refs_2_, ...), custom_call_target="tpu_custom_call" | custom-call | bytes 8306692 | tf_op jit(solution)/shard_map/pallas_call | solution.py:47
  157.7 3.8 %collective-permute-start.24 = (bf16[1,32,1024]{2,1,0:T(8,128)(2,1)S(1)}, bf16[1,32,1024]{2,1,0:T(8,128)(2,1)S(1)}, u32[]{:S(2)}, u32[]{:S(2)}) collective-permute-start(bf16[1,32,1024]{2,1,0:T(8,128)(2,1)S(1)} %get-tuple-element.53), channel_id=1, source_target_pairs={{0,4},{1,5},{2,6},{3,7},{4,8},{5,9},{6,10},{7,11},{8,12},{9,13},{1... | collective-permute-start | bytes 196616 | tf_op jit(solution)/shard_map/ppermute | solution.py:285
  161.5 5.6 %collective-permute-start.27 = (bf16[1,32,1024]{2,1,0:T(8,128)(2,1)S(1)}, bf16[1,32,1024]{2,1,0:T(8,128)(2,1)S(1)}, u32[]{:S(2)}, u32[]{:S(2)}) collective-permute-start(bf16[1,32,1024]{2,1,0:T(8,128)(2,1)S(1)} %get-tuple-element.53), channel_id=1, source_target_pairs={{0,6},{1,7},{2,4},{3,5},{4,10},{5,11},{6,8},{7,9},{8,14},{9,15},{1... | collective-permute-start | bytes 196616 | tf_op jit(solution)/shard_map/ppermute | solution.py:285
  174.9 15.8 %all-to-all-start.5 = ((bf16[32,27,256]{2,1,0:T(8,128)(2,1)}), bf16[32,27,256]{2,1,0:T(8,128)(2,1)}, u32[]{:S(2)}, u32[]{:S(2)}) async-start(bf16[32,27,256]{2,1,0:T(8,128)(2,1)} %reshape.91), calls=%async_computation.5 | async-start | bytes 1048576 | tf_op jit(solution)/shard_map/all_to_all | solution.py:303
  194.7 6.8 %all-to-all-done.5 = bf16[32,27,256]{2,1,0:T(8,128)(2,1)} async-done(((bf16[32,27,256]{2,1,0:T(8,128)(2,1)}), bf16[32,27,256]{2,1,0:T(8,128)(2,1)}, u32[]{:S(2)}, u32[]{:S(2)}) %all-to-all-start.5) | async-done | bytes 442400 | tf_op jit(solution)/shard_map/all_to_all | solution.py:303
  203.5 4.6 %all-to-all-start.6 = ((bf16[32,27,256]{2,1,0:T(8,128)(2,1)}), bf16[32,27,256]{2,1,0:T(8,128)(2,1)}, u32[]{:S(2)}, u32[]{:S(2)}) async-start(bf16[32,27,256]{2,1,0:T(8,128)(2,1)} %broadcast_in_dim.11), calls=%async_computation.6 | async-start | bytes 1048576 | tf_op jit(solution)/shard_map/all_to_all | solution.py:305
  211.1 3.5 %collective-permute-start.31 = (bf16[1,64,256]{2,1,0:T(8,128)(2,1)S(1)}, bf16[1,64,256]{2,1,0:T(8,128)(2,1)S(1)}, u32[]{:S(2)}, u32[]{:S(2)}) collective-permute-start(bf16[1,64,256]{2,1,0:T(8,128)(2,1)S(1)} %slice.81), channel_id=1, source_target_pairs={{0,4},{1,5},{2,6},{3,7},{4,8},{5,9},{6,10},{7,11},{8,12},{9,13},{1... | collective-permute-start | bytes 98312 | tf_op jit(solution)/shard_map/ppermute | solution.py:285
  216.7 6.2 %collective-permute-start.33 = (bf16[1,64,128]{2,1,0:T(8,128)(2,1)S(1)}, bf16[1,64,128]{2,1,0:T(8,128)(2,1)S(1)}, u32[]{:S(2)}, u32[]{:S(2)}) collective-permute-start(bf16[1,64,128]{2,1,0:T(8,128)(2,1)S(1)} %slice.83), channel_id=1, source_target_pairs={{0,5},{1,6},{2,7},{4,9},{5,10},{6,11},{8,13},{9,14},{10,15},{12,17... | collective-permute-start | bytes 49160 | tf_op jit(solution)/shard_map/ppermute | solution.py:285
  226.8 6.9 %all-to-all-start.3 = ((bf16[32,2,864]{2,1,0:T(2,128)(2,1)}), bf16[32,2,864]{2,1,0:T(2,128)(2,1)S(1)}, u32[]{:S(2)}, u32[]{:S(2)}) async-start(bf16[32,2,864]{2,1,0:T(2,128)(2,1)} %reshape.101), calls=%async_computation.3 | async-start | bytes 229376 | tf_op jit(solution)/shard_map/all_to_all | solution.py:303
  238.7 3.6 %all-to-all-done.3 = bf16[32,2,864]{2,1,0:T(2,128)(2,1)S(1)} async-done(((bf16[32,2,864]{2,1,0:T(2,128)(2,1)}), bf16[32,2,864]{2,1,0:T(2,128)(2,1)S(1)}, u32[]{:S(2)}, u32[]{:S(2)}) %all-to-all-start.3) | async-done | bytes 110624 | tf_op jit(solution)/shard_map/all_to_all | solution.py:303
  242.2 5.0 %all-to-all-start.1 = ((f32[128,8,128]{2,1,0:T(8,128)}), f32[128,8,128]{2,1,0:T(8,128)S(1)}, u32[]{:S(2)}, u32[]{:S(2)}) async-start(f32[128,8,128]{2,1,0:T(8,128)} %bitcast.20), calls=%async_computation.1 | async-start | bytes 1048576 | tf_op jit(solution)/shard_map/all_to_all | solution.py:303
  248.5 11.6 %all-to-all-done.1 = f32[128,8,128]{2,1,0:T(8,128)S(1)} async-done(((f32[128,8,128]{2,1,0:T(8,128)}), f32[128,8,128]{2,1,0:T(8,128)S(1)}, u32[]{:S(2)}, u32[]{:S(2)}) %all-to-all-start.1) | async-done | bytes 524320 | tf_op jit(solution)/shard_map/all_to_all | solution.py:303
  260.0 4.6 %all-to-all-start.4 = ((bf16[32,2,864]{2,1,0:T(2,128)(2,1)}), bf16[32,2,864]{2,1,0:T(2,128)(2,1)S(1)}, u32[]{:S(2)}, u32[]{:S(2)}) async-start(bf16[32,2,864]{2,1,0:T(2,128)(2,1)} %reshape.103), calls=%async_computation.4 | async-start | bytes 229376 | tf_op jit(solution)/shard_map/all_to_all | solution.py:305
  264.8 8.3 %all-to-all-done.4 = bf16[32,2,864]{2,1,0:T(2,128)(2,1)S(1)} async-done(((bf16[32,2,864]{2,1,0:T(2,128)(2,1)}), bf16[32,2,864]{2,1,0:T(2,128)(2,1)S(1)}, u32[]{:S(2)}, u32[]{:S(2)}) %all-to-all-start.4) | async-done | bytes 110624 | tf_op jit(solution)/shard_map/all_to_all | solution.py:305
  274.0 5.0 %all-to-all-start.2 = ((f32[128,8,128]{2,1,0:T(8,128)}), f32[128,8,128]{2,1,0:T(8,128)S(1)}, u32[]{:S(2)}, u32[]{:S(2)}) async-start(f32[128,8,128]{2,1,0:T(8,128)} %broadcast_in_dim.9), calls=%async_computation.2 | async-start | bytes 1048576 | tf_op jit(solution)/shard_map/all_to_all | solution.py:305
  283.2 8.7 %all-to-all-done.2 = f32[128,8,128]{2,1,0:T(8,128)S(1)} async-done(((f32[128,8,128]{2,1,0:T(8,128)}), f32[128,8,128]{2,1,0:T(8,128)S(1)}, u32[]{:S(2)}, u32[]{:S(2)}) %all-to-all-start.2) | async-done | bytes 524320 | tf_op jit(solution)/shard_map/all_to_all | solution.py:305
  (197 shorter events, 106.4 us)
Async XLA Ops:
  21.3 14.4 %collective-permute-start.5 = (bf16[4,64,256]{2,1,0:T(8,128)(2,1)S(1)}, bf16[4,64,256]{2,1,0:T(8,128)(2,1)S(1)}, u32[]{:S(2)}, u32[]{:S(2)}) collective-permute-start(bf16[4,64,256]{2,1,0:T(8,128)(2,1)S(1)} %get-tuple-element.19.refs_0_), channel_id=1, source_target_pairs={{0,2},{1,3},{2,0},{3,1},{4,6},{5,7},{6,4},{7,5},{8,10},{9,11},{10,... | collective-permute-start | bytes 393224 | tf_op jit(solution)/shard_map/ppermute | solution.py:285
  26.5 9.9 %collective-permute-start.3 = (bf16[1,64,256]{2,1,0:T(8,128)(2,1)S(1)}, bf16[1,64,256]{2,1,0:T(8,128)(2,1)S(1)}, u32[]{:S(2)}, u32[]{:S(2)}) collective-permute-start(bf16[1,64,256]{2,1,0:T(8,128)(2,1)S(1)} %get-tuple-element.60), channel_id=1, source_target_pairs={{0,4},{1,5},{2,6},{3,7},{4,8},{5,9},{6,10},{7,11},{8,12},{9,13},{1... | collective-permute-start | bytes 98312 | tf_op jit(solution)/shard_map/ppermute | solution.py:285
  30.2 10.8 %collective-permute-start.6 = (bf16[1,64,256]{2,1,0:T(8,128)(2,1)S(1)}, bf16[1,64,256]{2,1,0:T(8,128)(2,1)S(1)}, u32[]{:S(2)}, u32[]{:S(2)}) collective-permute-start(bf16[1,64,256]{2,1,0:T(8,128)(2,1)S(1)} %get-tuple-element.60), channel_id=1, source_target_pairs={{0,6},{1,7},{2,4},{3,5},{4,10},{5,11},{6,8},{7,9},{8,14},{9,15},{1... | collective-permute-start | bytes 98312 | tf_op jit(solution)/shard_map/ppermute | solution.py:285
  34.4 10.8 %collective-permute-start.7 = (bf16[1,64,256]{2,1,0:T(8,128)(2,1)S(1)}, bf16[1,64,256]{2,1,0:T(8,128)(2,1)S(1)}, u32[]{:S(2)}, u32[]{:S(2)}) collective-permute-start(bf16[1,64,256]{2,1,0:T(8,128)(2,1)S(1)} %get-tuple-element.59), channel_id=1, source_target_pairs={{4,2},{5,3},{6,0},{7,1},{8,6},{9,7},{10,4},{11,5},{12,10},{13,11},... | collective-permute-start | bytes 98312 | tf_op jit(solution)/shard_map/ppermute | solution.py:285
  35.7 21.0 %collective-permute-start.8 = (bf16[4,64,256]{2,1,0:T(8,128)(2,1)S(1)}, bf16[4,64,256]{2,1,0:T(8,128)(2,1)S(1)}, u32[]{:S(2)}, u32[]{:S(2)}) collective-permute-start(bf16[4,64,256]{2,1,0:T(8,128)(2,1)S(1)} %get-tuple-element.19.refs_0_), channel_id=1, source_target_pairs={{0,1},{1,0},{2,3},{3,2},{4,5},{5,4},{6,7},{7,6},{8,9},{9,8},{10,11... | collective-permute-start | bytes 393224 | tf_op jit(solution)/shard_map/ppermute | solution.py:285
  45.8 11.6 %collective-permute-start.9 = (bf16[8,64,256]{2,1,0:T(8,128)(2,1)}, bf16[8,64,256]{2,1,0:T(8,128)(2,1)S(1)}, u32[]{:S(2)}, u32[]{:S(2)}) collective-permute-start(bf16[8,64,256]{2,1,0:T(8,128)(2,1)} %constant_dynamic-update-slice_fusion), channel_id=1, source_target_pairs={{0,1},{1,0},{2,3},{3,2},{4,5},{5,4},{6,7},{7,6},{8,9},{9,8},{10,11... | collective-permute-start | bytes 786440 | tf_op jit(solution)/shard_map/ppermute | solution.py:285
  63.0 13.2 %collective-permute-start.12 = (bf16[4,32,1024]{2,1,0:T(8,128)(2,1)S(1)}, bf16[4,32,1024]{2,1,0:T(8,128)(2,1)S(1)}, u32[]{:S(2)}, u32[]{:S(2)}) collective-permute-start(bf16[4,32,1024]{2,1,0:T(8,128)(2,1)S(1)} %get-tuple-element.20.refs_0_.own), channel_id=1, source_target_pairs={{0,2},{1,3},{2,0},{3,1},{4,6},{5,7},{6,4},{7,5},{8,10},{9,11},{10,... | collective-permute-start | bytes 786440 | tf_op jit(solution)/shard_map/ppermute | solution.py:285
  64.0 12.9 %collective-permute-start.10 = (bf16[1,32,1024]{2,1,0:T(8,128)(2,1)S(1)}, bf16[1,32,1024]{2,1,0:T(8,128)(2,1)S(1)}, u32[]{:S(2)}, u32[]{:S(2)}) collective-permute-start(bf16[1,32,1024]{2,1,0:T(8,128)(2,1)S(1)} %get-tuple-element.55), channel_id=1, source_target_pairs={{0,4},{1,5},{2,6},{3,7},{4,8},{5,9},{6,10},{7,11},{8,12},{9,13},{1... | collective-permute-start | bytes 196616 | tf_op jit(solution)/shard_map/ppermute | solution.py:285
  69.9 11.5 %collective-permute-start.13 = (bf16[1,32,1024]{2,1,0:T(8,128)(2,1)S(1)}, bf16[1,32,1024]{2,1,0:T(8,128)(2,1)S(1)}, u32[]{:S(2)}, u32[]{:S(2)}) collective-permute-start(bf16[1,32,1024]{2,1,0:T(8,128)(2,1)S(1)} %get-tuple-element.55), channel_id=1, source_target_pairs={{0,6},{1,7},{2,4},{3,5},{4,10},{5,11},{6,8},{7,9},{8,14},{9,15},{1... | collective-permute-start | bytes 196616 | tf_op jit(solution)/shard_map/ppermute | solution.py:285
  74.9 10.6 %collective-permute-start.14 = (bf16[1,32,1024]{2,1,0:T(8,128)(2,1)S(1)}, bf16[1,32,1024]{2,1,0:T(8,128)(2,1)S(1)}, u32[]{:S(2)}, u32[]{:S(2)}) collective-permute-start(bf16[1,32,1024]{2,1,0:T(8,128)(2,1)S(1)} %get-tuple-element.54), channel_id=1, source_target_pairs={{4,2},{5,3},{6,0},{7,1},{8,6},{9,7},{10,4},{11,5},{12,10},{13,11},... | collective-permute-start | bytes 196616 | tf_op jit(solution)/shard_map/ppermute | solution.py:285
  86.1 31.1 %collective-permute-start.16 = (bf16[8,32,1024]{2,1,0:T(8,128)(2,1)}, bf16[8,32,1024]{2,1,0:T(8,128)(2,1)}, u32[]{:S(2)}, u32[]{:S(2)}) collective-permute-start(bf16[8,32,1024]{2,1,0:T(8,128)(2,1)} %constant_dynamic-update-slice_fusion.5), channel_id=1, source_target_pairs={{0,1},{1,0},{2,3},{3,2},{4,5},{5,4},{6,7},{7,6},{8,9},{9,8},{10,11... | collective-permute-start | bytes 1572872 | tf_op jit(solution)/shard_map/ppermute | solution.py:285
  93.8 12.9 %all-to-all-start = ((bf16[4,2,27648]{2,1,0:T(2,128)(2,1)}), bf16[4,2,27648]{2,1,0:T(2,128)(2,1)S(1)}, u32[]{:S(2)}, u32[]{:S(2)}) async-start(bf16[4,2,27648]{2,1,0:T(2,128)(2,1)} %reshape.99), calls=%async_computation | async-start | bytes 884736 | tf_op jit(solution)/shard_map/all_to_all | solution.py:348
  97.2 20.0 %collective-permute-start.15 = (bf16[4,32,1024]{2,1,0:T(8,128)(2,1)S(1)}, bf16[4,32,1024]{2,1,0:T(8,128)(2,1)}, u32[]{:S(2)}, u32[]{:S(2)}) collective-permute-start(bf16[4,32,1024]{2,1,0:T(8,128)(2,1)S(1)} %get-tuple-element.20.refs_0_.own), channel_id=1, source_target_pairs={{0,1},{1,0},{2,3},{3,2},{4,5},{5,4},{6,7},{7,6},{8,9},{9,8},{10,11... | collective-permute-start | bytes 786440 | tf_op jit(solution)/shard_map/ppermute | solution.py:285
  124.3 15.0 %collective-permute-start.19 = (bf16[4,64,1024]{2,1,0:T(8,128)(2,1)S(1)}, bf16[4,64,1024]{2,1,0:T(8,128)(2,1)S(1)}, u32[]{:S(2)}, u32[]{:S(2)}) collective-permute-start(bf16[4,64,1024]{2,1,0:T(8,128)(2,1)S(1)} %get-tuple-element.22.refs_0_), channel_id=1, source_target_pairs={{0,2},{1,3},{2,0},{3,1},{4,6},{5,7},{6,4},{7,5},{8,10},{9,11},{10,... | collective-permute-start | bytes 1572872 | tf_op jit(solution)/shard_map/ppermute | solution.py:285
  124.7 14.6 %collective-permute-start.17 = (bf16[1,64,1024]{2,1,0:T(8,128)(2,1)S(1)}, bf16[1,64,1024]{2,1,0:T(8,128)(2,1)S(1)}, u32[]{:S(2)}, u32[]{:S(2)}) collective-permute-start(bf16[1,64,1024]{2,1,0:T(8,128)(2,1)S(1)} %get-tuple-element.51), channel_id=1, source_target_pairs={{0,4},{1,5},{2,6},{3,7},{4,8},{5,9},{6,10},{7,11},{8,12},{9,13},{1... | collective-permute-start | bytes 393224 | tf_op jit(solution)/shard_map/ppermute | solution.py:285
  129.6 14.9 %collective-permute-start.20 = (bf16[1,64,1024]{2,1,0:T(8,128)(2,1)S(1)}, bf16[1,64,1024]{2,1,0:T(8,128)(2,1)S(1)}, u32[]{:S(2)}, u32[]{:S(2)}) collective-permute-start(bf16[1,64,1024]{2,1,0:T(8,128)(2,1)S(1)} %get-tuple-element.51), channel_id=1, source_target_pairs={{0,6},{1,7},{2,4},{3,5},{4,10},{5,11},{6,8},{7,9},{8,14},{9,15},{1... | collective-permute-start | bytes 393224 | tf_op jit(solution)/shard_map/ppermute | solution.py:285
  137.4 10.7 %collective-permute-start.21 = (bf16[1,64,1024]{2,1,0:T(8,128)(2,1)S(1)}, bf16[1,64,1024]{2,1,0:T(8,128)(2,1)S(1)}, u32[]{:S(2)}, u32[]{:S(2)}) collective-permute-start(bf16[1,64,1024]{2,1,0:T(8,128)(2,1)S(1)} %get-tuple-element.50), channel_id=1, source_target_pairs={{4,2},{5,3},{6,0},{7,1},{8,6},{9,7},{10,4},{11,5},{12,10},{13,11},... | collective-permute-start | bytes 393224 | tf_op jit(solution)/shard_map/ppermute | solution.py:285
  157.0 33.8 %collective-permute-start.26 = (bf16[4,32,1024]{2,1,0:T(8,128)(2,1)S(1)}, bf16[4,32,1024]{2,1,0:T(8,128)(2,1)S(1)}, u32[]{:S(2)}, u32[]{:S(2)}) collective-permute-start(bf16[4,32,1024]{2,1,0:T(8,128)(2,1)S(1)} %get-tuple-element.24.refs_0_), channel_id=1, source_target_pairs={{0,2},{1,3},{2,0},{3,1},{4,6},{5,7},{6,4},{7,5},{8,10},{9,11},{10,... | collective-permute-start | bytes 786440 | tf_op jit(solution)/shard_map/ppermute | solution.py:285
  157.7 33.7 %collective-permute-start.24 = (bf16[1,32,1024]{2,1,0:T(8,128)(2,1)S(1)}, bf16[1,32,1024]{2,1,0:T(8,128)(2,1)S(1)}, u32[]{:S(2)}, u32[]{:S(2)}) collective-permute-start(bf16[1,32,1024]{2,1,0:T(8,128)(2,1)S(1)} %get-tuple-element.53), channel_id=1, source_target_pairs={{0,4},{1,5},{2,6},{3,7},{4,8},{5,9},{6,10},{7,11},{8,12},{9,13},{1... | collective-permute-start | bytes 196616 | tf_op jit(solution)/shard_map/ppermute | solution.py:285
  161.5 31.2 %collective-permute-start.27 = (bf16[1,32,1024]{2,1,0:T(8,128)(2,1)S(1)}, bf16[1,32,1024]{2,1,0:T(8,128)(2,1)S(1)}, u32[]{:S(2)}, u32[]{:S(2)}) collective-permute-start(bf16[1,32,1024]{2,1,0:T(8,128)(2,1)S(1)} %get-tuple-element.53), channel_id=1, source_target_pairs={{0,6},{1,7},{2,4},{3,5},{4,10},{5,11},{6,8},{7,9},{8,14},{9,15},{1... | collective-permute-start | bytes 196616 | tf_op jit(solution)/shard_map/ppermute | solution.py:285
  167.1 25.0 %collective-permute-start.25 = (bf16[1,32,1024]{2,1,0:T(8,128)(2,1)S(1)}, bf16[1,32,1024]{2,1,0:T(8,128)(2,1)S(1)}, u32[]{:S(2)}, u32[]{:S(2)}) collective-permute-start(bf16[1,32,1024]{2,1,0:T(8,128)(2,1)S(1)} %get-tuple-element.52), channel_id=1, source_target_pairs={{4,0},{5,1},{6,2},{7,3},{8,4},{9,5},{10,6},{11,7},{12,8},{13,9},{1... | collective-permute-start | bytes 196616 | tf_op jit(solution)/shard_map/ppermute | solution.py:285
  168.4 25.0 %collective-permute-start.28 = (bf16[1,32,1024]{2,1,0:T(8,128)(2,1)S(1)}, bf16[1,32,1024]{2,1,0:T(8,128)(2,1)S(1)}, u32[]{:S(2)}, u32[]{:S(2)}) collective-permute-start(bf16[1,32,1024]{2,1,0:T(8,128)(2,1)S(1)} %get-tuple-element.52), channel_id=1, source_target_pairs={{4,2},{5,3},{6,0},{7,1},{8,6},{9,7},{10,4},{11,5},{12,10},{13,11},... | collective-permute-start | bytes 196616 | tf_op jit(solution)/shard_map/ppermute | solution.py:285
  174.9 26.6 %all-to-all-start.5 = ((bf16[32,27,256]{2,1,0:T(8,128)(2,1)}), bf16[32,27,256]{2,1,0:T(8,128)(2,1)}, u32[]{:S(2)}, u32[]{:S(2)}) async-start(bf16[32,27,256]{2,1,0:T(8,128)(2,1)} %reshape.91), calls=%async_computation.5 | async-start | bytes 1048576 | tf_op jit(solution)/shard_map/all_to_all | solution.py:303
  194.7 15.4 %collective-permute-start.30 = (bf16[8,32,1024]{2,1,0:T(8,128)(2,1)}, bf16[8,32,1024]{2,1,0:T(8,128)(2,1)S(1)}, u32[]{:S(2)}, u32[]{:S(2)}) collective-permute-start(bf16[8,32,1024]{2,1,0:T(8,128)(2,1)} %constant_dynamic-update-slice_fusion.15), channel_id=1, source_target_pairs={{0,1},{1,0},{2,3},{3,2},{4,5},{5,4},{6,7},{7,6},{8,9},{9,8},{10,11... | collective-permute-start | bytes 1572872 | tf_op jit(solution)/shard_map/ppermute | solution.py:285
  203.5 23.3 %all-to-all-start.6 = ((bf16[32,27,256]{2,1,0:T(8,128)(2,1)}), bf16[32,27,256]{2,1,0:T(8,128)(2,1)}, u32[]{:S(2)}, u32[]{:S(2)}) async-start(bf16[32,27,256]{2,1,0:T(8,128)(2,1)} %broadcast_in_dim.11), calls=%async_computation.6 | async-start | bytes 1048576 | tf_op jit(solution)/shard_map/all_to_all | solution.py:305
  211.1 23.7 %collective-permute-start.31 = (bf16[1,64,256]{2,1,0:T(8,128)(2,1)S(1)}, bf16[1,64,256]{2,1,0:T(8,128)(2,1)S(1)}, u32[]{:S(2)}, u32[]{:S(2)}) collective-permute-start(bf16[1,64,256]{2,1,0:T(8,128)(2,1)S(1)} %slice.81), channel_id=1, source_target_pairs={{0,4},{1,5},{2,6},{3,7},{4,8},{5,9},{6,10},{7,11},{8,12},{9,13},{1... | collective-permute-start | bytes 98312 | tf_op jit(solution)/shard_map/ppermute | solution.py:285
  214.6 20.2 %collective-permute-start.32 = (bf16[4,64,128]{2,1,0:T(8,128)(2,1)S(1)}, bf16[4,64,128]{2,1,0:T(8,128)(2,1)S(1)}, u32[]{:S(2)}, u32[]{:S(2)}) collective-permute-start(bf16[4,64,128]{2,1,0:T(8,128)(2,1)S(1)} %slice.82), channel_id=1, source_target_pairs={{0,1},{1,2},{2,3},{4,5},{5,6},{6,7},{8,9},{9,10},{10,11},{12,13},{... | collective-permute-start | bytes 196616 | tf_op jit(solution)/shard_map/ppermute | solution.py:285
  216.7 18.1 %collective-permute-start.33 = (bf16[1,64,128]{2,1,0:T(8,128)(2,1)S(1)}, bf16[1,64,128]{2,1,0:T(8,128)(2,1)S(1)}, u32[]{:S(2)}, u32[]{:S(2)}) collective-permute-start(bf16[1,64,128]{2,1,0:T(8,128)(2,1)S(1)} %slice.83), channel_id=1, source_target_pairs={{0,5},{1,6},{2,7},{4,9},{5,10},{6,11},{8,13},{9,14},{10,15},{12,17... | collective-permute-start | bytes 49160 | tf_op jit(solution)/shard_map/ppermute | solution.py:285
  226.8 15.4 %all-to-all-start.3 = ((bf16[32,2,864]{2,1,0:T(2,128)(2,1)}), bf16[32,2,864]{2,1,0:T(2,128)(2,1)S(1)}, u32[]{:S(2)}, u32[]{:S(2)}) async-start(bf16[32,2,864]{2,1,0:T(2,128)(2,1)} %reshape.101), calls=%async_computation.3 | async-start | bytes 229376 | tf_op jit(solution)/shard_map/all_to_all | solution.py:303
  242.2 17.8 %all-to-all-start.1 = ((f32[128,8,128]{2,1,0:T(8,128)}), f32[128,8,128]{2,1,0:T(8,128)S(1)}, u32[]{:S(2)}, u32[]{:S(2)}) async-start(f32[128,8,128]{2,1,0:T(8,128)} %bitcast.20), calls=%async_computation.1 | async-start | bytes 1048576 | tf_op jit(solution)/shard_map/all_to_all | solution.py:303
  260.0 13.1 %all-to-all-start.4 = ((bf16[32,2,864]{2,1,0:T(2,128)(2,1)}), bf16[32,2,864]{2,1,0:T(2,128)(2,1)S(1)}, u32[]{:S(2)}, u32[]{:S(2)}) async-start(bf16[32,2,864]{2,1,0:T(2,128)(2,1)} %reshape.103), calls=%async_computation.4 | async-start | bytes 229376 | tf_op jit(solution)/shard_map/all_to_all | solution.py:305
  274.0 17.8 %all-to-all-start.2 = ((f32[128,8,128]{2,1,0:T(8,128)}), f32[128,8,128]{2,1,0:T(8,128)S(1)}, u32[]{:S(2)}, u32[]{:S(2)}) async-start(f32[128,8,128]{2,1,0:T(8,128)} %broadcast_in_dim.9), calls=%async_computation.2 | async-start | bytes 1048576 | tf_op jit(solution)/shard_map/all_to_all | solution.py:305
  (43 other events, 385.7 us)

commit v2 on v1

v2 whole, which is shorter than its diff:
```python
import jax
import jax.numpy as jnp
import numpy as np
from jax import lax
from jax.experimental import pallas as pl
from jax.experimental.pallas import tpu as pltpu
from jax.sharding import PartitionSpec as P

BF = jnp.bfloat16
F32 = jnp.float32
BOTH = ("space", "chan")
LANES = 128
VMEM_LIMIT = 20 * 1024 * 1024


def mm(left, right):
    return lax.dot_general(left, right, (((1,), (0,)), ((), ())), preferred_element_type=F32)


def mm_nt(left, right):
    return lax.dot_general(left, right, (((1,), (1,)), ((), ())), preferred_element_type=F32)


def lane_of(shape):
    return lax.broadcasted_iota(jnp.int32, shape, len(shape) - 1)


def shifted(value, step):
    width = value.shape[1]
    turned = pltpu.roll(value, step % width, 1)
    edge = 0 if step == 1 else LANES - 1
    return jnp.where(lane_of(value.shape) % LANES == edge, 0.0, turned)


def activate(pre):
    sigma = jax.nn.sigmoid(pre)
    return pre * sigma, sigma * (1.0 + pre * (1.0 - sigma))


def call(kernel, outs, args, scratch=(), flops=0, anywhere=()):
    specs = []
    for place, a in enumerate(args):
        space = pltpu.SMEM if a.dtype == jnp.int32 else pltpu.VMEM
        specs.append(pl.BlockSpec(memory_space=pl.ANY if place in anywhere else space))
    size = sum(a.size * a.dtype.itemsize for a in args)
    size += sum(int(np.prod(s)) * jnp.dtype(t).itemsize for s, t in outs)
    buffers = [pltpu.VMEM(s, t) for s, t in scratch]
    if anywhere:
        buffers.append(pltpu.SemaphoreType.DMA((14,)))
    return pl.pallas_call(
        kernel,
        out_shape=[jax.ShapeDtypeStruct(s, t) for s, t in outs],
        in_specs=specs,
        out_specs=[pl.BlockSpec(memory_space=pltpu.VMEM)] * len(outs),
        scratch_shapes=buffers,
        compiler_params=pltpu.CompilerParams(vmem_limit_bytes=VMEM_LIMIT),
        cost_estimate=pl.CostEstimate(flops=flops, bytes_accessed=size, transcendentals=0),
    )(*args)


def first_layers_kernel(vol, phases, rows, w_one, w_two, field, act_one, slope_one, body, first, last, slope_two):
    for d in range(19):
        block = jnp.reshape(vol[:, d], (64, 512))
        split = mm(block, phases[...]).astype(BF)
        stacked = jnp.concatenate([split[:, p * 128 : p * 128 + 128] for p in range(5)], 0)
        field[d] = mm(rows[...], stacked).astype(BF)
    for d in range(9):
        columns = []
        for h in range(5):
            parts = [field[2 * d + a, h * 64 : h * 64 + 96] for a in range(3)]
            columns.append(jnp.concatenate(parts, 0))
        pre = mm(w_one[...], jnp.concatenate(columns, 1))
        act, slope = activate(pre)
        if d < 8:
            slope_one[d] = slope[:, :512]
        beside = shifted(act[:32], -1)
        for h in range(5):
            lanes = slice(h * 128, h * 128 + 128)
            act_one[d, h * 96 : h * 96 + 64] = act[:, lanes].astype(BF)
            act_one[d, h * 96 + 64 : h * 96 + 96] = beside[:, lanes].astype(BF)
    for d in range(4):
        columns = []
        for h in range(2):
            parts = [act_one[2 * d + a, h * 192 : h * 192 + 288] for a in range(3)]
            columns.append(jnp.concatenate(parts, 0))
        pre = mm(w_two[...], jnp.concatenate(columns, 1))
        act, slope = activate(pre)
        slope_two[d] = slope
        steep = slope.astype(BF)
        body[d, :, :256] = act.astype(BF)
        body[d, :, 256:] = steep[:, 128:]
        for rim, at in ((first, 0), (last, 3)):
            if d == at:
                rim[0, :, :256] = act.astype(BF)
                rim[0, :, 256:] = steep


def prepare_kernel(me_ref, packed, w_three, w_four, w_two_back):
    me = me_ref[0]

    def tap_of(t, four):
        if four:
            return jnp.concatenate([packed[j, t, :32] for j in range(4)], 0)
        return jnp.concatenate([packed[j, t, 32:, :128] for j in range(4)], 0)

    def own(count, wide):
        row = lax.broadcasted_iota(jnp.int32, (count, wide), 0)
        return jnp.where(lane_of((count, wide)) == row + me * count, 1.0, 0.0).astype(BF)

    for out, four, count in ((w_three, False, 32), (w_four, True, 64)):
        pick = own(count, 4 * count)
        for c in range(3):
            rows = jnp.concatenate([tap_of(ab * 3 + c, four) for ab in range(9)], 0)
            out[c * count : c * count + count] = mm_nt(pick, rows).astype(BF)
    w_two_back[...] = flipped_weights([tap_of(t, False) for t in range(27)])


def taps_of(field, d, start, width):
    parts = []
    for a in range(3):
        for b in range(3):
            parts.append(field[d + a, :, pl.ds(start + b * LANES, width)])
    return jnp.concatenate(parts, 0)


def shift_sum(product, channels):
    low = product[:channels]
    mid = product[channels : 2 * channels]
    high = product[2 * channels :]
    return shifted(low, 1) + mid + shifted(high, -1)


def clear_rims(field):
    depth, channels, lanes = field.shape
    rim = jnp.zeros((depth, channels, LANES), BF)
    field[:, :, :LANES] = rim
    field[:, :, lanes - LANES :] = rim


def arrive(refs, sems, target, up=1, width=1024):
    copies = []
    for k in range(4):
        body, rim = refs[2 * k], refs[2 * k + 1]
        lanes = pl.ds(0, width)
        sources = (body.at[:, :, lanes], rim.at[pl.ds(0, up), :, lanes], rim.at[pl.ds(up, 1), :, lanes])
        for piece, source in enumerate(sources):
            copies.append(pltpu.make_async_copy(source, target(k, piece), sems.at[3 * k + piece]))
    for copy in copies:
        copy.start()
    return copies


def assemble(field, me, refs, sems, channels, up=1, rim=1):
    planes = (pl.ds(up, 4), pl.ds(0, up), pl.ds(up + 4, 1))

    def target(k, piece):
        at = pl.multiple_of((me ^ k) * channels, channels)
        return field.at[planes[piece], pl.ds(at, channels), pl.ds(rim * LANES, 8 * LANES)]

    return arrive(refs, sems, target, up)


def third_kernel(me_ref, *refs):
    blocks, weights = refs[:8], refs[8]
    act, slope, field, steep_front, steep_row, sems = refs[9:]
    me = me_ref[0]
    planes = (pl.ds(1, 4), pl.ds(0, 1), pl.ds(5, 1))

    def target(k, piece):
        at = pl.multiple_of(LANES + (me ^ k) * (2 * LANES), LANES)
        return field.at[planes[piece], :, pl.ds(at, 2 * LANES)]

    copies = arrive(blocks, sems, target, 1, 2 * LANES)
    clear_rims(field)
    for copy in copies:
        copy.wait()

    @pl.when(me == 0)
    def _():
        steep_front[:, :LANES] = jnp.zeros((64, LANES), BF)
        steep_row[...] = jnp.zeros((4, 64, LANES), BF)

    plane = pltpu.make_async_copy(
        blocks[1].at[0, :, pl.ds(256, 256)], steep_front.at[:, pl.ds(LANES, 256)], sems.at[12]
    )
    plane.start()
    plane.wait()
    for k in (1, 3):

        @pl.when((me > 0) & (me ^ k == me - 1))
        def _(k=k):
            corner = pltpu.make_async_copy(
                blocks[2 * k + 1].at[0, :, pl.ds(384, LANES)], steep_front.at[:, pl.ds(0, LANES)], sems.at[12]
            )
            row = pltpu.make_async_copy(blocks[2 * k].at[:, :, pl.ds(256, LANES)], steep_row, sems.at[13])
            corner.start()
            row.start()
            corner.wait()
            row.wait()

    for d in range(4):
        product = mm(weights[...], taps_of(field, d, 0, 1024))
        value, steep = activate(shift_sum(product, 32))
        act[d] = value.astype(BF)
        slope[d] = steep


def fourth_kernel(me_ref, *refs):
    blocks, weights, cotangent = refs[:8], refs[8], refs[9]
    features, back, field, sems = refs[10:]
    copies = assemble(field, me_ref[0], blocks, sems, 32)
    clear_rims(field)
    for copy in copies:
        copy.wait()
    for d in range(4):
        product = mm(weights[...], taps_of(field, d, 0, 1024))
        value, steep = activate(shift_sum(product, 64))
        features[d] = value.astype(BF)
        back[d] = (cotangent[d].astype(F32) * steep).astype(BF)


def flipped_weights(kernel):
    columns = []
    for a in range(3):
        for b in range(3):
            taps = [((2 - a) * 3 + 2 - b) * 3 + 2 - c for c in range(3)]
            columns.append(jnp.concatenate([kernel[t] for t in taps], 0))
    return jnp.concatenate(columns, 1)


def into_three_kernel(me_ref, *refs):
    blocks, kernel, slope = refs[:8], refs[8], refs[9]
    back, field, sems = refs[10:]
    copies = assemble(field, me_ref[0], blocks, sems, 64)
    clear_rims(field)
    weights = flipped_weights(kernel)
    for copy in copies:
        copy.wait()
    for d in range(4):
        product = mm(weights, taps_of(field, d, 0, 1024))
        back[d] = (shift_sum(product, 32) * slope[d]).astype(BF)


def three_shifts(value):
    wide = value.astype(F32)
    return jnp.concatenate([shifted(wide, 1).astype(BF), value, shifted(wide, -1).astype(BF)], 0)


def filter_grad(wide, gradient, first, rim):
    total = None
    for d in range(4):
        own = gradient[d + first, :, rim * LANES : (rim + 8) * LANES]
        term = mm_nt(taps_of(wide, d, 0, 1024), own)
        total = term if total is None else total + term
    return total


def grad_four_kernel(own, rim, gradient, grad, wide):
    clear_rims(wide)
    inside = slice(LANES, 9 * LANES)
    wide[0, :, inside] = three_shifts(rim[0])
    for d in range(4):
        wide[d + 1, :, inside] = three_shifts(own[d])
    wide[5, :, inside] = three_shifts(rim[1])
    grad[...] = filter_grad(wide, gradient, 1, 1).astype(BF)


def last_kernel(me_ref, *refs):
    blocks = refs[:8]
    weights, slope, front, row, act_one, slope_one, volume, w_back, act_two, grad_four = refs[8:18]
    out, field, shifts, wide, back_one, sems = refs[18:]
    me = me_ref[0]
    copies = assemble(field, me, blocks, sems, 32, up=2, rim=2)
    field[:, :, : 2 * LANES] = jnp.zeros((7, 128, 2 * LANES), BF)
    field[:, :, 10 * LANES :] = jnp.zeros((7, 128, LANES), BF)
    clear_rims(shifts)
    inside = slice(LANES, 9 * LANES)
    channels = pl.ds(pl.multiple_of(me * 16, 16), 16)
    for d in range(6):
        shifts[d, :, inside] = three_shifts(act_two[d, channels, inside])
    for t in range(27):
        out[t, :32] = grad_four[t]
    for t in range(27, 32):
        out[t] = jnp.zeros((48, 256), BF)
    for copy in copies:
        copy.wait()

    start = pl.multiple_of(me * (2 * LANES), LANES)
    for d in range(5):
        steep = front[...].astype(F32)
        if d > 0:
            steep = jnp.concatenate([row[d - 1].astype(F32), slope[d - 1]], 1)
        product = mm(weights[...], taps_of(field, d, start, 3 * LANES))
        value = shift_sum(product, 64) * steep
        value = value.astype(BF)
        beside = shifted(value.astype(F32), 1).astype(BF)
        for h in range(3):
            wide[d, h, :64] = value[:, h * 128 : h * 128 + 128]
            wide[d, h, 64:] = beside[:, h * 128 : h * 128 + 128]
    for d_odd in range(2):
        for h_odd in range(2):
            taps = [(a, b) for a in ((1,) if d_odd else (0, 2)) for b in ((1,) if h_odd else (0, 2))]
            mixed = jnp.concatenate([w_back[a * 3 + b] for a, b in taps], 1)
            columns = []
            for d in range(4):
                for h in range(2):
                    parts = [wide[d + 1 - a // 2, h + 1 - b // 2] for a, b in taps]
                    columns.append(jnp.concatenate(parts, 0))
            into = mm(mixed, jnp.concatenate(columns, 1))
            for d in range(4):
                for h in range(2):
                    at = (d * 2 + h) * 128
                    lanes = slice((2 * h + h_odd) * 128, (2 * h + h_odd) * 128 + 128)
                    d_one = 2 * d + d_odd
                    value = into[:, at : at + 128] * slope_one[d_one, :, lanes]
                    back_one[d_one, :, lanes] = value.astype(BF)
    three = filter_grad(shifts, field, 2, 2).astype(BF)
    for t in range(27):
        out[t, 32:, :128] = three[t * 16 : t * 16 + 16]
    two = None
    for d in range(4):
        columns = []
        for h in range(2):
            parts = [act_one[2 * d + a, h * 192 : h * 192 + 288] for a in range(3)]
            columns.append(jnp.concatenate(parts, 0))
        own = jnp.concatenate([wide[d + 1, 1, :64], wide[d + 1, 2, :64]], 1)
        term = mm_nt(jnp.concatenate(columns, 1), own)
        two = term if two is None else two + term
    one = None
    for d in range(8):
        columns = []
        for h in range(4):
            parts = [volume[2 * d + a, h * 64 : h * 64 + 96] for a in range(3)]
            columns.append(jnp.concatenate(parts, 0))
        term = mm_nt(jnp.concatenate(columns, 1), back_one[d])
        one = term if one is None else one + term
    both = jnp.concatenate([two, one], 0)
    for t in range(32):
        pair = [both[32 * t + 16 * q : 32 * t + 16 * q + 16] for q in range(2)]
        out[t, 32:, 128:] = jnp.concatenate(pair, 1).astype(BF)
    rest = [both[1024 + 32 * q : 1056 + 32 * q] for q in range(4)]
    out[27, :32] = jnp.concatenate(rest, 1).astype(BF)


def unpack_kernel(packed, grad_one, grad_two, grad_three, grad_four, both):
    for t in range(27):
        grad_four[t] = packed[t, :32].astype(F32)
        grad_three[t] = packed[t, 32:, :128].astype(F32)
    for t in range(32):
        pair = packed[t, 32:, 128:].astype(F32)
        both[32 * t : 32 * t + 16] = pair[:, :64]
        both[32 * t + 16 : 32 * t + 32] = pair[:, 64:]
    rest = packed[27, :32].astype(F32)
    for q in range(4):
        both[1024 + 32 * q : 1056 + 32 * q] = rest[:, 64 * q : 64 * q + 64]
    grad_two[...] = both[:864]
    for t in range(9):
        at = 864 + 32 * t
        grad_one[t] = both[at : at + 12, :32] + both[at + 8 : at + 20, 32:]


def moved(block, depth_step, chan_of):
    depth, chans = lax.axis_size("space"), lax.axis_size("chan")
    route = []
    for s in range(depth):
        for c in range(chans):
            to = chan_of(c)
            if 0 <= s + depth_step < depth and 0 <= to < chans:
                route.append((s * chans + c, (s + depth_step) * chans + to))
    return lax.ppermute(block, BOTH, route)


def gathered(own, first, last):
    across = moved(own, 0, lambda c: c ^ 2)
    up = moved(last, 1, lambda c: c)
    down = moved(first, -1, lambda c: c)
    core = moved(own, 0, lambda c: c ^ 1)
    rim = jnp.concatenate([up, down], 0)
    across_rim = moved(rim, 0, lambda c: c ^ 2)
    core_rim = moved(rim, 0, lambda c: c ^ 1)
    across, across_rim = lax.optimization_barrier((across, across_rim))
    last_pair = [moved(piece, 0, lambda c: c ^ 1) for piece in (across, across_rim)]
    return [own, rim, core, core_rim, across, across_rim, *last_pair]


def summed(parts):
    terms = lax.all_to_all(parts, "space", 0, 0)
    own = jnp.sum(terms.astype(F32), 0)
    sent = own.astype(BF)
    others = [moved(sent, 0, lambda c, k=k: c ^ k).astype(F32) for k in (2, 3, 1)]
    shape = own.shape
    row = lax.broadcasted_iota(jnp.int32, shape, 0)
    shared = (row >= 32) & (lane_of(shape) >= 128) | (lax.axis_index("space") == 27)
    total = own + jnp.where(shared, others[0] + others[1] + others[2], 0.0)
    total = total.astype(BF)
    return lax.all_to_all(jnp.broadcast_to(total[None], parts.shape), "space", 0, 0)


def phase_matrix():
    pick = np.zeros((512, 640), np.float32)
    for p in range(5):
        for w in range(128):
            if 4 * w + p < 512:
                pick[4 * w + p, p * 128 + w] = 1.0
    return jnp.asarray(pick, BF)


def row_matrix():
    pick = np.zeros((11, 8, 4, 5, 4, 16), np.float32)
    for h in range(11):
        for p in range(5):
            for i in range(4):
                pick[h, p, i, p, i, h] = 1.0
    return jnp.asarray(pick.reshape(352, 320), BF)


def per_device(volume, kernel_one, kernel_two, kernel_three, kernel_four, cotangent):
    me = lax.axis_index("chan").astype(jnp.int32)[None]
    below = moved(volume[:, :3], -1, lambda c: c)
    beside = moved(volume[:, :, :3], 0, lambda c: c - 1)
    corner = moved(volume[:, :3, :3], -1, lambda c: c - 1)
    tall = jnp.concatenate([volume, below], 1)
    side = jnp.pad(jnp.concatenate([beside, corner], 1), ((0, 0), (0, 0), (0, 5), (0, 0)))
    tall = jnp.concatenate([tall, side], 2)

    three = jnp.pad(kernel_three.reshape(27, 16, 128), ((0, 0), (0, 0), (0, 128)))
    four = kernel_four.reshape(27, 32, 256)
    filters = lax.all_gather(jnp.concatenate([four, three], 1), "chan")
    cotangent = jnp.transpose(cotangent.reshape(64, 4, 1024), (1, 0, 2))

    even = jnp.pad(kernel_one, ((0, 0), (0, 0), (0, 5), (0, 0), (0, 0)))
    odd = jnp.pad(kernel_one, ((0, 0), (0, 0), (2, 3), (0, 0), (0, 0)))
    w_one = jnp.stack([even, odd]).reshape(2, 288, 32).transpose(0, 2, 1).reshape(64, 288)
    w_two = kernel_two.reshape(864, 64).T
    top = jnp.concatenate([kernel_two[:, :, 0], kernel_two[:, :, 2]], 3)
    bottom = jnp.pad(kernel_two[:, :, 1], ((0, 0), (0, 0), (0, 0), (0, 64)))
    w_back = jnp.concatenate([top, bottom], 2).reshape(9, 64, 128)

    field, act_one, slope_one, body, first, last, slope_two = call(
        first_layers_kernel,
        [
            ((19, 352, 128), BF),
            ((9, 480, 128), BF),
            ((8, 64, 512), F32),
            ((4, 64, 384), BF),
            ((1, 64, 512), BF),
            ((1, 64, 512), BF),
            ((4, 64, 256), F32),
        ],
        [tall, phase_matrix(), row_matrix(), w_one, w_two],
    )
    w_three, w_four, w_two_back = call(
        prepare_kernel,
        [((96, 576), BF), ((192, 1152), BF), ((192, 1152), BF)],
        [me, filters],
    )
    pieces = range(1, 9)
    act_three, slope_three, field_three, front, row = call(
        third_kernel,
        [((4, 32, 1024), BF), ((4, 32, 1024), F32), ((6, 64, 1280), BF), ((64, 384), BF), ((4, 64, 128), BF)],
        [me, *gathered(body, first, last), w_three],
        anywhere=pieces,
    )
    blocks = gathered(act_three, act_three[:1], act_three[3:])
    features, back_four = call(
        fourth_kernel,
        [((4, 64, 1024), BF), ((4, 64, 1024), BF)],
        [me, *blocks, w_four, cotangent],
        [((6, 128, 1280), BF)],
        anywhere=pieces,
    )
    features = jnp.transpose(features, (1, 0, 2)).reshape(64, 4, 8, 128)
    back_three, all_four = call(
        into_three_kernel,
        [((4, 32, 1024), BF), ((6, 256, 1280), BF)],
        [me, *gathered(back_four, back_four[:1], back_four[3:]), four, slope_three],
        anywhere=pieces,
    )
    (grad_four,) = call(
        grad_four_kernel,
        [((864, 256), BF)],
        [*blocks[:2], all_four],
        [((6, 96, 1280), BF)],
        flops=2 * 864 * 256 * 4096,
    )
    (grads,) = call(
        last_kernel,
        [((32, 48, 256), BF)],
        [
            me,
            *gathered(back_three, back_three[:1], back_three[2:]),
            w_two_back,
            slope_two,
            front,
            row,
            act_one,
            slope_one,
            field,
            w_back,
            field_three,
            grad_four.reshape(27, 32, 256),
        ],
        [
            ((7, 128, 1408), BF),
            ((6, 48, 1280), BF),
            ((5, 3, 128, 128), BF),
            ((8, 64, 512), BF),
        ],
        anywhere=pieces,
    )
    grad_one, grad_two, grad_three, grad_four = call(
        unpack_kernel,
        [((9, 12, 32), F32), ((864, 64), F32), ((27, 16, 128), F32), ((27, 32, 256), F32)],
        [summed(grads)],
        [((1152, 64), F32)],
    )
    grad_one = grad_one.reshape(3, 3, 3, 4, 32)
    grad_two = grad_two.reshape(3, 3, 3, 32, 64)
    grad_three = grad_three.reshape(3, 3, 3, 16, 128)
    grad_four = grad_four.reshape(3, 3, 3, 32, 256)
    return (features, grad_one, grad_two, grad_three, grad_four)


def solution(mesh):
    in_specs = (
        P(None, "space", "chan", None),
        P(),
        P(),
        P(None, None, None, "chan", None),
        P(None, None, None, "chan", None),
        P("chan", "space", None, None),
    )
    out_specs = (
        P("chan", "space", None, None),
        P(),
        P(),
        P(None, None, None, "chan", None),
        P(None, None, None, "chan", None),
    )
    return jax.shard_map(
        per_device, mesh=mesh, in_specs=in_specs, out_specs=out_specs, check_vma=False
    )
```

time: 297 us -> 215 us (0.72); the launches traced: 294 us -> 215 us
  starting transfers between devices: 118 us -> 67.6 us
  local copies, waits for them, and re-layouts: 62.5 us -> 15.2 us
  between operations: 1.46 us -> 14.8 us
  waiting for transfers between devices: 75.4 us -> 86.3 us
  blocking collectives: 8.5 us -> 0 us
  Pallas kernels: 24 us -> 28.1 us
    ppermute x34 -> x38, waiting for transfers between devices: 29.8 us -> 59.5 us  [moved(): return lax.ppermute(block, BOTH, route)]
    all_to_all x7 -> x2, starting transfers between devices: 45.5 us -> 18.8 us  [the longest x1 14.6 us: summed(): terms = lax.all_to_all(parts, 'space', 0, 0)]
    unnamed x93 -> x62, local copies, waits for them, and re-layouts: 35.7 us -> 9.24 us
    ppermute x34 -> x38, starting transfers between devices: 72 us -> 48.7 us  [moved(): return lax.ppermute(block, BOTH, route)]
    all_to_all x7 -> x2, waiting for transfers between devices: 45.5 us -> 26.8 us  [the longest x1 14.3 us: summed(): terms = lax.all_to_all(parts, 'space', 0, 0)]
    all_gather x1 -> x0, blocking collectives: 8.5 us -> none  [per_device(): all_kernel_three = lax.all_gather(kernel_three, 'chan', axis=3, tiled=True)]
    reshape x6 -> x1, local copies, waits for them, and re-layouts: 7.45 us -> 0.64 us  [per_device(): grad_one = grad_one.reshape(3, 3, 3, 4, 32)]
    pallas_call x8, Pallas kernels: 24 us -> 28.1 us  [call(): pl.pallas_call(kernel, out_shape=[jax.ShapeDtypeStruct(s, t) for s, t in...]
  transfers between devices with their start and end apart: 41 -> 41, of which waited for: 15 -> 17; matrix products, arithmetic and copies ran while one was open for 17% -> 3% of each run, Pallas kernels for 2% -> 5%
where the time goes in v2:
time: 215 us
  waiting for transfers between devices  86.3 us (40%)
  starting transfers between devices  67.6 us (31%)
  Pallas kernels  28.1 us (13%)
  local copies, waits for them, and re-layouts  15.2 us (7%)
  between operations  14.8 us (7%)
  other arithmetic  2.69 us (1%)
    ppermute x38, waiting for transfers between devices, moved(): return lax.ppermute(block, BOTH, route)  59.5 us
    ppermute x38, starting transfers between devices, moved(): return lax.ppermute(block, BOTH, route)  48.7 us
    pallas_call x8, Pallas kernels, call(): pl.pallas_call(kernel, out_shape=[jax.ShapeDtypeStruct(s, t) for s, t in...  28.1 us
    all_to_all x1, starting transfers between devices, summed(): terms = lax.all_to_all(parts, 'space', 0, 0)  14.6 us
    all_to_all x1, waiting for transfers between devices, summed(): terms = lax.all_to_all(parts, 'space', 0, 0)  14.3 us
    all_to_all x1, waiting for transfers between devices, summed(): lax.all_to_all(jnp.broadcast_to(total[None], parts.shape), 'space', 0, 0)  12.5 us
    unnamed x62, local copies, waits for them, and re-layouts  9.24 us
  transfers between devices with their start and end apart: 41, of which 17 were waited for; matrix products, arithmetic and copies ran while one was open for 3% of the time, Pallas kernels for 5%

profile of v2, /device:TPU:0, one launch (start us, length us, event | category | flops | bytes accessed | tf_op | source)
XLA Modules:
  0.0 214.6 jit_solution(3236756131500374092)
XLA Ops:
  7.2 2.0 fusion.3
  14.9 4.0 %collective-permute-done = bf16[4,3,8,512]{3,2,1,0:T(8,128)(2,1)S(1)} collective-permute-done((bf16[4,3,8,512]{3,2,1,0:T(8,128)(2,1)S(1)}, bf16[4,3,8,512]{3,2,1,0:T(8,128)(2,1)S(1)}, u32[]{:S(2)}, u32[]{:S(2)}) %collective-permute-start) | collective-permute-done | bytes 98336 | tf_op jit(solution)/shard_map/ppermute | solution.py:370
  19.1 7.1 %shard_map.119 = (bf16[19,352,128]{2,1,0:T(8,128)(2,1)S(1)}, bf16[9,480,128]{2,1,0:T(8,128)(2,1)S(1)}, f32[8,64,512]{2,1,0:T(8,128)S(1)}, bf16[4,64,384]{2,1,0:T...) custom-call(bf16[4,19,16,512]{3,2,1,0:T(8,128)(2,1)S(1)} %pad_maximum_fusi, ...), custom_call_target="tpu_custom_call" | custom-call | bytes 6729728 | tf_op jit(solution)/shard_map/pallas_call | solution.py:50
  27.3 3.5 %collective-permute-start.3 = (bf16[1,64,512]{2,1,0:T(8,128)(2,1)S(1)}, bf16[1,64,512]{2,1,0:T(8,128)(2,1)S(1)}, u32[]{:S(2)}, u32[]{:S(2)}) collective-permute-start(bf16[1,64,512]{2,1,0:T(8,128)(2,1)S(1)} %get-tuple-element.37), channel_id=1, source_target_pairs={{0,4},{1,5},{2,6},{3,7},{4,8},{5,9},{6,10},{7,11},{8,12},{9,13},{1... | collective-permute-start | bytes 196616 | tf_op jit(solution)/shard_map/ppermute | solution.py:370
  32.0 5.5 %collective-permute-start.7 = (bf16[4,64,384]{2,1,0:T(8,128)(2,1)}, bf16[4,64,384]{2,1,0:T(8,128)(2,1)}, u32[]{:S(2)}, u32[]{:S(2)}) collective-permute-start(bf16[4,64,384]{2,1,0:T(8,128)(2,1)} %get-tuple-element.36.refs_0_), channel_id=1, source_target_pairs={{0,2},{1,3},{2,0},{3,1},{4,6},{5,7},{6,4},{7,5},{8,10},{9,11},{10,... | collective-permute-start | bytes 589832 | tf_op jit(solution)/shard_map/ppermute | solution.py:370
  37.6 4.8 %collective-permute-start.8 = (bf16[2,64,512]{2,1,0:T(8,128)(2,1)S(1)}, bf16[2,64,512]{2,1,0:T(8,128)(2,1)S(1)}, u32[]{:S(2)}, u32[]{:S(2)}) collective-permute-start(bf16[2,64,512]{2,1,0:T(8,128)(2,1)S(1)} %constant_dynamic-update-slice_fusion.refs_1_), channel_id=1, source_target_pairs={{0,2},{1,3},{2,0},{3,1},{4,6},{5,7},{6,4},{7,5},{8,10},{9,11},{10,... | collective-permute-start | bytes 393224 | tf_op jit(solution)/shard_map/ppermute | solution.py:370
  42.4 7.0 %collective-permute-done.8.refs_5_ = bf16[2,64,512]{2,1,0:T(8,128)(2,1)S(1)} collective-permute-done((bf16[2,64,512]{2,1,0:T(8,128)(2,1)S(1)}, bf16[2,64,512]{2,1,0:T(8,128)(2,1)S(1)}, u32[]{:S(2)}, u32[]{:S(2)}) %collective-permute-start.8) | collective-permute-done | bytes 131104 | tf_op jit(solution)/shard_map/ppermute | solution.py:370
  55.2 2.4 %shard_map.121 = (bf16[4,32,1024]{2,1,0:T(8,128)(2,1)S(1)}, f32[4,32,1024]{2,1,0:T(8,128)S(1)}, bf16[6,64,1280]{2,1,0:T(8,128)(2,1)S(1)}, bf16[64,384]{1,0:T(8,128)(2,1)S(1)}, bf16[4,64,128]{2,1,0:T(8,128)(2,1)S(1)}) custom-call(s32[1]{0:T(128)} %bitcast.me_ref, bf16[4,64,384]{2,1,0:T(8,128)(2,1)} %get-tuple-element.36.refs_0_, ...), custom_call_target="tpu_custom_call" | custom-call | bytes 3305476 | tf_op jit(solution)/shard_map/pallas_call | solution.py:50
  59.9 2.1 collective-permute-start.11
  62.1 3.1 %collective-permute-start.15 = (bf16[4,32,1024]{2,1,0:T(8,128)(2,1)S(1)}, bf16[4,32,1024]{2,1,0:T(8,128)(2,1)}, u32[]{:S(2)}, u32[]{:S(2)}) collective-permute-start(bf16[4,32,1024]{2,1,0:T(8,128)(2,1)S(1)} %get-tuple-element.42.refs_0_.own), channel_id=1, source_target_pairs={{0,2},{1,3},{2,0},{3,1},{4,6},{5,7},{6,4},{7,5},{8,10},{9,11},{10,... | collective-permute-start | bytes 786440 | tf_op jit(solution)/shard_map/ppermute | solution.py:370
  67.1 4.2 %collective-permute-done.12 = bf16[1,32,1024]{2,1,0:T(8,128)(2,1)S(1)} collective-permute-done((bf16[1,32,1024]{2,1,0:T(8,128)(2,1)S(1)}, bf16[1,32,1024]{2,1,0:T(8,128)(2,1)S(1)}, u32[]{:S(2)}, u32[]{:S(2)}) %collective-permute-start.12) | collective-permute-done | bytes 65568 | tf_op jit(solution)/shard_map/ppermute | solution.py:370
  72.9 7.2 %collective-permute-done.16.refs_5_ = bf16[2,32,1024]{2,1,0:T(8,128)(2,1)} collective-permute-done((bf16[2,32,1024]{2,1,0:T(8,128)(2,1)}, bf16[2,32,1024]{2,1,0:T(8,128)(2,1)}, u32[]{:S(2)}, u32[]{:S(2)}) %collective-permute-start.16) | collective-permute-done | bytes 131104 | tf_op jit(solution)/shard_map/ppermute | solution.py:370
  80.7 2.0 reshape.65
  84.0 3.9 %shard_map.122 = (bf16[4,64,1024]{2,1,0:T(8,128)(2,1)S(1)}, bf16[4,64,1024]{2,1,0:T(8,128)(2,1)S(1)}) custom-call(s32[1]{0:T(128)} %bitcast.me_ref, bf16[4,32,1024]{2,1,0:T(8,128)(2,1)S(1)} %get-tuple-element.42.refs_0_.own, bf16[2,32,1024]{2,1,0:T(8,128)(2,1)} %constant_dynamic-update-slice_fusion.2.refs_1_.rim, ...), custom_call_target="tpu_custom_call" | custom-call | bytes 3588100 | tf_op jit(solution)/shard_map/pallas_call | solution.py:50
  88.0 3.6 %collective-permute-start.19 = (bf16[1,64,1024]{2,1,0:T(8,128)(2,1)S(1)}, bf16[1,64,1024]{2,1,0:T(8,128)(2,1)S(1)}, u32[]{:S(2)}, u32[]{:S(2)}) collective-permute-start(bf16[1,64,1024]{2,1,0:T(8,128)(2,1)S(1)} %get-tuple-element.83), channel_id=1, source_target_pairs={{0,4},{1,5},{2,6},{3,7},{4,8},{5,9},{6,10},{7,11},{8,12},{9,13},{1... | collective-permute-start | bytes 393224 | tf_op jit(solution)/shard_map/ppermute | solution.py:370
  91.6 1.8 collective-permute-start.23
  94.9 5.7 %collective-permute-done.20 = bf16[1,64,1024]{2,1,0:T(8,128)(2,1)S(1)} collective-permute-done((bf16[1,64,1024]{2,1,0:T(8,128)(2,1)S(1)}, bf16[1,64,1024]{2,1,0:T(8,128)(2,1)S(1)}, u32[]{:S(2)}, u32[]{:S(2)}) %collective-permute-start.20) | collective-permute-done | bytes 131104 | tf_op jit(solution)/shard_map/ppermute | solution.py:370
  100.6 2.1 collective-permute-start.24
  102.8 12.8 %collective-permute-done.24.refs_5_ = bf16[2,64,1024]{2,1,0:T(8,128)(2,1)S(1)} collective-permute-done((bf16[2,64,1024]{2,1,0:T(8,128)(2,1)S(1)}, bf16[2,64,1024]{2,1,0:T(8,128)(2,1)S(1)}, u32[]{:S(2)}, u32[]{:S(2)}) %collective-permute-start.24) | collective-permute-done | bytes 262176 | tf_op jit(solution)/shard_map/ppermute | solution.py:370
  116.1 1.8 collective-permute-done.22.refs_3_
  118.3 3.8 %shard_map.123 = (bf16[4,32,1024]{2,1,0:T(8,128)(2,1)S(1)}, bf16[6,256,1280]{2,1,0:T(8,128)(2,1)S(1)}) custom-call(s32[1]{0:T(128)} %bitcast.me_ref, bf16[4,64,1024]{2,1,0:T(8,128)(2,1)S(1)} %get-tuple-element.47.refs_0_, bf16[2,64,1024]{2,1,0:T(8,128)(2,1)S(1)} %constant_dynamic-update-slice_fusion.4.refs_1_, ...), custom_call_target="tpu_custom_call" | custom-call | bytes 8306692 | tf_op jit(solution)/shard_map/pallas_call | solution.py:50
  123.4 1.9 collective-permute-start.31
  126.7 5.5 %collective-permute-done.28 = bf16[1,32,1024]{2,1,0:T(8,128)(2,1)S(1)} collective-permute-done((bf16[1,32,1024]{2,1,0:T(8,128)(2,1)S(1)}, bf16[1,32,1024]{2,1,0:T(8,128)(2,1)S(1)}, u32[]{:S(2)}, u32[]{:S(2)}) %collective-permute-start.28) | collective-permute-done | bytes 65568 | tf_op jit(solution)/shard_map/ppermute | solution.py:370
  132.2 2.4 %collective-permute-start.32 = (bf16[3,32,1024]{2,1,0:T(8,128)(2,1)S(1)}, bf16[3,32,1024]{2,1,0:T(8,128)(2,1)S(1)}, u32[]{:S(2)}, u32[]{:S(2)}) collective-permute-start(bf16[3,32,1024]{2,1,0:T(8,128)(2,1)S(1)} %constant_dynamic-update-slice_fusion.6.refs_1_), channel_id=1, source_target_pairs={{0,2},{1,3},{2,0},{3,1},{4,6},{5,7},{6,4},{7,5},{8,10},{9,11},{10,... | collective-permute-start | bytes 589832 | tf_op jit(solution)/shard_map/ppermute | solution.py:370
  135.2 7.1 %collective-permute-done.32.refs_5_ = bf16[3,32,1024]{2,1,0:T(8,128)(2,1)S(1)} collective-permute-done((bf16[3,32,1024]{2,1,0:T(8,128)(2,1)S(1)}, bf16[3,32,1024]{2,1,0:T(8,128)(2,1)S(1)}, u32[]{:S(2)}, u32[]{:S(2)}) %collective-permute-start.32) | collective-permute-done | bytes 196640 | tf_op jit(solution)/shard_map/ppermute | solution.py:370
  143.0 3.1 %shard_map.124 = bf16[864,256]{1,0:T(8,128)(2,1)S(1)} custom-call(bf16[4,32,1024]{2,1,0:T(8,128)(2,1)S(1)} %get-tuple-element.42.refs_0_.own, bf16[2,32,1024]{2,1,0:T(8,128)(2,1)} %constant_dynamic-update-slice_fusion.2.refs_1_.rim, bf16[6,256,1280]{2,1,0:T(8,128)(2,1)S(1)} %get-tuple-element.62.gradient), custom_call_target="tpu_custom_call" | custom-call | flops 1811939328 | bytes 4767744 | tf_op jit(solution)/shard_map/pallas_call | solution.py:50
  146.2 5.7 %shard_map.125 = bf16[32,48,256]{2,1,0:T(8,128)(2,1)} custom-call(s32[1]{0:T(128)} %bitcast.me_ref, bf16[4,32,1024]{2,1,0:T(8,128)(2,1)S(1)} %get-tuple-element.51.refs_0_, bf16[3,32,1024]{2,1,0:T(8,128)(2,1)S(1)} %constant_dynamic-update-slice_fusion.6.refs_1_, bf16[4,32,1024]{2,1,0:T(8,128)(2,1)S(1)} %collective-permute-done.29.refs_2_, ...), custom_call_target="tpu_custom_call" | custom-call | bytes 8880132 | tf_op jit(solution)/shard_map/pallas_call | solution.py:50
  151.9 14.6 %all-to-all-start = ((bf16[32,48,256]{2,1,0:T(8,128)(2,1)}), bf16[32,48,256]{2,1,0:T(8,128)(2,1)S(1)}, u32[]{:S(2)}, u32[]{:S(2)}) async-start(bf16[32,48,256]{2,1,0:T(8,128)(2,1)} %shard_map.125), calls=%async_computation | async-start | bytes 1572864 | tf_op jit(solution)/shard_map/all_to_all | solution.py:387
  166.5 14.3 %all-to-all-done = bf16[32,48,256]{2,1,0:T(8,128)(2,1)S(1)} async-done(((bf16[32,48,256]{2,1,0:T(8,128)(2,1)}), bf16[32,48,256]{2,1,0:T(8,128)(2,1)S(1)}, u32[]{:S(2)}, u32[]{:S(2)}) %all-to-all-start) | async-done | bytes 786464 | tf_op jit(solution)/shard_map/all_to_all | solution.py:387
  181.8 2.9 %collective-permute-start.35 = (bf16[48,256]{1,0:T(8,128)(2,1)S(1)}, bf16[48,256]{1,0:T(8,128)(2,1)S(1)}, u32[]{:S(2)}, u32[]{:S(2)}) collective-permute-start(bf16[48,256]{1,0:T(8,128)(2,1)S(1)} %convert_element_type.29), channel_id=1, source_target_pairs={{0,2},{1,3},{2,0},{3,1},{4,6},{5,7},{6,4},{7,5},{8,10},{9,11},{10,... | collective-permute-start | bytes 73736 | tf_op jit(solution)/shard_map/ppermute | solution.py:370
  188.1 4.2 %all-to-all-start.1 = ((bf16[32,48,256]{2,1,0:T(8,128)(2,1)}), bf16[32,48,256]{2,1,0:T(8,128)(2,1)S(1)}, u32[]{:S(2)}, u32[]{:S(2)}) async-start(bf16[32,48,256]{2,1,0:T(8,128)(2,1)} %broadcast_in_dim.15), calls=%async_computation.1 | async-start | bytes 1572864 | tf_op jit(solution)/shard_map/all_to_all | solution.py:396
  193.4 12.5 %all-to-all-done.1.packed = bf16[32,48,256]{2,1,0:T(8,128)(2,1)S(1)} async-done(((bf16[32,48,256]{2,1,0:T(8,128)(2,1)}), bf16[32,48,256]{2,1,0:T(8,128)(2,1)S(1)}, u32[]{:S(2)}, u32[]{:S(2)}) %all-to-all-start.1) | async-done | bytes 786464 | tf_op jit(solution)/shard_map/all_to_all | solution.py:396
  (151 shorter events, 35.1 us)
Async XLA Ops:
  7.2 42.9 %all-gather.3.cloned.1.call-start = ((), (), s32[]{:S(2)}) async-start(), calls=%async_computation.2 | async-start | bytes 3317760 | tf_op jit(solution)/shard_map/all_gather | solution.py:428
  9.3 5.4 %collective-permute-start.2 = (bf16[4,3,3,512]{3,2,1,0:T(4,128)(2,1)S(1)}, bf16[4,3,3,512]{3,2,1,0:T(4,128)(2,1)S(1)}, u32[]{:S(2)}, u32[]{:S(2)}) collective-permute-start(bf16[4,3,3,512]{3,2,1,0:T(4,128)(2,1)S(1)} %slice.38), channel_id=1, source_target_pairs={{5,0},{6,1},{7,2},{9,4},{10,5},{11,6},{13,8},{14,9},{15,10},{17,12... | collective-permute-start | bytes 110600 | tf_op jit(solution)/shard_map/ppermute | solution.py:370
  10.7 4.0 %collective-permute-start.1 = (bf16[4,16,3,512]{3,2,1,0:T(4,128)(2,1)S(1)}, bf16[4,16,3,512]{3,2,1,0:T(4,128)(2,1)S(1)}, u32[]{:S(2)}, u32[]{:S(2)}) collective-permute-start(bf16[4,16,3,512]{3,2,1,0:T(4,128)(2,1)S(1)} %slice.37), channel_id=1, source_target_pairs={{1,0},{2,1},{3,2},{5,4},{6,5},{7,6},{9,8},{10,9},{11,10},{13,12},{... | collective-permute-start | bytes 589832 | tf_op jit(solution)/shard_map/ppermute | solution.py:370
  12.0 6.9 %collective-permute-start = (bf16[4,3,8,512]{3,2,1,0:T(8,128)(2,1)S(1)}, bf16[4,3,8,512]{3,2,1,0:T(8,128)(2,1)S(1)}, u32[]{:S(2)}, u32[]{:S(2)}) collective-permute-start(bf16[4,3,8,512]{3,2,1,0:T(8,128)(2,1)S(1)} %slice.36), channel_id=1, source_target_pairs={{4,0},{5,1},{6,2},{7,3},{8,4},{9,5},{10,6},{11,7},{12,8},{13,9},{1... | collective-permute-start | bytes 294920 | tf_op jit(solution)/shard_map/ppermute | solution.py:370
  27.3 10.3 %collective-permute-start.3 = (bf16[1,64,512]{2,1,0:T(8,128)(2,1)S(1)}, bf16[1,64,512]{2,1,0:T(8,128)(2,1)S(1)}, u32[]{:S(2)}, u32[]{:S(2)}) collective-permute-start(bf16[1,64,512]{2,1,0:T(8,128)(2,1)S(1)} %get-tuple-element.37), channel_id=1, source_target_pairs={{0,4},{1,5},{2,6},{3,7},{4,8},{5,9},{6,10},{7,11},{8,12},{9,13},{1... | collective-permute-start | bytes 196616 | tf_op jit(solution)/shard_map/ppermute | solution.py:370
  30.7 6.8 %collective-permute-start.4 = (bf16[1,64,512]{2,1,0:T(8,128)(2,1)S(1)}, bf16[1,64,512]{2,1,0:T(8,128)(2,1)S(1)}, u32[]{:S(2)}, u32[]{:S(2)}) collective-permute-start(bf16[1,64,512]{2,1,0:T(8,128)(2,1)S(1)} %get-tuple-element.38), channel_id=1, source_target_pairs={{4,0},{5,1},{6,2},{7,3},{8,4},{9,5},{10,6},{11,7},{12,8},{13,9},{1... | collective-permute-start | bytes 196616 | tf_op jit(solution)/shard_map/ppermute | solution.py:370
  32.0 17.4 %collective-permute-start.7 = (bf16[4,64,384]{2,1,0:T(8,128)(2,1)}, bf16[4,64,384]{2,1,0:T(8,128)(2,1)}, u32[]{:S(2)}, u32[]{:S(2)}) collective-permute-start(bf16[4,64,384]{2,1,0:T(8,128)(2,1)} %get-tuple-element.36.refs_0_), channel_id=1, source_target_pairs={{0,2},{1,3},{2,0},{3,1},{4,6},{5,7},{6,4},{7,5},{8,10},{9,11},{10,... | collective-permute-start | bytes 589832 | tf_op jit(solution)/shard_map/ppermute | solution.py:370
  37.6 11.8 %collective-permute-start.8 = (bf16[2,64,512]{2,1,0:T(8,128)(2,1)S(1)}, bf16[2,64,512]{2,1,0:T(8,128)(2,1)S(1)}, u32[]{:S(2)}, u32[]{:S(2)}) collective-permute-start(bf16[2,64,512]{2,1,0:T(8,128)(2,1)S(1)} %constant_dynamic-update-slice_fusion.refs_1_), channel_id=1, source_target_pairs={{0,2},{1,3},{2,0},{3,1},{4,6},{5,7},{6,4},{7,5},{8,10},{9,11},{10,... | collective-permute-start | bytes 393224 | tf_op jit(solution)/shard_map/ppermute | solution.py:370
  42.4 11.0 %collective-permute-start.5 = (bf16[4,64,384]{2,1,0:T(8,128)(2,1)}, bf16[4,64,384]{2,1,0:T(8,128)(2,1)}, u32[]{:S(2)}, u32[]{:S(2)}) collective-permute-start(bf16[4,64,384]{2,1,0:T(8,128)(2,1)} %get-tuple-element.36.refs_0_), channel_id=1, source_target_pairs={{0,1},{1,0},{2,3},{3,2},{4,5},{5,4},{6,7},{7,6},{8,9},{9,8},{10,11... | collective-permute-start | bytes 589832 | tf_op jit(solution)/shard_map/ppermute | solution.py:370
  49.4 4.0 %collective-permute-start.9 = (bf16[4,64,384]{2,1,0:T(8,128)(2,1)}, bf16[4,64,384]{2,1,0:T(8,128)(2,1)}, u32[]{:S(2)}, u32[]{:S(2)}) collective-permute-start(bf16[4,64,384]{2,1,0:T(8,128)(2,1)} %collective-permute-done.7.refs_4_), channel_id=1, source_target_pairs={{0,1},{1,0},{2,3},{3,2},{4,5},{5,4},{6,7},{7,6},{8,9},{9,8},{10,11... | collective-permute-start | bytes 589832 | tf_op jit(solution)/shard_map/ppermute | solution.py:370
  59.9 6.5 %collective-permute-start.11 = (bf16[1,32,1024]{2,1,0:T(8,128)(2,1)S(1)}, bf16[1,32,1024]{2,1,0:T(8,128)(2,1)S(1)}, u32[]{:S(2)}, u32[]{:S(2)}) collective-permute-start(bf16[1,32,1024]{2,1,0:T(8,128)(2,1)S(1)} %get-tuple-element.85), channel_id=1, source_target_pairs={{0,4},{1,5},{2,6},{3,7},{4,8},{5,9},{6,10},{7,11},{8,12},{9,13},{1... | collective-permute-start | bytes 196616 | tf_op jit(solution)/shard_map/ppermute | solution.py:370
  62.1 18.1 %collective-permute-start.15 = (bf16[4,32,1024]{2,1,0:T(8,128)(2,1)S(1)}, bf16[4,32,1024]{2,1,0:T(8,128)(2,1)}, u32[]{:S(2)}, u32[]{:S(2)}) collective-permute-start(bf16[4,32,1024]{2,1,0:T(8,128)(2,1)S(1)} %get-tuple-element.42.refs_0_.own), channel_id=1, source_target_pairs={{0,2},{1,3},{2,0},{3,1},{4,6},{5,7},{6,4},{7,5},{8,10},{9,11},{10,... | collective-permute-start | bytes 786440 | tf_op jit(solution)/shard_map/ppermute | solution.py:370
  65.1 6.2 %collective-permute-start.12 = (bf16[1,32,1024]{2,1,0:T(8,128)(2,1)S(1)}, bf16[1,32,1024]{2,1,0:T(8,128)(2,1)S(1)}, u32[]{:S(2)}, u32[]{:S(2)}) collective-permute-start(bf16[1,32,1024]{2,1,0:T(8,128)(2,1)S(1)} %get-tuple-element.84), channel_id=1, source_target_pairs={{4,0},{5,1},{6,2},{7,3},{8,4},{9,5},{10,6},{11,7},{12,8},{13,9},{1... | collective-permute-start | bytes 196616 | tf_op jit(solution)/shard_map/ppermute | solution.py:370
  71.9 8.2 %collective-permute-start.16 = (bf16[2,32,1024]{2,1,0:T(8,128)(2,1)}, bf16[2,32,1024]{2,1,0:T(8,128)(2,1)}, u32[]{:S(2)}, u32[]{:S(2)}) collective-permute-start(bf16[2,32,1024]{2,1,0:T(8,128)(2,1)} %constant_dynamic-update-slice_fusion.2.refs_1_.rim), channel_id=1, source_target_pairs={{0,2},{1,3},{2,0},{3,1},{4,6},{5,7},{6,4},{7,5},{8,10},{9,11},{10,... | collective-permute-start | bytes 393224 | tf_op jit(solution)/shard_map/ppermute | solution.py:370
  72.9 11.1 %collective-permute-start.13 = (bf16[4,32,1024]{2,1,0:T(8,128)(2,1)S(1)}, bf16[4,32,1024]{2,1,0:T(8,128)(2,1)}, u32[]{:S(2)}, u32[]{:S(2)}) collective-permute-start(bf16[4,32,1024]{2,1,0:T(8,128)(2,1)S(1)} %get-tuple-element.42.refs_0_.own), channel_id=1, source_target_pairs={{0,1},{1,0},{2,3},{3,2},{4,5},{5,4},{6,7},{7,6},{8,9},{9,8},{10,11... | collective-permute-start | bytes 786440 | tf_op jit(solution)/shard_map/ppermute | solution.py:370
  80.1 3.9 %collective-permute-start.17 = (bf16[4,32,1024]{2,1,0:T(8,128)(2,1)}, bf16[4,32,1024]{2,1,0:T(8,128)(2,1)}, u32[]{:S(2)}, u32[]{:S(2)}) collective-permute-start(bf16[4,32,1024]{2,1,0:T(8,128)(2,1)} %collective-permute-done.15.refs_4_), channel_id=1, source_target_pairs={{0,1},{1,0},{2,3},{3,2},{4,5},{5,4},{6,7},{7,6},{8,9},{9,8},{10,11... | collective-permute-start | bytes 786440 | tf_op jit(solution)/shard_map/ppermute | solution.py:370
  88.0 6.9 %collective-permute-start.19 = (bf16[1,64,1024]{2,1,0:T(8,128)(2,1)S(1)}, bf16[1,64,1024]{2,1,0:T(8,128)(2,1)S(1)}, u32[]{:S(2)}, u32[]{:S(2)}) collective-permute-start(bf16[1,64,1024]{2,1,0:T(8,128)(2,1)S(1)} %get-tuple-element.83), channel_id=1, source_target_pairs={{0,4},{1,5},{2,6},{3,7},{4,8},{5,9},{6,10},{7,11},{8,12},{9,13},{1... | collective-permute-start | bytes 393224 | tf_op jit(solution)/shard_map/ppermute | solution.py:370
  91.6 24.0 %collective-permute-start.23 = (bf16[4,64,1024]{2,1,0:T(8,128)(2,1)S(1)}, bf16[4,64,1024]{2,1,0:T(8,128)(2,1)S(1)}, u32[]{:S(2)}, u32[]{:S(2)}) collective-permute-start(bf16[4,64,1024]{2,1,0:T(8,128)(2,1)S(1)} %get-tuple-element.47.refs_0_), channel_id=1, source_target_pairs={{0,2},{1,3},{2,0},{3,1},{4,6},{5,7},{6,4},{7,5},{8,10},{9,11},{10,... | collective-permute-start | bytes 1572872 | tf_op jit(solution)/shard_map/ppermute | solution.py:370
  93.4 7.2 %collective-permute-start.20 = (bf16[1,64,1024]{2,1,0:T(8,128)(2,1)S(1)}, bf16[1,64,1024]{2,1,0:T(8,128)(2,1)S(1)}, u32[]{:S(2)}, u32[]{:S(2)}) collective-permute-start(bf16[1,64,1024]{2,1,0:T(8,128)(2,1)S(1)} %get-tuple-element.82), channel_id=1, source_target_pairs={{4,0},{5,1},{6,2},{7,3},{8,4},{9,5},{10,6},{11,7},{12,8},{13,9},{1... | collective-permute-start | bytes 393224 | tf_op jit(solution)/shard_map/ppermute | solution.py:370
  100.6 15.0 %collective-permute-start.24 = (bf16[2,64,1024]{2,1,0:T(8,128)(2,1)S(1)}, bf16[2,64,1024]{2,1,0:T(8,128)(2,1)S(1)}, u32[]{:S(2)}, u32[]{:S(2)}) collective-permute-start(bf16[2,64,1024]{2,1,0:T(8,128)(2,1)S(1)} %constant_dynamic-update-slice_fusion.4.refs_1_), channel_id=1, source_target_pairs={{0,2},{1,3},{2,0},{3,1},{4,6},{5,7},{6,4},{7,5},{8,10},{9,11},{10,... | collective-permute-start | bytes 786440 | tf_op jit(solution)/shard_map/ppermute | solution.py:370
  102.7 15.1 %collective-permute-start.21 = (bf16[4,64,1024]{2,1,0:T(8,128)(2,1)S(1)}, bf16[4,64,1024]{2,1,0:T(8,128)(2,1)S(1)}, u32[]{:S(2)}, u32[]{:S(2)}) collective-permute-start(bf16[4,64,1024]{2,1,0:T(8,128)(2,1)S(1)} %get-tuple-element.47.refs_0_), channel_id=1, source_target_pairs={{0,1},{1,0},{2,3},{3,2},{4,5},{5,4},{6,7},{7,6},{8,9},{9,8},{10,11... | collective-permute-start | bytes 1572872 | tf_op jit(solution)/shard_map/ppermute | solution.py:370
  122.1 4.6 %collective-permute-start.27 = (bf16[2,32,1024]{2,1,0:T(8,128)(2,1)S(1)}, bf16[2,32,1024]{2,1,0:T(8,128)(2,1)S(1)}, u32[]{:S(2)}, u32[]{:S(2)}) collective-permute-start(bf16[2,32,1024]{2,1,0:T(8,128)(2,1)S(1)} %slice.43), channel_id=1, source_target_pairs={{0,4},{1,5},{2,6},{3,7},{4,8},{5,9},{6,10},{7,11},{8,12},{9,13},{1... | collective-permute-start | bytes 393224 | tf_op jit(solution)/shard_map/ppermute | solution.py:370
  123.4 11.8 %collective-permute-start.31 = (bf16[4,32,1024]{2,1,0:T(8,128)(2,1)S(1)}, bf16[4,32,1024]{2,1,0:T(8,128)(2,1)S(1)}, u32[]{:S(2)}, u32[]{:S(2)}) collective-permute-start(bf16[4,32,1024]{2,1,0:T(8,128)(2,1)S(1)} %get-tuple-element.51.refs_0_), channel_id=1, source_target_pairs={{0,2},{1,3},{2,0},{3,1},{4,6},{5,7},{6,4},{7,5},{8,10},{9,11},{10,... | collective-permute-start | bytes 786440 | tf_op jit(solution)/shard_map/ppermute | solution.py:370
  125.3 6.9 %collective-permute-start.28 = (bf16[1,32,1024]{2,1,0:T(8,128)(2,1)S(1)}, bf16[1,32,1024]{2,1,0:T(8,128)(2,1)S(1)}, u32[]{:S(2)}, u32[]{:S(2)}) collective-permute-start(bf16[1,32,1024]{2,1,0:T(8,128)(2,1)S(1)} %slice.44), channel_id=1, source_target_pairs={{4,0},{5,1},{6,2},{7,3},{8,4},{9,5},{10,6},{11,7},{12,8},{13,9},{1... | collective-permute-start | bytes 196616 | tf_op jit(solution)/shard_map/ppermute | solution.py:370
  132.2 10.1 %collective-permute-start.32 = (bf16[3,32,1024]{2,1,0:T(8,128)(2,1)S(1)}, bf16[3,32,1024]{2,1,0:T(8,128)(2,1)S(1)}, u32[]{:S(2)}, u32[]{:S(2)}) collective-permute-start(bf16[3,32,1024]{2,1,0:T(8,128)(2,1)S(1)} %constant_dynamic-update-slice_fusion.6.refs_1_), channel_id=1, source_target_pairs={{0,2},{1,3},{2,0},{3,1},{4,6},{5,7},{6,4},{7,5},{8,10},{9,11},{10,... | collective-permute-start | bytes 589832 | tf_op jit(solution)/shard_map/ppermute | solution.py:370
  134.6 11.5 %collective-permute-start.29 = (bf16[4,32,1024]{2,1,0:T(8,128)(2,1)S(1)}, bf16[4,32,1024]{2,1,0:T(8,128)(2,1)S(1)}, u32[]{:S(2)}, u32[]{:S(2)}) collective-permute-start(bf16[4,32,1024]{2,1,0:T(8,128)(2,1)S(1)} %get-tuple-element.51.refs_0_), channel_id=1, source_target_pairs={{0,1},{1,0},{2,3},{3,2},{4,5},{5,4},{6,7},{7,6},{8,9},{9,8},{10,11... | collective-permute-start | bytes 786440 | tf_op jit(solution)/shard_map/ppermute | solution.py:370
  134.7 11.4 %collective-permute-start.30 = (bf16[3,32,1024]{2,1,0:T(8,128)(2,1)S(1)}, bf16[3,32,1024]{2,1,0:T(8,128)(2,1)S(1)}, u32[]{:S(2)}, u32[]{:S(2)}) collective-permute-start(bf16[3,32,1024]{2,1,0:T(8,128)(2,1)S(1)} %constant_dynamic-update-slice_fusion.6.refs_1_), channel_id=1, source_target_pairs={{0,1},{1,0},{2,3},{3,2},{4,5},{5,4},{6,7},{7,6},{8,9},{9,8},{10,11... | collective-permute-start | bytes 589832 | tf_op jit(solution)/shard_map/ppermute | solution.py:370
  142.3 3.8 %collective-permute-start.33 = (bf16[4,32,1024]{2,1,0:T(8,128)(2,1)S(1)}, bf16[4,32,1024]{2,1,0:T(8,128)(2,1)S(1)}, u32[]{:S(2)}, u32[]{:S(2)}) collective-permute-start(bf16[4,32,1024]{2,1,0:T(8,128)(2,1)S(1)} %collective-permute-done.31.refs_4_), channel_id=1, source_target_pairs={{0,1},{1,0},{2,3},{3,2},{4,5},{5,4},{6,7},{7,6},{8,9},{9,8},{10,11... | collective-permute-start | bytes 786440 | tf_op jit(solution)/shard_map/ppermute | solution.py:370
  151.9 28.9 %all-to-all-start = ((bf16[32,48,256]{2,1,0:T(8,128)(2,1)}), bf16[32,48,256]{2,1,0:T(8,128)(2,1)S(1)}, u32[]{:S(2)}, u32[]{:S(2)}) async-start(bf16[32,48,256]{2,1,0:T(8,128)(2,1)} %shard_map.125), calls=%async_computation | async-start | bytes 1572864 | tf_op jit(solution)/shard_map/all_to_all | solution.py:387
  181.0 4.8 %collective-permute-start.36 = (bf16[48,256]{1,0:T(8,128)(2,1)S(1)}, bf16[48,256]{1,0:T(8,128)(2,1)S(1)}, u32[]{:S(2)}, u32[]{:S(2)}) collective-permute-start(bf16[48,256]{1,0:T(8,128)(2,1)S(1)} %convert_element_type.29), channel_id=1, source_target_pairs={{0,3},{1,2},{2,1},{3,0},{4,7},{5,6},{6,5},{7,4},{8,11},{9,10},{10,... | collective-permute-start | bytes 73736 | tf_op jit(solution)/shard_map/ppermute | solution.py:370
  181.8 5.3 %collective-permute-start.35 = (bf16[48,256]{1,0:T(8,128)(2,1)S(1)}, bf16[48,256]{1,0:T(8,128)(2,1)S(1)}, u32[]{:S(2)}, u32[]{:S(2)}) collective-permute-start(bf16[48,256]{1,0:T(8,128)(2,1)S(1)} %convert_element_type.29), channel_id=1, source_target_pairs={{0,2},{1,3},{2,0},{3,1},{4,6},{5,7},{6,4},{7,5},{8,10},{9,11},{10,... | collective-permute-start | bytes 73736 | tf_op jit(solution)/shard_map/ppermute | solution.py:370
  188.1 17.7 %all-to-all-start.1 = ((bf16[32,48,256]{2,1,0:T(8,128)(2,1)}), bf16[32,48,256]{2,1,0:T(8,128)(2,1)S(1)}, u32[]{:S(2)}, u32[]{:S(2)}) async-start(bf16[32,48,256]{2,1,0:T(8,128)(2,1)} %broadcast_in_dim.15), calls=%async_computation.1 | async-start | bytes 1572864 | tf_op jit(solution)/shard_map/all_to_all | solution.py:396
  (37 other events, 246.6 us)
Sparse Core Ops, SparseCore 0:
  10.3 34.3 all-gather.2

commit v3 on v2

--- a/solution.py
+++ b/solution.py
@@ -37,33 +37,64 @@
     return pre * sigma, sigma * (1.0 + pre * (1.0 - sigma))
 
 
-def call(kernel, outs, args, scratch=(), flops=0, anywhere=()):
+def call(kernel, outs, args, scratch=(), flops=0, anywhere=(), away=(), far=()):
     specs = []
     for place, a in enumerate(args):
         space = pltpu.SMEM if a.dtype == jnp.int32 else pltpu.VMEM
         specs.append(pl.BlockSpec(memory_space=pl.ANY if place in anywhere else space))
     size = sum(a.size * a.dtype.itemsize for a in args)
+    args = [pltpu.with_memory_space_constraint(a, pltpu.HBM) if place in far else a for place, a in enumerate(args)]
     size += sum(int(np.prod(s)) * jnp.dtype(t).itemsize for s, t in outs)
     buffers = [pltpu.VMEM(s, t) for s, t in scratch]
-    if anywhere:
-        buffers.append(pltpu.SemaphoreType.DMA((14,)))
+    buffers.append(pltpu.SemaphoreType.DMA((20,)))
+    places = [pltpu.HBM if place in away else pltpu.VMEM for place in range(len(outs))]
     return pl.pallas_call(
         kernel,
-        out_shape=[jax.ShapeDtypeStruct(s, t) for s, t in outs],
+        out_shape=[
+            pltpu.HBM(s, t) if place in away else jax.ShapeDtypeStruct(s, t)
+            for place, (s, t) in enumerate(outs)
+        ],
         in_specs=specs,
-        out_specs=[pl.BlockSpec(memory_space=pltpu.VMEM)] * len(outs),
+        out_specs=[pl.BlockSpec(memory_space=place) for place in places],
         scratch_shapes=buffers,
         compiler_params=pltpu.CompilerParams(vmem_limit_bytes=VMEM_LIMIT),
         cost_estimate=pl.CostEstimate(flops=flops, bytes_accessed=size, transcendentals=0),
     )(*args)
 
 
-def first_layers_kernel(vol, phases, rows, w_one, w_two, field, act_one, slope_one, body, first, last, slope_two):
+def begin(source, target, sem):
+    copy = pltpu.make_async_copy(source, target, sem)
+    copy.start()
+    return copy
+
+
+def picks(shape, column_of):
+    row = lax.broadcasted_iota(jnp.int32, shape, 0)
+    return jnp.where(column_of(row, lane_of(shape)), 1.0, 0.0).astype(BF)
+
+
+def phase_matrix():
+    return picks((512, 640), lambda row, lane: row == 4 * (lane % 128) + lane // 128)
+
+
+def row_matrix():
+    def at(row, lane):
+        return lane == row // 4 % 8 * 64 + row % 4 * 16 + row // 32
+
+    return picks((352, 320), at)
+
+
+def first_layers_kernel(vol, w_one, w_two, *refs):
+    field_out, act_one_out, slope_one_out, body, first, last, slope_two = refs[:7]
+    field, act_one, slope_one, sems = refs[7:]
+    phases = phase_matrix()
+    rows = row_matrix()
     for d in range(19):
         block = jnp.reshape(vol[:, d], (64, 512))
-        split = mm(block, phases[...]).astype(BF)
+        split = mm(block, phases).astype(BF)
         stacked = jnp.concatenate([split[:, p * 128 : p * 128 + 128] for p in range(5)], 0)
-        field[d] = mm(rows[...], stacked).astype(BF)
+        field[d] = mm(rows, stacked).astype(BF)
+    leaving = [begin(field, field_out, sems.at[0])]
     for d in range(9):
         columns = []
         for h in range(5):
@@ -78,6 +109,8 @@
             lanes = slice(h * 128, h * 128 + 128)
             act_one[d, h * 96 : h * 96 + 64] = act[:, lanes].astype(BF)
             act_one[d, h * 96 + 64 : h * 96 + 96] = beside[:, lanes].astype(BF)
+    leaving.append(begin(slope_one, slope_one_out, sems.at[1]))
+    leaving.append(begin(act_one, act_one_out, sems.at[2]))
     for d in range(4):
         columns = []
         for h in range(2):
@@ -93,26 +126,19 @@
             if d == at:
                 rim[0, :, :256] = act.astype(BF)
                 rim[0, :, 256:] = steep
-
-
-def prepare_kernel(me_ref, packed, w_three, w_four, w_two_back):
-    me = me_ref[0]
-
-    def tap_of(t, four):
-        if four:
-            return jnp.concatenate([packed[j, t, :32] for j in range(4)], 0)
-        return jnp.concatenate([packed[j, t, 32:, :128] for j in range(4)], 0)
-
-    def own(count, wide):
-        row = lax.broadcasted_iota(jnp.int32, (count, wide), 0)
-        return jnp.where(lane_of((count, wide)) == row + me * count, 1.0, 0.0).astype(BF)
-
-    for out, four, count in ((w_three, False, 32), (w_four, True, 64)):
-        pick = own(count, 4 * count)
-        for c in range(3):
-            rows = jnp.concatenate([tap_of(ab * 3 + c, four) for ab in range(9)], 0)
-            out[c * count : c * count + count] = mm_nt(pick, rows).astype(BF)
-    w_two_back[...] = flipped_weights([tap_of(t, False) for t in range(27)])
+    for copy in leaving:
+        copy.wait()
+
+
+def turned(me, blocks, count):
+    wide = 4 * count
+    row = lax.broadcasted_iota(jnp.int32, (count, wide), 0)
+    pick = jnp.where(lane_of((count, wide)) == row + me * count, 1.0, 0.0).astype(BF)
+    parts = []
+    for c in range(3):
+        rows = [blocks[j, ab * 3 + c] for ab in range(9) for j in range(4)]
+        parts.append(mm_nt(pick, jnp.concatenate(rows, 0)).astype(BF))
+    return jnp.concatenate(parts, 0)
 
 
 def taps_of(field, d, start, width):
@@ -161,9 +187,11 @@
 
 
 def third_kernel(me_ref, *refs):
-    blocks, weights = refs[:8], refs[8]
-    act, slope, field, steep_front, steep_row, sems = refs[9:]
+    blocks, filters = refs[:8], refs[8]
+    act, first, last, slope_out, own_out, front_out, row_out = refs[9:16]
+    field, slope, front, row, kernel, sems = refs[16:]
     me = me_ref[0]
+    arrived = begin(filters.at[:, :, pl.ds(32, 16), pl.ds(0, LANES)], kernel, sems.at[12])
     planes = (pl.ds(1, 4), pl.ds(0, 1), pl.ds(5, 1))
 
     def target(k, piece):
@@ -171,52 +199,66 @@
         return field.at[planes[piece], :, pl.ds(at, 2 * LANES)]
 
     copies = arrive(blocks, sems, target, 1, 2 * LANES)
-    clear_rims(field)
-    for copy in copies:
-        copy.wait()
+    plane = begin(blocks[1].at[0, :, pl.ds(256, 256)], front.at[:, pl.ds(LANES, 256)], sems.at[13])
 
     @pl.when(me == 0)
     def _():
-        steep_front[:, :LANES] = jnp.zeros((64, LANES), BF)
-        steep_row[...] = jnp.zeros((4, 64, LANES), BF)
-
-    plane = pltpu.make_async_copy(
-        blocks[1].at[0, :, pl.ds(256, 256)], steep_front.at[:, pl.ds(LANES, 256)], sems.at[12]
-    )
-    plane.start()
-    plane.wait()
+        front[:, :LANES] = jnp.zeros((64, LANES), BF)
+        row[...] = jnp.zeros((4, 64, LANES), BF)
+
     for k in (1, 3):
 
         @pl.when((me > 0) & (me ^ k == me - 1))
         def _(k=k):
-            corner = pltpu.make_async_copy(
-                blocks[2 * k + 1].at[0, :, pl.ds(384, LANES)], steep_front.at[:, pl.ds(0, LANES)], sems.at[12]
-            )
-            row = pltpu.make_async_copy(blocks[2 * k].at[:, :, pl.ds(256, LANES)], steep_row, sems.at[13])
-            corner.start()
-            row.start()
-            corner.wait()
-            row.wait()
-
-    for d in range(4):
-        product = mm(weights[...], taps_of(field, d, 0, 1024))
+            begin(blocks[2 * k + 1].at[0, :, pl.ds(384, LANES)], front.at[:, pl.ds(0, LANES)], sems.at[14])
+            begin(blocks[2 * k].at[:, :, pl.ds(256, LANES)], row, sems.at[15])
+
+    clear_rims(field)
+    arrived.wait()
+    weights = turned(me, kernel, 32)
+    plane.wait()
+
+    @pl.when(me > 0)
+    def _():
+        corner = blocks[1].at[0, :, pl.ds(384, LANES)]
+        pltpu.make_async_copy(corner, front.at[:, pl.ds(0, LANES)], sems.at[14]).wait()
+        pltpu.make_async_copy(blocks[0].at[:, :, pl.ds(256, LANES)], row, sems.at[15]).wait()
+
+    leaving = [begin(front, front_out, sems.at[16]), begin(row, row_out, sems.at[17])]
+    for copy in copies:
+        copy.wait()
+    own = field.at[:, pl.ds(pl.multiple_of(me * 16, 16), 16), :]
+    leaving.append(begin(own, own_out, sems.at[18]))
+    for d in range(4):
+        product = mm(weights, taps_of(field, d, 0, 1024))
         value, steep = activate(shift_sum(product, 32))
         act[d] = value.astype(BF)
         slope[d] = steep
+    first[0] = act[0]
+    last[0] = act[3]
+    leaving.append(begin(slope, slope_out, sems.at[19]))
+    for copy in leaving:
+        copy.wait()
 
 
 def fourth_kernel(me_ref, *refs):
-    blocks, weights, cotangent = refs[:8], refs[8], refs[9]
-    features, back, field, sems = refs[10:]
-    copies = assemble(field, me_ref[0], blocks, sems, 32)
+    blocks, filters, cotangent = refs[:8], refs[8], refs[9]
+    features, back, first, last, field, kernel, sems = refs[10:]
+    me = me_ref[0]
+    arrived = begin(filters.at[:, :, pl.ds(0, 32), :], kernel, sems.at[12])
+    copies = assemble(field, me, blocks, sems, 32)
     clear_rims(field)
+    arrived.wait()
+    weights = turned(me, kernel, 64)
     for copy in copies:
         copy.wait()
     for d in range(4):
-        product = mm(weights[...], taps_of(field, d, 0, 1024))
+        product = mm(weights, taps_of(field, d, 0, 1024))
         value, steep = activate(shift_sum(product, 64))
         features[d] = value.astype(BF)
         back[d] = (cotangent[d].astype(F32) * steep).astype(BF)
+    first[0] = back[0]
+    last[0] = back[3]
 
 
 def flipped_weights(kernel):
@@ -229,9 +271,10 @@
 
 
 def into_three_kernel(me_ref, *refs):
-    blocks, kernel, slope = refs[:8], refs[8], refs[9]
-    back, field, sems = refs[10:]
+    blocks, kernel, steep = refs[:8], refs[8], refs[9]
+    back, first, last, field, slope, sems = refs[10:]
     copies = assemble(field, me_ref[0], blocks, sems, 64)
+    copies.append(begin(steep, slope, sems.at[12]))
     clear_rims(field)
     weights = flipped_weights(kernel)
     for copy in copies:
@@ -239,6 +282,8 @@
     for d in range(4):
         product = mm(weights, taps_of(field, d, 0, 1024))
         back[d] = (shift_sum(product, 32) * slope[d]).astype(BF)
+    first[0] = back[0]
+    last[...] = back[2:]
 
 
 def three_shifts(value):
@@ -246,43 +291,55 @@
     return jnp.concatenate([shifted(wide, 1).astype(BF), value, shifted(wide, -1).astype(BF)], 0)
 
 
-def filter_grad(wide, gradient, first, rim):
+def filter_grad(wide, gradients):
     total = None
     for d in range(4):
-        own = gradient[d + first, :, rim * LANES : (rim + 8) * LANES]
-        term = mm_nt(taps_of(wide, d, 0, 1024), own)
+        term = mm_nt(taps_of(wide, d, 0, 1024), gradients(d))
         total = term if total is None else total + term
     return total
 
 
-def grad_four_kernel(own, rim, gradient, grad, wide):
+def grad_four_kernel(me_ref, own, rim, *refs):
+    blocks, grad, wide, gradient, sems = refs[:4], *refs[4:]
+    copies = []
+    for k in range(4):
+        at = pl.multiple_of((me_ref[0] ^ k) * 64, 64)
+        copies.append(begin(blocks[k], gradient.at[:, pl.ds(at, 64), :], sems.at[k]))
     clear_rims(wide)
     inside = slice(LANES, 9 * LANES)
     wide[0, :, inside] = three_shifts(rim[0])
     for d in range(4):
         wide[d + 1, :, inside] = three_shifts(own[d])
     wide[5, :, inside] = three_shifts(rim[1])
-    grad[...] = filter_grad(wide, gradient, 1, 1).astype(BF)
+    for copy in copies:
+        copy.wait()
+    grad[...] = filter_grad(wide, lambda d: gradient[d]).astype(BF)
 
 
 def last_kernel(me_ref, *refs):
     blocks = refs[:8]
-    weights, slope, front, row, act_one, slope_one, volume, w_back, act_two, grad_four = refs[8:18]
-    out, field, shifts, wide, back_one, sems = refs[18:]
+    filters, w_back, act_two, grad_four = refs[8:12]
+    away, out, field, shifts, wide, back_one, kernel = refs[12:18], *refs[18:24]
+    slope, front, row, act_one, slope_one, volume = refs[24:30]
+    sems = refs[30]
     me = me_ref[0]
+    arrived = begin(filters.at[:, :, pl.ds(32, 16), pl.ds(0, LANES)], kernel, sems.at[12])
     copies = assemble(field, me, blocks, sems, 32, up=2, rim=2)
+    later = [begin(source, refs[24 + n], sems.at[13 + n]) for n, source in enumerate(away)]
     field[:, :, : 2 * LANES] = jnp.zeros((7, 128, 2 * LANES), BF)
     field[:, :, 10 * LANES :] = jnp.zeros((7, 128, LANES), BF)
     clear_rims(shifts)
     inside = slice(LANES, 9 * LANES)
-    channels = pl.ds(pl.multiple_of(me * 16, 16), 16)
     for d in range(6):
-        shifts[d, :, inside] = three_shifts(act_two[d, channels, inside])
+        shifts[d, :, inside] = three_shifts(act_two[d, :, inside])
     for t in range(27):
         out[t, :32] = grad_four[t]
     for t in range(27, 32):
         out[t] = jnp.zeros((48, 256), BF)
-    for copy in copies:
+    arrived.wait()
+    taps = [jnp.concatenate([kernel[j, t] for j in range(4)], 0) for t in range(27)]
+    weights = flipped_weights(taps)
+    for copy in copies + later:
         copy.wait()
 
     start = pl.multiple_of(me * (2 * LANES), LANES)
@@ -290,7 +347,7 @@
         steep = front[...].astype(F32)
         if d > 0:
             steep = jnp.concatenate([row[d - 1].astype(F32), slope[d - 1]], 1)
-        product = mm(weights[...], taps_of(field, d, start, 3 * LANES))
+        product = mm(weights, taps_of(field, d, start, 3 * LANES))
         value = shift_sum(product, 64) * steep
         value = value.astype(BF)
         beside = shifted(value.astype(F32), 1).astype(BF)
@@ -314,7 +371,7 @@
                     d_one = 2 * d + d_odd
                     value = into[:, at : at + 128] * slope_one[d_one, :, lanes]
                     back_one[d_one, :, lanes] = value.astype(BF)
-    three = filter_grad(shifts, field, 2, 2).astype(BF)
+    three = filter_grad(shifts, lambda d: field[d + 2, :, 2 * LANES : 10 * LANES]).astype(BF)
     for t in range(27):
         out[t, 32:, :128] = three[t * 16 : t * 16 + 16]
     two = None
@@ -342,7 +399,7 @@
     out[27, :32] = jnp.concatenate(rest, 1).astype(BF)
 
 
-def unpack_kernel(packed, grad_one, grad_two, grad_three, grad_four, both):
+def unpack_kernel(packed, grad_one, grad_two, grad_three, grad_four, both, sems):
     for t in range(27):
         grad_four[t] = packed[t, :32].astype(F32)
         grad_three[t] = packed[t, 32:, :128].astype(F32)
@@ -396,37 +453,17 @@
     return lax.all_to_all(jnp.broadcast_to(total[None], parts.shape), "space", 0, 0)
 
 
-def phase_matrix():
-    pick = np.zeros((512, 640), np.float32)
-    for p in range(5):
-        for w in range(128):
-            if 4 * w + p < 512:
-                pick[4 * w + p, p * 128 + w] = 1.0
-    return jnp.asarray(pick, BF)
-
-
-def row_matrix():
-    pick = np.zeros((11, 8, 4, 5, 4, 16), np.float32)
-    for h in range(11):
-        for p in range(5):
-            for i in range(4):
-                pick[h, p, i, p, i, h] = 1.0
-    return jnp.asarray(pick.reshape(352, 320), BF)
-
-
 def per_device(volume, kernel_one, kernel_two, kernel_three, kernel_four, cotangent):
     me = lax.axis_index("chan").astype(jnp.int32)[None]
     below = moved(volume[:, :3], -1, lambda c: c)
     beside = moved(volume[:, :, :3], 0, lambda c: c - 1)
     corner = moved(volume[:, :3, :3], -1, lambda c: c - 1)
-    tall = jnp.concatenate([volume, below], 1)
-    side = jnp.pad(jnp.concatenate([beside, corner], 1), ((0, 0), (0, 0), (0, 5), (0, 0)))
-    tall = jnp.concatenate([tall, side], 2)
 
     three = jnp.pad(kernel_three.reshape(27, 16, 128), ((0, 0), (0, 0), (0, 128)))
     four = kernel_four.reshape(27, 32, 256)
     filters = lax.all_gather(jnp.concatenate([four, three], 1), "chan")
     cotangent = jnp.transpose(cotangent.reshape(64, 4, 1024), (1, 0, 2))
+    corner, cotangent = lax.optimization_barrier((corner, cotangent))
 
     even = jnp.pad(kernel_one, ((0, 0), (0, 0), (0, 5), (0, 0), (0, 0)))
     odd = jnp.pad(kernel_one, ((0, 0), (0, 0), (2, 3), (0, 0), (0, 0)))
@@ -435,6 +472,10 @@
     top = jnp.concatenate([kernel_two[:, :, 0], kernel_two[:, :, 2]], 3)
     bottom = jnp.pad(kernel_two[:, :, 1], ((0, 0), (0, 0), (0, 0), (0, 64)))
     w_back = jnp.concatenate([top, bottom], 2).reshape(9, 64, 128)
+
+    tall = jnp.concatenate([volume, below], 1)
+    side = jnp.pad(jnp.concatenate([beside, corner], 1), ((0, 0), (0, 0), (0, 5), (0, 0)))
+    tall = jnp.concatenate([tall, side], 2)
 
     field, act_one, slope_one, body, first, last, slope_two = call(
         first_layers_kernel,
@@ -447,66 +488,76 @@
             ((1, 64, 512), BF),
             ((4, 64, 256), F32),
         ],
-        [tall, phase_matrix(), row_matrix(), w_one, w_two],
-    )
-    w_three, w_four, w_two_back = call(
-        prepare_kernel,
-        [((96, 576), BF), ((192, 1152), BF), ((192, 1152), BF)],
-        [me, filters],
-    )
-    pieces = range(1, 9)
-    act_three, slope_three, field_three, front, row = call(
+        [tall, w_one, w_two],
+        [((19, 352, 128), BF), ((9, 480, 128), BF), ((8, 64, 512), F32)],
+        away=(0, 1, 2),
+    )
+    pieces = range(1, 10)
+    act_three, first, last, slope_three, own_two, front, row = call(
         third_kernel,
-        [((4, 32, 1024), BF), ((4, 32, 1024), F32), ((6, 64, 1280), BF), ((64, 384), BF), ((4, 64, 128), BF)],
-        [me, *gathered(body, first, last), w_three],
+        [((4, 32, 1024), BF), ((1, 32, 1024), BF), ((1, 32, 1024), BF), ((4, 32, 1024), F32), ((6, 16, 1280), BF), ((64, 384), BF), ((4, 64, 128), BF)],
+        [me, *gathered(body, first, last), filters],
+        [((6, 64, 1280), BF), ((4, 32, 1024), F32), ((64, 384), BF), ((4, 64, 128), BF), ((4, 27, 16, 128), BF)],
         anywhere=pieces,
-    )
-    blocks = gathered(act_three, act_three[:1], act_three[3:])
-    features, back_four = call(
+        away=(3, 4, 5, 6),
+        far=(9,),
+    )
+    blocks = gathered(act_three, first, last)
+    features, back_four, first, last = call(
         fourth_kernel,
-        [((4, 64, 1024), BF), ((4, 64, 1024), BF)],
-        [me, *blocks, w_four, cotangent],
-        [((6, 128, 1280), BF)],
+        [((4, 64, 1024), BF), ((4, 64, 1024), BF), ((1, 64, 1024), BF), ((1, 64, 1024), BF)],
+        [me, *blocks, filters, cotangent],
+        [((6, 128, 1280), BF), ((4, 27, 32, 256), BF)],
         anywhere=pieces,
     )
     features = jnp.transpose(features, (1, 0, 2)).reshape(64, 4, 8, 128)
-    back_three, all_four = call(
+    all_four = gathered(back_four, first, last)
+    back_three, first, last = call(
         into_three_kernel,
-        [((4, 32, 1024), BF), ((6, 256, 1280), BF)],
-        [me, *gathered(back_four, back_four[:1], back_four[3:]), four, slope_three],
-        anywhere=pieces,
+        [((4, 32, 1024), BF), ((1, 32, 1024), BF), ((2, 32, 1024), BF)],
+        [me, *all_four, four, slope_three],
+        [((6, 256, 1280), BF), ((4, 32, 1024), F32)],
+        anywhere=[*range(1, 9), 10],
     )
     (grad_four,) = call(
         grad_four_kernel,
         [((864, 256), BF)],
-        [*blocks[:2], all_four],
-        [((6, 96, 1280), BF)],
+        [me, *blocks[:2], *all_four[::2]],
+        [((6, 96, 1280), BF), ((4, 256, 1024), BF)],
         flops=2 * 864 * 256 * 4096,
+        anywhere=range(3, 7),
     )
     (grads,) = call(
         last_kernel,
         [((32, 48, 256), BF)],
         [
             me,
-            *gathered(back_three, back_three[:1], back_three[2:]),
-            w_two_back,
+            *gathered(back_three, first, last),
+            filters,
+            w_back,
+            own_two,
+            grad_four.reshape(27, 32, 256),
             slope_two,
             front,
             row,
             act_one,
             slope_one,
             field,
-            w_back,
-            field_three,
-            grad_four.reshape(27, 32, 256),
         ],
         [
             ((7, 128, 1408), BF),
             ((6, 48, 1280), BF),
             ((5, 3, 128, 128), BF),
             ((8, 64, 512), BF),
+            ((4, 27, 16, 128), BF),
+            ((4, 64, 256), F32),
+            ((64, 384), BF),
+            ((4, 64, 128), BF),
+            ((9, 480, 128), BF),
+            ((8, 64, 512), F32),
+            ((19, 352, 128), BF),
         ],
-        anywhere=pieces,
+        anywhere=[*range(1, 10), *range(13, 19)],
     )
     grad_one, grad_two, grad_three, grad_four = call(
         unpack_kernel,

time: 215 us -> 206 us (0.958)
  local copies, waits for them, and re-layouts: 15.2 us -> 3.44 us
  starting transfers between devices: 67.6 us -> 71.2 us
  waiting for transfers between devices: 86.3 us -> 82.8 us
    unnamed x62 -> x32, local copies, waits for them, and re-layouts: 9.24 us -> 1.07 us
    ppermute x38, waiting for transfers between devices: 59.5 us -> 55.8 us  [moved(): return lax.ppermute(block, BOTH, route)]
    reshape x2, local copies, waits for them, and re-layouts: 3.21 us -> 0.28 us  [per_device(): cotangent = jnp.transpose(cotangent.reshape(64, 4, 1024), (1, 0, 2))]
    ppermute x38, starting transfers between devices: 48.7 us -> 50.9 us  [moved(): return lax.ppermute(block, BOTH, route)]
    pallas_call x8 -> x7, Pallas kernels: 28.1 us -> 30.1 us  [call(): pl.pallas_call(kernel, out_shape=[pltpu.HBM(s, t) if place in away else j...]
  transfers between devices with their start and end apart: 41 -> 41, of which waited for: 17 -> 20; matrix products, arithmetic and copies ran while one was open for 3% -> 1% of each run, Pallas kernels for 5% -> 5%
where the time goes in v3:
time: 206 us; the launch traced here: 205 us
  waiting for transfers between devices  82.8 us (40%)
  starting transfers between devices  71.2 us (35%)
  Pallas kernels  30.1 us (15%)
  between operations  14.6 us (7%)
  local copies, waits for them, and re-layouts  3.44 us (2%)
  other arithmetic  2.71 us (1%)
    ppermute x38, waiting for transfers between devices, moved(): return lax.ppermute(block, BOTH, route)  55.8 us
    ppermute x38, starting transfers between devices, moved(): return lax.ppermute(block, BOTH, route)  50.9 us
    pallas_call x7, Pallas kernels, call(): pl.pallas_call(kernel, out_shape=[pltpu.HBM(s, t) if place in away else j...  30.1 us
    all_to_all x1, starting transfers between devices, summed(): terms = lax.all_to_all(parts, 'space', 0, 0)  16.1 us
    all_to_all x1, waiting for transfers between devices, summed(): terms = lax.all_to_all(parts, 'space', 0, 0)  14.3 us
    all_to_all x1, waiting for transfers between devices, summed(): lax.all_to_all(jnp.broadcast_to(total[None], parts.shape), 'space', 0, 0)  12.7 us
    all_to_all x1, starting transfers between devices, summed(): lax.all_to_all(jnp.broadcast_to(total[None], parts.shape), 'space', 0, 0)  4.26 us
  transfers between devices with their start and end apart: 41, of which 20 were waited for; matrix products, arithmetic and copies ran while one was open for 1% of the time, Pallas kernels for 5%

profile of v3, /device:TPU:0, one launch (start us, length us, event | category | flops | bytes accessed | tf_op | source)
XLA Modules:
  0.0 204.9 jit_solution(2348459217242387910)
XLA Ops:
  7.2 2.0 fusion.3
  14.9 4.2 %collective-permute-done = bf16[4,3,8,512]{3,2,1,0:T(8,128)(2,1)S(1)} collective-permute-done((bf16[4,3,8,512]{3,2,1,0:T(8,128)(2,1)S(1)}, bf16[4,3,8,512]{3,2,1,0:T(8,128)(2,1)S(1)}, u32[]{:S(2)}, u32[]{:S(2)}) %collective-permute-start) | collective-permute-done | bytes 98336 | tf_op jit(solution)/shard_map/ppermute | solution.py:427
  19.3 8.3 %shard_map.101 = (bf16[19,352,128]{2,1,0:T(8,128)(2,1)}, bf16[9,480,128]{2,1,0:T(8,128)(2,1)}, f32[8,64,512]{2,1,0:T(8,128)}, bf16[4,64,384]{2,1,0:T(8,128)(2,1)...) custom-call(bf16[4,19,16,512]{3,2,1,0:T(8,128)(2,1)S(1)} %pad_maximum_fusion.vol, ...), custom_call_target="tpu_custom_call" | custom-call | bytes 5849088 | tf_op jit(solution)/shard_map/pallas_call | solution.py:51
  27.6 3.5 %collective-permute-start.3 = (bf16[1,64,512]{2,1,0:T(8,128)(2,1)S(1)}, bf16[1,64,512]{2,1,0:T(8,128)(2,1)S(1)}, u32[]{:S(2)}, u32[]{:S(2)}) collective-permute-start(bf16[1,64,512]{2,1,0:T(8,128)(2,1)S(1)} %get-tuple-element.42), channel_id=1, source_target_pairs={{0,4},{1,5},{2,6},{3,7},{4,8},{5,9},{6,10},{7,11},{8,12},{9,13},{1... | collective-permute-start | bytes 196616 | tf_op jit(solution)/shard_map/ppermute | solution.py:427
  32.4 5.5 %collective-permute-start.7 = (bf16[4,64,384]{2,1,0:T(8,128)(2,1)S(1)}, bf16[4,64,384]{2,1,0:T(8,128)(2,1)S(1)}, u32[]{:S(2)}, u32[]{:S(2)}) collective-permute-start(bf16[4,64,384]{2,1,0:T(8,128)(2,1)S(1)} %get-tuple-element.41.refs_0_), channel_id=1, source_target_pairs={{0,2},{1,3},{2,0},{3,1},{4,6},{5,7},{6,4},{7,5},{8,10},{9,11},{10,... | collective-permute-start | bytes 589832 | tf_op jit(solution)/shard_map/ppermute | solution.py:427
  37.9 4.7 %collective-permute-start.8 = (bf16[2,64,512]{2,1,0:T(8,128)(2,1)S(1)}, bf16[2,64,512]{2,1,0:T(8,128)(2,1)S(1)}, u32[]{:S(2)}, u32[]{:S(2)}) collective-permute-start(bf16[2,64,512]{2,1,0:T(8,128)(2,1)S(1)} %constant_dynamic-update-slice_fusion.refs_1_), channel_id=1, source_target_pairs={{0,2},{1,3},{2,0},{3,1},{4,6},{5,7},{6,4},{7,5},{8,10},{9,11},{10,... | collective-permute-start | bytes 393224 | tf_op jit(solution)/shard_map/ppermute | solution.py:427
  42.6 6.9 %collective-permute-done.8.refs_5_ = bf16[2,64,512]{2,1,0:T(8,128)(2,1)S(1)} collective-permute-done((bf16[2,64,512]{2,1,0:T(8,128)(2,1)S(1)}, bf16[2,64,512]{2,1,0:T(8,128)(2,1)S(1)}, u32[]{:S(2)}, u32[]{:S(2)}) %collective-permute-start.8) | collective-permute-done | bytes 131104 | tf_op jit(solution)/shard_map/ppermute | solution.py:427
  51.4 3.6 %shard_map.102 = (bf16[4,32,1024]{2,1,0:T(8,128)(2,1)S(1)}, bf16[1,32,1024]{2,1,0:T(8,128)(2,1)S(1)}, bf16[1,32,1024]{2,1,0:T(8,128)(2,1)S(1)}, f32[4,32,1024]{2...) custom-call(s32[1]{0:T(128)} %bitcast.me_ref, ...), custom_call_target="tpu_custom_call" | custom-call | bytes 5242884 | tf_op jit(solution)/shard_map/pallas_call | solution.py:51
  55.0 2.0 collective-permute-start.11
  58.3 2.5 %collective-permute-start.15 = (bf16[4,32,1024]{2,1,0:T(8,128)(2,1)S(1)}, bf16[4,32,1024]{2,1,0:T(8,128)(2,1)S(1)}, u32[]{:S(2)}, u32[]{:S(2)}) collective-permute-start(bf16[4,32,1024]{2,1,0:T(8,128)(2,1)S(1)} %get-tuple-element.46.refs_0_.own), channel_id=1, source_target_pairs={{0,2},{1,3},{2,0},{3,1},{4,6},{5,7},{6,4},{7,5},{8,10},{9,11},{10,... | collective-permute-start | bytes 786440 | tf_op jit(solution)/shard_map/ppermute | solution.py:427
  60.8 2.4 %collective-permute-done.12 = bf16[1,32,1024]{2,1,0:T(8,128)(2,1)S(1)} collective-permute-done((bf16[1,32,1024]{2,1,0:T(8,128)(2,1)S(1)}, bf16[1,32,1024]{2,1,0:T(8,128)(2,1)S(1)}, u32[]{:S(2)}, u32[]{:S(2)}) %collective-permute-start.12) | collective-permute-done | bytes 65568 | tf_op jit(solution)/shard_map/ppermute | solution.py:427
  63.2 2.5 %collective-permute-start.16 = (bf16[2,32,1024]{2,1,0:T(8,128)(2,1)S(1)}, bf16[2,32,1024]{2,1,0:T(8,128)(2,1)S(1)}, u32[]{:S(2)}, u32[]{:S(2)}) collective-permute-start(bf16[2,32,1024]{2,1,0:T(8,128)(2,1)S(1)} %constant_dynamic-update-slice_fusion.2.refs_1_.rim), channel_id=1, source_target_pairs={{0,2},{1,3},{2,0},{3,1},{4,6},{5,7},{6,4},{7,5},{8,10},{9,11},{10,... | collective-permute-start | bytes 393224 | tf_op jit(solution)/shard_map/ppermute | solution.py:427
  65.7 5.1 %collective-permute-done.16.refs_5_ = bf16[2,32,1024]{2,1,0:T(8,128)(2,1)S(1)} collective-permute-done((bf16[2,32,1024]{2,1,0:T(8,128)(2,1)S(1)}, bf16[2,32,1024]{2,1,0:T(8,128)(2,1)S(1)}, u32[]{:S(2)}, u32[]{:S(2)}) %collective-permute-start.16) | collective-permute-done | bytes 131104 | tf_op jit(solution)/shard_map/ppermute | solution.py:427
  72.8 3.8 %shard_map.103 = (bf16[4,64,1024]{2,1,0:T(8,128)(2,1)S(1)}, bf16[4,64,1024]{2,1,0:T(8,128)(2,1)S(1)}, bf16[1,64,1024]{2,1,0:T(8,128)(2,1)S(1)}, bf16[1,64,1024]{2,1,0:T(8,128)(2,1)S(1)}) custom-call(s32[1]{0:T(128)} %bitcast.me_ref, bf16[4,32,1024]{2,1,0:T(8,128)(2,1)S(1)} %get-tuple-element.46.refs_0_.own, ...), custom_call_target="tpu_custom_call" | custom-call | bytes 6062084 | tf_op jit(solution)/shard_map/pallas_call | solution.py:51
  76.5 4.3 %collective-permute-start.19 = (bf16[1,64,1024]{2,1,0:T(8,128)(2,1)S(1)}, bf16[1,64,1024]{2,1,0:T(8,128)(2,1)S(1)}, u32[]{:S(2)}, u32[]{:S(2)}) collective-permute-start(bf16[1,64,1024]{2,1,0:T(8,128)(2,1)S(1)} %get-tuple-element.54), channel_id=1, source_target_pairs={{0,4},{1,5},{2,6},{3,7},{4,8},{5,9},{6,10},{7,11},{8,12},{9,13},{1... | collective-permute-start | bytes 393224 | tf_op jit(solution)/shard_map/ppermute | solution.py:427
  80.8 2.8 %collective-permute-start.23 = (bf16[4,64,1024]{2,1,0:T(8,128)(2,1)S(1)}, bf16[4,64,1024]{2,1,0:T(8,128)(2,1)S(1)}, u32[]{:S(2)}, u32[]{:S(2)}) collective-permute-start(bf16[4,64,1024]{2,1,0:T(8,128)(2,1)S(1)} %get-tuple-element.53.refs_0_), channel_id=1, source_target_pairs={{0,2},{1,3},{2,0},{3,1},{4,6},{5,7},{6,4},{7,5},{8,10},{9,11},{10,... | collective-permute-start | bytes 1572872 | tf_op jit(solution)/shard_map/ppermute | solution.py:427
  84.9 6.9 %collective-permute-done.20 = bf16[1,64,1024]{2,1,0:T(8,128)(2,1)S(1)} collective-permute-done((bf16[1,64,1024]{2,1,0:T(8,128)(2,1)S(1)}, bf16[1,64,1024]{2,1,0:T(8,128)(2,1)S(1)}, u32[]{:S(2)}, u32[]{:S(2)}) %collective-permute-start.20) | collective-permute-done | bytes 131104 | tf_op jit(solution)/shard_map/ppermute | solution.py:427
  92.2 12.3 %collective-permute-done.24.refs_5_ = bf16[2,64,1024]{2,1,0:T(8,128)(2,1)S(1)} collective-permute-done((bf16[2,64,1024]{2,1,0:T(8,128)(2,1)S(1)}, bf16[2,64,1024]{2,1,0:T(8,128)(2,1)S(1)}, u32[]{:S(2)}, u32[]{:S(2)}) %collective-permute-start.24) | collective-permute-done | bytes 262176 | tf_op jit(solution)/shard_map/ppermute | solution.py:427
  105.0 1.8 collective-permute-done.22.refs_3_
  107.2 3.9 %shard_map.104 = (bf16[4,32,1024]{2,1,0:T(8,128)(2,1)S(1)}, bf16[1,32,1024]{2,1,0:T(8,128)(2,1)S(1)}, bf16[2,32,1024]{2,1,0:T(8,128)(2,1)S(1)}) custom-call(s32[1]{0:T(128)} %bitcast.me_ref, bf16[4,64,1024]{2,1,0:T(8,128)(2,1)S(1)} %get-tuple-element.53.refs_0_, bf16[2,64,1024]{2,1,0:T(8,128)(2,1)S(1)} %constant_dynamic-update-slice_fusion.4.refs_1_, ...), custom_call_target="tpu_custom_call" | custom-call | bytes 4571140 | tf_op jit(solution)/shard_map/pallas_call | solution.py:51
  114.0 3.3 %collective-permute-start.31 = (bf16[4,32,1024]{2,1,0:T(8,128)(2,1)S(1)}, bf16[4,32,1024]{2,1,0:T(8,128)(2,1)S(1)}, u32[]{:S(2)}, u32[]{:S(2)}) collective-permute-start(bf16[4,32,1024]{2,1,0:T(8,128)(2,1)S(1)} %get-tuple-element.59.refs_0_), channel_id=1, source_target_pairs={{0,2},{1,3},{2,0},{3,1},{4,6},{5,7},{6,4},{7,5},{8,10},{9,11},{10,... | collective-permute-start | bytes 786440 | tf_op jit(solution)/shard_map/ppermute | solution.py:427
  117.4 2.5 %collective-permute-done.28 = bf16[1,32,1024]{2,1,0:T(8,128)(2,1)S(1)} collective-permute-done((bf16[1,32,1024]{2,1,0:T(8,128)(2,1)S(1)}, bf16[1,32,1024]{2,1,0:T(8,128)(2,1)S(1)}, u32[]{:S(2)}, u32[]{:S(2)}) %collective-permute-start.28) | collective-permute-done | bytes 65568 | tf_op jit(solution)/shard_map/ppermute | solution.py:427
  119.9 2.2 %collective-permute-start.32 = (bf16[3,32,1024]{2,1,0:T(8,128)(2,1)S(1)}, bf16[3,32,1024]{2,1,0:T(8,128)(2,1)S(1)}, u32[]{:S(2)}, u32[]{:S(2)}) collective-permute-start(bf16[3,32,1024]{2,1,0:T(8,128)(2,1)S(1)} %constant_dynamic-update-slice_fusion.6.refs_1_), channel_id=1, source_target_pairs={{0,2},{1,3},{2,0},{3,1},{4,6},{5,7},{6,4},{7,5},{8,10},{9,11},{10,... | collective-permute-start | bytes 589832 | tf_op jit(solution)/shard_map/ppermute | solution.py:427
  124.3 5.7 %collective-permute-done.32.refs_5_ = bf16[3,32,1024]{2,1,0:T(8,128)(2,1)S(1)} collective-permute-done((bf16[3,32,1024]{2,1,0:T(8,128)(2,1)S(1)}, bf16[3,32,1024]{2,1,0:T(8,128)(2,1)S(1)}, u32[]{:S(2)}, u32[]{:S(2)}) %collective-permute-start.32) | collective-permute-done | bytes 196640 | tf_op jit(solution)/shard_map/ppermute | solution.py:427
  130.7 2.7 %shard_map.105 = bf16[864,256]{1,0:T(8,128)(2,1)S(1)} custom-call(s32[1]{0:T(128)} %bitcast.me_ref, bf16[4,32,1024]{2,1,0:T(8,128)(2,1)S(1)} %get-tuple-element.46.refs_0_.own, bf16[2,32,1024]{2,1,0:T(8,128)(2,1)S(1)} %constant_dynamic-update-slice_fusion.2.refs_1_.rim, bf16[4,64,1024]{2,1,0:T(8,128)(2,1)S(1)} %get-tuple-element.53.refs_0_, ...), custom_call_target="tpu_custom_call" | custom-call | flops 1811939328 | bytes 2932740 | tf_op jit(solution)/shard_map/pallas_call | solution.py:51
  133.5 6.5 %shard_map.106 = bf16[32,48,256]{2,1,0:T(8,128)(2,1)} custom-call(s32[1]{0:T(128)} %bitcast.me_ref, bf16[4,32,1024]{2,1,0:T(8,128)(2,1)S(1)} %get-tuple-element.59.refs_0_, bf16[3,32,1024]{2,1,0:T(8,128)(2,1)S(1)} %constant_dynamic-update-slice_fusion.6.refs_1_, bf16[4,32,1024]{2,1,0:T(8,128)(2,1)S(1)} %collective-permute-done.29.refs_2_, ...), custom_call_target="tpu_custom_call" | custom-call | bytes 10354692 | tf_op jit(solution)/shard_map/pallas_call | solution.py:51
  140.0 16.1 %all-to-all-start = ((bf16[32,48,256]{2,1,0:T(8,128)(2,1)}), bf16[32,48,256]{2,1,0:T(8,128)(2,1)S(1)}, u32[]{:S(2)}, u32[]{:S(2)}) async-start(bf16[32,48,256]{2,1,0:T(8,128)(2,1)} %shard_map.106), calls=%async_computation | async-start | bytes 1572864 | tf_op jit(solution)/shard_map/all_to_all | solution.py:444
  156.0 14.3 %all-to-all-done = bf16[32,48,256]{2,1,0:T(8,128)(2,1)S(1)} async-done(((bf16[32,48,256]{2,1,0:T(8,128)(2,1)}), bf16[32,48,256]{2,1,0:T(8,128)(2,1)S(1)}, u32[]{:S(2)}, u32[]{:S(2)}) %all-to-all-start) | async-done | bytes 786464 | tf_op jit(solution)/shard_map/all_to_all | solution.py:444
  170.5 1.8 collective-permute-start.35
  172.3 2.0 collective-permute-start.37
  178.0 4.3 %all-to-all-start.1 = ((bf16[32,48,256]{2,1,0:T(8,128)(2,1)}), bf16[32,48,256]{2,1,0:T(8,128)(2,1)S(1)}, u32[]{:S(2)}, u32[]{:S(2)}) async-start(bf16[32,48,256]{2,1,0:T(8,128)(2,1)} %broadcast_in_dim.15), calls=%async_computation.1 | async-start | bytes 1572864 | tf_op jit(solution)/shard_map/all_to_all | solution.py:453
  183.3 12.7 %all-to-all-done.1.packed = bf16[32,48,256]{2,1,0:T(8,128)(2,1)S(1)} async-done(((bf16[32,48,256]{2,1,0:T(8,128)(2,1)}), bf16[32,48,256]{2,1,0:T(8,128)(2,1)S(1)}, u32[]{:S(2)}, u32[]{:S(2)}) %all-to-all-start.1) | async-done | bytes 786464 | tf_op jit(solution)/shard_map/all_to_all | solution.py:453
  (116 shorter events, 27.5 us)
Async XLA Ops:
  7.2 44.3 %all-gather.3.cloned.1.call-start = ((), (), s32[]{:S(2)}) async-start(), calls=%async_computation.2 | async-start | bytes 3317760 | tf_op jit(solution)/shard_map/all_gather | solution.py:464
  9.3 5.4 %collective-permute-start.2 = (bf16[4,3,3,512]{3,2,1,0:T(4,128)(2,1)S(1)}, bf16[4,3,3,512]{3,2,1,0:T(4,128)(2,1)S(1)}, u32[]{:S(2)}, u32[]{:S(2)}) collective-permute-start(bf16[4,3,3,512]{3,2,1,0:T(4,128)(2,1)S(1)} %slice.20), channel_id=1, source_target_pairs={{5,0},{6,1},{7,2},{9,4},{10,5},{11,6},{13,8},{14,9},{15,10},{17,12... | collective-permute-start | bytes 110600 | tf_op jit(solution)/shard_map/ppermute | solution.py:427
  10.7 4.0 %collective-permute-start.1 = (bf16[4,16,3,512]{3,2,1,0:T(4,128)(2,1)S(1)}, bf16[4,16,3,512]{3,2,1,0:T(4,128)(2,1)S(1)}, u32[]{:S(2)}, u32[]{:S(2)}) collective-permute-start(bf16[4,16,3,512]{3,2,1,0:T(4,128)(2,1)S(1)} %slice.19), channel_id=1, source_target_pairs={{1,0},{2,1},{3,2},{5,4},{6,5},{7,6},{9,8},{10,9},{11,10},{13,12},{... | collective-permute-start | bytes 589832 | tf_op jit(solution)/shard_map/ppermute | solution.py:427
  12.0 7.1 %collective-permute-start = (bf16[4,3,8,512]{3,2,1,0:T(8,128)(2,1)S(1)}, bf16[4,3,8,512]{3,2,1,0:T(8,128)(2,1)S(1)}, u32[]{:S(2)}, u32[]{:S(2)}) collective-permute-start(bf16[4,3,8,512]{3,2,1,0:T(8,128)(2,1)S(1)} %slice.18), channel_id=1, source_target_pairs={{4,0},{5,1},{6,2},{7,3},{8,4},{9,5},{10,6},{11,7},{12,8},{13,9},{1... | collective-permute-start | bytes 294920 | tf_op jit(solution)/shard_map/ppermute | solution.py:427
  27.6 10.3 %collective-permute-start.3 = (bf16[1,64,512]{2,1,0:T(8,128)(2,1)S(1)}, bf16[1,64,512]{2,1,0:T(8,128)(2,1)S(1)}, u32[]{:S(2)}, u32[]{:S(2)}) collective-permute-start(bf16[1,64,512]{2,1,0:T(8,128)(2,1)S(1)} %get-tuple-element.42), channel_id=1, source_target_pairs={{0,4},{1,5},{2,6},{3,7},{4,8},{5,9},{6,10},{7,11},{8,12},{9,13},{1... | collective-permute-start | bytes 196616 | tf_op jit(solution)/shard_map/ppermute | solution.py:427
  31.1 6.8 %collective-permute-start.4 = (bf16[1,64,512]{2,1,0:T(8,128)(2,1)S(1)}, bf16[1,64,512]{2,1,0:T(8,128)(2,1)S(1)}, u32[]{:S(2)}, u32[]{:S(2)}) collective-permute-start(bf16[1,64,512]{2,1,0:T(8,128)(2,1)S(1)} %get-tuple-element.43), channel_id=1, source_target_pairs={{4,0},{5,1},{6,2},{7,3},{8,4},{9,5},{10,6},{11,7},{12,8},{13,9},{1... | collective-permute-start | bytes 196616 | tf_op jit(solution)/shard_map/ppermute | solution.py:427
  32.4 17.2 %collective-permute-start.7 = (bf16[4,64,384]{2,1,0:T(8,128)(2,1)S(1)}, bf16[4,64,384]{2,1,0:T(8,128)(2,1)S(1)}, u32[]{:S(2)}, u32[]{:S(2)}) collective-permute-start(bf16[4,64,384]{2,1,0:T(8,128)(2,1)S(1)} %get-tuple-element.41.refs_0_), channel_id=1, source_target_pairs={{0,2},{1,3},{2,0},{3,1},{4,6},{5,7},{6,4},{7,5},{8,10},{9,11},{10,... | collective-permute-start | bytes 589832 | tf_op jit(solution)/shard_map/ppermute | solution.py:427
  37.9 11.7 %collective-permute-start.8 = (bf16[2,64,512]{2,1,0:T(8,128)(2,1)S(1)}, bf16[2,64,512]{2,1,0:T(8,128)(2,1)S(1)}, u32[]{:S(2)}, u32[]{:S(2)}) collective-permute-start(bf16[2,64,512]{2,1,0:T(8,128)(2,1)S(1)} %constant_dynamic-update-slice_fusion.refs_1_), channel_id=1, source_target_pairs={{0,2},{1,3},{2,0},{3,1},{4,6},{5,7},{6,4},{7,5},{8,10},{9,11},{10,... | collective-permute-start | bytes 393224 | tf_op jit(solution)/shard_map/ppermute | solution.py:427
  42.6 8.6 %collective-permute-start.5 = (bf16[4,64,384]{2,1,0:T(8,128)(2,1)S(1)}, bf16[4,64,384]{2,1,0:T(8,128)(2,1)S(1)}, u32[]{:S(2)}, u32[]{:S(2)}) collective-permute-start(bf16[4,64,384]{2,1,0:T(8,128)(2,1)S(1)} %get-tuple-element.41.refs_0_), channel_id=1, source_target_pairs={{0,1},{1,0},{2,3},{3,2},{4,5},{5,4},{6,7},{7,6},{8,9},{9,8},{10,11... | collective-permute-start | bytes 589832 | tf_op jit(solution)/shard_map/ppermute | solution.py:427
  55.0 5.8 %collective-permute-start.11 = (bf16[1,32,1024]{2,1,0:T(8,128)(2,1)S(1)}, bf16[1,32,1024]{2,1,0:T(8,128)(2,1)S(1)}, u32[]{:S(2)}, u32[]{:S(2)}) collective-permute-start(bf16[1,32,1024]{2,1,0:T(8,128)(2,1)S(1)} %get-tuple-element.47), channel_id=1, source_target_pairs={{0,4},{1,5},{2,6},{3,7},{4,8},{5,9},{6,10},{7,11},{8,12},{9,13},{1... | collective-permute-start | bytes 196616 | tf_op jit(solution)/shard_map/ppermute | solution.py:427
  57.0 6.2 %collective-permute-start.12 = (bf16[1,32,1024]{2,1,0:T(8,128)(2,1)S(1)}, bf16[1,32,1024]{2,1,0:T(8,128)(2,1)S(1)}, u32[]{:S(2)}, u32[]{:S(2)}) collective-permute-start(bf16[1,32,1024]{2,1,0:T(8,128)(2,1)S(1)} %get-tuple-element.48), channel_id=1, source_target_pairs={{4,0},{5,1},{6,2},{7,3},{8,4},{9,5},{10,6},{11,7},{12,8},{13,9},{1... | collective-permute-start | bytes 196616 | tf_op jit(solution)/shard_map/ppermute | solution.py:427
  58.3 12.5 %collective-permute-start.15 = (bf16[4,32,1024]{2,1,0:T(8,128)(2,1)S(1)}, bf16[4,32,1024]{2,1,0:T(8,128)(2,1)S(1)}, u32[]{:S(2)}, u32[]{:S(2)}) collective-permute-start(bf16[4,32,1024]{2,1,0:T(8,128)(2,1)S(1)} %get-tuple-element.46.refs_0_.own), channel_id=1, source_target_pairs={{0,2},{1,3},{2,0},{3,1},{4,6},{5,7},{6,4},{7,5},{8,10},{9,11},{10,... | collective-permute-start | bytes 786440 | tf_op jit(solution)/shard_map/ppermute | solution.py:427
  63.2 7.6 %collective-permute-start.16 = (bf16[2,32,1024]{2,1,0:T(8,128)(2,1)S(1)}, bf16[2,32,1024]{2,1,0:T(8,128)(2,1)S(1)}, u32[]{:S(2)}, u32[]{:S(2)}) collective-permute-start(bf16[2,32,1024]{2,1,0:T(8,128)(2,1)S(1)} %constant_dynamic-update-slice_fusion.2.refs_1_.rim), channel_id=1, source_target_pairs={{0,2},{1,3},{2,0},{3,1},{4,6},{5,7},{6,4},{7,5},{8,10},{9,11},{10,... | collective-permute-start | bytes 393224 | tf_op jit(solution)/shard_map/ppermute | solution.py:427
  65.7 6.9 %collective-permute-start.13 = (bf16[4,32,1024]{2,1,0:T(8,128)(2,1)S(1)}, bf16[4,32,1024]{2,1,0:T(8,128)(2,1)S(1)}, u32[]{:S(2)}, u32[]{:S(2)}) collective-permute-start(bf16[4,32,1024]{2,1,0:T(8,128)(2,1)S(1)} %get-tuple-element.46.refs_0_.own), channel_id=1, source_target_pairs={{0,1},{1,0},{2,3},{3,2},{4,5},{5,4},{6,7},{7,6},{8,9},{9,8},{10,11... | collective-permute-start | bytes 786440 | tf_op jit(solution)/shard_map/ppermute | solution.py:427
  76.5 8.3 %collective-permute-start.19 = (bf16[1,64,1024]{2,1,0:T(8,128)(2,1)S(1)}, bf16[1,64,1024]{2,1,0:T(8,128)(2,1)S(1)}, u32[]{:S(2)}, u32[]{:S(2)}) collective-permute-start(bf16[1,64,1024]{2,1,0:T(8,128)(2,1)S(1)} %get-tuple-element.54), channel_id=1, source_target_pairs={{0,4},{1,5},{2,6},{3,7},{4,8},{5,9},{6,10},{7,11},{8,12},{9,13},{1... | collective-permute-start | bytes 393224 | tf_op jit(solution)/shard_map/ppermute | solution.py:427
  80.8 23.7 %collective-permute-start.23 = (bf16[4,64,1024]{2,1,0:T(8,128)(2,1)S(1)}, bf16[4,64,1024]{2,1,0:T(8,128)(2,1)S(1)}, u32[]{:S(2)}, u32[]{:S(2)}) collective-permute-start(bf16[4,64,1024]{2,1,0:T(8,128)(2,1)S(1)} %get-tuple-element.53.refs_0_), channel_id=1, source_target_pairs={{0,2},{1,3},{2,0},{3,1},{4,6},{5,7},{6,4},{7,5},{8,10},{9,11},{10,... | collective-permute-start | bytes 1572872 | tf_op jit(solution)/shard_map/ppermute | solution.py:427
  83.6 8.2 %collective-permute-start.20 = (bf16[1,64,1024]{2,1,0:T(8,128)(2,1)S(1)}, bf16[1,64,1024]{2,1,0:T(8,128)(2,1)S(1)}, u32[]{:S(2)}, u32[]{:S(2)}) collective-permute-start(bf16[1,64,1024]{2,1,0:T(8,128)(2,1)S(1)} %get-tuple-element.55), channel_id=1, source_target_pairs={{4,0},{5,1},{6,2},{7,3},{8,4},{9,5},{10,6},{11,7},{12,8},{13,9},{1... | collective-permute-start | bytes 393224 | tf_op jit(solution)/shard_map/ppermute | solution.py:427
  91.8 12.7 %collective-permute-start.24 = (bf16[2,64,1024]{2,1,0:T(8,128)(2,1)S(1)}, bf16[2,64,1024]{2,1,0:T(8,128)(2,1)S(1)}, u32[]{:S(2)}, u32[]{:S(2)}) collective-permute-start(bf16[2,64,1024]{2,1,0:T(8,128)(2,1)S(1)} %constant_dynamic-update-slice_fusion.4.refs_1_), channel_id=1, source_target_pairs={{0,2},{1,3},{2,0},{3,1},{4,6},{5,7},{6,4},{7,5},{8,10},{9,11},{10,... | collective-permute-start | bytes 786440 | tf_op jit(solution)/shard_map/ppermute | solution.py:427
  92.2 14.6 %collective-permute-start.21 = (bf16[4,64,1024]{2,1,0:T(8,128)(2,1)S(1)}, bf16[4,64,1024]{2,1,0:T(8,128)(2,1)S(1)}, u32[]{:S(2)}, u32[]{:S(2)}) collective-permute-start(bf16[4,64,1024]{2,1,0:T(8,128)(2,1)S(1)} %get-tuple-element.53.refs_0_), channel_id=1, source_target_pairs={{0,1},{1,0},{2,3},{3,2},{4,5},{5,4},{6,7},{7,6},{8,9},{9,8},{10,11... | collective-permute-start | bytes 1572872 | tf_op jit(solution)/shard_map/ppermute | solution.py:427
  111.1 6.3 %collective-permute-start.27 = (bf16[2,32,1024]{2,1,0:T(8,128)(2,1)S(1)}, bf16[2,32,1024]{2,1,0:T(8,128)(2,1)S(1)}, u32[]{:S(2)}, u32[]{:S(2)}) collective-permute-start(bf16[2,32,1024]{2,1,0:T(8,128)(2,1)S(1)} %get-tuple-element.60), channel_id=1, source_target_pairs={{0,4},{1,5},{2,6},{3,7},{4,8},{5,9},{6,10},{7,11},{8,12},{9,13},{1... | collective-permute-start | bytes 393224 | tf_op jit(solution)/shard_map/ppermute | solution.py:427
  112.7 7.2 %collective-permute-start.28 = (bf16[1,32,1024]{2,1,0:T(8,128)(2,1)S(1)}, bf16[1,32,1024]{2,1,0:T(8,128)(2,1)S(1)}, u32[]{:S(2)}, u32[]{:S(2)}) collective-permute-start(bf16[1,32,1024]{2,1,0:T(8,128)(2,1)S(1)} %get-tuple-element.61), channel_id=1, source_target_pairs={{4,0},{5,1},{6,2},{7,3},{8,4},{9,5},{10,6},{11,7},{12,8},{13,9},{1... | collective-permute-start | bytes 196616 | tf_op jit(solution)/shard_map/ppermute | solution.py:427
  114.0 10.3 %collective-permute-start.31 = (bf16[4,32,1024]{2,1,0:T(8,128)(2,1)S(1)}, bf16[4,32,1024]{2,1,0:T(8,128)(2,1)S(1)}, u32[]{:S(2)}, u32[]{:S(2)}) collective-permute-start(bf16[4,32,1024]{2,1,0:T(8,128)(2,1)S(1)} %get-tuple-element.59.refs_0_), channel_id=1, source_target_pairs={{0,2},{1,3},{2,0},{3,1},{4,6},{5,7},{6,4},{7,5},{8,10},{9,11},{10,... | collective-permute-start | bytes 786440 | tf_op jit(solution)/shard_map/ppermute | solution.py:427
  119.9 10.1 %collective-permute-start.32 = (bf16[3,32,1024]{2,1,0:T(8,128)(2,1)S(1)}, bf16[3,32,1024]{2,1,0:T(8,128)(2,1)S(1)}, u32[]{:S(2)}, u32[]{:S(2)}) collective-permute-start(bf16[3,32,1024]{2,1,0:T(8,128)(2,1)S(1)} %constant_dynamic-update-slice_fusion.6.refs_1_), channel_id=1, source_target_pairs={{0,2},{1,3},{2,0},{3,1},{4,6},{5,7},{6,4},{7,5},{8,10},{9,11},{10,... | collective-permute-start | bytes 589832 | tf_op jit(solution)/shard_map/ppermute | solution.py:427
  122.2 11.2 %collective-permute-start.29 = (bf16[4,32,1024]{2,1,0:T(8,128)(2,1)S(1)}, bf16[4,32,1024]{2,1,0:T(8,128)(2,1)S(1)}, u32[]{:S(2)}, u32[]{:S(2)}) collective-permute-start(bf16[4,32,1024]{2,1,0:T(8,128)(2,1)S(1)} %get-tuple-element.59.refs_0_), channel_id=1, source_target_pairs={{0,1},{1,0},{2,3},{3,2},{4,5},{5,4},{6,7},{7,6},{8,9},{9,8},{10,11... | collective-permute-start | bytes 786440 | tf_op jit(solution)/shard_map/ppermute | solution.py:427
  122.3 11.1 %collective-permute-start.30 = (bf16[3,32,1024]{2,1,0:T(8,128)(2,1)S(1)}, bf16[3,32,1024]{2,1,0:T(8,128)(2,1)S(1)}, u32[]{:S(2)}, u32[]{:S(2)}) collective-permute-start(bf16[3,32,1024]{2,1,0:T(8,128)(2,1)S(1)} %constant_dynamic-update-slice_fusion.6.refs_1_), channel_id=1, source_target_pairs={{0,1},{1,0},{2,3},{3,2},{4,5},{5,4},{6,7},{7,6},{8,9},{9,8},{10,11... | collective-permute-start | bytes 589832 | tf_op jit(solution)/shard_map/ppermute | solution.py:427
  130.0 3.4 %collective-permute-start.33 = (bf16[4,32,1024]{2,1,0:T(8,128)(2,1)S(1)}, bf16[4,32,1024]{2,1,0:T(8,128)(2,1)S(1)}, u32[]{:S(2)}, u32[]{:S(2)}) collective-permute-start(bf16[4,32,1024]{2,1,0:T(8,128)(2,1)S(1)} %collective-permute-done.31.refs_4_), channel_id=1, source_target_pairs={{0,1},{1,0},{2,3},{3,2},{4,5},{5,4},{6,7},{7,6},{8,9},{9,8},{10,11... | collective-permute-start | bytes 786440 | tf_op jit(solution)/shard_map/ppermute | solution.py:427
  130.0 3.4 %collective-permute-start.34 = (bf16[3,32,1024]{2,1,0:T(8,128)(2,1)S(1)}, bf16[3,32,1024]{2,1,0:T(8,128)(2,1)S(1)}, u32[]{:S(2)}, u32[]{:S(2)}) collective-permute-start(bf16[3,32,1024]{2,1,0:T(8,128)(2,1)S(1)} %collective-permute-done.32.refs_5_), channel_id=1, source_target_pairs={{0,1},{1,0},{2,3},{3,2},{4,5},{5,4},{6,7},{7,6},{8,9},{9,8},{10,11... | collective-permute-start | bytes 589832 | tf_op jit(solution)/shard_map/ppermute | solution.py:427
  140.0 30.4 %all-to-all-start = ((bf16[32,48,256]{2,1,0:T(8,128)(2,1)}), bf16[32,48,256]{2,1,0:T(8,128)(2,1)S(1)}, u32[]{:S(2)}, u32[]{:S(2)}) async-start(bf16[32,48,256]{2,1,0:T(8,128)(2,1)} %shard_map.106), calls=%async_computation | async-start | bytes 1572864 | tf_op jit(solution)/shard_map/all_to_all | solution.py:444
  170.5 5.4 %collective-permute-start.35 = (bf16[48,256]{1,0:T(8,128)(2,1)S(1)}, bf16[48,256]{1,0:T(8,128)(2,1)S(1)}, u32[]{:S(2)}, u32[]{:S(2)}) collective-permute-start(bf16[48,256]{1,0:T(8,128)(2,1)S(1)} %convert_element_type.29), channel_id=1, source_target_pairs={{0,2},{1,3},{2,0},{3,1},{4,6},{5,7},{6,4},{7,5},{8,10},{9,11},{10,... | collective-permute-start | bytes 73736 | tf_op jit(solution)/shard_map/ppermute | solution.py:427
  172.3 4.8 %collective-permute-start.36 = (bf16[48,256]{1,0:T(8,128)(2,1)S(1)}, bf16[48,256]{1,0:T(8,128)(2,1)S(1)}, u32[]{:S(2)}, u32[]{:S(2)}) collective-permute-start(bf16[48,256]{1,0:T(8,128)(2,1)S(1)} %convert_element_type.29), channel_id=1, source_target_pairs={{0,3},{1,2},{2,1},{3,0},{4,7},{5,6},{6,5},{7,4},{8,11},{9,10},{10,... | collective-permute-start | bytes 73736 | tf_op jit(solution)/shard_map/ppermute | solution.py:427
  172.3 4.8 %collective-permute-start.37 = (bf16[48,256]{1,0:T(8,128)(2,1)S(1)}, bf16[48,256]{1,0:T(8,128)(2,1)S(1)}, u32[]{:S(2)}, u32[]{:S(2)}) collective-permute-start(bf16[48,256]{1,0:T(8,128)(2,1)S(1)} %convert_element_type.29), channel_id=1, source_target_pairs={{0,1},{1,0},{2,3},{3,2},{4,5},{5,4},{6,7},{7,6},{8,9},{9,8},{10,11... | collective-permute-start | bytes 73736 | tf_op jit(solution)/shard_map/ppermute | solution.py:427
  178.0 17.9 %all-to-all-start.1 = ((bf16[32,48,256]{2,1,0:T(8,128)(2,1)}), bf16[32,48,256]{2,1,0:T(8,128)(2,1)S(1)}, u32[]{:S(2)}, u32[]{:S(2)}) async-start(bf16[32,48,256]{2,1,0:T(8,128)(2,1)} %broadcast_in_dim.15), calls=%async_computation.1 | async-start | bytes 1572864 | tf_op jit(solution)/shard_map/all_to_all | solution.py:453
  (22 other events, 160.0 us)
Sparse Core Ops, SparseCore 0:
  10.3 34.8 all-gather.2

commit v4 on v3

--- a/solution.py
+++ b/solution.py
@@ -89,11 +89,17 @@
     field, act_one, slope_one, sems = refs[7:]
     phases = phase_matrix()
     rows = row_matrix()
-    for d in range(19):
-        block = jnp.reshape(vol[:, d], (64, 512))
+    for start in range(0, 19, 4):
+        planes = range(start, min(start + 4, 19))
+        block = jnp.concatenate([jnp.reshape(vol[:, d], (64, 512)) for d in planes], 0)
         split = mm(block, phases).astype(BF)
-        stacked = jnp.concatenate([split[:, p * 128 : p * 128 + 128] for p in range(5)], 0)
-        field[d] = mm(rows, stacked).astype(BF)
+        columns = []
+        for n in range(len(planes)):
+            parts = [split[n * 64 : n * 64 + 64, p * 128 : p * 128 + 128] for p in range(5)]
+            columns.append(jnp.concatenate(parts, 0))
+        placed = mm(rows, jnp.concatenate(columns, 1)).astype(BF)
+        for n, d in enumerate(planes):
+            field[d] = placed[:, n * 128 : n * 128 + 128]
     leaving = [begin(field, field_out, sems.at[0])]
     for d in range(9):
         columns = []
@@ -413,7 +419,9 @@
     grad_two[...] = both[:864]
     for t in range(9):
         at = 864 + 32 * t
-        grad_one[t] = both[at : at + 12, :32] + both[at + 8 : at + 20, 32:]
+        value = both[at : at + 12, :32] + both[at + 8 : at + 20, 32:]
+        for c in range(3):
+            grad_one[t // 3, t % 3, c] = value[4 * c : 4 * c + 4]
 
 
 def moved(block, depth_step, chan_of):
@@ -427,7 +435,7 @@
     return lax.ppermute(block, BOTH, route)
 
 
-def gathered(own, first, last):
+def gathered(own, first, last, meanwhile=None):
     across = moved(own, 0, lambda c: c ^ 2)
     up = moved(last, 1, lambda c: c)
     down = moved(first, -1, lambda c: c)
@@ -435,21 +443,23 @@
     rim = jnp.concatenate([up, down], 0)
     across_rim = moved(rim, 0, lambda c: c ^ 2)
     core_rim = moved(rim, 0, lambda c: c ^ 1)
-    across, across_rim = lax.optimization_barrier((across, across_rim))
+    across, across_rim, meanwhile = lax.optimization_barrier((across, across_rim, meanwhile))
     last_pair = [moved(piece, 0, lambda c: c ^ 1) for piece in (across, across_rim)]
-    return [own, rim, core, core_rim, across, across_rim, *last_pair]
+    blocks = [own, rim, core, core_rim, across, across_rim, *last_pair]
+    return blocks if meanwhile is None else (blocks, meanwhile)
 
 
 def summed(parts):
     terms = lax.all_to_all(parts, "space", 0, 0)
     own = jnp.sum(terms.astype(F32), 0)
-    sent = own.astype(BF)
-    others = [moved(sent, 0, lambda c, k=k: c ^ k).astype(F32) for k in (2, 3, 1)]
     shape = own.shape
     row = lax.broadcasted_iota(jnp.int32, shape, 0)
     shared = (row >= 32) & (lane_of(shape) >= 128) | (lax.axis_index("space") == 27)
-    total = own + jnp.where(shared, others[0] + others[1] + others[2], 0.0)
-    total = total.astype(BF)
+    both = own
+    for step in (1, 2):
+        sent = lax.optimization_barrier(both.astype(BF))
+        both = sent.astype(F32) + moved(sent, 0, lambda c, step=step: c ^ step).astype(F32)
+    total = jnp.where(shared, both, own).astype(BF)
     return lax.all_to_all(jnp.broadcast_to(total[None], parts.shape), "space", 0, 0)
 
 
@@ -527,12 +537,13 @@
         flops=2 * 864 * 256 * 4096,
         anywhere=range(3, 7),
     )
+    blocks, grad_four = gathered(back_three, first, last, grad_four)
     (grads,) = call(
         last_kernel,
         [((32, 48, 256), BF)],
         [
             me,
-            *gathered(back_three, first, last),
+            *blocks,
             filters,
             w_back,
             own_two,
@@ -561,11 +572,10 @@
     )
     grad_one, grad_two, grad_three, grad_four = call(
         unpack_kernel,
-        [((9, 12, 32), F32), ((864, 64), F32), ((27, 16, 128), F32), ((27, 32, 256), F32)],
+        [((3, 3, 3, 4, 32), F32), ((864, 64), F32), ((27, 16, 128), F32), ((27, 32, 256), F32)],
         [summed(grads)],
         [((1152, 64), F32)],
     )
-    grad_one = grad_one.reshape(3, 3, 3, 4, 32)
     grad_two = grad_two.reshape(3, 3, 3, 32, 64)
     grad_three = grad_three.reshape(3, 3, 3, 16, 128)
     grad_four = grad_four.reshape(3, 3, 3, 32, 256)

time: 206 us -> 199 us (0.966)
  starting transfers between devices: 71.2 us -> 43.4 us
  blocking collectives: 0 us -> 26.3 us
  Pallas kernels: 30.1 us -> 25.7 us
    all_to_all x0 -> x1, blocking collectives: none -> 26.3 us  [summed(): terms = lax.all_to_all(parts, 'space', 0, 0)]
    all_to_all x1 -> x0, starting transfers between devices: 16.1 us -> none  [summed(): terms = lax.all_to_all(parts, 'space', 0, 0)]
    ppermute x38 -> x37, waiting for transfers between devices: 55.8 us -> 70.6 us  [moved(): return lax.ppermute(block, BOTH, route)]
    all_to_all x1 -> x0, waiting for transfers between devices: 14.3 us -> none  [summed(): terms = lax.all_to_all(parts, 'space', 0, 0)]
    ppermute x38 -> x37, starting transfers between devices: 50.9 us -> 39 us  [moved(): return lax.ppermute(block, BOTH, route)]
    pallas_call x7, Pallas kernels: 30.1 us -> 25.7 us  [call(): pl.pallas_call(kernel, out_shape=[pltpu.HBM(s, t) if place in away else j...]
  transfers between devices with their start and end apart: 41 -> 39, of which waited for: 20 -> 23; matrix products, arithmetic and copies ran while one was open for 1% -> 1% of each run, Pallas kernels for 5% -> 4%
where the time goes in v4:
time: 199 us; the launch traced here: 198 us
  waiting for transfers between devices  82.8 us (42%)
  starting transfers between devices  43.4 us (22%)
  blocking collectives  26.3 us (13%)
  Pallas kernels  25.7 us (13%)
  between operations  14.5 us (7%)
  local copies, waits for them, and re-layouts  2.79 us (1%)
  other arithmetic  2.7 us (1%)
    ppermute x37, waiting for transfers between devices, moved(): return lax.ppermute(block, BOTH, route)  70.6 us
    ppermute x37, starting transfers between devices, moved(): return lax.ppermute(block, BOTH, route)  39 us
    all_to_all x1, blocking collectives, summed(): terms = lax.all_to_all(parts, 'space', 0, 0)  26.3 us
    pallas_call x7, Pallas kernels, call(): pl.pallas_call(kernel, out_shape=[pltpu.HBM(s, t) if place in away else j...  25.7 us
    all_to_all x1, waiting for transfers between devices, summed(): lax.all_to_all(jnp.broadcast_to(total[None], parts.shape), 'space', 0, 0)  12.3 us
    all_to_all x1, starting transfers between devices, summed(): lax.all_to_all(jnp.broadcast_to(total[None], parts.shape), 'space', 0, 0)  4.35 us
  transfers between devices with their start and end apart: 39, of which 23 were waited for; matrix products, arithmetic and copies ran while one was open for 1% of the time, Pallas kernels for 4%

profile of v4, /device:TPU:0, one launch (start us, length us, event | category | flops | bytes accessed | tf_op | source)
XLA Modules:
  0.0 198.2 jit_solution(13838294975629128116)
XLA Ops:
  7.2 2.0 %fusion.3 = bf16[27,48,256]{2,1,0:T(8,128)(2,1)} fusion(bf16[27,16,128]{2,1,0:T(8,128)(2,1)} %bitcast.53, bf16[27,32,256]{2,1,0:T(8,128)(2,1)} %bitcast.42), kind=kLoop, calls=%fused_computation.7 | loop fusion | flops 1990656 | bytes 1216512 | tf_op jit(solution)/shard_map/concatenate | solution.py:474
  12.0 1.4 collective-permute-start
  14.9 4.2 %collective-permute-done = bf16[4,3,8,512]{3,2,1,0:T(8,128)(2,1)S(1)} collective-permute-done((bf16[4,3,8,512]{3,2,1,0:T(8,128)(2,1)S(1)}, bf16[4,3,8,512]{3,2,1,0:T(8,128)(2,1)S(1)}, u32[]{:S(2)}, u32[]{:S(2)}) %collective-permute-start) | collective-permute-done | bytes 98336 | tf_op jit(solution)/shard_map/ppermute | solution.py:435
  19.3 4.7 %shard_map.101 = (bf16[19,352,128]{2,1,0:T(8,128)(2,1)}, bf16[9,480,128]{2,1,0:T(8,128)(2,1)}, f32[8,64,512]{2,1,0:T(8,128)}, bf16[4,64,384]{2,1,0:T(8,128)(2,1)...) custom-call(bf16[4,19,16,512]{3,2,1,0:T(8,128)(2,1)S(1)} %pad_maximum_fusion.vol, ...), custom_call_target="tpu_custom_call" | custom-call | bytes 5849088 | tf_op jit(solution)/shard_map/pallas_call | solution.py:51
  24.0 3.5 %collective-permute-start.3 = (bf16[1,64,512]{2,1,0:T(8,128)(2,1)S(1)}, bf16[1,64,512]{2,1,0:T(8,128)(2,1)S(1)}, u32[]{:S(2)}, u32[]{:S(2)}) collective-permute-start(bf16[1,64,512]{2,1,0:T(8,128)(2,1)S(1)} %get-tuple-element.43), channel_id=1, source_target_pairs={{0,4},{1,5},{2,6},{3,7},{4,8},{5,9},{6,10},{7,11},{8,12},{9,13},{1... | collective-permute-start | bytes 196616 | tf_op jit(solution)/shard_map/ppermute | solution.py:435
  28.8 5.5 %collective-permute-start.7 = (bf16[4,64,384]{2,1,0:T(8,128)(2,1)S(1)}, bf16[4,64,384]{2,1,0:T(8,128)(2,1)S(1)}, u32[]{:S(2)}, u32[]{:S(2)}) collective-permute-start(bf16[4,64,384]{2,1,0:T(8,128)(2,1)S(1)} %get-tuple-element.42.refs_0_), channel_id=1, source_target_pairs={{0,2},{1,3},{2,0},{3,1},{4,6},{5,7},{6,4},{7,5},{8,10},{9,11},{10,... | collective-permute-start | bytes 589832 | tf_op jit(solution)/shard_map/ppermute | solution.py:435
  34.3 4.7 %collective-permute-start.8 = (bf16[2,64,512]{2,1,0:T(8,128)(2,1)S(1)}, bf16[2,64,512]{2,1,0:T(8,128)(2,1)S(1)}, u32[]{:S(2)}, u32[]{:S(2)}) collective-permute-start(bf16[2,64,512]{2,1,0:T(8,128)(2,1)S(1)} %constant_dynamic-update-slice_fusion.refs_1_), channel_id=1, source_target_pairs={{0,2},{1,3},{2,0},{3,1},{4,6},{5,7},{6,4},{7,5},{8,10},{9,11},{10,... | collective-permute-start | bytes 393224 | tf_op jit(solution)/shard_map/ppermute | solution.py:435
  39.0 10.5 %collective-permute-done.8.refs_5_ = bf16[2,64,512]{2,1,0:T(8,128)(2,1)S(1)} collective-permute-done((bf16[2,64,512]{2,1,0:T(8,128)(2,1)S(1)}, bf16[2,64,512]{2,1,0:T(8,128)(2,1)S(1)}, u32[]{:S(2)}, u32[]{:S(2)}) %collective-permute-start.8) | collective-permute-done | bytes 131104 | tf_op jit(solution)/shard_map/ppermute | solution.py:435
  51.4 3.6 %shard_map.102 = (bf16[4,32,1024]{2,1,0:T(8,128)(2,1)S(1)}, bf16[1,32,1024]{2,1,0:T(8,128)(2,1)S(1)}, bf16[1,32,1024]{2,1,0:T(8,128)(2,1)S(1)}, f32[4,32,1024]{2...) custom-call(s32[1]{0:T(128)} %bitcast.me_ref, ...), custom_call_target="tpu_custom_call" | custom-call | bytes 5242884 | tf_op jit(solution)/shard_map/pallas_call | solution.py:51
  55.0 2.0 %collective-permute-start.11 = (bf16[1,32,1024]{2,1,0:T(8,128)(2,1)S(1)}, bf16[1,32,1024]{2,1,0:T(8,128)(2,1)S(1)}, u32[]{:S(2)}, u32[]{:S(2)}) collective-permute-start(bf16[1,32,1024]{2,1,0:T(8,128)(2,1)S(1)} %get-tuple-element.48), channel_id=1, source_target_pairs={{0,4},{1,5},{2,6},{3,7},{4,8},{5,9},{6,10},{7,11},{8,12},{9,13},{1... | collective-permute-start | bytes 196616 | tf_op jit(solution)/shard_map/ppermute | solution.py:435
  58.9 4.3 %collective-permute-done.12 = bf16[1,32,1024]{2,1,0:T(8,128)(2,1)S(1)} collective-permute-done((bf16[1,32,1024]{2,1,0:T(8,128)(2,1)S(1)}, bf16[1,32,1024]{2,1,0:T(8,128)(2,1)S(1)}, u32[]{:S(2)}, u32[]{:S(2)}) %collective-permute-start.12) | collective-permute-done | bytes 65568 | tf_op jit(solution)/shard_map/ppermute | solution.py:435
  63.7 8.6 %collective-permute-done.16.refs_5_ = bf16[2,32,1024]{2,1,0:T(8,128)(2,1)S(1)} collective-permute-done((bf16[2,32,1024]{2,1,0:T(8,128)(2,1)S(1)}, bf16[2,32,1024]{2,1,0:T(8,128)(2,1)S(1)}, u32[]{:S(2)}, u32[]{:S(2)}) %collective-permute-start.16) | collective-permute-done | bytes 131104 | tf_op jit(solution)/shard_map/ppermute | solution.py:435
  74.2 3.8 %shard_map.103 = (bf16[4,64,1024]{2,1,0:T(8,128)(2,1)S(1)}, bf16[4,64,1024]{2,1,0:T(8,128)(2,1)S(1)}, bf16[1,64,1024]{2,1,0:T(8,128)(2,1)S(1)}, bf16[1,64,1024]{2,1,0:T(8,128)(2,1)S(1)}) custom-call(s32[1]{0:T(128)} %bitcast.me_ref, bf16[4,32,1024]{2,1,0:T(8,128)(2,1)S(1)} %get-tuple-element.47.refs_0_.own, ...), custom_call_target="tpu_custom_call" | custom-call | bytes 6062084 | tf_op jit(solution)/shard_map/pallas_call | solution.py:51
  77.9 2.9 %collective-permute-start.19 = (bf16[1,64,1024]{2,1,0:T(8,128)(2,1)S(1)}, bf16[1,64,1024]{2,1,0:T(8,128)(2,1)S(1)}, u32[]{:S(2)}, u32[]{:S(2)}) collective-permute-start(bf16[1,64,1024]{2,1,0:T(8,128)(2,1)S(1)} %get-tuple-element.55), channel_id=1, source_target_pairs={{0,4},{1,5},{2,6},{3,7},{4,8},{5,9},{6,10},{7,11},{8,12},{9,13},{1... | collective-permute-start | bytes 393224 | tf_op jit(solution)/shard_map/ppermute | solution.py:435
  83.9 4.3 %collective-permute-done.20 = bf16[1,64,1024]{2,1,0:T(8,128)(2,1)S(1)} collective-permute-done((bf16[1,64,1024]{2,1,0:T(8,128)(2,1)S(1)}, bf16[1,64,1024]{2,1,0:T(8,128)(2,1)S(1)}, u32[]{:S(2)}, u32[]{:S(2)}) %collective-permute-start.20) | collective-permute-done | bytes 131104 | tf_op jit(solution)/shard_map/ppermute | solution.py:435
  88.2 3.2 %collective-permute-start.24 = (bf16[2,64,1024]{2,1,0:T(8,128)(2,1)S(1)}, bf16[2,64,1024]{2,1,0:T(8,128)(2,1)S(1)}, u32[]{:S(2)}, u32[]{:S(2)}) collective-permute-start(bf16[2,64,1024]{2,1,0:T(8,128)(2,1)S(1)} %constant_dynamic-update-slice_fusion.4.refs_1_), channel_id=1, source_target_pairs={{0,2},{1,3},{2,0},{3,1},{4,6},{5,7},{6,4},{7,5},{8,10},{9,11},{10,... | collective-permute-start | bytes 786440 | tf_op jit(solution)/shard_map/ppermute | solution.py:435
  91.4 13.1 %collective-permute-done.24.refs_5_ = bf16[2,64,1024]{2,1,0:T(8,128)(2,1)S(1)} collective-permute-done((bf16[2,64,1024]{2,1,0:T(8,128)(2,1)S(1)}, bf16[2,64,1024]{2,1,0:T(8,128)(2,1)S(1)}, u32[]{:S(2)}, u32[]{:S(2)}) %collective-permute-start.24) | collective-permute-done | bytes 262176 | tf_op jit(solution)/shard_map/ppermute | solution.py:435
  105.0 1.8 collective-permute-done.22.refs_3_
  107.2 3.9 %shard_map.104 = (bf16[4,32,1024]{2,1,0:T(8,128)(2,1)S(1)}, bf16[1,32,1024]{2,1,0:T(8,128)(2,1)S(1)}, bf16[2,32,1024]{2,1,0:T(8,128)(2,1)S(1)}) custom-call(s32[1]{0:T(128)} %bitcast.me_ref, bf16[4,64,1024]{2,1,0:T(8,128)(2,1)S(1)} %get-tuple-element.54.refs_0_, bf16[2,64,1024]{2,1,0:T(8,128)(2,1)S(1)} %constant_dynamic-update-slice_fusion.4.refs_1_, ...), custom_call_target="tpu_custom_call" | custom-call | bytes 4571140 | tf_op jit(solution)/shard_map/pallas_call | solution.py:51
  111.1 1.3 collective-permute-start.27
  114.1 1.5 collective-permute-done.27
  115.7 2.8 %collective-permute-done.28 = bf16[1,32,1024]{2,1,0:T(8,128)(2,1)S(1)} collective-permute-done((bf16[1,32,1024]{2,1,0:T(8,128)(2,1)S(1)}, bf16[1,32,1024]{2,1,0:T(8,128)(2,1)S(1)}, u32[]{:S(2)}, u32[]{:S(2)}) %collective-permute-start.28) | collective-permute-done | bytes 65568 | tf_op jit(solution)/shard_map/ppermute | solution.py:435
  119.0 2.7 %shard_map.105 = bf16[864,256]{1,0:T(8,128)(2,1)S(1)} custom-call(s32[1]{0:T(128)} %bitcast.me_ref, bf16[4,32,1024]{2,1,0:T(8,128)(2,1)S(1)} %get-tuple-element.47.refs_0_.own, bf16[2,32,1024]{2,1,0:T(8,128)(2,1)S(1)} %constant_dynamic-update-slice_fusion.2.refs_1_.rim, bf16[4,64,1024]{2,1,0:T(8,128)(2,1)S(1)} %get-tuple-element.54.refs_0_, ...), custom_call_target="tpu_custom_call" | custom-call | flops 1811939328 | bytes 2932740 | tf_op jit(solution)/shard_map/pallas_call | solution.py:51
  122.3 2.1 %collective-permute-done.31.refs_4_ = bf16[4,32,1024]{2,1,0:T(8,128)(2,1)S(1)} collective-permute-done((bf16[4,32,1024]{2,1,0:T(8,128)(2,1)S(1)}, bf16[4,32,1024]{2,1,0:T(8,128)(2,1)S(1)}, u32[]{:S(2)}, u32[]{:S(2)}) %collective-permute-start.31) | collective-permute-done | bytes 262176 | tf_op jit(solution)/shard_map/ppermute | solution.py:435
  124.4 6.2 %collective-permute-done.32.refs_5_ = bf16[3,32,1024]{2,1,0:T(8,128)(2,1)S(1)} collective-permute-done((bf16[3,32,1024]{2,1,0:T(8,128)(2,1)S(1)}, bf16[3,32,1024]{2,1,0:T(8,128)(2,1)S(1)}, u32[]{:S(2)}, u32[]{:S(2)}) %collective-permute-start.32) | collective-permute-done | bytes 196640 | tf_op jit(solution)/shard_map/ppermute | solution.py:435
  132.5 5.6 %shard_map.106 = bf16[32,48,256]{2,1,0:T(8,128)(2,1)S(1)} custom-call(s32[1]{0:T(128)} %bitcast.me_ref, bf16[4,32,1024]{2,1,0:T(8,128)(2,1)S(1)} %get-tuple-element.60.refs_0_, bf16[3,32,1024]{2,1,0:T(8,128)(2,1)S(1)} %constant_dynamic-update-slice_fusion.6.refs_1_, bf16[4,32,1024]{2,1,0:T(8,128)(2,1)S(1)} %collective-permute-done.29.refs_2_, ...), custom_call_target="tpu_custom_call" | custom-call | bytes 10354692 | tf_op jit(solution)/shard_map/pallas_call | solution.py:51
  138.1 26.3 %all_to_all.10 = bf16[32,48,256]{2,1,0:T(8,128)(2,1)S(1)} all-to-all(bf16[32,48,256]{2,1,0:T(8,128)(2,1)S(1)} %shard_map.106), channel_id=1, replica_groups=mesh['space'=32,'chan'=4] {'space'}, dimensions={0} | all-to-all | bytes 1572864 | tf_op jit(solution)/shard_map/all_to_all | solution.py:453
  165.8 1.7 collective-permute-start.36
  167.6 3.7 %collective-permute-done.36 = bf16[48,256]{1,0:T(8,128)(2,1)S(1)} collective-permute-done((bf16[48,256]{1,0:T(8,128)(2,1)S(1)}, bf16[48,256]{1,0:T(8,128)(2,1)S(1)}, u32[]{:S(2)}, u32[]{:S(2)}) %collective-permute-start.36) | collective-permute-done | bytes 24608 | tf_op jit(solution)/shard_map/ppermute | solution.py:435
  172.3 4.4 %all-to-all-start.1 = ((bf16[32,48,256]{2,1,0:T(8,128)(2,1)}), bf16[32,48,256]{2,1,0:T(8,128)(2,1)S(1)}, u32[]{:S(2)}, u32[]{:S(2)}) async-start(bf16[32,48,256]{2,1,0:T(8,128)(2,1)} %broadcast_in_dim.10), calls=%async_computation.1 | async-start | bytes 1572864 | tf_op jit(solution)/shard_map/all_to_all | solution.py:463
  177.6 12.3 %all-to-all-done.1.packed = bf16[32,48,256]{2,1,0:T(8,128)(2,1)S(1)} async-done(((bf16[32,48,256]{2,1,0:T(8,128)(2,1)}), bf16[32,48,256]{2,1,0:T(8,128)(2,1)S(1)}, u32[]{:S(2)}, u32[]{:S(2)}) %all-to-all-start.1) | async-done | bytes 786464 | tf_op jit(solution)/shard_map/all_to_all | solution.py:463
  189.9 1.5 shard_map.107
  (112 shorter events, 23.7 us)
Async XLA Ops:
  7.2 44.3 %all-gather.3.cloned.1.call-start = ((), (), s32[]{:S(2)}) async-start(), calls=%async_computation.2 | async-start | bytes 3317760 | tf_op jit(solution)/shard_map/all_gather | solution.py:474
  9.3 5.4 %collective-permute-start.2 = (bf16[4,3,3,512]{3,2,1,0:T(4,128)(2,1)S(1)}, bf16[4,3,3,512]{3,2,1,0:T(4,128)(2,1)S(1)}, u32[]{:S(2)}, u32[]{:S(2)}) collective-permute-start(bf16[4,3,3,512]{3,2,1,0:T(4,128)(2,1)S(1)} %slice.20), channel_id=1, source_target_pairs={{5,0},{6,1},{7,2},{9,4},{10,5},{11,6},{13,8},{14,9},{15,10},{17,12... | collective-permute-start | bytes 110600 | tf_op jit(solution)/shard_map/ppermute | solution.py:435
  10.7 4.0 %collective-permute-start.1 = (bf16[4,16,3,512]{3,2,1,0:T(4,128)(2,1)S(1)}, bf16[4,16,3,512]{3,2,1,0:T(4,128)(2,1)S(1)}, u32[]{:S(2)}, u32[]{:S(2)}) collective-permute-start(bf16[4,16,3,512]{3,2,1,0:T(4,128)(2,1)S(1)} %slice.19), channel_id=1, source_target_pairs={{1,0},{2,1},{3,2},{5,4},{6,5},{7,6},{9,8},{10,9},{11,10},{13,12},{... | collective-permute-start | bytes 589832 | tf_op jit(solution)/shard_map/ppermute | solution.py:435
  12.0 7.1 %collective-permute-start = (bf16[4,3,8,512]{3,2,1,0:T(8,128)(2,1)S(1)}, bf16[4,3,8,512]{3,2,1,0:T(8,128)(2,1)S(1)}, u32[]{:S(2)}, u32[]{:S(2)}) collective-permute-start(bf16[4,3,8,512]{3,2,1,0:T(8,128)(2,1)S(1)} %slice.18), channel_id=1, source_target_pairs={{4,0},{5,1},{6,2},{7,3},{8,4},{9,5},{10,6},{11,7},{12,8},{13,9},{1... | collective-permute-start | bytes 294920 | tf_op jit(solution)/shard_map/ppermute | solution.py:435
  24.0 10.3 %collective-permute-start.3 = (bf16[1,64,512]{2,1,0:T(8,128)(2,1)S(1)}, bf16[1,64,512]{2,1,0:T(8,128)(2,1)S(1)}, u32[]{:S(2)}, u32[]{:S(2)}) collective-permute-start(bf16[1,64,512]{2,1,0:T(8,128)(2,1)S(1)} %get-tuple-element.43), channel_id=1, source_target_pairs={{0,4},{1,5},{2,6},{3,7},{4,8},{5,9},{6,10},{7,11},{8,12},{9,13},{1... | collective-permute-start | bytes 196616 | tf_op jit(solution)/shard_map/ppermute | solution.py:435
  27.5 6.8 %collective-permute-start.4 = (bf16[1,64,512]{2,1,0:T(8,128)(2,1)S(1)}, bf16[1,64,512]{2,1,0:T(8,128)(2,1)S(1)}, u32[]{:S(2)}, u32[]{:S(2)}) collective-permute-start(bf16[1,64,512]{2,1,0:T(8,128)(2,1)S(1)} %get-tuple-element.44), channel_id=1, source_target_pairs={{4,0},{5,1},{6,2},{7,3},{8,4},{9,5},{10,6},{11,7},{12,8},{13,9},{1... | collective-permute-start | bytes 196616 | tf_op jit(solution)/shard_map/ppermute | solution.py:435
  28.8 20.8 %collective-permute-start.7 = (bf16[4,64,384]{2,1,0:T(8,128)(2,1)S(1)}, bf16[4,64,384]{2,1,0:T(8,128)(2,1)S(1)}, u32[]{:S(2)}, u32[]{:S(2)}) collective-permute-start(bf16[4,64,384]{2,1,0:T(8,128)(2,1)S(1)} %get-tuple-element.42.refs_0_), channel_id=1, source_target_pairs={{0,2},{1,3},{2,0},{3,1},{4,6},{5,7},{6,4},{7,5},{8,10},{9,11},{10,... | collective-permute-start | bytes 589832 | tf_op jit(solution)/shard_map/ppermute | solution.py:435
  34.3 15.3 %collective-permute-start.8 = (bf16[2,64,512]{2,1,0:T(8,128)(2,1)S(1)}, bf16[2,64,512]{2,1,0:T(8,128)(2,1)S(1)}, u32[]{:S(2)}, u32[]{:S(2)}) collective-permute-start(bf16[2,64,512]{2,1,0:T(8,128)(2,1)S(1)} %constant_dynamic-update-slice_fusion.refs_1_), channel_id=1, source_target_pairs={{0,2},{1,3},{2,0},{3,1},{4,6},{5,7},{6,4},{7,5},{8,10},{9,11},{10,... | collective-permute-start | bytes 393224 | tf_op jit(solution)/shard_map/ppermute | solution.py:435
  39.0 12.2 %collective-permute-start.5 = (bf16[4,64,384]{2,1,0:T(8,128)(2,1)S(1)}, bf16[4,64,384]{2,1,0:T(8,128)(2,1)S(1)}, u32[]{:S(2)}, u32[]{:S(2)}) collective-permute-start(bf16[4,64,384]{2,1,0:T(8,128)(2,1)S(1)} %get-tuple-element.42.refs_0_), channel_id=1, source_target_pairs={{0,1},{1,0},{2,3},{3,2},{4,5},{5,4},{6,7},{7,6},{8,9},{9,8},{10,11... | collective-permute-start | bytes 589832 | tf_op jit(solution)/shard_map/ppermute | solution.py:435
  49.6 1.9 collective-permute-start.9
  55.0 3.9 %collective-permute-start.11 = (bf16[1,32,1024]{2,1,0:T(8,128)(2,1)S(1)}, bf16[1,32,1024]{2,1,0:T(8,128)(2,1)S(1)}, u32[]{:S(2)}, u32[]{:S(2)}) collective-permute-start(bf16[1,32,1024]{2,1,0:T(8,128)(2,1)S(1)} %get-tuple-element.48), channel_id=1, source_target_pairs={{0,4},{1,5},{2,6},{3,7},{4,8},{5,9},{6,10},{7,11},{8,12},{9,13},{1... | collective-permute-start | bytes 196616 | tf_op jit(solution)/shard_map/ppermute | solution.py:435
  57.0 6.2 %collective-permute-start.12 = (bf16[1,32,1024]{2,1,0:T(8,128)(2,1)S(1)}, bf16[1,32,1024]{2,1,0:T(8,128)(2,1)S(1)}, u32[]{:S(2)}, u32[]{:S(2)}) collective-permute-start(bf16[1,32,1024]{2,1,0:T(8,128)(2,1)S(1)} %get-tuple-element.49), channel_id=1, source_target_pairs={{4,0},{5,1},{6,2},{7,3},{8,4},{9,5},{10,6},{11,7},{12,8},{13,9},{1... | collective-permute-start | bytes 196616 | tf_op jit(solution)/shard_map/ppermute | solution.py:435
  58.3 13.9 %collective-permute-start.15 = (bf16[4,32,1024]{2,1,0:T(8,128)(2,1)S(1)}, bf16[4,32,1024]{2,1,0:T(8,128)(2,1)S(1)}, u32[]{:S(2)}, u32[]{:S(2)}) collective-permute-start(bf16[4,32,1024]{2,1,0:T(8,128)(2,1)S(1)} %get-tuple-element.47.refs_0_.own), channel_id=1, source_target_pairs={{0,2},{1,3},{2,0},{3,1},{4,6},{5,7},{6,4},{7,5},{8,10},{9,11},{10,... | collective-permute-start | bytes 786440 | tf_op jit(solution)/shard_map/ppermute | solution.py:435
  63.2 9.0 %collective-permute-start.16 = (bf16[2,32,1024]{2,1,0:T(8,128)(2,1)S(1)}, bf16[2,32,1024]{2,1,0:T(8,128)(2,1)S(1)}, u32[]{:S(2)}, u32[]{:S(2)}) collective-permute-start(bf16[2,32,1024]{2,1,0:T(8,128)(2,1)S(1)} %constant_dynamic-update-slice_fusion.2.refs_1_.rim), channel_id=1, source_target_pairs={{0,2},{1,3},{2,0},{3,1},{4,6},{5,7},{6,4},{7,5},{8,10},{9,11},{10,... | collective-permute-start | bytes 393224 | tf_op jit(solution)/shard_map/ppermute | solution.py:435
  63.7 10.3 %collective-permute-start.13 = (bf16[4,32,1024]{2,1,0:T(8,128)(2,1)S(1)}, bf16[4,32,1024]{2,1,0:T(8,128)(2,1)S(1)}, u32[]{:S(2)}, u32[]{:S(2)}) collective-permute-start(bf16[4,32,1024]{2,1,0:T(8,128)(2,1)S(1)} %get-tuple-element.47.refs_0_.own), channel_id=1, source_target_pairs={{0,1},{1,0},{2,3},{3,2},{4,5},{5,4},{6,7},{7,6},{8,9},{9,8},{10,11... | collective-permute-start | bytes 786440 | tf_op jit(solution)/shard_map/ppermute | solution.py:435
  72.2 1.9 collective-permute-start.17
  77.9 5.9 %collective-permute-start.19 = (bf16[1,64,1024]{2,1,0:T(8,128)(2,1)S(1)}, bf16[1,64,1024]{2,1,0:T(8,128)(2,1)S(1)}, u32[]{:S(2)}, u32[]{:S(2)}) collective-permute-start(bf16[1,64,1024]{2,1,0:T(8,128)(2,1)S(1)} %get-tuple-element.55), channel_id=1, source_target_pairs={{0,4},{1,5},{2,6},{3,7},{4,8},{5,9},{6,10},{7,11},{8,12},{9,13},{1... | collective-permute-start | bytes 393224 | tf_op jit(solution)/shard_map/ppermute | solution.py:435
  80.8 23.7 %collective-permute-start.23 = (bf16[4,64,1024]{2,1,0:T(8,128)(2,1)S(1)}, bf16[4,64,1024]{2,1,0:T(8,128)(2,1)S(1)}, u32[]{:S(2)}, u32[]{:S(2)}) collective-permute-start(bf16[4,64,1024]{2,1,0:T(8,128)(2,1)S(1)} %get-tuple-element.54.refs_0_), channel_id=1, source_target_pairs={{0,2},{1,3},{2,0},{3,1},{4,6},{5,7},{6,4},{7,5},{8,10},{9,11},{10,... | collective-permute-start | bytes 1572872 | tf_op jit(solution)/shard_map/ppermute | solution.py:435
  81.3 6.9 %collective-permute-start.20 = (bf16[1,64,1024]{2,1,0:T(8,128)(2,1)S(1)}, bf16[1,64,1024]{2,1,0:T(8,128)(2,1)S(1)}, u32[]{:S(2)}, u32[]{:S(2)}) collective-permute-start(bf16[1,64,1024]{2,1,0:T(8,128)(2,1)S(1)} %get-tuple-element.56), channel_id=1, source_target_pairs={{4,0},{5,1},{6,2},{7,3},{8,4},{9,5},{10,6},{11,7},{12,8},{13,9},{1... | collective-permute-start | bytes 393224 | tf_op jit(solution)/shard_map/ppermute | solution.py:435
  88.2 16.3 %collective-permute-start.24 = (bf16[2,64,1024]{2,1,0:T(8,128)(2,1)S(1)}, bf16[2,64,1024]{2,1,0:T(8,128)(2,1)S(1)}, u32[]{:S(2)}, u32[]{:S(2)}) collective-permute-start(bf16[2,64,1024]{2,1,0:T(8,128)(2,1)S(1)} %constant_dynamic-update-slice_fusion.4.refs_1_), channel_id=1, source_target_pairs={{0,2},{1,3},{2,0},{3,1},{4,6},{5,7},{6,4},{7,5},{8,10},{9,11},{10,... | collective-permute-start | bytes 786440 | tf_op jit(solution)/shard_map/ppermute | solution.py:435
  91.4 15.4 %collective-permute-start.21 = (bf16[4,64,1024]{2,1,0:T(8,128)(2,1)S(1)}, bf16[4,64,1024]{2,1,0:T(8,128)(2,1)S(1)}, u32[]{:S(2)}, u32[]{:S(2)}) collective-permute-start(bf16[4,64,1024]{2,1,0:T(8,128)(2,1)S(1)} %get-tuple-element.54.refs_0_), channel_id=1, source_target_pairs={{0,1},{1,0},{2,3},{3,2},{4,5},{5,4},{6,7},{7,6},{8,9},{9,8},{10,11... | collective-permute-start | bytes 1572872 | tf_op jit(solution)/shard_map/ppermute | solution.py:435
  104.5 2.7 %collective-permute-start.25 = (bf16[4,64,1024]{2,1,0:T(8,128)(2,1)S(1)}, bf16[4,64,1024]{2,1,0:T(8,128)(2,1)S(1)}, u32[]{:S(2)}, u32[]{:S(2)}) collective-permute-start(bf16[4,64,1024]{2,1,0:T(8,128)(2,1)S(1)} %collective-permute-done.23.refs_4_.refs_2_), channel_id=1, source_target_pairs={{0,1},{1,0},{2,3},{3,2},{4,5},{5,4},{6,7},{7,6},{8,9},{9,8},{10,11... | collective-permute-start | bytes 1572872 | tf_op jit(solution)/shard_map/ppermute | solution.py:435
  104.5 2.3 %collective-permute-start.22 = (bf16[2,64,1024]{2,1,0:T(8,128)(2,1)S(1)}, bf16[2,64,1024]{2,1,0:T(8,128)(2,1)S(1)}, u32[]{:S(2)}, u32[]{:S(2)}) collective-permute-start(bf16[2,64,1024]{2,1,0:T(8,128)(2,1)S(1)} %constant_dynamic-update-slice_fusion.4.refs_1_), channel_id=1, source_target_pairs={{0,1},{1,0},{2,3},{3,2},{4,5},{5,4},{6,7},{7,6},{8,9},{9,8},{10,11... | collective-permute-start | bytes 786440 | tf_op jit(solution)/shard_map/ppermute | solution.py:435
  105.0 2.1 %collective-permute-start.26 = (bf16[2,64,1024]{2,1,0:T(8,128)(2,1)S(1)}, bf16[2,64,1024]{2,1,0:T(8,128)(2,1)S(1)}, u32[]{:S(2)}, u32[]{:S(2)}) collective-permute-start(bf16[2,64,1024]{2,1,0:T(8,128)(2,1)S(1)} %collective-permute-done.24.refs_5_), channel_id=1, source_target_pairs={{0,1},{1,0},{2,3},{3,2},{4,5},{5,4},{6,7},{7,6},{8,9},{9,8},{10,11... | collective-permute-start | bytes 786440 | tf_op jit(solution)/shard_map/ppermute | solution.py:435
  111.1 4.6 %collective-permute-start.27 = (bf16[2,32,1024]{2,1,0:T(8,128)(2,1)S(1)}, bf16[2,32,1024]{2,1,0:T(8,128)(2,1)S(1)}, u32[]{:S(2)}, u32[]{:S(2)}) collective-permute-start(bf16[2,32,1024]{2,1,0:T(8,128)(2,1)S(1)} %get-tuple-element.61), channel_id=1, source_target_pairs={{0,4},{1,5},{2,6},{3,7},{4,8},{5,9},{6,10},{7,11},{8,12},{9,13},{1... | collective-permute-start | bytes 393224 | tf_op jit(solution)/shard_map/ppermute | solution.py:435
  112.4 6.2 %collective-permute-start.28 = (bf16[1,32,1024]{2,1,0:T(8,128)(2,1)S(1)}, bf16[1,32,1024]{2,1,0:T(8,128)(2,1)S(1)}, u32[]{:S(2)}, u32[]{:S(2)}) collective-permute-start(bf16[1,32,1024]{2,1,0:T(8,128)(2,1)S(1)} %get-tuple-element.62), channel_id=1, source_target_pairs={{4,0},{5,1},{6,2},{7,3},{8,4},{9,5},{10,6},{11,7},{12,8},{13,9},{1... | collective-permute-start | bytes 196616 | tf_op jit(solution)/shard_map/ppermute | solution.py:435
  113.7 10.7 %collective-permute-start.31 = (bf16[4,32,1024]{2,1,0:T(8,128)(2,1)S(1)}, bf16[4,32,1024]{2,1,0:T(8,128)(2,1)S(1)}, u32[]{:S(2)}, u32[]{:S(2)}) collective-permute-start(bf16[4,32,1024]{2,1,0:T(8,128)(2,1)S(1)} %get-tuple-element.60.refs_0_), channel_id=1, source_target_pairs={{0,2},{1,3},{2,0},{3,1},{4,6},{5,7},{6,4},{7,5},{8,10},{9,11},{10,... | collective-permute-start | bytes 786440 | tf_op jit(solution)/shard_map/ppermute | solution.py:435
  118.6 12.1 %collective-permute-start.32 = (bf16[3,32,1024]{2,1,0:T(8,128)(2,1)S(1)}, bf16[3,32,1024]{2,1,0:T(8,128)(2,1)S(1)}, u32[]{:S(2)}, u32[]{:S(2)}) collective-permute-start(bf16[3,32,1024]{2,1,0:T(8,128)(2,1)S(1)} %constant_dynamic-update-slice_fusion.6.refs_1_), channel_id=1, source_target_pairs={{0,2},{1,3},{2,0},{3,1},{4,6},{5,7},{6,4},{7,5},{8,10},{9,11},{10,... | collective-permute-start | bytes 589832 | tf_op jit(solution)/shard_map/ppermute | solution.py:435
  119.0 12.2 %collective-permute-start.29 = (bf16[4,32,1024]{2,1,0:T(8,128)(2,1)S(1)}, bf16[4,32,1024]{2,1,0:T(8,128)(2,1)S(1)}, u32[]{:S(2)}, u32[]{:S(2)}) collective-permute-start(bf16[4,32,1024]{2,1,0:T(8,128)(2,1)S(1)} %get-tuple-element.60.refs_0_), channel_id=1, source_target_pairs={{0,1},{1,0},{2,3},{3,2},{4,5},{5,4},{6,7},{7,6},{8,9},{9,8},{10,11... | collective-permute-start | bytes 786440 | tf_op jit(solution)/shard_map/ppermute | solution.py:435
  121.7 9.5 %collective-permute-start.30 = (bf16[3,32,1024]{2,1,0:T(8,128)(2,1)S(1)}, bf16[3,32,1024]{2,1,0:T(8,128)(2,1)S(1)}, u32[]{:S(2)}, u32[]{:S(2)}) collective-permute-start(bf16[3,32,1024]{2,1,0:T(8,128)(2,1)S(1)} %constant_dynamic-update-slice_fusion.6.refs_1_), channel_id=1, source_target_pairs={{0,1},{1,0},{2,3},{3,2},{4,5},{5,4},{6,7},{7,6},{8,9},{9,8},{10,11... | collective-permute-start | bytes 589832 | tf_op jit(solution)/shard_map/ppermute | solution.py:435
  165.8 5.4 %collective-permute-start.36 = (bf16[48,256]{1,0:T(8,128)(2,1)S(1)}, bf16[48,256]{1,0:T(8,128)(2,1)S(1)}, u32[]{:S(2)}, u32[]{:S(2)}) collective-permute-start(bf16[48,256]{1,0:T(8,128)(2,1)S(1)} %add_convert_fusion), channel_id=1, source_target_pairs={{0,2},{1,3},{2,0},{3,1},{4,6},{5,7},{6,4},{7,5},{8,10},{9,11},{10,... | collective-permute-start | bytes 73736 | tf_op jit(solution)/shard_map/ppermute | solution.py:435
  172.3 17.6 %all-to-all-start.1 = ((bf16[32,48,256]{2,1,0:T(8,128)(2,1)}), bf16[32,48,256]{2,1,0:T(8,128)(2,1)S(1)}, u32[]{:S(2)}, u32[]{:S(2)}) async-start(bf16[32,48,256]{2,1,0:T(8,128)(2,1)} %broadcast_in_dim.10), calls=%async_computation.1 | async-start | bytes 1572864 | tf_op jit(solution)/shard_map/all_to_all | solution.py:463
  (20 other events, 220.7 us)
Sparse Core Ops, SparseCore 0:
  10.3 39.8 all-gather.2

commit v5 on v4

--- a/solution.py
+++ b/solution.py
@@ -46,7 +46,7 @@
     args = [pltpu.with_memory_space_constraint(a, pltpu.HBM) if place in far else a for place, a in enumerate(args)]
     size += sum(int(np.prod(s)) * jnp.dtype(t).itemsize for s, t in outs)
     buffers = [pltpu.VMEM(s, t) for s, t in scratch]
-    buffers.append(pltpu.SemaphoreType.DMA((20,)))
+    buffers.append(pltpu.SemaphoreType.DMA((28,)))
     places = [pltpu.HBM if place in away else pltpu.VMEM for place in range(len(outs))]
     return pl.pallas_call(
         kernel,
@@ -170,42 +170,48 @@
 
 
 def arrive(refs, sems, target, up=1, width=1024):
+    parts = len(refs) // 4 - 1
     copies = []
     for k in range(4):
-        body, rim = refs[2 * k], refs[2 * k + 1]
+        *bodies, rim = refs[k * (parts + 1) : (k + 1) * (parts + 1)]
         lanes = pl.ds(0, width)
-        sources = (body.at[:, :, lanes], rim.at[pl.ds(0, up), :, lanes], rim.at[pl.ds(up, 1), :, lanes])
-        for piece, source in enumerate(sources):
-            copies.append(pltpu.make_async_copy(source, target(k, piece), sems.at[3 * k + piece]))
+        planes = 4 // parts
+        pieces = [(body.at[:, :, lanes], up + n * planes, planes) for n, body in enumerate(bodies)]
+        pieces.append((rim.at[pl.ds(0, up), :, lanes], 0, up))
+        pieces.append((rim.at[pl.ds(up, 1), :, lanes], up + 4, 1))
+        for n, (source, first, count) in enumerate(pieces):
+            copies.append(pltpu.make_async_copy(source, target(k, first, count), sems.at[4 * k + n]))
     for copy in copies:
         copy.start()
     return copies
 
 
 def assemble(field, me, refs, sems, channels, up=1, rim=1):
-    planes = (pl.ds(up, 4), pl.ds(0, up), pl.ds(up + 4, 1))
-
-    def target(k, piece):
+    def target(k, first, count):
         at = pl.multiple_of((me ^ k) * channels, channels)
-        return field.at[planes[piece], pl.ds(at, channels), pl.ds(rim * LANES, 8 * LANES)]
+        return field.at[pl.ds(first, count), pl.ds(at, channels), pl.ds(rim * LANES, 8 * LANES)]
 
     return arrive(refs, sems, target, up)
 
 
+def turn_kernel(me_ref, filters, weights, kernel, sems):
+    arrived = begin(filters.at[:, :, pl.ds(32, 16), pl.ds(0, LANES)], kernel, sems.at[0])
+    arrived.wait()
+    weights[...] = turned(me_ref[0], kernel, 32)
+
+
 def third_kernel(me_ref, *refs):
-    blocks, filters = refs[:8], refs[8]
+    blocks, weights = refs[:8], refs[8]
     act, first, last, slope_out, own_out, front_out, row_out = refs[9:16]
-    field, slope, front, row, kernel, sems = refs[16:]
+    field, slope, front, row, sems = refs[16:]
     me = me_ref[0]
-    arrived = begin(filters.at[:, :, pl.ds(32, 16), pl.ds(0, LANES)], kernel, sems.at[12])
-    planes = (pl.ds(1, 4), pl.ds(0, 1), pl.ds(5, 1))
-
-    def target(k, piece):
+
+    def target(k, first, count):
         at = pl.multiple_of(LANES + (me ^ k) * (2 * LANES), LANES)
-        return field.at[planes[piece], :, pl.ds(at, 2 * LANES)]
+        return field.at[pl.ds(first, count), :, pl.ds(at, 2 * LANES)]
 
     copies = arrive(blocks, sems, target, 1, 2 * LANES)
-    plane = begin(blocks[1].at[0, :, pl.ds(256, 256)], front.at[:, pl.ds(LANES, 256)], sems.at[13])
+    plane = begin(blocks[1].at[0, :, pl.ds(256, 256)], front.at[:, pl.ds(LANES, 256)], sems.at[21])
 
     @pl.when(me == 0)
     def _():
@@ -216,33 +222,31 @@
 
         @pl.when((me > 0) & (me ^ k == me - 1))
         def _(k=k):
-            begin(blocks[2 * k + 1].at[0, :, pl.ds(384, LANES)], front.at[:, pl.ds(0, LANES)], sems.at[14])
-            begin(blocks[2 * k].at[:, :, pl.ds(256, LANES)], row, sems.at[15])
+            begin(blocks[2 * k + 1].at[0, :, pl.ds(384, LANES)], front.at[:, pl.ds(0, LANES)], sems.at[22])
+            begin(blocks[2 * k].at[:, :, pl.ds(256, LANES)], row, sems.at[23])
 
     clear_rims(field)
-    arrived.wait()
-    weights = turned(me, kernel, 32)
     plane.wait()
 
     @pl.when(me > 0)
     def _():
         corner = blocks[1].at[0, :, pl.ds(384, LANES)]
-        pltpu.make_async_copy(corner, front.at[:, pl.ds(0, LANES)], sems.at[14]).wait()
-        pltpu.make_async_copy(blocks[0].at[:, :, pl.ds(256, LANES)], row, sems.at[15]).wait()
-
-    leaving = [begin(front, front_out, sems.at[16]), begin(row, row_out, sems.at[17])]
+        pltpu.make_async_copy(corner, front.at[:, pl.ds(0, LANES)], sems.at[22]).wait()
+        pltpu.make_async_copy(blocks[0].at[:, :, pl.ds(256, LANES)], row, sems.at[23]).wait()
+
+    leaving = [begin(front, front_out, sems.at[24]), begin(row, row_out, sems.at[25])]
     for copy in copies:
         copy.wait()
     own = field.at[:, pl.ds(pl.multiple_of(me * 16, 16), 16), :]
-    leaving.append(begin(own, own_out, sems.at[18]))
+    leaving.append(begin(own, own_out, sems.at[26]))
     for d in range(4):
-        product = mm(weights, taps_of(field, d, 0, 1024))
+        product = mm(weights[...], taps_of(field, d, 0, 1024))
         value, steep = activate(shift_sum(product, 32))
         act[d] = value.astype(BF)
         slope[d] = steep
     first[0] = act[0]
     last[0] = act[3]
-    leaving.append(begin(slope, slope_out, sems.at[19]))
+    leaving.append(begin(slope, slope_out, sems.at[27]))
     for copy in leaving:
         copy.wait()
 
@@ -251,7 +255,7 @@
     blocks, filters, cotangent = refs[:8], refs[8], refs[9]
     features, back, first, last, field, kernel, sems = refs[10:]
     me = me_ref[0]
-    arrived = begin(filters.at[:, :, pl.ds(0, 32), :], kernel, sems.at[12])
+    arrived = begin(filters.at[:, :, pl.ds(0, 32), :], kernel, sems.at[20])
     copies = assemble(field, me, blocks, sems, 32)
     clear_rims(field)
     arrived.wait()
@@ -280,7 +284,7 @@
     blocks, kernel, steep = refs[:8], refs[8], refs[9]
     back, first, last, field, slope, sems = refs[10:]
     copies = assemble(field, me_ref[0], blocks, sems, 64)
-    copies.append(begin(steep, slope, sems.at[12]))
+    copies.append(begin(steep, slope, sems.at[20]))
     clear_rims(field)
     weights = flipped_weights(kernel)
     for copy in copies:
@@ -329,9 +333,9 @@
     slope, front, row, act_one, slope_one, volume = refs[24:30]
     sems = refs[30]
     me = me_ref[0]
-    arrived = begin(filters.at[:, :, pl.ds(32, 16), pl.ds(0, LANES)], kernel, sems.at[12])
+    arrived = begin(filters.at[:, :, pl.ds(32, 16), pl.ds(0, LANES)], kernel, sems.at[20])
     copies = assemble(field, me, blocks, sems, 32, up=2, rim=2)
-    later = [begin(source, refs[24 + n], sems.at[13 + n]) for n, source in enumerate(away)]
+    later = [begin(source, refs[24 + n], sems.at[21 + n]) for n, source in enumerate(away)]
     field[:, :, : 2 * LANES] = jnp.zeros((7, 128, 2 * LANES), BF)
     field[:, :, 10 * LANES :] = jnp.zeros((7, 128, LANES), BF)
     clear_rims(shifts)
@@ -436,16 +440,16 @@
 
 
 def gathered(own, first, last, meanwhile=None):
-    across = moved(own, 0, lambda c: c ^ 2)
+    across = [moved(part, 0, lambda c: c ^ 2) for part in own]
     up = moved(last, 1, lambda c: c)
     down = moved(first, -1, lambda c: c)
-    core = moved(own, 0, lambda c: c ^ 1)
+    core = [moved(part, 0, lambda c: c ^ 1) for part in own]
     rim = jnp.concatenate([up, down], 0)
     across_rim = moved(rim, 0, lambda c: c ^ 2)
-    core_rim = moved(rim, 0, lambda c: c ^ 1)
-    across, across_rim, meanwhile = lax.optimization_barrier((across, across_rim, meanwhile))
-    last_pair = [moved(piece, 0, lambda c: c ^ 1) for piece in (across, across_rim)]
-    blocks = [own, rim, core, core_rim, across, across_rim, *last_pair]
+    across, held, meanwhile = lax.optimization_barrier((across, rim, meanwhile))
+    core_rim = moved(held, 0, lambda c: c ^ 1)
+    pair = [moved(piece, 0, lambda c: c ^ 1) for piece in (*across, across_rim)]
+    blocks = [*own, rim, *core, core_rim, *across, across_rim, *pair]
     return blocks if meanwhile is None else (blocks, meanwhile)
 
 
@@ -502,26 +506,29 @@
         [((19, 352, 128), BF), ((9, 480, 128), BF), ((8, 64, 512), F32)],
         away=(0, 1, 2),
     )
-    pieces = range(1, 10)
+    pieces = range(1, 9)
+    (w_three,) = call(
+        turn_kernel, [((96, 576), BF)], [me, filters], [((4, 27, 16, 128), BF)], anywhere=(1,), far=(1,)
+    )
+    blocks, w_three = gathered([body], first, last, w_three)
     act_three, first, last, slope_three, own_two, front, row = call(
         third_kernel,
         [((4, 32, 1024), BF), ((1, 32, 1024), BF), ((1, 32, 1024), BF), ((4, 32, 1024), F32), ((6, 16, 1280), BF), ((64, 384), BF), ((4, 64, 128), BF)],
-        [me, *gathered(body, first, last), filters],
-        [((6, 64, 1280), BF), ((4, 32, 1024), F32), ((64, 384), BF), ((4, 64, 128), BF), ((4, 27, 16, 128), BF)],
+        [me, *blocks, w_three],
+        [((6, 64, 1280), BF), ((4, 32, 1024), F32), ((64, 384), BF), ((4, 64, 128), BF)],
         anywhere=pieces,
         away=(3, 4, 5, 6),
-        far=(9,),
-    )
-    blocks = gathered(act_three, first, last)
+    )
+    blocks = gathered([act_three], first, last)
     features, back_four, first, last = call(
         fourth_kernel,
         [((4, 64, 1024), BF), ((4, 64, 1024), BF), ((1, 64, 1024), BF), ((1, 64, 1024), BF)],
         [me, *blocks, filters, cotangent],
         [((6, 128, 1280), BF), ((4, 27, 32, 256), BF)],
-        anywhere=pieces,
+        anywhere=range(1, 10),
     )
     features = jnp.transpose(features, (1, 0, 2)).reshape(64, 4, 8, 128)
-    all_four = gathered(back_four, first, last)
+    all_four = gathered([back_four], first, last)
     back_three, first, last = call(
         into_three_kernel,
         [((4, 32, 1024), BF), ((1, 32, 1024), BF), ((2, 32, 1024), BF)],
@@ -537,7 +544,7 @@
         flops=2 * 864 * 256 * 4096,
         anywhere=range(3, 7),
     )
-    blocks, grad_four = gathered(back_three, first, last, grad_four)
+    blocks, grad_four = gathered([back_three], first, last, grad_four)
     (grads,) = call(
         last_kernel,
         [((32, 48, 256), BF)],

time: 199 us -> 196 us (0.985)
  waiting for transfers between devices: 82.8 us -> 72.5 us
  starting transfers between devices: 43.4 us -> 48.5 us
    ppermute x37, waiting for transfers between devices: 70.6 us -> 49.3 us  [moved(): return lax.ppermute(block, BOTH, route)]
    all_gather x1, waiting for transfers between devices: 0.01 us -> 11 us  [per_device(): filters = lax.all_gather(jnp.concatenate([four, three], 1), 'chan')]
    ppermute x37, starting transfers between devices: 39 us -> 44.1 us  [moved(): return lax.ppermute(block, BOTH, route)]
    pallas_call x7 -> x8, Pallas kernels: 25.7 us -> 26.6 us  [call(): pl.pallas_call(kernel, out_shape=[pltpu.HBM(s, t) if place in away else j...]
  transfers between devices with their start and end apart: 39 -> 39, of which waited for: 23 -> 24; matrix products, arithmetic and copies ran while one was open for 1% -> 1% of each run, Pallas kernels for 4% -> 5%
where the time goes in v5:
time: 196 us; the launch traced here: 195 us
  waiting for transfers between devices  72.5 us (37%)
  starting transfers between devices  48.5 us (25%)
  blocking collectives  27.7 us (14%)
  Pallas kernels  26.6 us (14%)
  between operations  14.6 us (7%)
  local copies, waits for them, and re-layouts  2.79 us (1%)
  other arithmetic  2.7 us (1%)
    ppermute x37, waiting for transfers between devices, moved(): return lax.ppermute(block, BOTH, route)  49.3 us
    ppermute x37, starting transfers between devices, moved(): return lax.ppermute(block, BOTH, route)  44.1 us
    all_to_all x1, blocking collectives, summed(): terms = lax.all_to_all(parts, 'space', 0, 0)  27.7 us
    pallas_call x8, Pallas kernels, call(): pl.pallas_call(kernel, out_shape=[pltpu.HBM(s, t) if place in away else j...  26.6 us
    all_to_all x1, waiting for transfers between devices, summed(): lax.all_to_all(jnp.broadcast_to(total[None], parts.shape), 'space', 0, 0)  12.3 us
    all_gather x1, waiting for transfers between devices, per_device(): filters = lax.all_gather(jnp.concatenate([four, three], 1), 'chan')  11 us
    all_to_all x1, starting transfers between devices, summed(): lax.all_to_all(jnp.broadcast_to(total[None], parts.shape), 'space', 0, 0)  4.35 us
  transfers between devices with their start and end apart: 39, of which 24 were waited for; matrix products, arithmetic and copies ran while one was open for 1% of the time, Pallas kernels for 5%

profile of v5, /device:TPU:0, one launch (start us, length us, event | category | flops | bytes accessed | tf_op | source)
XLA Modules:
  0.0 195.3 jit_solution(919851662183633495)
XLA Ops:
  7.2 2.0 %fusion.3 = bf16[27,48,256]{2,1,0:T(8,128)(2,1)} fusion(bf16[27,16,128]{2,1,0:T(8,128)(2,1)} %bitcast.53, bf16[27,32,256]{2,1,0:T(8,128)(2,1)} %bitcast.42), kind=kLoop, calls=%fused_computation.7 | loop fusion | flops 1990656 | bytes 1216512 | tf_op jit(solution)/shard_map/concatenate | solution.py:478
  14.9 4.2 %collective-permute-done = bf16[4,3,8,512]{3,2,1,0:T(8,128)(2,1)S(1)} collective-permute-done((bf16[4,3,8,512]{3,2,1,0:T(8,128)(2,1)S(1)}, bf16[4,3,8,512]{3,2,1,0:T(8,128)(2,1)S(1)}, u32[]{:S(2)}, u32[]{:S(2)}) %collective-permute-start) | collective-permute-done | bytes 98336 | tf_op jit(solution)/shard_map/ppermute | solution.py:439
  19.3 4.8 %shard_map.101 = (bf16[19,352,128]{2,1,0:T(8,128)(2,1)}, bf16[9,480,128]{2,1,0:T(8,128)(2,1)}, f32[8,64,512]{2,1,0:T(8,128)}, bf16[4,64,384]{2,1,0:T(8,128)(2,1)...) custom-call(bf16[4,19,16,512]{3,2,1,0:T(8,128)(2,1)S(1)} %pad_maximum_fusion.vol, ...), custom_call_target="tpu_custom_call" | custom-call | bytes 5849088 | tf_op jit(solution)/shard_map/pallas_call | solution.py:51
  24.0 3.5 %collective-permute-start.3 = (bf16[1,64,512]{2,1,0:T(8,128)(2,1)S(1)}, bf16[1,64,512]{2,1,0:T(8,128)(2,1)S(1)}, u32[]{:S(2)}, u32[]{:S(2)}) collective-permute-start(bf16[1,64,512]{2,1,0:T(8,128)(2,1)S(1)} %get-tuple-element.44), channel_id=1, source_target_pairs={{0,4},{1,5},{2,6},{3,7},{4,8},{5,9},{6,10},{7,11},{8,12},{9,13},{1... | collective-permute-start | bytes 196616 | tf_op jit(solution)/shard_map/ppermute | solution.py:439
  28.8 5.5 %collective-permute-start.6 = (bf16[4,64,384]{2,1,0:T(8,128)(2,1)S(1)}, bf16[4,64,384]{2,1,0:T(8,128)(2,1)S(1)}, u32[]{:S(2)}, u32[]{:S(2)}) collective-permute-start(bf16[4,64,384]{2,1,0:T(8,128)(2,1)S(1)} %get-tuple-element.43.refs_0_), channel_id=1, source_target_pairs={{0,2},{1,3},{2,0},{3,1},{4,6},{5,7},{6,4},{7,5},{8,10},{9,11},{10,... | collective-permute-start | bytes 589832 | tf_op jit(solution)/shard_map/ppermute | solution.py:439
  34.3 4.7 %collective-permute-start.8 = (bf16[2,64,512]{2,1,0:T(8,128)(2,1)S(1)}, bf16[2,64,512]{2,1,0:T(8,128)(2,1)S(1)}, u32[]{:S(2)}, u32[]{:S(2)}) collective-permute-start(bf16[2,64,512]{2,1,0:T(8,128)(2,1)S(1)} %constant_dynamic-update-slice_fusion.refs_1_), channel_id=1, source_target_pairs={{0,2},{1,3},{2,0},{3,1},{4,6},{5,7},{6,4},{7,5},{8,10},{9,11},{10,... | collective-permute-start | bytes 393224 | tf_op jit(solution)/shard_map/ppermute | solution.py:439
  39.1 11.0 %all-gather.3.cloned.1.call-done = bf16[108,48,256]{2,1,0:T(8,128)(2,1)} async-done(((bf16[27,48,256]{2,1,0:T(8,128)(2,1)}), bf16[108,48,256]{2,1,0:T(8,128)(2,1)}) %all-gather.3.cloned.1.call-update) | async-done | bytes 2654224 | tf_op jit(solution)/shard_map/all_gather | solution.py:478
  50.1 1.7 shard_map.102.refs_8_
  53.7 2.3 %shard_map.103 = (bf16[4,32,1024]{2,1,0:T(8,128)(2,1)S(1)}, bf16[1,32,1024]{2,1,0:T(8,128)(2,1)S(1)}, bf16[1,32,1024]{2,1,0:T(8,128)(2,1)S(1)}, f32[4,32,1024]{2...) custom-call(s32[1]{0:T(128)} %bitcast.me_ref, ...), custom_call_target="tpu_custom_call" | custom-call | bytes 2699268 | tf_op jit(solution)/shard_map/pallas_call | solution.py:51
  59.4 4.5 %collective-permute-done.12 = bf16[1,32,1024]{2,1,0:T(8,128)(2,1)S(1)} collective-permute-done((bf16[1,32,1024]{2,1,0:T(8,128)(2,1)S(1)}, bf16[1,32,1024]{2,1,0:T(8,128)(2,1)S(1)}, u32[]{:S(2)}, u32[]{:S(2)}) %collective-permute-start.12) | collective-permute-done | bytes 65568 | tf_op jit(solution)/shard_map/ppermute | solution.py:439
  64.0 3.5 %collective-permute-start.16 = (bf16[2,32,1024]{2,1,0:T(8,128)(2,1)S(1)}, bf16[2,32,1024]{2,1,0:T(8,128)(2,1)S(1)}, u32[]{:S(2)}, u32[]{:S(2)}) collective-permute-start(bf16[2,32,1024]{2,1,0:T(8,128)(2,1)S(1)} %constant_dynamic-update-slice_fusion.2.refs_1_.rim), channel_id=1, source_target_pairs={{0,2},{1,3},{2,0},{3,1},{4,6},{5,7},{6,4},{7,5},{8,10},{9,11},{10,... | collective-permute-start | bytes 393224 | tf_op jit(solution)/shard_map/ppermute | solution.py:439
  67.5 2.0 %collective-permute-done.14.refs_4_ = bf16[4,32,1024]{2,1,0:T(8,128)(2,1)S(1)} collective-permute-done((bf16[4,32,1024]{2,1,0:T(8,128)(2,1)S(1)}, bf16[4,32,1024]{2,1,0:T(8,128)(2,1)S(1)}, u32[]{:S(2)}, u32[]{:S(2)}) %collective-permute-start.14) | collective-permute-done | bytes 262176 | tf_op jit(solution)/shard_map/ppermute | solution.py:439
  69.5 2.1 %collective-permute-done.16.refs_5_ = bf16[2,32,1024]{2,1,0:T(8,128)(2,1)S(1)} collective-permute-done((bf16[2,32,1024]{2,1,0:T(8,128)(2,1)S(1)}, bf16[2,32,1024]{2,1,0:T(8,128)(2,1)S(1)}, u32[]{:S(2)}, u32[]{:S(2)}) %collective-permute-start.16) | collective-permute-done | bytes 131104 | tf_op jit(solution)/shard_map/ppermute | solution.py:439
  73.2 3.8 %shard_map.104 = (bf16[4,64,1024]{2,1,0:T(8,128)(2,1)S(1)}, bf16[4,64,1024]{2,1,0:T(8,128)(2,1)S(1)}, bf16[1,64,1024]{2,1,0:T(8,128)(2,1)S(1)}, bf16[1,64,1024]{2,1,0:T(8,128)(2,1)S(1)}) custom-call(s32[1]{0:T(128)} %bitcast.me_ref, bf16[4,32,1024]{2,1,0:T(8,128)(2,1)S(1)} %get-tuple-element.49.refs_0_.own, ...), custom_call_target="tpu_custom_call" | custom-call | bytes 6062084 | tf_op jit(solution)/shard_map/pallas_call | solution.py:51
  77.0 2.6 %collective-permute-start.22 = (bf16[4,64,1024]{2,1,0:T(8,128)(2,1)S(1)}, bf16[4,64,1024]{2,1,0:T(8,128)(2,1)S(1)}, u32[]{:S(2)}, u32[]{:S(2)}) collective-permute-start(bf16[4,64,1024]{2,1,0:T(8,128)(2,1)S(1)} %get-tuple-element.56.refs_0_), channel_id=1, source_target_pairs={{0,2},{1,3},{2,0},{3,1},{4,6},{5,7},{6,4},{7,5},{8,10},{9,11},{10,... | collective-permute-start | bytes 1572872 | tf_op jit(solution)/shard_map/ppermute | solution.py:439
  79.6 1.9 collective-permute-start.19
  84.5 4.1 %collective-permute-done.20 = bf16[1,64,1024]{2,1,0:T(8,128)(2,1)S(1)} collective-permute-done((bf16[1,64,1024]{2,1,0:T(8,128)(2,1)S(1)}, bf16[1,64,1024]{2,1,0:T(8,128)(2,1)S(1)}, u32[]{:S(2)}, u32[]{:S(2)}) %collective-permute-start.20) | collective-permute-done | bytes 131104 | tf_op jit(solution)/shard_map/ppermute | solution.py:439
  89.4 4.0 %collective-permute-done.22.refs_4_.refs_2_ = bf16[4,64,1024]{2,1,0:T(8,128)(2,1)S(1)} collective-permute-done((bf16[4,64,1024]{2,1,0:T(8,128)(2,1)S(1)}, bf16[4,64,1024]{2,1,0:T(8,128)(2,1)S(1)}, u32[]{:S(2)}, u32[]{:S(2)}) %collective-permute-start.22) | collective-permute-done | bytes 524320 | tf_op jit(solution)/shard_map/ppermute | solution.py:439
  93.4 7.8 %collective-permute-done.24.refs_5_ = bf16[2,64,1024]{2,1,0:T(8,128)(2,1)S(1)} collective-permute-done((bf16[2,64,1024]{2,1,0:T(8,128)(2,1)S(1)}, bf16[2,64,1024]{2,1,0:T(8,128)(2,1)S(1)}, u32[]{:S(2)}, u32[]{:S(2)}) %collective-permute-start.24) | collective-permute-done | bytes 262176 | tf_op jit(solution)/shard_map/ppermute | solution.py:439
  103.1 3.9 %shard_map.105 = (bf16[4,32,1024]{2,1,0:T(8,128)(2,1)S(1)}, bf16[1,32,1024]{2,1,0:T(8,128)(2,1)S(1)}, bf16[2,32,1024]{2,1,0:T(8,128)(2,1)S(1)}) custom-call(s32[1]{0:T(128)} %bitcast.me_ref, bf16[4,64,1024]{2,1,0:T(8,128)(2,1)S(1)} %get-tuple-element.56.refs_0_, bf16[2,64,1024]{2,1,0:T(8,128)(2,1)S(1)} %constant_dynamic-update-slice_fusion.4.refs_1_, ...), custom_call_target="tpu_custom_call" | custom-call | bytes 4571140 | tf_op jit(solution)/shard_map/pallas_call | solution.py:51
  109.7 2.6 %collective-permute-start.30 = (bf16[4,32,1024]{2,1,0:T(8,128)(2,1)S(1)}, bf16[4,32,1024]{2,1,0:T(8,128)(2,1)S(1)}, u32[]{:S(2)}, u32[]{:S(2)}) collective-permute-start(bf16[4,32,1024]{2,1,0:T(8,128)(2,1)S(1)} %get-tuple-element.62.refs_0_), channel_id=1, source_target_pairs={{0,2},{1,3},{2,0},{3,1},{4,6},{5,7},{6,4},{7,5},{8,10},{9,11},{10,... | collective-permute-start | bytes 786440 | tf_op jit(solution)/shard_map/ppermute | solution.py:439
  112.3 2.3 %collective-permute-done.28 = bf16[1,32,1024]{2,1,0:T(8,128)(2,1)S(1)} collective-permute-done((bf16[1,32,1024]{2,1,0:T(8,128)(2,1)S(1)}, bf16[1,32,1024]{2,1,0:T(8,128)(2,1)S(1)}, u32[]{:S(2)}, u32[]{:S(2)}) %collective-permute-start.28) | collective-permute-done | bytes 65568 | tf_op jit(solution)/shard_map/ppermute | solution.py:439
  114.6 2.6 %collective-permute-start.32 = (bf16[3,32,1024]{2,1,0:T(8,128)(2,1)S(1)}, bf16[3,32,1024]{2,1,0:T(8,128)(2,1)S(1)}, u32[]{:S(2)}, u32[]{:S(2)}) collective-permute-start(bf16[3,32,1024]{2,1,0:T(8,128)(2,1)S(1)} %constant_dynamic-update-slice_fusion.6.refs_1_), channel_id=1, source_target_pairs={{0,2},{1,3},{2,0},{3,1},{4,6},{5,7},{6,4},{7,5},{8,10},{9,11},{10,... | collective-permute-start | bytes 589832 | tf_op jit(solution)/shard_map/ppermute | solution.py:439
  117.1 2.8 %shard_map.106 = bf16[864,256]{1,0:T(8,128)(2,1)S(1)} custom-call(s32[1]{0:T(128)} %bitcast.me_ref, bf16[4,32,1024]{2,1,0:T(8,128)(2,1)S(1)} %get-tuple-element.49.refs_0_.own, bf16[2,32,1024]{2,1,0:T(8,128)(2,1)S(1)} %constant_dynamic-update-slice_fusion.2.refs_1_.rim, bf16[4,64,1024]{2,1,0:T(8,128)(2,1)S(1)} %get-tuple-element.56.refs_0_, ...), custom_call_target="tpu_custom_call" | custom-call | flops 1811939328 | bytes 2932740 | tf_op jit(solution)/shard_map/pallas_call | solution.py:51
  120.9 5.7 %collective-permute-done.32.refs_5_ = bf16[3,32,1024]{2,1,0:T(8,128)(2,1)S(1)} collective-permute-done((bf16[3,32,1024]{2,1,0:T(8,128)(2,1)S(1)}, bf16[3,32,1024]{2,1,0:T(8,128)(2,1)S(1)}, u32[]{:S(2)}, u32[]{:S(2)}) %collective-permute-start.32) | collective-permute-done | bytes 196640 | tf_op jit(solution)/shard_map/ppermute | solution.py:439
  128.1 5.7 %shard_map.107 = bf16[32,48,256]{2,1,0:T(8,128)(2,1)S(1)} custom-call(s32[1]{0:T(128)} %bitcast.me_ref, bf16[4,32,1024]{2,1,0:T(8,128)(2,1)S(1)} %get-tuple-element.62.refs_0_, bf16[3,32,1024]{2,1,0:T(8,128)(2,1)S(1)} %constant_dynamic-update-slice_fusion.6.refs_1_, bf16[4,32,1024]{2,1,0:T(8,128)(2,1)S(1)} %collective-permute-done.29.refs_2_, ...), custom_call_target="tpu_custom_call" | custom-call | bytes 10354692 | tf_op jit(solution)/shard_map/pallas_call | solution.py:51
  133.8 27.7 %all_to_all.10 = bf16[32,48,256]{2,1,0:T(8,128)(2,1)S(1)} all-to-all(bf16[32,48,256]{2,1,0:T(8,128)(2,1)S(1)} %shard_map.107), channel_id=1, replica_groups=mesh['space'=32,'chan'=4] {'space'}, dimensions={0} | all-to-all | bytes 1572864 | tf_op jit(solution)/shard_map/all_to_all | solution.py:457
  162.9 1.8 collective-permute-start.36
  164.7 3.6 %collective-permute-done.36 = bf16[48,256]{1,0:T(8,128)(2,1)S(1)} collective-permute-done((bf16[48,256]{1,0:T(8,128)(2,1)S(1)}, bf16[48,256]{1,0:T(8,128)(2,1)S(1)}, u32[]{:S(2)}, u32[]{:S(2)}) %collective-permute-start.36) | collective-permute-done | bytes 24608 | tf_op jit(solution)/shard_map/ppermute | solution.py:439
  169.3 4.4 %all-to-all-start.1 = ((bf16[32,48,256]{2,1,0:T(8,128)(2,1)}), bf16[32,48,256]{2,1,0:T(8,128)(2,1)S(1)}, u32[]{:S(2)}, u32[]{:S(2)}) async-start(bf16[32,48,256]{2,1,0:T(8,128)(2,1)} %broadcast_in_dim.10), calls=%async_computation.1 | async-start | bytes 1572864 | tf_op jit(solution)/shard_map/all_to_all | solution.py:467
  174.7 12.3 %all-to-all-done.1.packed = bf16[32,48,256]{2,1,0:T(8,128)(2,1)S(1)} async-done(((bf16[32,48,256]{2,1,0:T(8,128)(2,1)}), bf16[32,48,256]{2,1,0:T(8,128)(2,1)S(1)}, u32[]{:S(2)}, u32[]{:S(2)}) %all-to-all-start.1) | async-done | bytes 786464 | tf_op jit(solution)/shard_map/all_to_all | solution.py:467
  186.9 1.5 shard_map.108
  (113 shorter events, 27.9 us)
Async XLA Ops:
  7.2 42.9 %all-gather.3.cloned.1.call-start = ((), (), s32[]{:S(2)}) async-start(), calls=%async_computation.2 | async-start | bytes 3317760 | tf_op jit(solution)/shard_map/all_gather | solution.py:478
  9.3 5.4 %collective-permute-start.2 = (bf16[4,3,3,512]{3,2,1,0:T(4,128)(2,1)S(1)}, bf16[4,3,3,512]{3,2,1,0:T(4,128)(2,1)S(1)}, u32[]{:S(2)}, u32[]{:S(2)}) collective-permute-start(bf16[4,3,3,512]{3,2,1,0:T(4,128)(2,1)S(1)} %slice.20), channel_id=1, source_target_pairs={{5,0},{6,1},{7,2},{9,4},{10,5},{11,6},{13,8},{14,9},{15,10},{17,12... | collective-permute-start | bytes 110600 | tf_op jit(solution)/shard_map/ppermute | solution.py:439
  10.7 4.0 %collective-permute-start.1 = (bf16[4,16,3,512]{3,2,1,0:T(4,128)(2,1)S(1)}, bf16[4,16,3,512]{3,2,1,0:T(4,128)(2,1)S(1)}, u32[]{:S(2)}, u32[]{:S(2)}) collective-permute-start(bf16[4,16,3,512]{3,2,1,0:T(4,128)(2,1)S(1)} %slice.19), channel_id=1, source_target_pairs={{1,0},{2,1},{3,2},{5,4},{6,5},{7,6},{9,8},{10,9},{11,10},{13,12},{... | collective-permute-start | bytes 589832 | tf_op jit(solution)/shard_map/ppermute | solution.py:439
  12.0 7.1 %collective-permute-start = (bf16[4,3,8,512]{3,2,1,0:T(8,128)(2,1)S(1)}, bf16[4,3,8,512]{3,2,1,0:T(8,128)(2,1)S(1)}, u32[]{:S(2)}, u32[]{:S(2)}) collective-permute-start(bf16[4,3,8,512]{3,2,1,0:T(8,128)(2,1)S(1)} %slice.18), channel_id=1, source_target_pairs={{4,0},{5,1},{6,2},{7,3},{8,4},{9,5},{10,6},{11,7},{12,8},{13,9},{1... | collective-permute-start | bytes 294920 | tf_op jit(solution)/shard_map/ppermute | solution.py:439
  24.0 10.3 %collective-permute-start.3 = (bf16[1,64,512]{2,1,0:T(8,128)(2,1)S(1)}, bf16[1,64,512]{2,1,0:T(8,128)(2,1)S(1)}, u32[]{:S(2)}, u32[]{:S(2)}) collective-permute-start(bf16[1,64,512]{2,1,0:T(8,128)(2,1)S(1)} %get-tuple-element.44), channel_id=1, source_target_pairs={{0,4},{1,5},{2,6},{3,7},{4,8},{5,9},{6,10},{7,11},{8,12},{9,13},{1... | collective-permute-start | bytes 196616 | tf_op jit(solution)/shard_map/ppermute | solution.py:439
  27.5 6.8 %collective-permute-start.4 = (bf16[1,64,512]{2,1,0:T(8,128)(2,1)S(1)}, bf16[1,64,512]{2,1,0:T(8,128)(2,1)S(1)}, u32[]{:S(2)}, u32[]{:S(2)}) collective-permute-start(bf16[1,64,512]{2,1,0:T(8,128)(2,1)S(1)} %get-tuple-element.45), channel_id=1, source_target_pairs={{4,0},{5,1},{6,2},{7,3},{8,4},{9,5},{10,6},{11,7},{12,8},{13,9},{1... | collective-permute-start | bytes 196616 | tf_op jit(solution)/shard_map/ppermute | solution.py:439
  28.8 22.9 %collective-permute-start.6 = (bf16[4,64,384]{2,1,0:T(8,128)(2,1)S(1)}, bf16[4,64,384]{2,1,0:T(8,128)(2,1)S(1)}, u32[]{:S(2)}, u32[]{:S(2)}) collective-permute-start(bf16[4,64,384]{2,1,0:T(8,128)(2,1)S(1)} %get-tuple-element.43.refs_0_), channel_id=1, source_target_pairs={{0,2},{1,3},{2,0},{3,1},{4,6},{5,7},{6,4},{7,5},{8,10},{9,11},{10,... | collective-permute-start | bytes 589832 | tf_op jit(solution)/shard_map/ppermute | solution.py:439
  34.3 17.8 %collective-permute-start.8 = (bf16[2,64,512]{2,1,0:T(8,128)(2,1)S(1)}, bf16[2,64,512]{2,1,0:T(8,128)(2,1)S(1)}, u32[]{:S(2)}, u32[]{:S(2)}) collective-permute-start(bf16[2,64,512]{2,1,0:T(8,128)(2,1)S(1)} %constant_dynamic-update-slice_fusion.refs_1_), channel_id=1, source_target_pairs={{0,2},{1,3},{2,0},{3,1},{4,6},{5,7},{6,4},{7,5},{8,10},{9,11},{10,... | collective-permute-start | bytes 393224 | tf_op jit(solution)/shard_map/ppermute | solution.py:439
  39.1 13.5 %collective-permute-start.5 = (bf16[4,64,384]{2,1,0:T(8,128)(2,1)S(1)}, bf16[4,64,384]{2,1,0:T(8,128)(2,1)S(1)}, u32[]{:S(2)}, u32[]{:S(2)}) collective-permute-start(bf16[4,64,384]{2,1,0:T(8,128)(2,1)S(1)} %get-tuple-element.43.refs_0_), channel_id=1, source_target_pairs={{0,1},{1,0},{2,3},{3,2},{4,5},{5,4},{6,7},{7,6},{8,9},{9,8},{10,11... | collective-permute-start | bytes 589832 | tf_op jit(solution)/shard_map/ppermute | solution.py:439
  51.8 1.9 collective-permute-start.9
  56.1 3.3 %collective-permute-start.11 = (bf16[1,32,1024]{2,1,0:T(8,128)(2,1)S(1)}, bf16[1,32,1024]{2,1,0:T(8,128)(2,1)S(1)}, u32[]{:S(2)}, u32[]{:S(2)}) collective-permute-start(bf16[1,32,1024]{2,1,0:T(8,128)(2,1)S(1)} %get-tuple-element.50), channel_id=1, source_target_pairs={{0,4},{1,5},{2,6},{3,7},{4,8},{5,9},{6,10},{7,11},{8,12},{9,13},{1... | collective-permute-start | bytes 196616 | tf_op jit(solution)/shard_map/ppermute | solution.py:439
  57.4 12.1 %collective-permute-start.14 = (bf16[4,32,1024]{2,1,0:T(8,128)(2,1)S(1)}, bf16[4,32,1024]{2,1,0:T(8,128)(2,1)S(1)}, u32[]{:S(2)}, u32[]{:S(2)}) collective-permute-start(bf16[4,32,1024]{2,1,0:T(8,128)(2,1)S(1)} %get-tuple-element.49.refs_0_.own), channel_id=1, source_target_pairs={{0,2},{1,3},{2,0},{3,1},{4,6},{5,7},{6,4},{7,5},{8,10},{9,11},{10,... | collective-permute-start | bytes 786440 | tf_op jit(solution)/shard_map/ppermute | solution.py:439
  57.5 14.7 %collective-permute-start.13 = (bf16[4,32,1024]{2,1,0:T(8,128)(2,1)S(1)}, bf16[4,32,1024]{2,1,0:T(8,128)(2,1)S(1)}, u32[]{:S(2)}, u32[]{:S(2)}) collective-permute-start(bf16[4,32,1024]{2,1,0:T(8,128)(2,1)S(1)} %get-tuple-element.49.refs_0_.own), channel_id=1, source_target_pairs={{0,1},{1,0},{2,3},{3,2},{4,5},{5,4},{6,7},{7,6},{8,9},{9,8},{10,11... | collective-permute-start | bytes 786440 | tf_op jit(solution)/shard_map/ppermute | solution.py:439
  57.8 6.1 %collective-permute-start.12 = (bf16[1,32,1024]{2,1,0:T(8,128)(2,1)S(1)}, bf16[1,32,1024]{2,1,0:T(8,128)(2,1)S(1)}, u32[]{:S(2)}, u32[]{:S(2)}) collective-permute-start(bf16[1,32,1024]{2,1,0:T(8,128)(2,1)S(1)} %get-tuple-element.51), channel_id=1, source_target_pairs={{4,0},{5,1},{6,2},{7,3},{8,4},{9,5},{10,6},{11,7},{12,8},{13,9},{1... | collective-permute-start | bytes 196616 | tf_op jit(solution)/shard_map/ppermute | solution.py:439
  64.0 7.7 %collective-permute-start.16 = (bf16[2,32,1024]{2,1,0:T(8,128)(2,1)S(1)}, bf16[2,32,1024]{2,1,0:T(8,128)(2,1)S(1)}, u32[]{:S(2)}, u32[]{:S(2)}) collective-permute-start(bf16[2,32,1024]{2,1,0:T(8,128)(2,1)S(1)} %constant_dynamic-update-slice_fusion.2.refs_1_.rim), channel_id=1, source_target_pairs={{0,2},{1,3},{2,0},{3,1},{4,6},{5,7},{6,4},{7,5},{8,10},{9,11},{10,... | collective-permute-start | bytes 393224 | tf_op jit(solution)/shard_map/ppermute | solution.py:439
  69.5 3.7 %collective-permute-start.17 = (bf16[4,32,1024]{2,1,0:T(8,128)(2,1)S(1)}, bf16[4,32,1024]{2,1,0:T(8,128)(2,1)S(1)}, u32[]{:S(2)}, u32[]{:S(2)}) collective-permute-start(bf16[4,32,1024]{2,1,0:T(8,128)(2,1)S(1)} %collective-permute-done.14.refs_4_), channel_id=1, source_target_pairs={{0,1},{1,0},{2,3},{3,2},{4,5},{5,4},{6,7},{7,6},{8,9},{9,8},{10,11... | collective-permute-start | bytes 786440 | tf_op jit(solution)/shard_map/ppermute | solution.py:439
  77.0 16.3 %collective-permute-start.22 = (bf16[4,64,1024]{2,1,0:T(8,128)(2,1)S(1)}, bf16[4,64,1024]{2,1,0:T(8,128)(2,1)S(1)}, u32[]{:S(2)}, u32[]{:S(2)}) collective-permute-start(bf16[4,64,1024]{2,1,0:T(8,128)(2,1)S(1)} %get-tuple-element.56.refs_0_), channel_id=1, source_target_pairs={{0,2},{1,3},{2,0},{3,1},{4,6},{5,7},{6,4},{7,5},{8,10},{9,11},{10,... | collective-permute-start | bytes 1572872 | tf_op jit(solution)/shard_map/ppermute | solution.py:439
  79.6 4.9 %collective-permute-start.19 = (bf16[1,64,1024]{2,1,0:T(8,128)(2,1)S(1)}, bf16[1,64,1024]{2,1,0:T(8,128)(2,1)S(1)}, u32[]{:S(2)}, u32[]{:S(2)}) collective-permute-start(bf16[1,64,1024]{2,1,0:T(8,128)(2,1)S(1)} %get-tuple-element.57), channel_id=1, source_target_pairs={{0,4},{1,5},{2,6},{3,7},{4,8},{5,9},{6,10},{7,11},{8,12},{9,13},{1... | collective-permute-start | bytes 393224 | tf_op jit(solution)/shard_map/ppermute | solution.py:439
  81.5 7.1 %collective-permute-start.20 = (bf16[1,64,1024]{2,1,0:T(8,128)(2,1)S(1)}, bf16[1,64,1024]{2,1,0:T(8,128)(2,1)S(1)}, u32[]{:S(2)}, u32[]{:S(2)}) collective-permute-start(bf16[1,64,1024]{2,1,0:T(8,128)(2,1)S(1)} %get-tuple-element.58), channel_id=1, source_target_pairs={{4,0},{5,1},{6,2},{7,3},{8,4},{9,5},{10,6},{11,7},{12,8},{13,9},{1... | collective-permute-start | bytes 393224 | tf_op jit(solution)/shard_map/ppermute | solution.py:439
  82.8 18.9 %collective-permute-start.21 = (bf16[4,64,1024]{2,1,0:T(8,128)(2,1)S(1)}, bf16[4,64,1024]{2,1,0:T(8,128)(2,1)S(1)}, u32[]{:S(2)}, u32[]{:S(2)}) collective-permute-start(bf16[4,64,1024]{2,1,0:T(8,128)(2,1)S(1)} %get-tuple-element.56.refs_0_), channel_id=1, source_target_pairs={{0,1},{1,0},{2,3},{3,2},{4,5},{5,4},{6,7},{7,6},{8,9},{9,8},{10,11... | collective-permute-start | bytes 1572872 | tf_op jit(solution)/shard_map/ppermute | solution.py:439
  88.6 12.6 %collective-permute-start.24 = (bf16[2,64,1024]{2,1,0:T(8,128)(2,1)S(1)}, bf16[2,64,1024]{2,1,0:T(8,128)(2,1)S(1)}, u32[]{:S(2)}, u32[]{:S(2)}) collective-permute-start(bf16[2,64,1024]{2,1,0:T(8,128)(2,1)S(1)} %constant_dynamic-update-slice_fusion.4.refs_1_), channel_id=1, source_target_pairs={{0,2},{1,3},{2,0},{3,1},{4,6},{5,7},{6,4},{7,5},{8,10},{9,11},{10,... | collective-permute-start | bytes 786440 | tf_op jit(solution)/shard_map/ppermute | solution.py:439
  93.3 9.7 %collective-permute-start.25 = (bf16[4,64,1024]{2,1,0:T(8,128)(2,1)S(1)}, bf16[4,64,1024]{2,1,0:T(8,128)(2,1)S(1)}, u32[]{:S(2)}, u32[]{:S(2)}) collective-permute-start(bf16[4,64,1024]{2,1,0:T(8,128)(2,1)S(1)} %collective-permute-done.22.refs_4_.refs_2_), channel_id=1, source_target_pairs={{0,1},{1,0},{2,3},{3,2},{4,5},{5,4},{6,7},{7,6},{8,9},{9,8},{10,11... | collective-permute-start | bytes 1572872 | tf_op jit(solution)/shard_map/ppermute | solution.py:439
  101.2 1.9 collective-permute-start.23
  107.1 5.2 %collective-permute-start.27 = (bf16[2,32,1024]{2,1,0:T(8,128)(2,1)S(1)}, bf16[2,32,1024]{2,1,0:T(8,128)(2,1)S(1)}, u32[]{:S(2)}, u32[]{:S(2)}) collective-permute-start(bf16[2,32,1024]{2,1,0:T(8,128)(2,1)S(1)} %get-tuple-element.63), channel_id=1, source_target_pairs={{0,4},{1,5},{2,6},{3,7},{4,8},{5,9},{6,10},{7,11},{8,12},{9,13},{1... | collective-permute-start | bytes 393224 | tf_op jit(solution)/shard_map/ppermute | solution.py:439
  108.4 6.2 %collective-permute-start.28 = (bf16[1,32,1024]{2,1,0:T(8,128)(2,1)S(1)}, bf16[1,32,1024]{2,1,0:T(8,128)(2,1)S(1)}, u32[]{:S(2)}, u32[]{:S(2)}) collective-permute-start(bf16[1,32,1024]{2,1,0:T(8,128)(2,1)S(1)} %get-tuple-element.64), channel_id=1, source_target_pairs={{4,0},{5,1},{6,2},{7,3},{8,4},{9,5},{10,6},{11,7},{12,8},{13,9},{1... | collective-permute-start | bytes 196616 | tf_op jit(solution)/shard_map/ppermute | solution.py:439
  109.7 10.7 %collective-permute-start.30 = (bf16[4,32,1024]{2,1,0:T(8,128)(2,1)S(1)}, bf16[4,32,1024]{2,1,0:T(8,128)(2,1)S(1)}, u32[]{:S(2)}, u32[]{:S(2)}) collective-permute-start(bf16[4,32,1024]{2,1,0:T(8,128)(2,1)S(1)} %get-tuple-element.62.refs_0_), channel_id=1, source_target_pairs={{0,2},{1,3},{2,0},{3,1},{4,6},{5,7},{6,4},{7,5},{8,10},{9,11},{10,... | collective-permute-start | bytes 786440 | tf_op jit(solution)/shard_map/ppermute | solution.py:439
  114.6 12.1 %collective-permute-start.32 = (bf16[3,32,1024]{2,1,0:T(8,128)(2,1)S(1)}, bf16[3,32,1024]{2,1,0:T(8,128)(2,1)S(1)}, u32[]{:S(2)}, u32[]{:S(2)}) collective-permute-start(bf16[3,32,1024]{2,1,0:T(8,128)(2,1)S(1)} %constant_dynamic-update-slice_fusion.6.refs_1_), channel_id=1, source_target_pairs={{0,2},{1,3},{2,0},{3,1},{4,6},{5,7},{6,4},{7,5},{8,10},{9,11},{10,... | collective-permute-start | bytes 589832 | tf_op jit(solution)/shard_map/ppermute | solution.py:439
  117.1 9.6 %collective-permute-start.29 = (bf16[4,32,1024]{2,1,0:T(8,128)(2,1)S(1)}, bf16[4,32,1024]{2,1,0:T(8,128)(2,1)S(1)}, u32[]{:S(2)}, u32[]{:S(2)}) collective-permute-start(bf16[4,32,1024]{2,1,0:T(8,128)(2,1)S(1)} %get-tuple-element.62.refs_0_), channel_id=1, source_target_pairs={{0,1},{1,0},{2,3},{3,2},{4,5},{5,4},{6,7},{7,6},{8,9},{9,8},{10,11... | collective-permute-start | bytes 786440 | tf_op jit(solution)/shard_map/ppermute | solution.py:439
  120.4 6.4 %collective-permute-start.31 = (bf16[3,32,1024]{2,1,0:T(8,128)(2,1)S(1)}, bf16[3,32,1024]{2,1,0:T(8,128)(2,1)S(1)}, u32[]{:S(2)}, u32[]{:S(2)}) collective-permute-start(bf16[3,32,1024]{2,1,0:T(8,128)(2,1)S(1)} %constant_dynamic-update-slice_fusion.6.refs_1_), channel_id=1, source_target_pairs={{0,1},{1,0},{2,3},{3,2},{4,5},{5,4},{6,7},{7,6},{8,9},{9,8},{10,11... | collective-permute-start | bytes 589832 | tf_op jit(solution)/shard_map/ppermute | solution.py:439
  120.5 6.3 %collective-permute-start.33 = (bf16[4,32,1024]{2,1,0:T(8,128)(2,1)S(1)}, bf16[4,32,1024]{2,1,0:T(8,128)(2,1)S(1)}, u32[]{:S(2)}, u32[]{:S(2)}) collective-permute-start(bf16[4,32,1024]{2,1,0:T(8,128)(2,1)S(1)} %collective-permute-done.30.refs_4_), channel_id=1, source_target_pairs={{0,1},{1,0},{2,3},{3,2},{4,5},{5,4},{6,7},{7,6},{8,9},{9,8},{10,11... | collective-permute-start | bytes 786440 | tf_op jit(solution)/shard_map/ppermute | solution.py:439
  162.9 5.4 %collective-permute-start.36 = (bf16[48,256]{1,0:T(8,128)(2,1)S(1)}, bf16[48,256]{1,0:T(8,128)(2,1)S(1)}, u32[]{:S(2)}, u32[]{:S(2)}) collective-permute-start(bf16[48,256]{1,0:T(8,128)(2,1)S(1)} %add_convert_fusion), channel_id=1, source_target_pairs={{0,2},{1,3},{2,0},{3,1},{4,6},{5,7},{6,4},{7,5},{8,10},{9,11},{10,... | collective-permute-start | bytes 73736 | tf_op jit(solution)/shard_map/ppermute | solution.py:439
  169.3 17.6 %all-to-all-start.1 = ((bf16[32,48,256]{2,1,0:T(8,128)(2,1)}), bf16[32,48,256]{2,1,0:T(8,128)(2,1)S(1)}, u32[]{:S(2)}, u32[]{:S(2)}) async-start(bf16[32,48,256]{2,1,0:T(8,128)(2,1)} %broadcast_in_dim.10), calls=%async_computation.1 | async-start | bytes 1572864 | tf_op jit(solution)/shard_map/all_to_all | solution.py:467
  (20 other events, 201.7 us)
Sparse Core Ops, SparseCore 0:
  10.3 39.7 all-gather.2

commit v6 on v5

--- a/solution.py
+++ b/solution.py
@@ -253,13 +253,11 @@
 
 def fourth_kernel(me_ref, *refs):
     blocks, filters, cotangent = refs[:8], refs[8], refs[9]
-    features, back, first, last, field, kernel, sems = refs[10:]
+    features, back, first, last, field, sems = refs[10:]
     me = me_ref[0]
-    arrived = begin(filters.at[:, :, pl.ds(0, 32), :], kernel, sems.at[20])
     copies = assemble(field, me, blocks, sems, 32)
     clear_rims(field)
-    arrived.wait()
-    weights = turned(me, kernel, 64)
+    weights = turned(me, filters.at[:, :, :32], 64)
     for copy in copies:
         copy.wait()
     for d in range(4):
@@ -281,10 +279,9 @@
 
 
 def into_three_kernel(me_ref, *refs):
-    blocks, kernel, steep = refs[:8], refs[8], refs[9]
-    back, first, last, field, slope, sems = refs[10:]
+    blocks, kernel, slope = refs[:8], refs[8], refs[9]
+    back, first, last, field, sems = refs[10:]
     copies = assemble(field, me_ref[0], blocks, sems, 64)
-    copies.append(begin(steep, slope, sems.at[20]))
     clear_rims(field)
     weights = flipped_weights(kernel)
     for copy in copies:
@@ -329,13 +326,10 @@
 def last_kernel(me_ref, *refs):
     blocks = refs[:8]
     filters, w_back, act_two, grad_four = refs[8:12]
-    away, out, field, shifts, wide, back_one, kernel = refs[12:18], *refs[18:24]
-    slope, front, row, act_one, slope_one, volume = refs[24:30]
-    sems = refs[30]
+    slope, front, row, act_one, slope_one, volume = refs[12:18]
+    out, field, shifts, wide, back_one, sems = refs[18:]
     me = me_ref[0]
-    arrived = begin(filters.at[:, :, pl.ds(32, 16), pl.ds(0, LANES)], kernel, sems.at[20])
     copies = assemble(field, me, blocks, sems, 32, up=2, rim=2)
-    later = [begin(source, refs[24 + n], sems.at[21 + n]) for n, source in enumerate(away)]
     field[:, :, : 2 * LANES] = jnp.zeros((7, 128, 2 * LANES), BF)
     field[:, :, 10 * LANES :] = jnp.zeros((7, 128, LANES), BF)
     clear_rims(shifts)
@@ -346,10 +340,9 @@
         out[t, :32] = grad_four[t]
     for t in range(27, 32):
         out[t] = jnp.zeros((48, 256), BF)
-    arrived.wait()
-    taps = [jnp.concatenate([kernel[j, t] for j in range(4)], 0) for t in range(27)]
+    taps = [jnp.concatenate([filters[j, t, 32:, :LANES] for j in range(4)], 0) for t in range(27)]
     weights = flipped_weights(taps)
-    for copy in copies + later:
+    for copy in copies:
         copy.wait()
 
     start = pl.multiple_of(me * (2 * LANES), LANES)
@@ -524,8 +517,8 @@
         fourth_kernel,
         [((4, 64, 1024), BF), ((4, 64, 1024), BF), ((1, 64, 1024), BF), ((1, 64, 1024), BF)],
         [me, *blocks, filters, cotangent],
-        [((6, 128, 1280), BF), ((4, 27, 32, 256), BF)],
-        anywhere=range(1, 10),
+        [((6, 128, 1280), BF)],
+        anywhere=pieces,
     )
     features = jnp.transpose(features, (1, 0, 2)).reshape(64, 4, 8, 128)
     all_four = gathered([back_four], first, last)
@@ -533,8 +526,8 @@
         into_three_kernel,
         [((4, 32, 1024), BF), ((1, 32, 1024), BF), ((2, 32, 1024), BF)],
         [me, *all_four, four, slope_three],
-        [((6, 256, 1280), BF), ((4, 32, 1024), F32)],
-        anywhere=[*range(1, 9), 10],
+        [((6, 256, 1280), BF)],
+        anywhere=pieces,
     )
     (grad_four,) = call(
         grad_four_kernel,
@@ -567,15 +560,8 @@
             ((6, 48, 1280), BF),
             ((5, 3, 128, 128), BF),
             ((8, 64, 512), BF),
-            ((4, 27, 16, 128), BF),
-            ((4, 64, 256), F32),
-            ((64, 384), BF),
-            ((4, 64, 128), BF),
-            ((9, 480, 128), BF),
-            ((8, 64, 512), F32),
-            ((19, 352, 128), BF),
         ],
-        anywhere=[*range(1, 10), *range(13, 19)],
+        anywhere=pieces,
     )
     grad_one, grad_two, grad_three, grad_four = call(
         unpack_kernel,

time: 196 us -> 195 us (level)
  no operation moved by 1% of the time
where the time goes in v6:
time: 195 us; the launch traced here: 194 us
  waiting for transfers between devices  72.5 us (37%)
  starting transfers between devices  48.5 us (25%)
  blocking collectives  27.7 us (14%)
  Pallas kernels  25.6 us (13%)
  between operations  14.6 us (7%)
  local copies, waits for them, and re-layouts  2.79 us (1%)
  other arithmetic  2.7 us (1%)
    ppermute x37, waiting for transfers between devices, moved(): return lax.ppermute(block, BOTH, route)  49.3 us
    ppermute x37, starting transfers between devices, moved(): return lax.ppermute(block, BOTH, route)  44.1 us
    all_to_all x1, blocking collectives, summed(): terms = lax.all_to_all(parts, 'space', 0, 0)  27.7 us
    pallas_call x8, Pallas kernels, call(): pl.pallas_call(kernel, out_shape=[pltpu.HBM(s, t) if place in away else j...  25.6 us
    all_to_all x1, waiting for transfers between devices, summed(): lax.all_to_all(jnp.broadcast_to(total[None], parts.shape), 'space', 0, 0)  12.3 us
    all_gather x1, waiting for transfers between devices, per_device(): filters = lax.all_gather(jnp.concatenate([four, three], 1), 'chan')  11 us
    all_to_all x1, starting transfers between devices, summed(): lax.all_to_all(jnp.broadcast_to(total[None], parts.shape), 'space', 0, 0)  4.35 us
  transfers between devices with their start and end apart: 39, of which 24 were waited for; matrix products, arithmetic and copies ran while one was open for 1% of the time, Pallas kernels for 5%

profile of v6, /device:TPU:0, one launch (start us, length us, event | category | flops | bytes accessed | tf_op | source)
XLA Modules:
  0.0 194.3 jit_solution(2090692147628451068)
XLA Ops:
  7.2 2.0 %fusion.3 = bf16[27,48,256]{2,1,0:T(8,128)(2,1)} fusion(bf16[27,16,128]{2,1,0:T(8,128)(2,1)} %bitcast.53, bf16[27,32,256]{2,1,0:T(8,128)(2,1)} %bitcast.42), kind=kLoop, calls=%fused_computation.7 | loop fusion | flops 1990656 | bytes 1216512 | tf_op jit(solution)/shard_map/concatenate | solution.py:471
  14.9 4.2 %collective-permute-done = bf16[4,3,8,512]{3,2,1,0:T(8,128)(2,1)S(1)} collective-permute-done((bf16[4,3,8,512]{3,2,1,0:T(8,128)(2,1)S(1)}, bf16[4,3,8,512]{3,2,1,0:T(8,128)(2,1)S(1)}, u32[]{:S(2)}, u32[]{:S(2)}) %collective-permute-start) | collective-permute-done | bytes 98336 | tf_op jit(solution)/shard_map/ppermute | solution.py:432
  19.3 4.8 %shard_map.101 = (bf16[19,352,128]{2,1,0:T(8,128)(2,1)}, bf16[9,480,128]{2,1,0:T(8,128)(2,1)}, f32[8,64,512]{2,1,0:T(8,128)}, bf16[4,64,384]{2,1,0:T(8,128)(2,1)...) custom-call(bf16[4,19,16,512]{3,2,1,0:T(8,128)(2,1)S(1)} %pad_maximum_fusion.vol, ...), custom_call_target="tpu_custom_call" | custom-call | bytes 5849088 | tf_op jit(solution)/shard_map/pallas_call | solution.py:51
  24.0 3.5 %collective-permute-start.3 = (bf16[1,64,512]{2,1,0:T(8,128)(2,1)S(1)}, bf16[1,64,512]{2,1,0:T(8,128)(2,1)S(1)}, u32[]{:S(2)}, u32[]{:S(2)}) collective-permute-start(bf16[1,64,512]{2,1,0:T(8,128)(2,1)S(1)} %get-tuple-element.44), channel_id=1, source_target_pairs={{0,4},{1,5},{2,6},{3,7},{4,8},{5,9},{6,10},{7,11},{8,12},{9,13},{1... | collective-permute-start | bytes 196616 | tf_op jit(solution)/shard_map/ppermute | solution.py:432
  28.8 5.5 %collective-permute-start.6 = (bf16[4,64,384]{2,1,0:T(8,128)(2,1)S(1)}, bf16[4,64,384]{2,1,0:T(8,128)(2,1)S(1)}, u32[]{:S(2)}, u32[]{:S(2)}) collective-permute-start(bf16[4,64,384]{2,1,0:T(8,128)(2,1)S(1)} %get-tuple-element.43.refs_0_), channel_id=1, source_target_pairs={{0,2},{1,3},{2,0},{3,1},{4,6},{5,7},{6,4},{7,5},{8,10},{9,11},{10,... | collective-permute-start | bytes 589832 | tf_op jit(solution)/shard_map/ppermute | solution.py:432
  34.3 4.7 %collective-permute-start.8 = (bf16[2,64,512]{2,1,0:T(8,128)(2,1)S(1)}, bf16[2,64,512]{2,1,0:T(8,128)(2,1)S(1)}, u32[]{:S(2)}, u32[]{:S(2)}) collective-permute-start(bf16[2,64,512]{2,1,0:T(8,128)(2,1)S(1)} %constant_dynamic-update-slice_fusion.refs_1_), channel_id=1, source_target_pairs={{0,2},{1,3},{2,0},{3,1},{4,6},{5,7},{6,4},{7,5},{8,10},{9,11},{10,... | collective-permute-start | bytes 393224 | tf_op jit(solution)/shard_map/ppermute | solution.py:432
  39.1 11.0 %all-gather.3.cloned.1.call-done = bf16[108,48,256]{2,1,0:T(8,128)(2,1)} async-done(((bf16[27,48,256]{2,1,0:T(8,128)(2,1)}), bf16[108,48,256]{2,1,0:T(8,128)(2,1)}) %all-gather.3.cloned.1.call-update) | async-done | bytes 2654224 | tf_op jit(solution)/shard_map/all_gather | solution.py:471
  50.1 1.7 shard_map.102.refs_8_
  53.7 2.3 %shard_map.103 = (bf16[4,32,1024]{2,1,0:T(8,128)(2,1)S(1)}, bf16[1,32,1024]{2,1,0:T(8,128)(2,1)S(1)}, bf16[1,32,1024]{2,1,0:T(8,128)(2,1)S(1)}, f32[4,32,1024]{2...) custom-call(s32[1]{0:T(128)} %bitcast.me_ref, ...), custom_call_target="tpu_custom_call" | custom-call | bytes 2699268 | tf_op jit(solution)/shard_map/pallas_call | solution.py:51
  59.4 4.5 %collective-permute-done.12 = bf16[1,32,1024]{2,1,0:T(8,128)(2,1)S(1)} collective-permute-done((bf16[1,32,1024]{2,1,0:T(8,128)(2,1)S(1)}, bf16[1,32,1024]{2,1,0:T(8,128)(2,1)S(1)}, u32[]{:S(2)}, u32[]{:S(2)}) %collective-permute-start.12) | collective-permute-done | bytes 65568 | tf_op jit(solution)/shard_map/ppermute | solution.py:432
  64.0 3.5 %collective-permute-start.16 = (bf16[2,32,1024]{2,1,0:T(8,128)(2,1)S(1)}, bf16[2,32,1024]{2,1,0:T(8,128)(2,1)S(1)}, u32[]{:S(2)}, u32[]{:S(2)}) collective-permute-start(bf16[2,32,1024]{2,1,0:T(8,128)(2,1)S(1)} %constant_dynamic-update-slice_fusion.2.refs_1_.rim), channel_id=1, source_target_pairs={{0,2},{1,3},{2,0},{3,1},{4,6},{5,7},{6,4},{7,5},{8,10},{9,11},{10,... | collective-permute-start | bytes 393224 | tf_op jit(solution)/shard_map/ppermute | solution.py:432
  67.5 2.0 %collective-permute-done.14.refs_4_ = bf16[4,32,1024]{2,1,0:T(8,128)(2,1)S(1)} collective-permute-done((bf16[4,32,1024]{2,1,0:T(8,128)(2,1)S(1)}, bf16[4,32,1024]{2,1,0:T(8,128)(2,1)S(1)}, u32[]{:S(2)}, u32[]{:S(2)}) %collective-permute-start.14) | collective-permute-done | bytes 262176 | tf_op jit(solution)/shard_map/ppermute | solution.py:432
  69.5 2.1 %collective-permute-done.16.refs_5_ = bf16[2,32,1024]{2,1,0:T(8,128)(2,1)S(1)} collective-permute-done((bf16[2,32,1024]{2,1,0:T(8,128)(2,1)S(1)}, bf16[2,32,1024]{2,1,0:T(8,128)(2,1)S(1)}, u32[]{:S(2)}, u32[]{:S(2)}) %collective-permute-start.16) | collective-permute-done | bytes 131104 | tf_op jit(solution)/shard_map/ppermute | solution.py:432
  73.2 3.6 %shard_map.104 = (bf16[4,64,1024]{2,1,0:T(8,128)(2,1)S(1)}, bf16[4,64,1024]{2,1,0:T(8,128)(2,1)S(1)}, bf16[1,64,1024]{2,1,0:T(8,128)(2,1)S(1)}, bf16[1,64,1024]{2,1,0:T(8,128)(2,1)S(1)}) custom-call(s32[1]{0:T(128)} %bitcast.me_ref, bf16[4,32,1024]{2,1,0:T(8,128)(2,1)S(1)} %get-tuple-element.49.refs_0_.own, ...), custom_call_target="tpu_custom_call" | custom-call | bytes 6062084 | tf_op jit(solution)/shard_map/pallas_call | solution.py:51
  76.7 2.6 %collective-permute-start.22 = (bf16[4,64,1024]{2,1,0:T(8,128)(2,1)S(1)}, bf16[4,64,1024]{2,1,0:T(8,128)(2,1)S(1)}, u32[]{:S(2)}, u32[]{:S(2)}) collective-permute-start(bf16[4,64,1024]{2,1,0:T(8,128)(2,1)S(1)} %get-tuple-element.56.refs_0_), channel_id=1, source_target_pairs={{0,2},{1,3},{2,0},{3,1},{4,6},{5,7},{6,4},{7,5},{8,10},{9,11},{10,... | collective-permute-start | bytes 1572872 | tf_op jit(solution)/shard_map/ppermute | solution.py:432
  79.3 1.9 collective-permute-start.19
  84.2 4.1 %collective-permute-done.20 = bf16[1,64,1024]{2,1,0:T(8,128)(2,1)S(1)} collective-permute-done((bf16[1,64,1024]{2,1,0:T(8,128)(2,1)S(1)}, bf16[1,64,1024]{2,1,0:T(8,128)(2,1)S(1)}, u32[]{:S(2)}, u32[]{:S(2)}) %collective-permute-start.20) | collective-permute-done | bytes 131104 | tf_op jit(solution)/shard_map/ppermute | solution.py:432
  89.1 4.0 %collective-permute-done.22.refs_4_.refs_2_ = bf16[4,64,1024]{2,1,0:T(8,128)(2,1)S(1)} collective-permute-done((bf16[4,64,1024]{2,1,0:T(8,128)(2,1)S(1)}, bf16[4,64,1024]{2,1,0:T(8,128)(2,1)S(1)}, u32[]{:S(2)}, u32[]{:S(2)}) %collective-permute-start.22) | collective-permute-done | bytes 524320 | tf_op jit(solution)/shard_map/ppermute | solution.py:432
  93.1 7.8 %collective-permute-done.24.refs_5_ = bf16[2,64,1024]{2,1,0:T(8,128)(2,1)S(1)} collective-permute-done((bf16[2,64,1024]{2,1,0:T(8,128)(2,1)S(1)}, bf16[2,64,1024]{2,1,0:T(8,128)(2,1)S(1)}, u32[]{:S(2)}, u32[]{:S(2)}) %collective-permute-start.24) | collective-permute-done | bytes 262176 | tf_op jit(solution)/shard_map/ppermute | solution.py:432
  102.8 4.0 %shard_map.105 = (bf16[4,32,1024]{2,1,0:T(8,128)(2,1)S(1)}, bf16[1,32,1024]{2,1,0:T(8,128)(2,1)S(1)}, bf16[2,32,1024]{2,1,0:T(8,128)(2,1)S(1)}) custom-call(s32[1]{0:T(128)} %bitcast.me_ref, bf16[4,64,1024]{2,1,0:T(8,128)(2,1)S(1)} %get-tuple-element.56.refs_0_, bf16[2,64,1024]{2,1,0:T(8,128)(2,1)S(1)} %constant_dynamic-update-slice_fusion.4.refs_1_, ...), custom_call_target="tpu_custom_call" | custom-call | bytes 4571140 | tf_op jit(solution)/shard_map/pallas_call | solution.py:51
  109.4 2.6 %collective-permute-start.30 = (bf16[4,32,1024]{2,1,0:T(8,128)(2,1)S(1)}, bf16[4,32,1024]{2,1,0:T(8,128)(2,1)S(1)}, u32[]{:S(2)}, u32[]{:S(2)}) collective-permute-start(bf16[4,32,1024]{2,1,0:T(8,128)(2,1)S(1)} %get-tuple-element.62.refs_0_), channel_id=1, source_target_pairs={{0,2},{1,3},{2,0},{3,1},{4,6},{5,7},{6,4},{7,5},{8,10},{9,11},{10,... | collective-permute-start | bytes 786440 | tf_op jit(solution)/shard_map/ppermute | solution.py:432
  112.0 2.3 %collective-permute-done.28 = bf16[1,32,1024]{2,1,0:T(8,128)(2,1)S(1)} collective-permute-done((bf16[1,32,1024]{2,1,0:T(8,128)(2,1)S(1)}, bf16[1,32,1024]{2,1,0:T(8,128)(2,1)S(1)}, u32[]{:S(2)}, u32[]{:S(2)}) %collective-permute-start.28) | collective-permute-done | bytes 65568 | tf_op jit(solution)/shard_map/ppermute | solution.py:432
  114.3 2.6 %collective-permute-start.32 = (bf16[3,32,1024]{2,1,0:T(8,128)(2,1)S(1)}, bf16[3,32,1024]{2,1,0:T(8,128)(2,1)S(1)}, u32[]{:S(2)}, u32[]{:S(2)}) collective-permute-start(bf16[3,32,1024]{2,1,0:T(8,128)(2,1)S(1)} %constant_dynamic-update-slice_fusion.6.refs_1_), channel_id=1, source_target_pairs={{0,2},{1,3},{2,0},{3,1},{4,6},{5,7},{6,4},{7,5},{8,10},{9,11},{10,... | collective-permute-start | bytes 589832 | tf_op jit(solution)/shard_map/ppermute | solution.py:432
  116.9 2.8 %shard_map.106 = bf16[864,256]{1,0:T(8,128)(2,1)S(1)} custom-call(s32[1]{0:T(128)} %bitcast.me_ref, bf16[4,32,1024]{2,1,0:T(8,128)(2,1)S(1)} %get-tuple-element.49.refs_0_.own, bf16[2,32,1024]{2,1,0:T(8,128)(2,1)S(1)} %constant_dynamic-update-slice_fusion.2.refs_1_.rim, bf16[4,64,1024]{2,1,0:T(8,128)(2,1)S(1)} %get-tuple-element.56.refs_0_, ...), custom_call_target="tpu_custom_call" | custom-call | flops 1811939328 | bytes 2932740 | tf_op jit(solution)/shard_map/pallas_call | solution.py:51
  120.6 5.7 %collective-permute-done.32.refs_5_ = bf16[3,32,1024]{2,1,0:T(8,128)(2,1)S(1)} collective-permute-done((bf16[3,32,1024]{2,1,0:T(8,128)(2,1)S(1)}, bf16[3,32,1024]{2,1,0:T(8,128)(2,1)S(1)}, u32[]{:S(2)}, u32[]{:S(2)}) %collective-permute-start.32) | collective-permute-done | bytes 196640 | tf_op jit(solution)/shard_map/ppermute | solution.py:432
  127.8 4.9 %shard_map.107 = bf16[32,48,256]{2,1,0:T(8,128)(2,1)S(1)} custom-call(s32[1]{0:T(128)} %bitcast.me_ref, bf16[4,32,1024]{2,1,0:T(8,128)(2,1)S(1)} %get-tuple-element.62.refs_0_, bf16[3,32,1024]{2,1,0:T(8,128)(2,1)S(1)} %constant_dynamic-update-slice_fusion.6.refs_1_, bf16[4,32,1024]{2,1,0:T(8,128)(2,1)S(1)} %collective-permute-done.29.refs_2_, ...), custom_call_target="tpu_custom_call" | custom-call | bytes 10354692 | tf_op jit(solution)/shard_map/pallas_call | solution.py:51
  132.8 27.7 %all_to_all.10 = bf16[32,48,256]{2,1,0:T(8,128)(2,1)S(1)} all-to-all(bf16[32,48,256]{2,1,0:T(8,128)(2,1)S(1)} %shard_map.107), channel_id=1, replica_groups=mesh['space'=32,'chan'=4] {'space'}, dimensions={0} | all-to-all | bytes 1572864 | tf_op jit(solution)/shard_map/all_to_all | solution.py:450
  161.9 1.8 collective-permute-start.36
  163.7 3.6 %collective-permute-done.36 = bf16[48,256]{1,0:T(8,128)(2,1)S(1)} collective-permute-done((bf16[48,256]{1,0:T(8,128)(2,1)S(1)}, bf16[48,256]{1,0:T(8,128)(2,1)S(1)}, u32[]{:S(2)}, u32[]{:S(2)}) %collective-permute-start.36) | collective-permute-done | bytes 24608 | tf_op jit(solution)/shard_map/ppermute | solution.py:432
  168.3 4.3 %all-to-all-start.1 = ((bf16[32,48,256]{2,1,0:T(8,128)(2,1)}), bf16[32,48,256]{2,1,0:T(8,128)(2,1)S(1)}, u32[]{:S(2)}, u32[]{:S(2)}) async-start(bf16[32,48,256]{2,1,0:T(8,128)(2,1)} %broadcast_in_dim.10), calls=%async_computation.1 | async-start | bytes 1572864 | tf_op jit(solution)/shard_map/all_to_all | solution.py:460
  173.7 12.3 %all-to-all-done.1.packed = bf16[32,48,256]{2,1,0:T(8,128)(2,1)S(1)} async-done(((bf16[32,48,256]{2,1,0:T(8,128)(2,1)}), bf16[32,48,256]{2,1,0:T(8,128)(2,1)S(1)}, u32[]{:S(2)}, u32[]{:S(2)}) %all-to-all-start.1) | async-done | bytes 786464 | tf_op jit(solution)/shard_map/all_to_all | solution.py:460
  185.9 1.5 shard_map.108
  (113 shorter events, 27.9 us)
Async XLA Ops:
  7.2 42.9 %all-gather.3.cloned.1.call-start = ((), (), s32[]{:S(2)}) async-start(), calls=%async_computation.2 | async-start | bytes 3317760 | tf_op jit(solution)/shard_map/all_gather | solution.py:471
  9.3 5.4 %collective-permute-start.2 = (bf16[4,3,3,512]{3,2,1,0:T(4,128)(2,1)S(1)}, bf16[4,3,3,512]{3,2,1,0:T(4,128)(2,1)S(1)}, u32[]{:S(2)}, u32[]{:S(2)}) collective-permute-start(bf16[4,3,3,512]{3,2,1,0:T(4,128)(2,1)S(1)} %slice.20), channel_id=1, source_target_pairs={{5,0},{6,1},{7,2},{9,4},{10,5},{11,6},{13,8},{14,9},{15,10},{17,12... | collective-permute-start | bytes 110600 | tf_op jit(solution)/shard_map/ppermute | solution.py:432
  10.7 4.0 %collective-permute-start.1 = (bf16[4,16,3,512]{3,2,1,0:T(4,128)(2,1)S(1)}, bf16[4,16,3,512]{3,2,1,0:T(4,128)(2,1)S(1)}, u32[]{:S(2)}, u32[]{:S(2)}) collective-permute-start(bf16[4,16,3,512]{3,2,1,0:T(4,128)(2,1)S(1)} %slice.19), channel_id=1, source_target_pairs={{1,0},{2,1},{3,2},{5,4},{6,5},{7,6},{9,8},{10,9},{11,10},{13,12},{... | collective-permute-start | bytes 589832 | tf_op jit(solution)/shard_map/ppermute | solution.py:432
  12.0 7.1 %collective-permute-start = (bf16[4,3,8,512]{3,2,1,0:T(8,128)(2,1)S(1)}, bf16[4,3,8,512]{3,2,1,0:T(8,128)(2,1)S(1)}, u32[]{:S(2)}, u32[]{:S(2)}) collective-permute-start(bf16[4,3,8,512]{3,2,1,0:T(8,128)(2,1)S(1)} %slice.18), channel_id=1, source_target_pairs={{4,0},{5,1},{6,2},{7,3},{8,4},{9,5},{10,6},{11,7},{12,8},{13,9},{1... | collective-permute-start | bytes 294920 | tf_op jit(solution)/shard_map/ppermute | solution.py:432
  24.0 10.3 %collective-permute-start.3 = (bf16[1,64,512]{2,1,0:T(8,128)(2,1)S(1)}, bf16[1,64,512]{2,1,0:T(8,128)(2,1)S(1)}, u32[]{:S(2)}, u32[]{:S(2)}) collective-permute-start(bf16[1,64,512]{2,1,0:T(8,128)(2,1)S(1)} %get-tuple-element.44), channel_id=1, source_target_pairs={{0,4},{1,5},{2,6},{3,7},{4,8},{5,9},{6,10},{7,11},{8,12},{9,13},{1... | collective-permute-start | bytes 196616 | tf_op jit(solution)/shard_map/ppermute | solution.py:432
  27.5 6.8 %collective-permute-start.4 = (bf16[1,64,512]{2,1,0:T(8,128)(2,1)S(1)}, bf16[1,64,512]{2,1,0:T(8,128)(2,1)S(1)}, u32[]{:S(2)}, u32[]{:S(2)}) collective-permute-start(bf16[1,64,512]{2,1,0:T(8,128)(2,1)S(1)} %get-tuple-element.45), channel_id=1, source_target_pairs={{4,0},{5,1},{6,2},{7,3},{8,4},{9,5},{10,6},{11,7},{12,8},{13,9},{1... | collective-permute-start | bytes 196616 | tf_op jit(solution)/shard_map/ppermute | solution.py:432
  28.8 22.9 %collective-permute-start.6 = (bf16[4,64,384]{2,1,0:T(8,128)(2,1)S(1)}, bf16[4,64,384]{2,1,0:T(8,128)(2,1)S(1)}, u32[]{:S(2)}, u32[]{:S(2)}) collective-permute-start(bf16[4,64,384]{2,1,0:T(8,128)(2,1)S(1)} %get-tuple-element.43.refs_0_), channel_id=1, source_target_pairs={{0,2},{1,3},{2,0},{3,1},{4,6},{5,7},{6,4},{7,5},{8,10},{9,11},{10,... | collective-permute-start | bytes 589832 | tf_op jit(solution)/shard_map/ppermute | solution.py:432
  34.3 17.8 %collective-permute-start.8 = (bf16[2,64,512]{2,1,0:T(8,128)(2,1)S(1)}, bf16[2,64,512]{2,1,0:T(8,128)(2,1)S(1)}, u32[]{:S(2)}, u32[]{:S(2)}) collective-permute-start(bf16[2,64,512]{2,1,0:T(8,128)(2,1)S(1)} %constant_dynamic-update-slice_fusion.refs_1_), channel_id=1, source_target_pairs={{0,2},{1,3},{2,0},{3,1},{4,6},{5,7},{6,4},{7,5},{8,10},{9,11},{10,... | collective-permute-start | bytes 393224 | tf_op jit(solution)/shard_map/ppermute | solution.py:432
  39.1 13.5 %collective-permute-start.5 = (bf16[4,64,384]{2,1,0:T(8,128)(2,1)S(1)}, bf16[4,64,384]{2,1,0:T(8,128)(2,1)S(1)}, u32[]{:S(2)}, u32[]{:S(2)}) collective-permute-start(bf16[4,64,384]{2,1,0:T(8,128)(2,1)S(1)} %get-tuple-element.43.refs_0_), channel_id=1, source_target_pairs={{0,1},{1,0},{2,3},{3,2},{4,5},{5,4},{6,7},{7,6},{8,9},{9,8},{10,11... | collective-permute-start | bytes 589832 | tf_op jit(solution)/shard_map/ppermute | solution.py:432
  51.8 1.9 %collective-permute-start.9 = (bf16[4,64,384]{2,1,0:T(8,128)(2,1)S(1)}, bf16[4,64,384]{2,1,0:T(8,128)(2,1)S(1)}, u32[]{:S(2)}, u32[]{:S(2)}) collective-permute-start(bf16[4,64,384]{2,1,0:T(8,128)(2,1)S(1)} %collective-permute-done.6.refs_4_), channel_id=1, source_target_pairs={{0,1},{1,0},{2,3},{3,2},{4,5},{5,4},{6,7},{7,6},{8,9},{9,8},{10,11... | collective-permute-start | bytes 589832 | tf_op jit(solution)/shard_map/ppermute | solution.py:432
  56.1 3.3 %collective-permute-start.11 = (bf16[1,32,1024]{2,1,0:T(8,128)(2,1)S(1)}, bf16[1,32,1024]{2,1,0:T(8,128)(2,1)S(1)}, u32[]{:S(2)}, u32[]{:S(2)}) collective-permute-start(bf16[1,32,1024]{2,1,0:T(8,128)(2,1)S(1)} %get-tuple-element.50), channel_id=1, source_target_pairs={{0,4},{1,5},{2,6},{3,7},{4,8},{5,9},{6,10},{7,11},{8,12},{9,13},{1... | collective-permute-start | bytes 196616 | tf_op jit(solution)/shard_map/ppermute | solution.py:432
  57.4 12.1 %collective-permute-start.14 = (bf16[4,32,1024]{2,1,0:T(8,128)(2,1)S(1)}, bf16[4,32,1024]{2,1,0:T(8,128)(2,1)S(1)}, u32[]{:S(2)}, u32[]{:S(2)}) collective-permute-start(bf16[4,32,1024]{2,1,0:T(8,128)(2,1)S(1)} %get-tuple-element.49.refs_0_.own), channel_id=1, source_target_pairs={{0,2},{1,3},{2,0},{3,1},{4,6},{5,7},{6,4},{7,5},{8,10},{9,11},{10,... | collective-permute-start | bytes 786440 | tf_op jit(solution)/shard_map/ppermute | solution.py:432
  57.5 14.7 %collective-permute-start.13 = (bf16[4,32,1024]{2,1,0:T(8,128)(2,1)S(1)}, bf16[4,32,1024]{2,1,0:T(8,128)(2,1)S(1)}, u32[]{:S(2)}, u32[]{:S(2)}) collective-permute-start(bf16[4,32,1024]{2,1,0:T(8,128)(2,1)S(1)} %get-tuple-element.49.refs_0_.own), channel_id=1, source_target_pairs={{0,1},{1,0},{2,3},{3,2},{4,5},{5,4},{6,7},{7,6},{8,9},{9,8},{10,11... | collective-permute-start | bytes 786440 | tf_op jit(solution)/shard_map/ppermute | solution.py:432
  57.8 6.1 %collective-permute-start.12 = (bf16[1,32,1024]{2,1,0:T(8,128)(2,1)S(1)}, bf16[1,32,1024]{2,1,0:T(8,128)(2,1)S(1)}, u32[]{:S(2)}, u32[]{:S(2)}) collective-permute-start(bf16[1,32,1024]{2,1,0:T(8,128)(2,1)S(1)} %get-tuple-element.51), channel_id=1, source_target_pairs={{4,0},{5,1},{6,2},{7,3},{8,4},{9,5},{10,6},{11,7},{12,8},{13,9},{1... | collective-permute-start | bytes 196616 | tf_op jit(solution)/shard_map/ppermute | solution.py:432
  64.0 7.7 %collective-permute-start.16 = (bf16[2,32,1024]{2,1,0:T(8,128)(2,1)S(1)}, bf16[2,32,1024]{2,1,0:T(8,128)(2,1)S(1)}, u32[]{:S(2)}, u32[]{:S(2)}) collective-permute-start(bf16[2,32,1024]{2,1,0:T(8,128)(2,1)S(1)} %constant_dynamic-update-slice_fusion.2.refs_1_.rim), channel_id=1, source_target_pairs={{0,2},{1,3},{2,0},{3,1},{4,6},{5,7},{6,4},{7,5},{8,10},{9,11},{10,... | collective-permute-start | bytes 393224 | tf_op jit(solution)/shard_map/ppermute | solution.py:432
  69.5 3.7 %collective-permute-start.17 = (bf16[4,32,1024]{2,1,0:T(8,128)(2,1)S(1)}, bf16[4,32,1024]{2,1,0:T(8,128)(2,1)S(1)}, u32[]{:S(2)}, u32[]{:S(2)}) collective-permute-start(bf16[4,32,1024]{2,1,0:T(8,128)(2,1)S(1)} %collective-permute-done.14.refs_4_), channel_id=1, source_target_pairs={{0,1},{1,0},{2,3},{3,2},{4,5},{5,4},{6,7},{7,6},{8,9},{9,8},{10,11... | collective-permute-start | bytes 786440 | tf_op jit(solution)/shard_map/ppermute | solution.py:432
  76.7 16.3 %collective-permute-start.22 = (bf16[4,64,1024]{2,1,0:T(8,128)(2,1)S(1)}, bf16[4,64,1024]{2,1,0:T(8,128)(2,1)S(1)}, u32[]{:S(2)}, u32[]{:S(2)}) collective-permute-start(bf16[4,64,1024]{2,1,0:T(8,128)(2,1)S(1)} %get-tuple-element.56.refs_0_), channel_id=1, source_target_pairs={{0,2},{1,3},{2,0},{3,1},{4,6},{5,7},{6,4},{7,5},{8,10},{9,11},{10,... | collective-permute-start | bytes 1572872 | tf_op jit(solution)/shard_map/ppermute | solution.py:432
  79.3 4.9 %collective-permute-start.19 = (bf16[1,64,1024]{2,1,0:T(8,128)(2,1)S(1)}, bf16[1,64,1024]{2,1,0:T(8,128)(2,1)S(1)}, u32[]{:S(2)}, u32[]{:S(2)}) collective-permute-start(bf16[1,64,1024]{2,1,0:T(8,128)(2,1)S(1)} %get-tuple-element.57), channel_id=1, source_target_pairs={{0,4},{1,5},{2,6},{3,7},{4,8},{5,9},{6,10},{7,11},{8,12},{9,13},{1... | collective-permute-start | bytes 393224 | tf_op jit(solution)/shard_map/ppermute | solution.py:432
  81.2 7.1 %collective-permute-start.20 = (bf16[1,64,1024]{2,1,0:T(8,128)(2,1)S(1)}, bf16[1,64,1024]{2,1,0:T(8,128)(2,1)S(1)}, u32[]{:S(2)}, u32[]{:S(2)}) collective-permute-start(bf16[1,64,1024]{2,1,0:T(8,128)(2,1)S(1)} %get-tuple-element.58), channel_id=1, source_target_pairs={{4,0},{5,1},{6,2},{7,3},{8,4},{9,5},{10,6},{11,7},{12,8},{13,9},{1... | collective-permute-start | bytes 393224 | tf_op jit(solution)/shard_map/ppermute | solution.py:432
  82.5 18.9 %collective-permute-start.21 = (bf16[4,64,1024]{2,1,0:T(8,128)(2,1)S(1)}, bf16[4,64,1024]{2,1,0:T(8,128)(2,1)S(1)}, u32[]{:S(2)}, u32[]{:S(2)}) collective-permute-start(bf16[4,64,1024]{2,1,0:T(8,128)(2,1)S(1)} %get-tuple-element.56.refs_0_), channel_id=1, source_target_pairs={{0,1},{1,0},{2,3},{3,2},{4,5},{5,4},{6,7},{7,6},{8,9},{9,8},{10,11... | collective-permute-start | bytes 1572872 | tf_op jit(solution)/shard_map/ppermute | solution.py:432
  88.3 12.6 %collective-permute-start.24 = (bf16[2,64,1024]{2,1,0:T(8,128)(2,1)S(1)}, bf16[2,64,1024]{2,1,0:T(8,128)(2,1)S(1)}, u32[]{:S(2)}, u32[]{:S(2)}) collective-permute-start(bf16[2,64,1024]{2,1,0:T(8,128)(2,1)S(1)} %constant_dynamic-update-slice_fusion.4.refs_1_), channel_id=1, source_target_pairs={{0,2},{1,3},{2,0},{3,1},{4,6},{5,7},{6,4},{7,5},{8,10},{9,11},{10,... | collective-permute-start | bytes 786440 | tf_op jit(solution)/shard_map/ppermute | solution.py:432
  93.1 9.7 %collective-permute-start.25 = (bf16[4,64,1024]{2,1,0:T(8,128)(2,1)S(1)}, bf16[4,64,1024]{2,1,0:T(8,128)(2,1)S(1)}, u32[]{:S(2)}, u32[]{:S(2)}) collective-permute-start(bf16[4,64,1024]{2,1,0:T(8,128)(2,1)S(1)} %collective-permute-done.22.refs_4_.refs_2_), channel_id=1, source_target_pairs={{0,1},{1,0},{2,3},{3,2},{4,5},{5,4},{6,7},{7,6},{8,9},{9,8},{10,11... | collective-permute-start | bytes 1572872 | tf_op jit(solution)/shard_map/ppermute | solution.py:432
  100.9 1.9 collective-permute-start.23
  106.8 5.2 %collective-permute-start.27 = (bf16[2,32,1024]{2,1,0:T(8,128)(2,1)S(1)}, bf16[2,32,1024]{2,1,0:T(8,128)(2,1)S(1)}, u32[]{:S(2)}, u32[]{:S(2)}) collective-permute-start(bf16[2,32,1024]{2,1,0:T(8,128)(2,1)S(1)} %get-tuple-element.63), channel_id=1, source_target_pairs={{0,4},{1,5},{2,6},{3,7},{4,8},{5,9},{6,10},{7,11},{8,12},{9,13},{1... | collective-permute-start | bytes 393224 | tf_op jit(solution)/shard_map/ppermute | solution.py:432
  108.1 6.2 %collective-permute-start.28 = (bf16[1,32,1024]{2,1,0:T(8,128)(2,1)S(1)}, bf16[1,32,1024]{2,1,0:T(8,128)(2,1)S(1)}, u32[]{:S(2)}, u32[]{:S(2)}) collective-permute-start(bf16[1,32,1024]{2,1,0:T(8,128)(2,1)S(1)} %get-tuple-element.64), channel_id=1, source_target_pairs={{4,0},{5,1},{6,2},{7,3},{8,4},{9,5},{10,6},{11,7},{12,8},{13,9},{1... | collective-permute-start | bytes 196616 | tf_op jit(solution)/shard_map/ppermute | solution.py:432
  109.4 10.7 %collective-permute-start.30 = (bf16[4,32,1024]{2,1,0:T(8,128)(2,1)S(1)}, bf16[4,32,1024]{2,1,0:T(8,128)(2,1)S(1)}, u32[]{:S(2)}, u32[]{:S(2)}) collective-permute-start(bf16[4,32,1024]{2,1,0:T(8,128)(2,1)S(1)} %get-tuple-element.62.refs_0_), channel_id=1, source_target_pairs={{0,2},{1,3},{2,0},{3,1},{4,6},{5,7},{6,4},{7,5},{8,10},{9,11},{10,... | collective-permute-start | bytes 786440 | tf_op jit(solution)/shard_map/ppermute | solution.py:432
  114.3 12.1 %collective-permute-start.32 = (bf16[3,32,1024]{2,1,0:T(8,128)(2,1)S(1)}, bf16[3,32,1024]{2,1,0:T(8,128)(2,1)S(1)}, u32[]{:S(2)}, u32[]{:S(2)}) collective-permute-start(bf16[3,32,1024]{2,1,0:T(8,128)(2,1)S(1)} %constant_dynamic-update-slice_fusion.6.refs_1_), channel_id=1, source_target_pairs={{0,2},{1,3},{2,0},{3,1},{4,6},{5,7},{6,4},{7,5},{8,10},{9,11},{10,... | collective-permute-start | bytes 589832 | tf_op jit(solution)/shard_map/ppermute | solution.py:432
  116.9 9.6 %collective-permute-start.29 = (bf16[4,32,1024]{2,1,0:T(8,128)(2,1)S(1)}, bf16[4,32,1024]{2,1,0:T(8,128)(2,1)S(1)}, u32[]{:S(2)}, u32[]{:S(2)}) collective-permute-start(bf16[4,32,1024]{2,1,0:T(8,128)(2,1)S(1)} %get-tuple-element.62.refs_0_), channel_id=1, source_target_pairs={{0,1},{1,0},{2,3},{3,2},{4,5},{5,4},{6,7},{7,6},{8,9},{9,8},{10,11... | collective-permute-start | bytes 786440 | tf_op jit(solution)/shard_map/ppermute | solution.py:432
  120.1 6.4 %collective-permute-start.31 = (bf16[3,32,1024]{2,1,0:T(8,128)(2,1)S(1)}, bf16[3,32,1024]{2,1,0:T(8,128)(2,1)S(1)}, u32[]{:S(2)}, u32[]{:S(2)}) collective-permute-start(bf16[3,32,1024]{2,1,0:T(8,128)(2,1)S(1)} %constant_dynamic-update-slice_fusion.6.refs_1_), channel_id=1, source_target_pairs={{0,1},{1,0},{2,3},{3,2},{4,5},{5,4},{6,7},{7,6},{8,9},{9,8},{10,11... | collective-permute-start | bytes 589832 | tf_op jit(solution)/shard_map/ppermute | solution.py:432
  120.2 6.3 %collective-permute-start.33 = (bf16[4,32,1024]{2,1,0:T(8,128)(2,1)S(1)}, bf16[4,32,1024]{2,1,0:T(8,128)(2,1)S(1)}, u32[]{:S(2)}, u32[]{:S(2)}) collective-permute-start(bf16[4,32,1024]{2,1,0:T(8,128)(2,1)S(1)} %collective-permute-done.30.refs_4_), channel_id=1, source_target_pairs={{0,1},{1,0},{2,3},{3,2},{4,5},{5,4},{6,7},{7,6},{8,9},{9,8},{10,11... | collective-permute-start | bytes 786440 | tf_op jit(solution)/shard_map/ppermute | solution.py:432
  161.9 5.4 %collective-permute-start.36 = (bf16[48,256]{1,0:T(8,128)(2,1)S(1)}, bf16[48,256]{1,0:T(8,128)(2,1)S(1)}, u32[]{:S(2)}, u32[]{:S(2)}) collective-permute-start(bf16[48,256]{1,0:T(8,128)(2,1)S(1)} %add_convert_fusion), channel_id=1, source_target_pairs={{0,2},{1,3},{2,0},{3,1},{4,6},{5,7},{6,4},{7,5},{8,10},{9,11},{10,... | collective-permute-start | bytes 73736 | tf_op jit(solution)/shard_map/ppermute | solution.py:432
  168.3 17.6 %all-to-all-start.1 = ((bf16[32,48,256]{2,1,0:T(8,128)(2,1)}), bf16[32,48,256]{2,1,0:T(8,128)(2,1)S(1)}, u32[]{:S(2)}, u32[]{:S(2)}) async-start(bf16[32,48,256]{2,1,0:T(8,128)(2,1)} %broadcast_in_dim.10), calls=%async_computation.1 | async-start | bytes 1572864 | tf_op jit(solution)/shard_map/all_to_all | solution.py:460
  (20 other events, 201.1 us)
Sparse Core Ops, SparseCore 0:
  10.3 39.7 all-gather.2

commit v7 on v6

--- a/solution.py
+++ b/solution.py
@@ -128,10 +128,11 @@
         steep = slope.astype(BF)
         body[d, :, :256] = act.astype(BF)
         body[d, :, 256:] = steep[:, 128:]
-        for rim, at in ((first, 0), (last, 3)):
-            if d == at:
-                rim[0, :, :256] = act.astype(BF)
-                rim[0, :, 256:] = steep
+        if d == 0:
+            first[0] = act.astype(BF)
+        if d == 3:
+            last[0] = act.astype(BF)
+            last[1] = steep
     for copy in leaving:
         copy.wait()
 
@@ -178,7 +179,7 @@
         planes = 4 // parts
         pieces = [(body.at[:, :, lanes], up + n * planes, planes) for n, body in enumerate(bodies)]
         pieces.append((rim.at[pl.ds(0, up), :, lanes], 0, up))
-        pieces.append((rim.at[pl.ds(up, 1), :, lanes], up + 4, 1))
+        pieces.append((rim.at[pl.ds(rim.shape[0] - 1, 1), :, lanes], up + 4, 1))
         for n, (source, first, count) in enumerate(pieces):
             copies.append(pltpu.make_async_copy(source, target(k, first, count), sems.at[4 * k + n]))
     for copy in copies:
@@ -211,7 +212,7 @@
         return field.at[pl.ds(first, count), :, pl.ds(at, 2 * LANES)]
 
     copies = arrive(blocks, sems, target, 1, 2 * LANES)
-    plane = begin(blocks[1].at[0, :, pl.ds(256, 256)], front.at[:, pl.ds(LANES, 256)], sems.at[21])
+    plane = begin(blocks[1].at[1], front.at[:, pl.ds(LANES, 256)], sems.at[21])
 
     @pl.when(me == 0)
     def _():
@@ -222,7 +223,7 @@
 
         @pl.when((me > 0) & (me ^ k == me - 1))
         def _(k=k):
-            begin(blocks[2 * k + 1].at[0, :, pl.ds(384, LANES)], front.at[:, pl.ds(0, LANES)], sems.at[22])
+            begin(blocks[2 * k + 1].at[1, :, pl.ds(LANES, LANES)], front.at[:, pl.ds(0, LANES)], sems.at[22])
             begin(blocks[2 * k].at[:, :, pl.ds(256, LANES)], row, sems.at[23])
 
     clear_rims(field)
@@ -230,7 +231,7 @@
 
     @pl.when(me > 0)
     def _():
-        corner = blocks[1].at[0, :, pl.ds(384, LANES)]
+        corner = blocks[1].at[1, :, pl.ds(LANES, LANES)]
         pltpu.make_async_copy(corner, front.at[:, pl.ds(0, LANES)], sems.at[22]).wait()
         pltpu.make_async_copy(blocks[0].at[:, :, pl.ds(256, LANES)], row, sems.at[23]).wait()
 
@@ -491,8 +492,8 @@
             ((9, 480, 128), BF),
             ((8, 64, 512), F32),
             ((4, 64, 384), BF),
-            ((1, 64, 512), BF),
-            ((1, 64, 512), BF),
+            ((1, 64, 256), BF),
+            ((2, 64, 256), BF),
             ((4, 64, 256), F32),
         ],
         [tall, w_one, w_two],

time: 195 us -> 196 us (level)
  starting transfers between devices: 48.5 us -> 42.2 us
  waiting for transfers between devices: 72.5 us -> 78.7 us
    ppermute x37, waiting for transfers between devices: 49.3 us -> 55.6 us  [moved(): return lax.ppermute(block, BOTH, route)]
    ppermute x37, starting transfers between devices: 44.1 us -> 37.8 us  [moved(): return lax.ppermute(block, BOTH, route)]
  transfers between devices with their start and end apart: 39 -> 39, of which waited for: 24 -> 25; matrix products, arithmetic and copies ran while one was open for 1% -> 1% of each run, Pallas kernels for 5% -> 5%
where the time goes in v7:
time: 196 us; the launch traced here: 195 us
  waiting for transfers between devices  78.7 us (40%)
  starting transfers between devices  42.2 us (22%)
  blocking collectives  28.1 us (14%)
  Pallas kernels  26 us (13%)
  between operations  14.6 us (7%)
  local copies, waits for them, and re-layouts  2.79 us (1%)
  other arithmetic  2.7 us (1%)
    ppermute x37, waiting for transfers between devices, moved(): return lax.ppermute(block, BOTH, route)  55.6 us
    ppermute x37, starting transfers between devices, moved(): return lax.ppermute(block, BOTH, route)  37.8 us
    all_to_all x1, blocking collectives, summed(): terms = lax.all_to_all(parts, 'space', 0, 0)  28.1 us
    pallas_call x8, Pallas kernels, call(): pl.pallas_call(kernel, out_shape=[pltpu.HBM(s, t) if place in away else j...  26 us
    all_to_all x1, waiting for transfers between devices, summed(): lax.all_to_all(jnp.broadcast_to(total[None], parts.shape), 'space', 0, 0)  12.3 us
    all_gather x1, waiting for transfers between devices, per_device(): filters = lax.all_gather(jnp.concatenate([four, three], 1), 'chan')  10.8 us
    all_to_all x1, starting transfers between devices, summed(): lax.all_to_all(jnp.broadcast_to(total[None], parts.shape), 'space', 0, 0)  4.34 us
  transfers between devices with their start and end apart: 39, of which 25 were waited for; matrix products, arithmetic and copies ran while one was open for 1% of the time, Pallas kernels for 5%

profile of v7, /device:TPU:0, one launch (start us, length us, event | category | flops | bytes accessed | tf_op | source)
XLA Modules:
  0.0 195.1 jit_solution(8190868909846851528)
XLA Ops:
  7.2 2.0 %fusion.3 = bf16[27,48,256]{2,1,0:T(8,128)(2,1)} fusion(bf16[27,16,128]{2,1,0:T(8,128)(2,1)} %bitcast.53, bf16[27,32,256]{2,1,0:T(8,128)(2,1)} %bitcast.42), kind=kLoop, calls=%fused_computation.7 | loop fusion | flops 1990656 | bytes 1216512 | tf_op jit(solution)/shard_map/concatenate | solution.py:472
  14.9 4.2 %collective-permute-done = bf16[4,3,8,512]{3,2,1,0:T(8,128)(2,1)S(1)} collective-permute-done((bf16[4,3,8,512]{3,2,1,0:T(8,128)(2,1)S(1)}, bf16[4,3,8,512]{3,2,1,0:T(8,128)(2,1)S(1)}, u32[]{:S(2)}, u32[]{:S(2)}) %collective-permute-start) | collective-permute-done | bytes 98336 | tf_op jit(solution)/shard_map/ppermute | solution.py:433
  19.3 5.3 %shard_map.101 = (bf16[19,352,128]{2,1,0:T(8,128)(2,1)}, bf16[9,480,128]{2,1,0:T(8,128)(2,1)}, f32[8,64,512]{2,1,0:T(8,128)}, bf16[4,64,384]{2,1,0:T(8,128)(2,1)...) custom-call(bf16[4,19,16,512]{3,2,1,0:T(8,128)(2,1)S(1)} %pad_maximum_fusion.vol, ...), custom_call_target="tpu_custom_call" | custom-call | bytes 5816320 | tf_op jit(solution)/shard_map/pallas_call | solution.py:51
  24.5 3.5 %collective-permute-start.3 = (bf16[2,64,256]{2,1,0:T(8,128)(2,1)S(1)}, bf16[2,64,256]{2,1,0:T(8,128)(2,1)S(1)}, u32[]{:S(2)}, u32[]{:S(2)}) collective-permute-start(bf16[2,64,256]{2,1,0:T(8,128)(2,1)S(1)} %get-tuple-element.44), channel_id=1, source_target_pairs={{0,4},{1,5},{2,6},{3,7},{4,8},{5,9},{6,10},{7,11},{8,12},{9,13},{1... | collective-permute-start | bytes 196616 | tf_op jit(solution)/shard_map/ppermute | solution.py:433
  28.0 2.2 %collective-permute-start.5 = (bf16[4,64,384]{2,1,0:T(8,128)(2,1)S(1)}, bf16[4,64,384]{2,1,0:T(8,128)(2,1)S(1)}, u32[]{:S(2)}, u32[]{:S(2)}) collective-permute-start(bf16[4,64,384]{2,1,0:T(8,128)(2,1)S(1)} %get-tuple-element.43.refs_0_), channel_id=1, source_target_pairs={{0,1},{1,0},{2,3},{3,2},{4,5},{5,4},{6,7},{7,6},{8,9},{9,8},{10,11... | collective-permute-start | bytes 589832 | tf_op jit(solution)/shard_map/ppermute | solution.py:433
  30.2 3.3 %collective-permute-start.6 = (bf16[4,64,384]{2,1,0:T(8,128)(2,1)S(1)}, bf16[4,64,384]{2,1,0:T(8,128)(2,1)S(1)}, u32[]{:S(2)}, u32[]{:S(2)}) collective-permute-start(bf16[4,64,384]{2,1,0:T(8,128)(2,1)S(1)} %get-tuple-element.43.refs_0_), channel_id=1, source_target_pairs={{0,2},{1,3},{2,0},{3,1},{4,6},{5,7},{6,4},{7,5},{8,10},{9,11},{10,... | collective-permute-start | bytes 589832 | tf_op jit(solution)/shard_map/ppermute | solution.py:433
  34.9 4.5 %collective-permute-done.4 = bf16[1,64,256]{2,1,0:T(8,128)(2,1)S(1)} collective-permute-done((bf16[1,64,256]{2,1,0:T(8,128)(2,1)S(1)}, bf16[1,64,256]{2,1,0:T(8,128)(2,1)S(1)}, u32[]{:S(2)}, u32[]{:S(2)}) %collective-permute-start.4) | collective-permute-done | bytes 32800 | tf_op jit(solution)/shard_map/ppermute | solution.py:433
  39.6 10.8 %all-gather.3.cloned.1.call-done = bf16[108,48,256]{2,1,0:T(8,128)(2,1)} async-done(((bf16[27,48,256]{2,1,0:T(8,128)(2,1)}), bf16[108,48,256]{2,1,0:T(8,128)(2,1)}) %all-gather.3.cloned.1.call-update) | async-done | bytes 2654224 | tf_op jit(solution)/shard_map/all_gather | solution.py:472
  50.4 1.7 shard_map.102.refs_8_
  54.0 2.4 %shard_map.103 = (bf16[4,32,1024]{2,1,0:T(8,128)(2,1)S(1)}, bf16[1,32,1024]{2,1,0:T(8,128)(2,1)S(1)}, bf16[1,32,1024]{2,1,0:T(8,128)(2,1)S(1)}, f32[4,32,1024]{2...) custom-call(s32[1]{0:T(128)} %bitcast.me_ref, ...), custom_call_target="tpu_custom_call" | custom-call | bytes 2568196 | tf_op jit(solution)/shard_map/pallas_call | solution.py:51
  59.7 4.5 %collective-permute-done.12 = bf16[1,32,1024]{2,1,0:T(8,128)(2,1)S(1)} collective-permute-done((bf16[1,32,1024]{2,1,0:T(8,128)(2,1)S(1)}, bf16[1,32,1024]{2,1,0:T(8,128)(2,1)S(1)}, u32[]{:S(2)}, u32[]{:S(2)}) %collective-permute-start.12) | collective-permute-done | bytes 65568 | tf_op jit(solution)/shard_map/ppermute | solution.py:433
  64.2 3.5 %collective-permute-start.16 = (bf16[2,32,1024]{2,1,0:T(8,128)(2,1)S(1)}, bf16[2,32,1024]{2,1,0:T(8,128)(2,1)S(1)}, u32[]{:S(2)}, u32[]{:S(2)}) collective-permute-start(bf16[2,32,1024]{2,1,0:T(8,128)(2,1)S(1)} %constant_dynamic-update-slice_fusion.2.refs_1_.rim), channel_id=1, source_target_pairs={{0,2},{1,3},{2,0},{3,1},{4,6},{5,7},{6,4},{7,5},{8,10},{9,11},{10,... | collective-permute-start | bytes 393224 | tf_op jit(solution)/shard_map/ppermute | solution.py:433
  67.7 2.0 %collective-permute-done.14.refs_4_ = bf16[4,32,1024]{2,1,0:T(8,128)(2,1)S(1)} collective-permute-done((bf16[4,32,1024]{2,1,0:T(8,128)(2,1)S(1)}, bf16[4,32,1024]{2,1,0:T(8,128)(2,1)S(1)}, u32[]{:S(2)}, u32[]{:S(2)}) %collective-permute-start.14) | collective-permute-done | bytes 262176 | tf_op jit(solution)/shard_map/ppermute | solution.py:433
  69.8 2.1 %collective-permute-done.16.refs_5_ = bf16[2,32,1024]{2,1,0:T(8,128)(2,1)S(1)} collective-permute-done((bf16[2,32,1024]{2,1,0:T(8,128)(2,1)S(1)}, bf16[2,32,1024]{2,1,0:T(8,128)(2,1)S(1)}, u32[]{:S(2)}, u32[]{:S(2)}) %collective-permute-start.16) | collective-permute-done | bytes 131104 | tf_op jit(solution)/shard_map/ppermute | solution.py:433
  73.4 3.6 %shard_map.104 = (bf16[4,64,1024]{2,1,0:T(8,128)(2,1)S(1)}, bf16[4,64,1024]{2,1,0:T(8,128)(2,1)S(1)}, bf16[1,64,1024]{2,1,0:T(8,128)(2,1)S(1)}, bf16[1,64,1024]{2,1,0:T(8,128)(2,1)S(1)}) custom-call(s32[1]{0:T(128)} %bitcast.me_ref, bf16[4,32,1024]{2,1,0:T(8,128)(2,1)S(1)} %get-tuple-element.49.refs_0_.own, ...), custom_call_target="tpu_custom_call" | custom-call | bytes 6062084 | tf_op jit(solution)/shard_map/pallas_call | solution.py:51
  77.0 2.6 %collective-permute-start.22 = (bf16[4,64,1024]{2,1,0:T(8,128)(2,1)S(1)}, bf16[4,64,1024]{2,1,0:T(8,128)(2,1)S(1)}, u32[]{:S(2)}, u32[]{:S(2)}) collective-permute-start(bf16[4,64,1024]{2,1,0:T(8,128)(2,1)S(1)} %get-tuple-element.56.refs_0_), channel_id=1, source_target_pairs={{0,2},{1,3},{2,0},{3,1},{4,6},{5,7},{6,4},{7,5},{8,10},{9,11},{10,... | collective-permute-start | bytes 1572872 | tf_op jit(solution)/shard_map/ppermute | solution.py:433
  79.6 2.2 %collective-permute-start.19 = (bf16[1,64,1024]{2,1,0:T(8,128)(2,1)S(1)}, bf16[1,64,1024]{2,1,0:T(8,128)(2,1)S(1)}, u32[]{:S(2)}, u32[]{:S(2)}) collective-permute-start(bf16[1,64,1024]{2,1,0:T(8,128)(2,1)S(1)} %get-tuple-element.57), channel_id=1, source_target_pairs={{0,4},{1,5},{2,6},{3,7},{4,8},{5,9},{6,10},{7,11},{8,12},{9,13},{1... | collective-permute-start | bytes 393224 | tf_op jit(solution)/shard_map/ppermute | solution.py:433
  84.7 4.1 %collective-permute-done.20 = bf16[1,64,1024]{2,1,0:T(8,128)(2,1)S(1)} collective-permute-done((bf16[1,64,1024]{2,1,0:T(8,128)(2,1)S(1)}, bf16[1,64,1024]{2,1,0:T(8,128)(2,1)S(1)}, u32[]{:S(2)}, u32[]{:S(2)}) %collective-permute-start.20) | collective-permute-done | bytes 131104 | tf_op jit(solution)/shard_map/ppermute | solution.py:433
  89.3 4.0 %collective-permute-done.22.refs_4_.refs_2_ = bf16[4,64,1024]{2,1,0:T(8,128)(2,1)S(1)} collective-permute-done((bf16[4,64,1024]{2,1,0:T(8,128)(2,1)S(1)}, bf16[4,64,1024]{2,1,0:T(8,128)(2,1)S(1)}, u32[]{:S(2)}, u32[]{:S(2)}) %collective-permute-start.22) | collective-permute-done | bytes 524320 | tf_op jit(solution)/shard_map/ppermute | solution.py:433
  93.4 7.8 %collective-permute-done.24.refs_5_ = bf16[2,64,1024]{2,1,0:T(8,128)(2,1)S(1)} collective-permute-done((bf16[2,64,1024]{2,1,0:T(8,128)(2,1)S(1)}, bf16[2,64,1024]{2,1,0:T(8,128)(2,1)S(1)}, u32[]{:S(2)}, u32[]{:S(2)}) %collective-permute-start.24) | collective-permute-done | bytes 262176 | tf_op jit(solution)/shard_map/ppermute | solution.py:433
  103.1 4.0 %shard_map.105 = (bf16[4,32,1024]{2,1,0:T(8,128)(2,1)S(1)}, bf16[1,32,1024]{2,1,0:T(8,128)(2,1)S(1)}, bf16[2,32,1024]{2,1,0:T(8,128)(2,1)S(1)}) custom-call(s32[1]{0:T(128)} %bitcast.me_ref, bf16[4,64,1024]{2,1,0:T(8,128)(2,1)S(1)} %get-tuple-element.56.refs_0_, bf16[2,64,1024]{2,1,0:T(8,128)(2,1)S(1)} %constant_dynamic-update-slice_fusion.4.refs_1_, ...), custom_call_target="tpu_custom_call" | custom-call | bytes 4571140 | tf_op jit(solution)/shard_map/pallas_call | solution.py:51
  107.1 1.7 collective-permute-start.27
  110.0 2.2 %collective-permute-start.30 = (bf16[4,32,1024]{2,1,0:T(8,128)(2,1)S(1)}, bf16[4,32,1024]{2,1,0:T(8,128)(2,1)S(1)}, u32[]{:S(2)}, u32[]{:S(2)}) collective-permute-start(bf16[4,32,1024]{2,1,0:T(8,128)(2,1)S(1)} %get-tuple-element.62.refs_0_), channel_id=1, source_target_pairs={{0,2},{1,3},{2,0},{3,1},{4,6},{5,7},{6,4},{7,5},{8,10},{9,11},{10,... | collective-permute-start | bytes 786440 | tf_op jit(solution)/shard_map/ppermute | solution.py:433
  112.2 2.7 %collective-permute-done.28 = bf16[1,32,1024]{2,1,0:T(8,128)(2,1)S(1)} collective-permute-done((bf16[1,32,1024]{2,1,0:T(8,128)(2,1)S(1)}, bf16[1,32,1024]{2,1,0:T(8,128)(2,1)S(1)}, u32[]{:S(2)}, u32[]{:S(2)}) %collective-permute-start.28) | collective-permute-done | bytes 65568 | tf_op jit(solution)/shard_map/ppermute | solution.py:433
  114.9 2.2 %collective-permute-start.32 = (bf16[3,32,1024]{2,1,0:T(8,128)(2,1)S(1)}, bf16[3,32,1024]{2,1,0:T(8,128)(2,1)S(1)}, u32[]{:S(2)}, u32[]{:S(2)}) collective-permute-start(bf16[3,32,1024]{2,1,0:T(8,128)(2,1)S(1)} %constant_dynamic-update-slice_fusion.6.refs_1_), channel_id=1, source_target_pairs={{0,2},{1,3},{2,0},{3,1},{4,6},{5,7},{6,4},{7,5},{8,10},{9,11},{10,... | collective-permute-start | bytes 589832 | tf_op jit(solution)/shard_map/ppermute | solution.py:433
  117.1 2.8 %shard_map.106 = bf16[864,256]{1,0:T(8,128)(2,1)S(1)} custom-call(s32[1]{0:T(128)} %bitcast.me_ref, bf16[4,32,1024]{2,1,0:T(8,128)(2,1)S(1)} %get-tuple-element.49.refs_0_.own, bf16[2,32,1024]{2,1,0:T(8,128)(2,1)S(1)} %constant_dynamic-update-slice_fusion.2.refs_1_.rim, bf16[4,64,1024]{2,1,0:T(8,128)(2,1)S(1)} %get-tuple-element.56.refs_0_, ...), custom_call_target="tpu_custom_call" | custom-call | flops 1811939328 | bytes 2932740 | tf_op jit(solution)/shard_map/pallas_call | solution.py:51
  121.3 5.4 %collective-permute-done.32.refs_5_ = bf16[3,32,1024]{2,1,0:T(8,128)(2,1)S(1)} collective-permute-done((bf16[3,32,1024]{2,1,0:T(8,128)(2,1)S(1)}, bf16[3,32,1024]{2,1,0:T(8,128)(2,1)S(1)}, u32[]{:S(2)}, u32[]{:S(2)}) %collective-permute-start.32) | collective-permute-done | bytes 196640 | tf_op jit(solution)/shard_map/ppermute | solution.py:433
  128.2 4.9 %shard_map.107 = bf16[32,48,256]{2,1,0:T(8,128)(2,1)S(1)} custom-call(s32[1]{0:T(128)} %bitcast.me_ref, bf16[4,32,1024]{2,1,0:T(8,128)(2,1)S(1)} %get-tuple-element.62.refs_0_, bf16[3,32,1024]{2,1,0:T(8,128)(2,1)S(1)} %constant_dynamic-update-slice_fusion.6.refs_1_, bf16[4,32,1024]{2,1,0:T(8,128)(2,1)S(1)} %collective-permute-done.29.refs_2_, ...), custom_call_target="tpu_custom_call" | custom-call | bytes 10354692 | tf_op jit(solution)/shard_map/pallas_call | solution.py:51
  133.2 28.1 %all_to_all.10 = bf16[32,48,256]{2,1,0:T(8,128)(2,1)S(1)} all-to-all(bf16[32,48,256]{2,1,0:T(8,128)(2,1)S(1)} %shard_map.107), channel_id=1, replica_groups=mesh['space'=32,'chan'=4] {'space'}, dimensions={0} | all-to-all | bytes 1572864 | tf_op jit(solution)/shard_map/all_to_all | solution.py:451
  163.0 5.0 %collective-permute-done.36 = bf16[48,256]{1,0:T(8,128)(2,1)S(1)} collective-permute-done((bf16[48,256]{1,0:T(8,128)(2,1)S(1)}, bf16[48,256]{1,0:T(8,128)(2,1)S(1)}, u32[]{:S(2)}, u32[]{:S(2)}) %collective-permute-start.36) | collective-permute-done | bytes 24608 | tf_op jit(solution)/shard_map/ppermute | solution.py:433
  169.1 4.3 %all-to-all-start.1 = ((bf16[32,48,256]{2,1,0:T(8,128)(2,1)}), bf16[32,48,256]{2,1,0:T(8,128)(2,1)S(1)}, u32[]{:S(2)}, u32[]{:S(2)}) async-start(bf16[32,48,256]{2,1,0:T(8,128)(2,1)} %broadcast_in_dim.10), calls=%async_computation.1 | async-start | bytes 1572864 | tf_op jit(solution)/shard_map/all_to_all | solution.py:461
  174.4 12.3 %all-to-all-done.1.packed = bf16[32,48,256]{2,1,0:T(8,128)(2,1)S(1)} async-done(((bf16[32,48,256]{2,1,0:T(8,128)(2,1)}), bf16[32,48,256]{2,1,0:T(8,128)(2,1)S(1)}, u32[]{:S(2)}, u32[]{:S(2)}) %all-to-all-start.1) | async-done | bytes 786464 | tf_op jit(solution)/shard_map/all_to_all | solution.py:461
  (113 shorter events, 28.8 us)
Async XLA Ops:
  7.2 43.2 %all-gather.3.cloned.1.call-start = ((), (), s32[]{:S(2)}) async-start(), calls=%async_computation.2 | async-start | bytes 3317760 | tf_op jit(solution)/shard_map/all_gather | solution.py:472
  9.3 5.4 %collective-permute-start.2 = (bf16[4,3,3,512]{3,2,1,0:T(4,128)(2,1)S(1)}, bf16[4,3,3,512]{3,2,1,0:T(4,128)(2,1)S(1)}, u32[]{:S(2)}, u32[]{:S(2)}) collective-permute-start(bf16[4,3,3,512]{3,2,1,0:T(4,128)(2,1)S(1)} %slice.20), channel_id=1, source_target_pairs={{5,0},{6,1},{7,2},{9,4},{10,5},{11,6},{13,8},{14,9},{15,10},{17,12... | collective-permute-start | bytes 110600 | tf_op jit(solution)/shard_map/ppermute | solution.py:433
  10.7 4.0 %collective-permute-start.1 = (bf16[4,16,3,512]{3,2,1,0:T(4,128)(2,1)S(1)}, bf16[4,16,3,512]{3,2,1,0:T(4,128)(2,1)S(1)}, u32[]{:S(2)}, u32[]{:S(2)}) collective-permute-start(bf16[4,16,3,512]{3,2,1,0:T(4,128)(2,1)S(1)} %slice.19), channel_id=1, source_target_pairs={{1,0},{2,1},{3,2},{5,4},{6,5},{7,6},{9,8},{10,9},{11,10},{13,12},{... | collective-permute-start | bytes 589832 | tf_op jit(solution)/shard_map/ppermute | solution.py:433
  12.0 7.1 %collective-permute-start = (bf16[4,3,8,512]{3,2,1,0:T(8,128)(2,1)S(1)}, bf16[4,3,8,512]{3,2,1,0:T(8,128)(2,1)S(1)}, u32[]{:S(2)}, u32[]{:S(2)}) collective-permute-start(bf16[4,3,8,512]{3,2,1,0:T(8,128)(2,1)S(1)} %slice.18), channel_id=1, source_target_pairs={{4,0},{5,1},{6,2},{7,3},{8,4},{9,5},{10,6},{11,7},{12,8},{13,9},{1... | collective-permute-start | bytes 294920 | tf_op jit(solution)/shard_map/ppermute | solution.py:433
  24.5 10.3 %collective-permute-start.3 = (bf16[2,64,256]{2,1,0:T(8,128)(2,1)S(1)}, bf16[2,64,256]{2,1,0:T(8,128)(2,1)S(1)}, u32[]{:S(2)}, u32[]{:S(2)}) collective-permute-start(bf16[2,64,256]{2,1,0:T(8,128)(2,1)S(1)} %get-tuple-element.44), channel_id=1, source_target_pairs={{0,4},{1,5},{2,6},{3,7},{4,8},{5,9},{6,10},{7,11},{8,12},{9,13},{1... | collective-permute-start | bytes 196616 | tf_op jit(solution)/shard_map/ppermute | solution.py:433
  28.0 24.9 %collective-permute-start.5 = (bf16[4,64,384]{2,1,0:T(8,128)(2,1)S(1)}, bf16[4,64,384]{2,1,0:T(8,128)(2,1)S(1)}, u32[]{:S(2)}, u32[]{:S(2)}) collective-permute-start(bf16[4,64,384]{2,1,0:T(8,128)(2,1)S(1)} %get-tuple-element.43.refs_0_), channel_id=1, source_target_pairs={{0,1},{1,0},{2,3},{3,2},{4,5},{5,4},{6,7},{7,6},{8,9},{9,8},{10,11... | collective-permute-start | bytes 589832 | tf_op jit(solution)/shard_map/ppermute | solution.py:433
  30.2 21.8 %collective-permute-start.6 = (bf16[4,64,384]{2,1,0:T(8,128)(2,1)S(1)}, bf16[4,64,384]{2,1,0:T(8,128)(2,1)S(1)}, u32[]{:S(2)}, u32[]{:S(2)}) collective-permute-start(bf16[4,64,384]{2,1,0:T(8,128)(2,1)S(1)} %get-tuple-element.43.refs_0_), channel_id=1, source_target_pairs={{0,2},{1,3},{2,0},{3,1},{4,6},{5,7},{6,4},{7,5},{8,10},{9,11},{10,... | collective-permute-start | bytes 589832 | tf_op jit(solution)/shard_map/ppermute | solution.py:433
  33.5 5.8 %collective-permute-start.4 = (bf16[1,64,256]{2,1,0:T(8,128)(2,1)S(1)}, bf16[1,64,256]{2,1,0:T(8,128)(2,1)S(1)}, u32[]{:S(2)}, u32[]{:S(2)}) collective-permute-start(bf16[1,64,256]{2,1,0:T(8,128)(2,1)S(1)} %get-tuple-element.45), channel_id=1, source_target_pairs={{4,0},{5,1},{6,2},{7,3},{8,4},{9,5},{10,6},{11,7},{12,8},{13,9},{1... | collective-permute-start | bytes 98312 | tf_op jit(solution)/shard_map/ppermute | solution.py:433
  39.3 13.1 %collective-permute-start.8 = (bf16[3,64,256]{2,1,0:T(8,128)(2,1)S(1)}, bf16[3,64,256]{2,1,0:T(8,128)(2,1)S(1)}, u32[]{:S(2)}, u32[]{:S(2)}) collective-permute-start(bf16[3,64,256]{2,1,0:T(8,128)(2,1)S(1)} %constant_dynamic-update-slice_fusion.refs_1_), channel_id=1, source_target_pairs={{0,2},{1,3},{2,0},{3,1},{4,6},{5,7},{6,4},{7,5},{8,10},{9,11},{10,... | collective-permute-start | bytes 294920 | tf_op jit(solution)/shard_map/ppermute | solution.py:433
  52.1 1.9 collective-permute-start.9
  56.3 3.3 %collective-permute-start.11 = (bf16[1,32,1024]{2,1,0:T(8,128)(2,1)S(1)}, bf16[1,32,1024]{2,1,0:T(8,128)(2,1)S(1)}, u32[]{:S(2)}, u32[]{:S(2)}) collective-permute-start(bf16[1,32,1024]{2,1,0:T(8,128)(2,1)S(1)} %get-tuple-element.50), channel_id=1, source_target_pairs={{0,4},{1,5},{2,6},{3,7},{4,8},{5,9},{6,10},{7,11},{8,12},{9,13},{1... | collective-permute-start | bytes 196616 | tf_op jit(solution)/shard_map/ppermute | solution.py:433
  57.6 12.1 %collective-permute-start.14 = (bf16[4,32,1024]{2,1,0:T(8,128)(2,1)S(1)}, bf16[4,32,1024]{2,1,0:T(8,128)(2,1)S(1)}, u32[]{:S(2)}, u32[]{:S(2)}) collective-permute-start(bf16[4,32,1024]{2,1,0:T(8,128)(2,1)S(1)} %get-tuple-element.49.refs_0_.own), channel_id=1, source_target_pairs={{0,2},{1,3},{2,0},{3,1},{4,6},{5,7},{6,4},{7,5},{8,10},{9,11},{10,... | collective-permute-start | bytes 786440 | tf_op jit(solution)/shard_map/ppermute | solution.py:433
  57.7 14.7 %collective-permute-start.13 = (bf16[4,32,1024]{2,1,0:T(8,128)(2,1)S(1)}, bf16[4,32,1024]{2,1,0:T(8,128)(2,1)S(1)}, u32[]{:S(2)}, u32[]{:S(2)}) collective-permute-start(bf16[4,32,1024]{2,1,0:T(8,128)(2,1)S(1)} %get-tuple-element.49.refs_0_.own), channel_id=1, source_target_pairs={{0,1},{1,0},{2,3},{3,2},{4,5},{5,4},{6,7},{7,6},{8,9},{9,8},{10,11... | collective-permute-start | bytes 786440 | tf_op jit(solution)/shard_map/ppermute | solution.py:433
  58.1 6.1 %collective-permute-start.12 = (bf16[1,32,1024]{2,1,0:T(8,128)(2,1)S(1)}, bf16[1,32,1024]{2,1,0:T(8,128)(2,1)S(1)}, u32[]{:S(2)}, u32[]{:S(2)}) collective-permute-start(bf16[1,32,1024]{2,1,0:T(8,128)(2,1)S(1)} %get-tuple-element.51), channel_id=1, source_target_pairs={{4,0},{5,1},{6,2},{7,3},{8,4},{9,5},{10,6},{11,7},{12,8},{13,9},{1... | collective-permute-start | bytes 196616 | tf_op jit(solution)/shard_map/ppermute | solution.py:433
  64.2 7.7 %collective-permute-start.16 = (bf16[2,32,1024]{2,1,0:T(8,128)(2,1)S(1)}, bf16[2,32,1024]{2,1,0:T(8,128)(2,1)S(1)}, u32[]{:S(2)}, u32[]{:S(2)}) collective-permute-start(bf16[2,32,1024]{2,1,0:T(8,128)(2,1)S(1)} %constant_dynamic-update-slice_fusion.2.refs_1_.rim), channel_id=1, source_target_pairs={{0,2},{1,3},{2,0},{3,1},{4,6},{5,7},{6,4},{7,5},{8,10},{9,11},{10,... | collective-permute-start | bytes 393224 | tf_op jit(solution)/shard_map/ppermute | solution.py:433
  69.8 3.7 %collective-permute-start.17 = (bf16[4,32,1024]{2,1,0:T(8,128)(2,1)S(1)}, bf16[4,32,1024]{2,1,0:T(8,128)(2,1)S(1)}, u32[]{:S(2)}, u32[]{:S(2)}) collective-permute-start(bf16[4,32,1024]{2,1,0:T(8,128)(2,1)S(1)} %collective-permute-done.14.refs_4_), channel_id=1, source_target_pairs={{0,1},{1,0},{2,3},{3,2},{4,5},{5,4},{6,7},{7,6},{8,9},{9,8},{10,11... | collective-permute-start | bytes 786440 | tf_op jit(solution)/shard_map/ppermute | solution.py:433
  77.0 16.3 %collective-permute-start.22 = (bf16[4,64,1024]{2,1,0:T(8,128)(2,1)S(1)}, bf16[4,64,1024]{2,1,0:T(8,128)(2,1)S(1)}, u32[]{:S(2)}, u32[]{:S(2)}) collective-permute-start(bf16[4,64,1024]{2,1,0:T(8,128)(2,1)S(1)} %get-tuple-element.56.refs_0_), channel_id=1, source_target_pairs={{0,2},{1,3},{2,0},{3,1},{4,6},{5,7},{6,4},{7,5},{8,10},{9,11},{10,... | collective-permute-start | bytes 1572872 | tf_op jit(solution)/shard_map/ppermute | solution.py:433
  79.6 5.1 %collective-permute-start.19 = (bf16[1,64,1024]{2,1,0:T(8,128)(2,1)S(1)}, bf16[1,64,1024]{2,1,0:T(8,128)(2,1)S(1)}, u32[]{:S(2)}, u32[]{:S(2)}) collective-permute-start(bf16[1,64,1024]{2,1,0:T(8,128)(2,1)S(1)} %get-tuple-element.57), channel_id=1, source_target_pairs={{0,4},{1,5},{2,6},{3,7},{4,8},{5,9},{6,10},{7,11},{8,12},{9,13},{1... | collective-permute-start | bytes 393224 | tf_op jit(solution)/shard_map/ppermute | solution.py:433
  81.8 7.1 %collective-permute-start.20 = (bf16[1,64,1024]{2,1,0:T(8,128)(2,1)S(1)}, bf16[1,64,1024]{2,1,0:T(8,128)(2,1)S(1)}, u32[]{:S(2)}, u32[]{:S(2)}) collective-permute-start(bf16[1,64,1024]{2,1,0:T(8,128)(2,1)S(1)} %get-tuple-element.58), channel_id=1, source_target_pairs={{4,0},{5,1},{6,2},{7,3},{8,4},{9,5},{10,6},{11,7},{12,8},{13,9},{1... | collective-permute-start | bytes 393224 | tf_op jit(solution)/shard_map/ppermute | solution.py:433
  83.1 18.6 %collective-permute-start.21 = (bf16[4,64,1024]{2,1,0:T(8,128)(2,1)S(1)}, bf16[4,64,1024]{2,1,0:T(8,128)(2,1)S(1)}, u32[]{:S(2)}, u32[]{:S(2)}) collective-permute-start(bf16[4,64,1024]{2,1,0:T(8,128)(2,1)S(1)} %get-tuple-element.56.refs_0_), channel_id=1, source_target_pairs={{0,1},{1,0},{2,3},{3,2},{4,5},{5,4},{6,7},{7,6},{8,9},{9,8},{10,11... | collective-permute-start | bytes 1572872 | tf_op jit(solution)/shard_map/ppermute | solution.py:433
  88.8 12.3 %collective-permute-start.24 = (bf16[2,64,1024]{2,1,0:T(8,128)(2,1)S(1)}, bf16[2,64,1024]{2,1,0:T(8,128)(2,1)S(1)}, u32[]{:S(2)}, u32[]{:S(2)}) collective-permute-start(bf16[2,64,1024]{2,1,0:T(8,128)(2,1)S(1)} %constant_dynamic-update-slice_fusion.4.refs_1_), channel_id=1, source_target_pairs={{0,2},{1,3},{2,0},{3,1},{4,6},{5,7},{6,4},{7,5},{8,10},{9,11},{10,... | collective-permute-start | bytes 786440 | tf_op jit(solution)/shard_map/ppermute | solution.py:433
  93.4 9.7 %collective-permute-start.25 = (bf16[4,64,1024]{2,1,0:T(8,128)(2,1)S(1)}, bf16[4,64,1024]{2,1,0:T(8,128)(2,1)S(1)}, u32[]{:S(2)}, u32[]{:S(2)}) collective-permute-start(bf16[4,64,1024]{2,1,0:T(8,128)(2,1)S(1)} %collective-permute-done.22.refs_4_.refs_2_), channel_id=1, source_target_pairs={{0,1},{1,0},{2,3},{3,2},{4,5},{5,4},{6,7},{7,6},{8,9},{9,8},{10,11... | collective-permute-start | bytes 1572872 | tf_op jit(solution)/shard_map/ppermute | solution.py:433
  101.2 1.9 collective-permute-start.23
  107.1 5.2 %collective-permute-start.27 = (bf16[2,32,1024]{2,1,0:T(8,128)(2,1)S(1)}, bf16[2,32,1024]{2,1,0:T(8,128)(2,1)S(1)}, u32[]{:S(2)}, u32[]{:S(2)}) collective-permute-start(bf16[2,32,1024]{2,1,0:T(8,128)(2,1)S(1)} %get-tuple-element.63), channel_id=1, source_target_pairs={{0,4},{1,5},{2,6},{3,7},{4,8},{5,9},{6,10},{7,11},{8,12},{9,13},{1... | collective-permute-start | bytes 393224 | tf_op jit(solution)/shard_map/ppermute | solution.py:433
  108.7 6.2 %collective-permute-start.28 = (bf16[1,32,1024]{2,1,0:T(8,128)(2,1)S(1)}, bf16[1,32,1024]{2,1,0:T(8,128)(2,1)S(1)}, u32[]{:S(2)}, u32[]{:S(2)}) collective-permute-start(bf16[1,32,1024]{2,1,0:T(8,128)(2,1)S(1)} %get-tuple-element.64), channel_id=1, source_target_pairs={{4,0},{5,1},{6,2},{7,3},{8,4},{9,5},{10,6},{11,7},{12,8},{13,9},{1... | collective-permute-start | bytes 196616 | tf_op jit(solution)/shard_map/ppermute | solution.py:433
  110.0 10.8 %collective-permute-start.30 = (bf16[4,32,1024]{2,1,0:T(8,128)(2,1)S(1)}, bf16[4,32,1024]{2,1,0:T(8,128)(2,1)S(1)}, u32[]{:S(2)}, u32[]{:S(2)}) collective-permute-start(bf16[4,32,1024]{2,1,0:T(8,128)(2,1)S(1)} %get-tuple-element.62.refs_0_), channel_id=1, source_target_pairs={{0,2},{1,3},{2,0},{3,1},{4,6},{5,7},{6,4},{7,5},{8,10},{9,11},{10,... | collective-permute-start | bytes 786440 | tf_op jit(solution)/shard_map/ppermute | solution.py:433
  114.9 11.8 %collective-permute-start.32 = (bf16[3,32,1024]{2,1,0:T(8,128)(2,1)S(1)}, bf16[3,32,1024]{2,1,0:T(8,128)(2,1)S(1)}, u32[]{:S(2)}, u32[]{:S(2)}) collective-permute-start(bf16[3,32,1024]{2,1,0:T(8,128)(2,1)S(1)} %constant_dynamic-update-slice_fusion.6.refs_1_), channel_id=1, source_target_pairs={{0,2},{1,3},{2,0},{3,1},{4,6},{5,7},{6,4},{7,5},{8,10},{9,11},{10,... | collective-permute-start | bytes 589832 | tf_op jit(solution)/shard_map/ppermute | solution.py:433
  117.1 9.7 %collective-permute-start.29 = (bf16[4,32,1024]{2,1,0:T(8,128)(2,1)S(1)}, bf16[4,32,1024]{2,1,0:T(8,128)(2,1)S(1)}, u32[]{:S(2)}, u32[]{:S(2)}) collective-permute-start(bf16[4,32,1024]{2,1,0:T(8,128)(2,1)S(1)} %get-tuple-element.62.refs_0_), channel_id=1, source_target_pairs={{0,1},{1,0},{2,3},{3,2},{4,5},{5,4},{6,7},{7,6},{8,9},{9,8},{10,11... | collective-permute-start | bytes 786440 | tf_op jit(solution)/shard_map/ppermute | solution.py:433
  120.8 6.0 %collective-permute-start.31 = (bf16[3,32,1024]{2,1,0:T(8,128)(2,1)S(1)}, bf16[3,32,1024]{2,1,0:T(8,128)(2,1)S(1)}, u32[]{:S(2)}, u32[]{:S(2)}) collective-permute-start(bf16[3,32,1024]{2,1,0:T(8,128)(2,1)S(1)} %constant_dynamic-update-slice_fusion.6.refs_1_), channel_id=1, source_target_pairs={{0,1},{1,0},{2,3},{3,2},{4,5},{5,4},{6,7},{7,6},{8,9},{9,8},{10,11... | collective-permute-start | bytes 589832 | tf_op jit(solution)/shard_map/ppermute | solution.py:433
  120.8 6.0 %collective-permute-start.33 = (bf16[4,32,1024]{2,1,0:T(8,128)(2,1)S(1)}, bf16[4,32,1024]{2,1,0:T(8,128)(2,1)S(1)}, u32[]{:S(2)}, u32[]{:S(2)}) collective-permute-start(bf16[4,32,1024]{2,1,0:T(8,128)(2,1)S(1)} %collective-permute-done.30.refs_4_), channel_id=1, source_target_pairs={{0,1},{1,0},{2,3},{3,2},{4,5},{5,4},{6,7},{7,6},{8,9},{9,8},{10,11... | collective-permute-start | bytes 786440 | tf_op jit(solution)/shard_map/ppermute | solution.py:433
  162.7 5.4 %collective-permute-start.36 = (bf16[48,256]{1,0:T(8,128)(2,1)S(1)}, bf16[48,256]{1,0:T(8,128)(2,1)S(1)}, u32[]{:S(2)}, u32[]{:S(2)}) collective-permute-start(bf16[48,256]{1,0:T(8,128)(2,1)S(1)} %add_convert_fusion), channel_id=1, source_target_pairs={{0,2},{1,3},{2,0},{3,1},{4,6},{5,7},{6,4},{7,5},{8,10},{9,11},{10,... | collective-permute-start | bytes 73736 | tf_op jit(solution)/shard_map/ppermute | solution.py:433
  169.1 17.6 %all-to-all-start.1 = ((bf16[32,48,256]{2,1,0:T(8,128)(2,1)}), bf16[32,48,256]{2,1,0:T(8,128)(2,1)S(1)}, u32[]{:S(2)}, u32[]{:S(2)}) async-start(bf16[32,48,256]{2,1,0:T(8,128)(2,1)} %broadcast_in_dim.10), calls=%async_computation.1 | async-start | bytes 1572864 | tf_op jit(solution)/shard_map/all_to_all | solution.py:461
  (20 other events, 200.5 us)
Sparse Core Ops, SparseCore 0:
  10.3 40.0 all-gather.2

commit v8 on v7

--- a/solution.py
+++ b/solution.py
@@ -10,7 +10,7 @@
 F32 = jnp.float32
 BOTH = ("space", "chan")
 LANES = 128
-VMEM_LIMIT = 20 * 1024 * 1024
+VMEM_LIMIT = 14 * 1024 * 1024
 
 
 def mm(left, right):

time: 196 us -> 196 us (level)
  no operation moved by 1% of the time
where the time goes in v8:
time: 196 us; the launch traced here: 195 us
  waiting for transfers between devices  78.7 us (40%)
  starting transfers between devices  42.2 us (22%)
  blocking collectives  28.1 us (14%)
  Pallas kernels  26.1 us (13%)
  between operations  14.6 us (7%)
  local copies, waits for them, and re-layouts  2.79 us (1%)
  other arithmetic  2.7 us (1%)
    ppermute x37, waiting for transfers between devices, moved(): return lax.ppermute(block, BOTH, route)  55.6 us
    ppermute x37, starting transfers between devices, moved(): return lax.ppermute(block, BOTH, route)  37.8 us
    all_to_all x1, blocking collectives, summed(): terms = lax.all_to_all(parts, 'space', 0, 0)  28.1 us
    pallas_call x8, Pallas kernels, call(): pl.pallas_call(kernel, out_shape=[pltpu.HBM(s, t) if place in away else j...  26.1 us
    all_to_all x1, waiting for transfers between devices, summed(): lax.all_to_all(jnp.broadcast_to(total[None], parts.shape), 'space', 0, 0)  12.3 us
    all_gather x1, waiting for transfers between devices, per_device(): filters = lax.all_gather(jnp.concatenate([four, three], 1), 'chan')  10.8 us
    all_to_all x1, starting transfers between devices, summed(): lax.all_to_all(jnp.broadcast_to(total[None], parts.shape), 'space', 0, 0)  4.34 us
  transfers between devices with their start and end apart: 39, of which 25 were waited for; matrix products, arithmetic and copies ran while one was open for 1% of the time, Pallas kernels for 5%

profile of v8, /device:TPU:0, one launch (start us, length us, event | category | flops | bytes accessed | tf_op | source)
XLA Modules:
  0.0 195.1 jit_solution(14178283142154337308)
XLA Ops:
  7.2 2.0 %fusion.3 = bf16[27,48,256]{2,1,0:T(8,128)(2,1)} fusion(bf16[27,16,128]{2,1,0:T(8,128)(2,1)} %bitcast.53, bf16[27,32,256]{2,1,0:T(8,128)(2,1)} %bitcast.42), kind=kLoop, calls=%fused_computation.7 | loop fusion | flops 1990656 | bytes 1216512 | tf_op jit(solution)/shard_map/concatenate | solution.py:472
  14.9 4.2 %collective-permute-done = bf16[4,3,8,512]{3,2,1,0:T(8,128)(2,1)S(1)} collective-permute-done((bf16[4,3,8,512]{3,2,1,0:T(8,128)(2,1)S(1)}, bf16[4,3,8,512]{3,2,1,0:T(8,128)(2,1)S(1)}, u32[]{:S(2)}, u32[]{:S(2)}) %collective-permute-start) | collective-permute-done | bytes 98336 | tf_op jit(solution)/shard_map/ppermute | solution.py:433
  19.3 5.3 %shard_map.101 = (bf16[19,352,128]{2,1,0:T(8,128)(2,1)}, bf16[9,480,128]{2,1,0:T(8,128)(2,1)}, f32[8,64,512]{2,1,0:T(8,128)}, bf16[4,64,384]{2,1,0:T(8,128)(2,1)...) custom-call(bf16[4,19,16,512]{3,2,1,0:T(8,128)(2,1)S(1)} %pad_maximum_fusion.vol, ...), custom_call_target="tpu_custom_call" | custom-call | bytes 5816320 | tf_op jit(solution)/shard_map/pallas_call | solution.py:51
  24.5 3.5 %collective-permute-start.3 = (bf16[2,64,256]{2,1,0:T(8,128)(2,1)S(1)}, bf16[2,64,256]{2,1,0:T(8,128)(2,1)S(1)}, u32[]{:S(2)}, u32[]{:S(2)}) collective-permute-start(bf16[2,64,256]{2,1,0:T(8,128)(2,1)S(1)} %get-tuple-element.44), channel_id=1, source_target_pairs={{0,4},{1,5},{2,6},{3,7},{4,8},{5,9},{6,10},{7,11},{8,12},{9,13},{1... | collective-permute-start | bytes 196616 | tf_op jit(solution)/shard_map/ppermute | solution.py:433
  28.0 2.2 %collective-permute-start.5 = (bf16[4,64,384]{2,1,0:T(8,128)(2,1)S(1)}, bf16[4,64,384]{2,1,0:T(8,128)(2,1)S(1)}, u32[]{:S(2)}, u32[]{:S(2)}) collective-permute-start(bf16[4,64,384]{2,1,0:T(8,128)(2,1)S(1)} %get-tuple-element.43.refs_0_), channel_id=1, source_target_pairs={{0,1},{1,0},{2,3},{3,2},{4,5},{5,4},{6,7},{7,6},{8,9},{9,8},{10,11... | collective-permute-start | bytes 589832 | tf_op jit(solution)/shard_map/ppermute | solution.py:433
  30.3 3.3 %collective-permute-start.6 = (bf16[4,64,384]{2,1,0:T(8,128)(2,1)S(1)}, bf16[4,64,384]{2,1,0:T(8,128)(2,1)S(1)}, u32[]{:S(2)}, u32[]{:S(2)}) collective-permute-start(bf16[4,64,384]{2,1,0:T(8,128)(2,1)S(1)} %get-tuple-element.43.refs_0_), channel_id=1, source_target_pairs={{0,2},{1,3},{2,0},{3,1},{4,6},{5,7},{6,4},{7,5},{8,10},{9,11},{10,... | collective-permute-start | bytes 589832 | tf_op jit(solution)/shard_map/ppermute | solution.py:433
  34.9 4.5 %collective-permute-done.4 = bf16[1,64,256]{2,1,0:T(8,128)(2,1)S(1)} collective-permute-done((bf16[1,64,256]{2,1,0:T(8,128)(2,1)S(1)}, bf16[1,64,256]{2,1,0:T(8,128)(2,1)S(1)}, u32[]{:S(2)}, u32[]{:S(2)}) %collective-permute-start.4) | collective-permute-done | bytes 32800 | tf_op jit(solution)/shard_map/ppermute | solution.py:433
  39.6 10.8 %all-gather.3.cloned.1.call-done = bf16[108,48,256]{2,1,0:T(8,128)(2,1)} async-done(((bf16[27,48,256]{2,1,0:T(8,128)(2,1)}), bf16[108,48,256]{2,1,0:T(8,128)(2,1)}) %all-gather.3.cloned.1.call-update) | async-done | bytes 2654224 | tf_op jit(solution)/shard_map/all_gather | solution.py:472
  50.4 1.7 shard_map.102.refs_8_
  54.0 2.4 %shard_map.103 = (bf16[4,32,1024]{2,1,0:T(8,128)(2,1)S(1)}, bf16[1,32,1024]{2,1,0:T(8,128)(2,1)S(1)}, bf16[1,32,1024]{2,1,0:T(8,128)(2,1)S(1)}, f32[4,32,1024]{2...) custom-call(s32[1]{0:T(128)} %bitcast.me_ref, ...), custom_call_target="tpu_custom_call" | custom-call | bytes 2568196 | tf_op jit(solution)/shard_map/pallas_call | solution.py:51
  59.7 4.5 %collective-permute-done.12 = bf16[1,32,1024]{2,1,0:T(8,128)(2,1)S(1)} collective-permute-done((bf16[1,32,1024]{2,1,0:T(8,128)(2,1)S(1)}, bf16[1,32,1024]{2,1,0:T(8,128)(2,1)S(1)}, u32[]{:S(2)}, u32[]{:S(2)}) %collective-permute-start.12) | collective-permute-done | bytes 65568 | tf_op jit(solution)/shard_map/ppermute | solution.py:433
  64.2 3.5 %collective-permute-start.16 = (bf16[2,32,1024]{2,1,0:T(8,128)(2,1)S(1)}, bf16[2,32,1024]{2,1,0:T(8,128)(2,1)S(1)}, u32[]{:S(2)}, u32[]{:S(2)}) collective-permute-start(bf16[2,32,1024]{2,1,0:T(8,128)(2,1)S(1)} %constant_dynamic-update-slice_fusion.2.refs_1_.rim), channel_id=1, source_target_pairs={{0,2},{1,3},{2,0},{3,1},{4,6},{5,7},{6,4},{7,5},{8,10},{9,11},{10,... | collective-permute-start | bytes 393224 | tf_op jit(solution)/shard_map/ppermute | solution.py:433
  67.7 2.0 %collective-permute-done.14.refs_4_ = bf16[4,32,1024]{2,1,0:T(8,128)(2,1)S(1)} collective-permute-done((bf16[4,32,1024]{2,1,0:T(8,128)(2,1)S(1)}, bf16[4,32,1024]{2,1,0:T(8,128)(2,1)S(1)}, u32[]{:S(2)}, u32[]{:S(2)}) %collective-permute-start.14) | collective-permute-done | bytes 262176 | tf_op jit(solution)/shard_map/ppermute | solution.py:433
  69.8 2.1 %collective-permute-done.16.refs_5_ = bf16[2,32,1024]{2,1,0:T(8,128)(2,1)S(1)} collective-permute-done((bf16[2,32,1024]{2,1,0:T(8,128)(2,1)S(1)}, bf16[2,32,1024]{2,1,0:T(8,128)(2,1)S(1)}, u32[]{:S(2)}, u32[]{:S(2)}) %collective-permute-start.16) | collective-permute-done | bytes 131104 | tf_op jit(solution)/shard_map/ppermute | solution.py:433
  73.4 3.6 %shard_map.104 = (bf16[4,64,1024]{2,1,0:T(8,128)(2,1)S(1)}, bf16[4,64,1024]{2,1,0:T(8,128)(2,1)S(1)}, bf16[1,64,1024]{2,1,0:T(8,128)(2,1)S(1)}, bf16[1,64,1024]{2,1,0:T(8,128)(2,1)S(1)}) custom-call(s32[1]{0:T(128)} %bitcast.me_ref, bf16[4,32,1024]{2,1,0:T(8,128)(2,1)S(1)} %get-tuple-element.49.refs_0_.own, ...), custom_call_target="tpu_custom_call" | custom-call | bytes 6062084 | tf_op jit(solution)/shard_map/pallas_call | solution.py:51
  77.0 2.6 %collective-permute-start.22 = (bf16[4,64,1024]{2,1,0:T(8,128)(2,1)S(1)}, bf16[4,64,1024]{2,1,0:T(8,128)(2,1)S(1)}, u32[]{:S(2)}, u32[]{:S(2)}) collective-permute-start(bf16[4,64,1024]{2,1,0:T(8,128)(2,1)S(1)} %get-tuple-element.56.refs_0_), channel_id=1, source_target_pairs={{0,2},{1,3},{2,0},{3,1},{4,6},{5,7},{6,4},{7,5},{8,10},{9,11},{10,... | collective-permute-start | bytes 1572872 | tf_op jit(solution)/shard_map/ppermute | solution.py:433
  79.6 2.2 %collective-permute-start.19 = (bf16[1,64,1024]{2,1,0:T(8,128)(2,1)S(1)}, bf16[1,64,1024]{2,1,0:T(8,128)(2,1)S(1)}, u32[]{:S(2)}, u32[]{:S(2)}) collective-permute-start(bf16[1,64,1024]{2,1,0:T(8,128)(2,1)S(1)} %get-tuple-element.57), channel_id=1, source_target_pairs={{0,4},{1,5},{2,6},{3,7},{4,8},{5,9},{6,10},{7,11},{8,12},{9,13},{1... | collective-permute-start | bytes 393224 | tf_op jit(solution)/shard_map/ppermute | solution.py:433
  84.7 4.1 %collective-permute-done.20 = bf16[1,64,1024]{2,1,0:T(8,128)(2,1)S(1)} collective-permute-done((bf16[1,64,1024]{2,1,0:T(8,128)(2,1)S(1)}, bf16[1,64,1024]{2,1,0:T(8,128)(2,1)S(1)}, u32[]{:S(2)}, u32[]{:S(2)}) %collective-permute-start.20) | collective-permute-done | bytes 131104 | tf_op jit(solution)/shard_map/ppermute | solution.py:433
  89.3 4.0 %collective-permute-done.22.refs_4_.refs_2_ = bf16[4,64,1024]{2,1,0:T(8,128)(2,1)S(1)} collective-permute-done((bf16[4,64,1024]{2,1,0:T(8,128)(2,1)S(1)}, bf16[4,64,1024]{2,1,0:T(8,128)(2,1)S(1)}, u32[]{:S(2)}, u32[]{:S(2)}) %collective-permute-start.22) | collective-permute-done | bytes 524320 | tf_op jit(solution)/shard_map/ppermute | solution.py:433
  93.4 7.8 %collective-permute-done.24.refs_5_ = bf16[2,64,1024]{2,1,0:T(8,128)(2,1)S(1)} collective-permute-done((bf16[2,64,1024]{2,1,0:T(8,128)(2,1)S(1)}, bf16[2,64,1024]{2,1,0:T(8,128)(2,1)S(1)}, u32[]{:S(2)}, u32[]{:S(2)}) %collective-permute-start.24) | collective-permute-done | bytes 262176 | tf_op jit(solution)/shard_map/ppermute | solution.py:433
  103.1 4.0 %shard_map.105 = (bf16[4,32,1024]{2,1,0:T(8,128)(2,1)S(1)}, bf16[1,32,1024]{2,1,0:T(8,128)(2,1)S(1)}, bf16[2,32,1024]{2,1,0:T(8,128)(2,1)S(1)}) custom-call(s32[1]{0:T(128)} %bitcast.me_ref, bf16[4,64,1024]{2,1,0:T(8,128)(2,1)S(1)} %get-tuple-element.56.refs_0_, bf16[2,64,1024]{2,1,0:T(8,128)(2,1)S(1)} %constant_dynamic-update-slice_fusion.4.refs_1_, ...), custom_call_target="tpu_custom_call" | custom-call | bytes 4571140 | tf_op jit(solution)/shard_map/pallas_call | solution.py:51
  107.1 1.7 collective-permute-start.27
  110.0 2.2 %collective-permute-start.30 = (bf16[4,32,1024]{2,1,0:T(8,128)(2,1)S(1)}, bf16[4,32,1024]{2,1,0:T(8,128)(2,1)S(1)}, u32[]{:S(2)}, u32[]{:S(2)}) collective-permute-start(bf16[4,32,1024]{2,1,0:T(8,128)(2,1)S(1)} %get-tuple-element.62.refs_0_), channel_id=1, source_target_pairs={{0,2},{1,3},{2,0},{3,1},{4,6},{5,7},{6,4},{7,5},{8,10},{9,11},{10,... | collective-permute-start | bytes 786440 | tf_op jit(solution)/shard_map/ppermute | solution.py:433
  112.2 2.7 %collective-permute-done.28 = bf16[1,32,1024]{2,1,0:T(8,128)(2,1)S(1)} collective-permute-done((bf16[1,32,1024]{2,1,0:T(8,128)(2,1)S(1)}, bf16[1,32,1024]{2,1,0:T(8,128)(2,1)S(1)}, u32[]{:S(2)}, u32[]{:S(2)}) %collective-permute-start.28) | collective-permute-done | bytes 65568 | tf_op jit(solution)/shard_map/ppermute | solution.py:433
  114.9 2.2 %collective-permute-start.32 = (bf16[3,32,1024]{2,1,0:T(8,128)(2,1)S(1)}, bf16[3,32,1024]{2,1,0:T(8,128)(2,1)S(1)}, u32[]{:S(2)}, u32[]{:S(2)}) collective-permute-start(bf16[3,32,1024]{2,1,0:T(8,128)(2,1)S(1)} %constant_dynamic-update-slice_fusion.6.refs_1_), channel_id=1, source_target_pairs={{0,2},{1,3},{2,0},{3,1},{4,6},{5,7},{6,4},{7,5},{8,10},{9,11},{10,... | collective-permute-start | bytes 589832 | tf_op jit(solution)/shard_map/ppermute | solution.py:433
  117.1 2.8 %shard_map.106 = bf16[864,256]{1,0:T(8,128)(2,1)S(1)} custom-call(s32[1]{0:T(128)} %bitcast.me_ref, bf16[4,32,1024]{2,1,0:T(8,128)(2,1)S(1)} %get-tuple-element.49.refs_0_.own, bf16[2,32,1024]{2,1,0:T(8,128)(2,1)S(1)} %constant_dynamic-update-slice_fusion.2.refs_1_.rim, bf16[4,64,1024]{2,1,0:T(8,128)(2,1)S(1)} %get-tuple-element.56.refs_0_, ...), custom_call_target="tpu_custom_call" | custom-call | flops 1811939328 | bytes 2932740 | tf_op jit(solution)/shard_map/pallas_call | solution.py:51
  121.3 5.4 %collective-permute-done.32.refs_5_ = bf16[3,32,1024]{2,1,0:T(8,128)(2,1)S(1)} collective-permute-done((bf16[3,32,1024]{2,1,0:T(8,128)(2,1)S(1)}, bf16[3,32,1024]{2,1,0:T(8,128)(2,1)S(1)}, u32[]{:S(2)}, u32[]{:S(2)}) %collective-permute-start.32) | collective-permute-done | bytes 196640 | tf_op jit(solution)/shard_map/ppermute | solution.py:433
  128.2 4.9 %shard_map.107 = bf16[32,48,256]{2,1,0:T(8,128)(2,1)S(1)} custom-call(s32[1]{0:T(128)} %bitcast.me_ref, bf16[4,32,1024]{2,1,0:T(8,128)(2,1)S(1)} %get-tuple-element.62.refs_0_, bf16[3,32,1024]{2,1,0:T(8,128)(2,1)S(1)} %constant_dynamic-update-slice_fusion.6.refs_1_, bf16[4,32,1024]{2,1,0:T(8,128)(2,1)S(1)} %collective-permute-done.29.refs_2_, ...), custom_call_target="tpu_custom_call" | custom-call | bytes 10354692 | tf_op jit(solution)/shard_map/pallas_call | solution.py:51
  133.2 28.1 %all_to_all.10 = bf16[32,48,256]{2,1,0:T(8,128)(2,1)S(1)} all-to-all(bf16[32,48,256]{2,1,0:T(8,128)(2,1)S(1)} %shard_map.107), channel_id=1, replica_groups=mesh['space'=32,'chan'=4] {'space'}, dimensions={0} | all-to-all | bytes 1572864 | tf_op jit(solution)/shard_map/all_to_all | solution.py:451
  163.0 5.0 %collective-permute-done.36 = bf16[48,256]{1,0:T(8,128)(2,1)S(1)} collective-permute-done((bf16[48,256]{1,0:T(8,128)(2,1)S(1)}, bf16[48,256]{1,0:T(8,128)(2,1)S(1)}, u32[]{:S(2)}, u32[]{:S(2)}) %collective-permute-start.36) | collective-permute-done | bytes 24608 | tf_op jit(solution)/shard_map/ppermute | solution.py:433
  169.1 4.3 %all-to-all-start.1 = ((bf16[32,48,256]{2,1,0:T(8,128)(2,1)}), bf16[32,48,256]{2,1,0:T(8,128)(2,1)S(1)}, u32[]{:S(2)}, u32[]{:S(2)}) async-start(bf16[32,48,256]{2,1,0:T(8,128)(2,1)} %broadcast_in_dim.10), calls=%async_computation.1 | async-start | bytes 1572864 | tf_op jit(solution)/shard_map/all_to_all | solution.py:461
  174.4 12.3 %all-to-all-done.1.packed = bf16[32,48,256]{2,1,0:T(8,128)(2,1)S(1)} async-done(((bf16[32,48,256]{2,1,0:T(8,128)(2,1)}), bf16[32,48,256]{2,1,0:T(8,128)(2,1)S(1)}, u32[]{:S(2)}, u32[]{:S(2)}) %all-to-all-start.1) | async-done | bytes 786464 | tf_op jit(solution)/shard_map/all_to_all | solution.py:461
  (113 shorter events, 28.9 us)
Async XLA Ops:
  7.2 43.2 %all-gather.3.cloned.1.call-start = ((), (), s32[]{:S(2)}) async-start(), calls=%async_computation.2 | async-start | bytes 3317760 | tf_op jit(solution)/shard_map/all_gather | solution.py:472
  9.3 5.4 %collective-permute-start.2 = (bf16[4,3,3,512]{3,2,1,0:T(4,128)(2,1)S(1)}, bf16[4,3,3,512]{3,2,1,0:T(4,128)(2,1)S(1)}, u32[]{:S(2)}, u32[]{:S(2)}) collective-permute-start(bf16[4,3,3,512]{3,2,1,0:T(4,128)(2,1)S(1)} %slice.20), channel_id=1, source_target_pairs={{5,0},{6,1},{7,2},{9,4},{10,5},{11,6},{13,8},{14,9},{15,10},{17,12... | collective-permute-start | bytes 110600 | tf_op jit(solution)/shard_map/ppermute | solution.py:433
  10.7 4.0 %collective-permute-start.1 = (bf16[4,16,3,512]{3,2,1,0:T(4,128)(2,1)S(1)}, bf16[4,16,3,512]{3,2,1,0:T(4,128)(2,1)S(1)}, u32[]{:S(2)}, u32[]{:S(2)}) collective-permute-start(bf16[4,16,3,512]{3,2,1,0:T(4,128)(2,1)S(1)} %slice.19), channel_id=1, source_target_pairs={{1,0},{2,1},{3,2},{5,4},{6,5},{7,6},{9,8},{10,9},{11,10},{13,12},{... | collective-permute-start | bytes 589832 | tf_op jit(solution)/shard_map/ppermute | solution.py:433
  12.0 7.1 %collective-permute-start = (bf16[4,3,8,512]{3,2,1,0:T(8,128)(2,1)S(1)}, bf16[4,3,8,512]{3,2,1,0:T(8,128)(2,1)S(1)}, u32[]{:S(2)}, u32[]{:S(2)}) collective-permute-start(bf16[4,3,8,512]{3,2,1,0:T(8,128)(2,1)S(1)} %slice.18), channel_id=1, source_target_pairs={{4,0},{5,1},{6,2},{7,3},{8,4},{9,5},{10,6},{11,7},{12,8},{13,9},{1... | collective-permute-start | bytes 294920 | tf_op jit(solution)/shard_map/ppermute | solution.py:433
  24.5 10.3 %collective-permute-start.3 = (bf16[2,64,256]{2,1,0:T(8,128)(2,1)S(1)}, bf16[2,64,256]{2,1,0:T(8,128)(2,1)S(1)}, u32[]{:S(2)}, u32[]{:S(2)}) collective-permute-start(bf16[2,64,256]{2,1,0:T(8,128)(2,1)S(1)} %get-tuple-element.44), channel_id=1, source_target_pairs={{0,4},{1,5},{2,6},{3,7},{4,8},{5,9},{6,10},{7,11},{8,12},{9,13},{1... | collective-permute-start | bytes 196616 | tf_op jit(solution)/shard_map/ppermute | solution.py:433
  28.0 24.9 %collective-permute-start.5 = (bf16[4,64,384]{2,1,0:T(8,128)(2,1)S(1)}, bf16[4,64,384]{2,1,0:T(8,128)(2,1)S(1)}, u32[]{:S(2)}, u32[]{:S(2)}) collective-permute-start(bf16[4,64,384]{2,1,0:T(8,128)(2,1)S(1)} %get-tuple-element.43.refs_0_), channel_id=1, source_target_pairs={{0,1},{1,0},{2,3},{3,2},{4,5},{5,4},{6,7},{7,6},{8,9},{9,8},{10,11... | collective-permute-start | bytes 589832 | tf_op jit(solution)/shard_map/ppermute | solution.py:433
  30.3 21.8 %collective-permute-start.6 = (bf16[4,64,384]{2,1,0:T(8,128)(2,1)S(1)}, bf16[4,64,384]{2,1,0:T(8,128)(2,1)S(1)}, u32[]{:S(2)}, u32[]{:S(2)}) collective-permute-start(bf16[4,64,384]{2,1,0:T(8,128)(2,1)S(1)} %get-tuple-element.43.refs_0_), channel_id=1, source_target_pairs={{0,2},{1,3},{2,0},{3,1},{4,6},{5,7},{6,4},{7,5},{8,10},{9,11},{10,... | collective-permute-start | bytes 589832 | tf_op jit(solution)/shard_map/ppermute | solution.py:433
  33.5 5.8 %collective-permute-start.4 = (bf16[1,64,256]{2,1,0:T(8,128)(2,1)S(1)}, bf16[1,64,256]{2,1,0:T(8,128)(2,1)S(1)}, u32[]{:S(2)}, u32[]{:S(2)}) collective-permute-start(bf16[1,64,256]{2,1,0:T(8,128)(2,1)S(1)} %get-tuple-element.45), channel_id=1, source_target_pairs={{4,0},{5,1},{6,2},{7,3},{8,4},{9,5},{10,6},{11,7},{12,8},{13,9},{1... | collective-permute-start | bytes 98312 | tf_op jit(solution)/shard_map/ppermute | solution.py:433
  39.3 13.1 %collective-permute-start.8 = (bf16[3,64,256]{2,1,0:T(8,128)(2,1)S(1)}, bf16[3,64,256]{2,1,0:T(8,128)(2,1)S(1)}, u32[]{:S(2)}, u32[]{:S(2)}) collective-permute-start(bf16[3,64,256]{2,1,0:T(8,128)(2,1)S(1)} %constant_dynamic-update-slice_fusion.refs_1_), channel_id=1, source_target_pairs={{0,2},{1,3},{2,0},{3,1},{4,6},{5,7},{6,4},{7,5},{8,10},{9,11},{10,... | collective-permute-start | bytes 294920 | tf_op jit(solution)/shard_map/ppermute | solution.py:433
  52.1 1.9 collective-permute-start.9
  56.3 3.3 %collective-permute-start.11 = (bf16[1,32,1024]{2,1,0:T(8,128)(2,1)S(1)}, bf16[1,32,1024]{2,1,0:T(8,128)(2,1)S(1)}, u32[]{:S(2)}, u32[]{:S(2)}) collective-permute-start(bf16[1,32,1024]{2,1,0:T(8,128)(2,1)S(1)} %get-tuple-element.50), channel_id=1, source_target_pairs={{0,4},{1,5},{2,6},{3,7},{4,8},{5,9},{6,10},{7,11},{8,12},{9,13},{1... | collective-permute-start | bytes 196616 | tf_op jit(solution)/shard_map/ppermute | solution.py:433
  57.6 12.1 %collective-permute-start.14 = (bf16[4,32,1024]{2,1,0:T(8,128)(2,1)S(1)}, bf16[4,32,1024]{2,1,0:T(8,128)(2,1)S(1)}, u32[]{:S(2)}, u32[]{:S(2)}) collective-permute-start(bf16[4,32,1024]{2,1,0:T(8,128)(2,1)S(1)} %get-tuple-element.49.refs_0_.own), channel_id=1, source_target_pairs={{0,2},{1,3},{2,0},{3,1},{4,6},{5,7},{6,4},{7,5},{8,10},{9,11},{10,... | collective-permute-start | bytes 786440 | tf_op jit(solution)/shard_map/ppermute | solution.py:433
  57.7 14.7 %collective-permute-start.13 = (bf16[4,32,1024]{2,1,0:T(8,128)(2,1)S(1)}, bf16[4,32,1024]{2,1,0:T(8,128)(2,1)S(1)}, u32[]{:S(2)}, u32[]{:S(2)}) collective-permute-start(bf16[4,32,1024]{2,1,0:T(8,128)(2,1)S(1)} %get-tuple-element.49.refs_0_.own), channel_id=1, source_target_pairs={{0,1},{1,0},{2,3},{3,2},{4,5},{5,4},{6,7},{7,6},{8,9},{9,8},{10,11... | collective-permute-start | bytes 786440 | tf_op jit(solution)/shard_map/ppermute | solution.py:433
  58.1 6.1 %collective-permute-start.12 = (bf16[1,32,1024]{2,1,0:T(8,128)(2,1)S(1)}, bf16[1,32,1024]{2,1,0:T(8,128)(2,1)S(1)}, u32[]{:S(2)}, u32[]{:S(2)}) collective-permute-start(bf16[1,32,1024]{2,1,0:T(8,128)(2,1)S(1)} %get-tuple-element.51), channel_id=1, source_target_pairs={{4,0},{5,1},{6,2},{7,3},{8,4},{9,5},{10,6},{11,7},{12,8},{13,9},{1... | collective-permute-start | bytes 196616 | tf_op jit(solution)/shard_map/ppermute | solution.py:433
  64.2 7.7 %collective-permute-start.16 = (bf16[2,32,1024]{2,1,0:T(8,128)(2,1)S(1)}, bf16[2,32,1024]{2,1,0:T(8,128)(2,1)S(1)}, u32[]{:S(2)}, u32[]{:S(2)}) collective-permute-start(bf16[2,32,1024]{2,1,0:T(8,128)(2,1)S(1)} %constant_dynamic-update-slice_fusion.2.refs_1_.rim), channel_id=1, source_target_pairs={{0,2},{1,3},{2,0},{3,1},{4,6},{5,7},{6,4},{7,5},{8,10},{9,11},{10,... | collective-permute-start | bytes 393224 | tf_op jit(solution)/shard_map/ppermute | solution.py:433
  69.8 3.7 %collective-permute-start.17 = (bf16[4,32,1024]{2,1,0:T(8,128)(2,1)S(1)}, bf16[4,32,1024]{2,1,0:T(8,128)(2,1)S(1)}, u32[]{:S(2)}, u32[]{:S(2)}) collective-permute-start(bf16[4,32,1024]{2,1,0:T(8,128)(2,1)S(1)} %collective-permute-done.14.refs_4_), channel_id=1, source_target_pairs={{0,1},{1,0},{2,3},{3,2},{4,5},{5,4},{6,7},{7,6},{8,9},{9,8},{10,11... | collective-permute-start | bytes 786440 | tf_op jit(solution)/shard_map/ppermute | solution.py:433
  77.0 16.3 %collective-permute-start.22 = (bf16[4,64,1024]{2,1,0:T(8,128)(2,1)S(1)}, bf16[4,64,1024]{2,1,0:T(8,128)(2,1)S(1)}, u32[]{:S(2)}, u32[]{:S(2)}) collective-permute-start(bf16[4,64,1024]{2,1,0:T(8,128)(2,1)S(1)} %get-tuple-element.56.refs_0_), channel_id=1, source_target_pairs={{0,2},{1,3},{2,0},{3,1},{4,6},{5,7},{6,4},{7,5},{8,10},{9,11},{10,... | collective-permute-start | bytes 1572872 | tf_op jit(solution)/shard_map/ppermute | solution.py:433
  79.6 5.1 %collective-permute-start.19 = (bf16[1,64,1024]{2,1,0:T(8,128)(2,1)S(1)}, bf16[1,64,1024]{2,1,0:T(8,128)(2,1)S(1)}, u32[]{:S(2)}, u32[]{:S(2)}) collective-permute-start(bf16[1,64,1024]{2,1,0:T(8,128)(2,1)S(1)} %get-tuple-element.57), channel_id=1, source_target_pairs={{0,4},{1,5},{2,6},{3,7},{4,8},{5,9},{6,10},{7,11},{8,12},{9,13},{1... | collective-permute-start | bytes 393224 | tf_op jit(solution)/shard_map/ppermute | solution.py:433
  81.8 7.1 %collective-permute-start.20 = (bf16[1,64,1024]{2,1,0:T(8,128)(2,1)S(1)}, bf16[1,64,1024]{2,1,0:T(8,128)(2,1)S(1)}, u32[]{:S(2)}, u32[]{:S(2)}) collective-permute-start(bf16[1,64,1024]{2,1,0:T(8,128)(2,1)S(1)} %get-tuple-element.58), channel_id=1, source_target_pairs={{4,0},{5,1},{6,2},{7,3},{8,4},{9,5},{10,6},{11,7},{12,8},{13,9},{1... | collective-permute-start | bytes 393224 | tf_op jit(solution)/shard_map/ppermute | solution.py:433
  83.1 18.6 %collective-permute-start.21 = (bf16[4,64,1024]{2,1,0:T(8,128)(2,1)S(1)}, bf16[4,64,1024]{2,1,0:T(8,128)(2,1)S(1)}, u32[]{:S(2)}, u32[]{:S(2)}) collective-permute-start(bf16[4,64,1024]{2,1,0:T(8,128)(2,1)S(1)} %get-tuple-element.56.refs_0_), channel_id=1, source_target_pairs={{0,1},{1,0},{2,3},{3,2},{4,5},{5,4},{6,7},{7,6},{8,9},{9,8},{10,11... | collective-permute-start | bytes 1572872 | tf_op jit(solution)/shard_map/ppermute | solution.py:433
  88.8 12.3 %collective-permute-start.24 = (bf16[2,64,1024]{2,1,0:T(8,128)(2,1)S(1)}, bf16[2,64,1024]{2,1,0:T(8,128)(2,1)S(1)}, u32[]{:S(2)}, u32[]{:S(2)}) collective-permute-start(bf16[2,64,1024]{2,1,0:T(8,128)(2,1)S(1)} %constant_dynamic-update-slice_fusion.4.refs_1_), channel_id=1, source_target_pairs={{0,2},{1,3},{2,0},{3,1},{4,6},{5,7},{6,4},{7,5},{8,10},{9,11},{10,... | collective-permute-start | bytes 786440 | tf_op jit(solution)/shard_map/ppermute | solution.py:433
  93.4 9.7 %collective-permute-start.25 = (bf16[4,64,1024]{2,1,0:T(8,128)(2,1)S(1)}, bf16[4,64,1024]{2,1,0:T(8,128)(2,1)S(1)}, u32[]{:S(2)}, u32[]{:S(2)}) collective-permute-start(bf16[4,64,1024]{2,1,0:T(8,128)(2,1)S(1)} %collective-permute-done.22.refs_4_.refs_2_), channel_id=1, source_target_pairs={{0,1},{1,0},{2,3},{3,2},{4,5},{5,4},{6,7},{7,6},{8,9},{9,8},{10,11... | collective-permute-start | bytes 1572872 | tf_op jit(solution)/shard_map/ppermute | solution.py:433
  101.2 1.9 collective-permute-start.23
  107.1 5.2 %collective-permute-start.27 = (bf16[2,32,1024]{2,1,0:T(8,128)(2,1)S(1)}, bf16[2,32,1024]{2,1,0:T(8,128)(2,1)S(1)}, u32[]{:S(2)}, u32[]{:S(2)}) collective-permute-start(bf16[2,32,1024]{2,1,0:T(8,128)(2,1)S(1)} %get-tuple-element.63), channel_id=1, source_target_pairs={{0,4},{1,5},{2,6},{3,7},{4,8},{5,9},{6,10},{7,11},{8,12},{9,13},{1... | collective-permute-start | bytes 393224 | tf_op jit(solution)/shard_map/ppermute | solution.py:433
  108.7 6.2 %collective-permute-start.28 = (bf16[1,32,1024]{2,1,0:T(8,128)(2,1)S(1)}, bf16[1,32,1024]{2,1,0:T(8,128)(2,1)S(1)}, u32[]{:S(2)}, u32[]{:S(2)}) collective-permute-start(bf16[1,32,1024]{2,1,0:T(8,128)(2,1)S(1)} %get-tuple-element.64), channel_id=1, source_target_pairs={{4,0},{5,1},{6,2},{7,3},{8,4},{9,5},{10,6},{11,7},{12,8},{13,9},{1... | collective-permute-start | bytes 196616 | tf_op jit(solution)/shard_map/ppermute | solution.py:433
  110.0 10.8 %collective-permute-start.30 = (bf16[4,32,1024]{2,1,0:T(8,128)(2,1)S(1)}, bf16[4,32,1024]{2,1,0:T(8,128)(2,1)S(1)}, u32[]{:S(2)}, u32[]{:S(2)}) collective-permute-start(bf16[4,32,1024]{2,1,0:T(8,128)(2,1)S(1)} %get-tuple-element.62.refs_0_), channel_id=1, source_target_pairs={{0,2},{1,3},{2,0},{3,1},{4,6},{5,7},{6,4},{7,5},{8,10},{9,11},{10,... | collective-permute-start | bytes 786440 | tf_op jit(solution)/shard_map/ppermute | solution.py:433
  114.9 11.8 %collective-permute-start.32 = (bf16[3,32,1024]{2,1,0:T(8,128)(2,1)S(1)}, bf16[3,32,1024]{2,1,0:T(8,128)(2,1)S(1)}, u32[]{:S(2)}, u32[]{:S(2)}) collective-permute-start(bf16[3,32,1024]{2,1,0:T(8,128)(2,1)S(1)} %constant_dynamic-update-slice_fusion.6.refs_1_), channel_id=1, source_target_pairs={{0,2},{1,3},{2,0},{3,1},{4,6},{5,7},{6,4},{7,5},{8,10},{9,11},{10,... | collective-permute-start | bytes 589832 | tf_op jit(solution)/shard_map/ppermute | solution.py:433
  117.1 9.7 %collective-permute-start.29 = (bf16[4,32,1024]{2,1,0:T(8,128)(2,1)S(1)}, bf16[4,32,1024]{2,1,0:T(8,128)(2,1)S(1)}, u32[]{:S(2)}, u32[]{:S(2)}) collective-permute-start(bf16[4,32,1024]{2,1,0:T(8,128)(2,1)S(1)} %get-tuple-element.62.refs_0_), channel_id=1, source_target_pairs={{0,1},{1,0},{2,3},{3,2},{4,5},{5,4},{6,7},{7,6},{8,9},{9,8},{10,11... | collective-permute-start | bytes 786440 | tf_op jit(solution)/shard_map/ppermute | solution.py:433
  120.8 6.0 %collective-permute-start.31 = (bf16[3,32,1024]{2,1,0:T(8,128)(2,1)S(1)}, bf16[3,32,1024]{2,1,0:T(8,128)(2,1)S(1)}, u32[]{:S(2)}, u32[]{:S(2)}) collective-permute-start(bf16[3,32,1024]{2,1,0:T(8,128)(2,1)S(1)} %constant_dynamic-update-slice_fusion.6.refs_1_), channel_id=1, source_target_pairs={{0,1},{1,0},{2,3},{3,2},{4,5},{5,4},{6,7},{7,6},{8,9},{9,8},{10,11... | collective-permute-start | bytes 589832 | tf_op jit(solution)/shard_map/ppermute | solution.py:433
  120.8 6.0 %collective-permute-start.33 = (bf16[4,32,1024]{2,1,0:T(8,128)(2,1)S(1)}, bf16[4,32,1024]{2,1,0:T(8,128)(2,1)S(1)}, u32[]{:S(2)}, u32[]{:S(2)}) collective-permute-start(bf16[4,32,1024]{2,1,0:T(8,128)(2,1)S(1)} %collective-permute-done.30.refs_4_), channel_id=1, source_target_pairs={{0,1},{1,0},{2,3},{3,2},{4,5},{5,4},{6,7},{7,6},{8,9},{9,8},{10,11... | collective-permute-start | bytes 786440 | tf_op jit(solution)/shard_map/ppermute | solution.py:433
  162.7 5.4 %collective-permute-start.36 = (bf16[48,256]{1,0:T(8,128)(2,1)S(1)}, bf16[48,256]{1,0:T(8,128)(2,1)S(1)}, u32[]{:S(2)}, u32[]{:S(2)}) collective-permute-start(bf16[48,256]{1,0:T(8,128)(2,1)S(1)} %add_convert_fusion), channel_id=1, source_target_pairs={{0,2},{1,3},{2,0},{3,1},{4,6},{5,7},{6,4},{7,5},{8,10},{9,11},{10,... | collective-permute-start | bytes 73736 | tf_op jit(solution)/shard_map/ppermute | solution.py:433
  169.1 17.6 %all-to-all-start.1 = ((bf16[32,48,256]{2,1,0:T(8,128)(2,1)}), bf16[32,48,256]{2,1,0:T(8,128)(2,1)S(1)}, u32[]{:S(2)}, u32[]{:S(2)}) async-start(bf16[32,48,256]{2,1,0:T(8,128)(2,1)} %broadcast_in_dim.10), calls=%async_computation.1 | async-start | bytes 1572864 | tf_op jit(solution)/shard_map/all_to_all | solution.py:461
  (20 other events, 200.5 us)
Sparse Core Ops, SparseCore 0:
  10.3 40.0 all-gather.2
